TPU v7x, 32 devices: a whole 2x2x4 slice. The times are simulated.
32 devices in a mesh: groups: 2 (over x), section: 8 (over z, y), tensor: 2 (over core).
Axes of the slice: x: 2, y: 2, z: 4, core: 2. Of those that a mesh axis runs over, the one named last changes fastest.
Arguments:
- text_rows: bfloat16 [4096, 8192], P(('groups', 'section'), 'tensor'), parts along dimension 0, may hold values from -6 to 6
- vis_rows: bfloat16 [1024, 8192], P(('groups', 'section'), 'tensor'), parts along dimension 0, may hold values from -6 to 6
- img_route: int32 [1024, 1], P('groups'), parts along dimension 0, may hold values from 0 to 7; in each aligned block of 64 rows (0 to 63, 64 to 127, ...) at most 16 rows name the same one
- norm_gain: float32 [8192], replicated, may hold values from 0.1 to 1.9
- w_key: bfloat16 [8192, 512], P(None, 'tensor'), may hold values from -0.0625 to 0.0625
- w_value: bfloat16 [8192, 512], P(None, 'tensor'), may hold values from -0.0625 to 0.0625
- page_count: int32 [16], P('groups'), parts along dimension 0, may hold values from 1 to 32, 128 in all
- tail_len: int32 [16], P('groups'), parts along dimension 0, may hold values from 1 to 16
- page_dest: int32 [256, 1], P('groups'), parts along dimension 0, may hold values from 0 to 7; in each aligned block of 16 rows (0 to 15, 16 to 31, ...) at most 2 rows name the same one
- dec_req: int32 [16], P('groups'), parts along dimension 0, may hold values from 0 to 7, each once
- dec_query: bfloat16 [16, 4, 4096], P(('groups', 'section'), None, 'tensor'), parts along dimension 0, may hold values from -90 to 90
- dec_key: bfloat16 [16, 4, 512], P(('groups', 'section'), None, 'tensor'), parts along dimension 0, may hold values from -3.1 to 3.1
- dec_value: bfloat16 [16, 4, 512], P(('groups', 'section'), None, 'tensor'), parts along dimension 0, may hold values from -6 to 6
Outputs:
- attended: bfloat16 [16, 4, 4096], P(('groups', 'section'), None, 'tensor'), parts along dimension 0
- cache_key: bfloat16 [256, 16, 512], P(('groups', 'section'), None, 'tensor'), parts along dimension 0
- cache_value: bfloat16 [256, 16, 512], P(('groups', 'section'), None, 'tensor'), parts along dimension 0
There are 2 independent parts, one for each index of `groups`. A program takes and returns all parts, laid end to end along the dimension named above; an argument that names none is the same for every part. Nothing has to cross between parts.
Inputs may be any that keep to these rules, and one draw needn't show every extreme that they name: `img_route`: of the rows of one encoder device (aligned blocks of 64 rows) at most 16 go to one prefill device. `page_count`: they sum to 128. `page_dest`: of the pages of one prefill device (aligned blocks of 16 pages) at most 2 go to one decode device. `dec_req`: each request is served by exactly one slot.
All inputs are finite; a program needn't handle non-finite values.
Results may differ from a plain program's by a relative error of at most 0.0061.
Values may be sent and summed in bfloat16 or wider, within the bound.
No kernel may reach another device: no remote copies, remote signals or barrier semaphores. Data moves between devices by JAX's collectives and lax.ppermute only.
A program may use at most 128 MiB of HBM per device.

v0:
```python
import jax
import jax.numpy as jnp
from jax import lax
from jax.sharding import PartitionSpec as P

HD = 128
PAGE = 16


lowest_score = -1e30
norm_epsilon = 1e-06


def joined(part, axis, combine):
    gathered = jax.tree.map(lambda a: lax.all_gather(a, axis), part)

    def take(source):
        return jax.tree.map(lambda a: lax.dynamic_index_in_dim(a, source, 0, False), gathered)

    return lax.fori_loop(
        1, lax.axis_size(axis), lambda source, state: combine(state, take(source)), take(0)
    )


def prior_rank(marked, axis_number):
    earlier = jnp.cumsum(marked, axis=axis_number) - marked
    return jnp.sum(earlier * marked, axis=-1)


def partial_combine(first_part, second_part):
    num_a, top_a, total_a = first_part
    num_b, top_b, total_b = second_part
    highest = jnp.maximum(top_a, top_b)
    scale_a = jnp.exp(top_a - highest)
    scale_b = jnp.exp(top_b - highest)
    head_width = num_a.shape[-1] // top_a.shape[-1]
    shaped_a = num_a.reshape(top_a.shape + (head_width,))
    shaped_b = num_b.reshape(top_b.shape + (head_width,))
    merged = shaped_a * scale_a[..., None] + shaped_b * scale_b[..., None]
    return (merged.reshape(num_a.shape), highest, total_a * scale_a + total_b * scale_b)


def prompt_partials(
    all_queries, key_pages, value_pages, global_page, present, page_count, tail_len, dec_req
):
    page_total, page_len, kv_width = key_pages.shape
    starts = jnp.cumsum(page_count) - page_count
    request_of = jnp.sum((starts[None, :] <= global_page[:, None]).astype(jnp.int32), axis=1) - 1
    prompt_length = (page_count - 1) * PAGE + tail_len
    inner_page = global_page - starts[request_of]
    token_place = inner_page[:, None] * PAGE + jnp.arange(PAGE, dtype=jnp.int32)[None, :]
    token_usable = present[:, None] & (token_place < prompt_length[request_of][:, None])
    request_count = page_count.shape[0]
    request_index = jnp.arange(request_count, dtype=jnp.int32)
    slot_of = jnp.sum(
        jnp.where(dec_req[None, :] == request_index[:, None], request_index[None, :], 0), axis=1
    )
    page_slot = slot_of[request_of]
    step_count, query_width = (all_queries.shape[1], all_queries.shape[2])
    head_count = query_width // HD
    kv_heads = kv_width // HD
    head_group = head_count // kv_heads
    score_scale = HD ** (-0.5)
    page_query = all_queries[page_slot].reshape(page_total, step_count, kv_heads, head_group, HD)
    page_keys = key_pages.reshape(page_total, PAGE, kv_heads, HD)
    page_values = value_pages.reshape(page_total, PAGE, kv_heads, HD)
    scores = (
        jnp.einsum("nsghd,njgd->nsghj", page_query, page_keys, preferred_element_type=jnp.float32)
        * score_scale
    )
    usable = token_usable[:, None, None, None, :]
    masked = jnp.where(usable, scores, lowest_score)
    page_top = jnp.max(masked, axis=-1)
    slot_match = (page_slot[None, :] == request_index[:, None]) & present[None, :]
    slot_top = jnp.max(
        jnp.where(slot_match[:, :, None, None, None], page_top[None], lowest_score), axis=1
    )
    weights = jnp.where(usable, jnp.exp(masked - slot_top[page_slot][..., None]), 0.0)
    page_total_weight = jnp.sum(weights, axis=-1)
    page_numerator = jnp.einsum(
        "nsghj,njgd->nsghd",
        weights.astype(jnp.bfloat16),
        page_values,
        preferred_element_type=jnp.float32,
    )
    match_float = slot_match.astype(jnp.float32)
    slot_numerator = jnp.dot(
        match_float,
        page_numerator.reshape(page_total, -1),
        precision=lax.Precision.HIGHEST,
        preferred_element_type=jnp.float32,
    ).reshape(request_count, step_count, query_width)
    slot_total = jnp.dot(
        match_float,
        page_total_weight.reshape(page_total, -1),
        precision=lax.Precision.HIGHEST,
        preferred_element_type=jnp.float32,
    ).reshape(request_count, step_count, head_count)
    slot_maxima = slot_top.reshape(request_count, step_count, head_count)
    return (slot_numerator, slot_maxima, slot_total)


def body(
    text_rows,
    vis_rows,
    img_route,
    norm_gain,
    w_key,
    w_value,
    page_count,
    tail_len,
    page_dest,
    dec_req,
    dec_query,
    dec_key,
    dec_value,
):
    sections = lax.axis_size("section")
    position = lax.axis_index("section")
    tok_rows, half_width = text_rows.shape
    img_rows = vis_rows.shape[0]
    img_cap = max(2, (2 * img_rows + sections - 1) // sections)
    station = jnp.arange(sections, dtype=jnp.int32)
    targets = img_route[:, 0]
    grouped_marks = (
        (targets[:, None] == station[None, :])
        .astype(jnp.int32)
        .reshape(sections, img_rows, sections)
    )
    row_rank = prior_rank(grouped_marks, 1)
    own_targets = lax.dynamic_index_in_dim(
        targets.reshape(sections, img_rows), position, 0, keepdims=False
    )
    own_rank = lax.dynamic_index_in_dim(row_rank, position, 0, keepdims=False)
    send_slot = own_targets * img_cap + own_rank
    outgoing = jnp.zeros((sections * img_cap, half_width), jnp.bfloat16).at[send_slot].set(vis_rows)
    incoming = lax.all_to_all(outgoing, "section", split_axis=0, concat_axis=0, tiled=True)
    per_source = jnp.sum(grouped_marks, axis=1)
    arriving = lax.dynamic_index_in_dim(per_source, position, 1, keepdims=False)
    offsets = jnp.cumsum(arriving) - arriving
    columns = jnp.arange(img_cap, dtype=jnp.int32)
    places = jnp.where(
        columns[None, :] < arriving[:, None], offsets[:, None] + columns[None, :], tok_rows
    )
    hidden = text_rows.at[places.reshape(-1)].set(incoming, mode="drop")
    full_rows = lax.all_gather(hidden, "tensor", axis=1, tiled=True)
    widened = full_rows.astype(jnp.float32)
    mean_square = jnp.mean(widened * widened, axis=1, keepdims=True)
    normed = (widened * lax.rsqrt(mean_square + norm_epsilon) * norm_gain[None, :]).astype(
        jnp.bfloat16
    )
    keys_local = jnp.dot(normed, w_key, preferred_element_type=jnp.float32).astype(jnp.bfloat16)
    values_local = jnp.dot(normed, w_value, preferred_element_type=jnp.float32).astype(jnp.bfloat16)
    blocks = tok_rows // PAGE
    page_cap = max(1, (blocks + sections - 1) // sections)
    kv_width = keys_local.shape[1]
    holders = page_dest[:, 0].reshape(sections, blocks)
    holder_marks = (holders[:, :, None] == station[None, None, :]).astype(jnp.int32)
    holder_rank = prior_rank(holder_marks, 1)
    own_holders = lax.dynamic_index_in_dim(holders, position, 0, keepdims=False)
    own_page_rank = lax.dynamic_index_in_dim(holder_rank, position, 0, keepdims=False)
    send_page = own_holders * page_cap + own_page_rank
    key_pages_local = keys_local.reshape(blocks, PAGE, kv_width)
    value_pages_local = values_local.reshape(blocks, PAGE, kv_width)
    key_out = (
        jnp.zeros((sections * page_cap, PAGE, kv_width), jnp.bfloat16)
        .at[send_page]
        .set(key_pages_local)
    )
    value_out = (
        jnp.zeros((sections * page_cap, PAGE, kv_width), jnp.bfloat16)
        .at[send_page]
        .set(value_pages_local)
    )
    cache_key, cache_value = (
        lax.all_to_all(key_out, "section", split_axis=0, concat_axis=0, tiled=True),
        lax.all_to_all(value_out, "section", split_axis=0, concat_axis=0, tiled=True),
    )
    all_queries = lax.all_gather(dec_query, "section", axis=0, tiled=True)
    batch_rows, step_count, query_width = dec_query.shape
    head_count = query_width // HD
    kv_heads = kv_width // HD
    head_group = head_count // kv_heads
    score_scale = HD ** (-0.5)
    own_query = dec_query.reshape(batch_rows, step_count, kv_heads, head_group, HD)
    new_keys = dec_key.reshape(batch_rows, step_count, kv_heads, HD)
    new_values = dec_value.reshape(batch_rows, step_count, kv_heads, HD)
    fresh_scores = (
        jnp.einsum("bsghd,btgd->bsght", own_query, new_keys, preferred_element_type=jnp.float32)
        * score_scale
    )
    causal = (jnp.arange(step_count)[None, :] <= jnp.arange(step_count)[:, None])[
        None, :, None, None, :
    ]
    fresh_scores = jnp.where(causal, fresh_scores, lowest_score)
    fresh_top = jnp.max(fresh_scores, axis=-1)
    fresh_weights = jnp.where(causal, jnp.exp(fresh_scores - fresh_top[..., None]), 0.0)
    fresh_total = jnp.sum(fresh_weights, axis=-1)
    fresh_numerator = jnp.einsum(
        "bsght,btgd->bsghd",
        fresh_weights.astype(jnp.bfloat16),
        new_values,
        preferred_element_type=jnp.float32,
    )
    own_part = (
        fresh_numerator.reshape(batch_rows, step_count, query_width),
        fresh_top.reshape(batch_rows, step_count, head_count),
        fresh_total.reshape(batch_rows, step_count, head_count),
    )
    slot_index = jnp.arange(page_cap, dtype=jnp.int32)
    block_index = jnp.arange(blocks, dtype=jnp.int32)
    matched = (holders[:, None, :] == position) & (
        holder_rank[:, None, :] == slot_index[None, :, None]
    )
    present = jnp.any(matched, axis=2).reshape(-1)
    local_page = jnp.sum(jnp.where(matched, block_index[None, None, :], 0), axis=2)
    global_page = (station[:, None] * blocks + local_page).reshape(-1)
    slot_sums = prompt_partials(
        all_queries, cache_key, cache_value, global_page, present, page_count, tail_len, dec_req
    )
    merged = joined(slot_sums, "section", partial_combine)
    prompt_part = tuple(
        (
            lax.dynamic_slice_in_dim(member, position * batch_rows, batch_rows, 0)
            for member in merged
        )
    )
    total_numerator, total_top, total_weight = partial_combine(prompt_part, own_part)
    attended = (
        (total_numerator.reshape(batch_rows, step_count, head_count, HD) / total_weight[..., None])
        .reshape(batch_rows, step_count, query_width)
        .astype(jnp.bfloat16)
    )
    return (attended, cache_key, cache_value)


def solution(mesh):
    return jax.shard_map(
        body,
        mesh=mesh,
        in_specs=(
            P(("groups", "section"), "tensor"),
            P(("groups", "section"), "tensor"),
            P("groups", None),
            P(),
            P(None, "tensor"),
            P(None, "tensor"),
            P("groups"),
            P("groups"),
            P("groups", None),
            P("groups"),
            P(("groups", "section"), None, "tensor"),
            P(("groups", "section"), None, "tensor"),
            P(("groups", "section"), None, "tensor"),
        ),
        out_specs=(
            P(("groups", "section"), None, "tensor"),
            P(("groups", "section"), None, "tensor"),
            P(("groups", "section"), None, "tensor"),
        ),
        check_vma=False,
    )
```

profile of v0, /device:TPU:0, one launch (start us, length us, event | category | flops | bytes accessed | tf_op | source)
XLA Modules:
  0.0 210.1 jit_solution(13012472607995762242)
XLA Ops:
  7.2 0.5 broadcast.384
  7.7 0.3 copy-done.5
  8.0 0.7 reduce.16
  8.9 1.4 fusion.82
  10.4 2.9 %scatter_custom_fusion = bf16[128,4096]{1,0:T(8,128)(2,1)} fusion(s32[64]{0:T(128)S(1)} %fusion.72, bf16[64,4096]{1,0:T(8,128)(2,1)} %param.16, bf16[]{:T(256)} %constant.121.clone.1), kind=kCustom, calls=%fused_computation.48 | custom fusion | bytes 1049088 | tf_op jit(solution)/shard_map/scatter | solution.py:136
  13.4 7.3 %all-to-all-start = ((bf16[8,16,4096]{2,1,0:T(8,128)(2,1)}), bf16[8,16,4096]{2,1,0:T(8,128)(2,1)S(1)}, u32[]{:S(2)}, u32[]{:S(2)}) async-start(bf16[8,16,4096]{2,1,0:T(8,128)(2,1)} %bitcast.141), calls=%async_computation | async-start | bytes 2097152 | tf_op jit(solution)/shard_map/all_to_all | solution.py:137
  21.3 25.1 %all-to-all-done = bf16[8,16,4096]{2,1,0:T(8,128)(2,1)S(1)} async-done(((bf16[8,16,4096]{2,1,0:T(8,128)(2,1)}), bf16[8,16,4096]{2,1,0:T(8,128)(2,1)S(1)}, u32[]{:S(2)}, u32[]{:S(2)}) %all-to-all-start) | async-done | bytes 1048608 | tf_op jit(solution)/shard_map/all_to_all | solution.py:137
  46.4 3.1 %scatter_fusion = bf16[256,4096]{1,0:T(8,128)(2,1)S(1)} fusion(bf16[256,4096]{1,0:T(8,128)(2,1)S(1)} %copy-done.2, s32[128]{0:T(128)S(1)} %fusion.71, bf16[128,4096]{1,0:T(8,128)(2,1)S(1)} %bitcast.140), kind=kCustom, calls=%fused_computation.6 | custom fusion | bytes 3146240 | tf_op jit(solution)/shard_map/scatter | solution.py:145
  49.6 1.3 copy-done.1
  50.9 0.7 reduce.15
  51.8 0.4 fusion.81
  52.9 0.7 gather_fusion.1
  53.6 0.7 gather_fusion.2
  54.7 0.7 gather_fusion
  55.4 30.7 %all_gather.16 = bf16[8,4,2048]{2,1,0:T(4,128)(2,1)S(1)} all-gather(bf16[1,4,2048]{2,1,0:T(4,128)(2,1)S(1)} %copy-done.4), channel_id=1, replica_groups=mesh['groups'=2,'section'=8,'tensor'=2] {'section'}, dimensions={0}, use_global_device_ids=true | all-gather | bytes 147456 | tf_op jit(solution)/shard_map/all_gather | solution.py:179
  86.0 0.8 gather_fusion.3
  87.3 3.3 %fusion.5 = f32[256]{0:T(256)S(1)} fusion(bf16[256,8192]{1,0:T(8,128)(2,1)} %all-gather.5.cloned.1.call-done), kind=kLoop, calls=%fused_computation.24 | loop fusion | flops 6291200 | bytes 4195328 | tf_op jit(solution)/shard_map/reduce_sum | solution.py:148
  90.7 3.5 %fusion.17 = bf16[256,256]{1,0:T(8,128)(2,1)S(1)} fusion(bf16[8192,256]{1,0:T(8,128)(2,1)} %param.19, bf16[256,8192]{1,0:T(8,128)(2,1)S(1)} %copy-done.3, f32[8192]{0:T(1024)S(1)} %copy-done.8, f32[256]{0:T(256)S(1)} %add_rsqrt_fusion), kind=kOutput, calls=%fused_computation.34 | convolution fusion | flops 1082195968 | bytes 8553472 | tf_op jit(solution)/shard_map/dot_general | solution.py:152
  94.2 0.7 broadcast.340.clone
  94.9 2.2 %scatter_fusion.2 = bf16[16,16,256]{2,1,0:T(8,128)(2,1)} fusion(bf16[16,16,256]{2,1,0:T(8,128)(2,1)} %broadcast.340.clone, s32[16]{0:T(128)S(1)} %fusion.70, bf16[16,16,256]{2,1,0:T(8,128)(2,1)S(1)} %bitcast.148), kind=kCustom, calls=%fused_computation.8 | custom fusion | bytes 393280 | tf_op jit(solution)/shard_map/scatter | solution.py:168
  97.1 3.5 %all-to-all-start.2 = ((bf16[16,16,256]{2,1,0:T(8,128)(2,1)}), bf16[16,16,256]{2,1,0:T(8,128)(2,1)S(1)}, u32[]{:S(2)}, u32[]{:S(2)}) async-start(bf16[16,16,256]{2,1,0:T(8,128)(2,1)} %scatter_fusion.2), calls=%async_computation.2 | async-start | bytes 262144 | tf_op jit(solution)/shard_map/all_to_all | solution.py:176
  100.6 4.8 %fusion.14 = bf16[256,256]{1,0:T(8,128)(2,1)S(1)} fusion(bf16[8192,256]{1,0:T(8,128)(2,1)} %param.20, bf16[256,8192]{1,0:T(8,128)(2,1)} %all-gather.5.cloned.1.call-done, f32[8192]{0:T(1024)S(1)} %copy-done.8, f32[256]{0:T(256)S(1)} %add_rsqrt_fusion), kind=kOutput, calls=%fused_computation.33 | convolution fusion | flops 1082195968 | bytes 8553472 | tf_op jit(solution)/shard_map/dot_general | solution.py:153
  105.4 0.7 broadcast.340.clone.1
  106.1 2.2 %scatter_fusion.1 = bf16[16,16,256]{2,1,0:T(8,128)(2,1)} fusion(bf16[16,16,256]{2,1,0:T(8,128)(2,1)} %broadcast.340.clone.1, s32[16]{0:T(128)S(1)} %fusion.70, bf16[16,16,256]{2,1,0:T(8,128)(2,1)S(1)} %bitcast.147), kind=kCustom, calls=%fused_computation.7 | custom fusion | bytes 393280 | tf_op jit(solution)/shard_map/scatter | solution.py:173
  108.3 6.0 %all-to-all-start.1 = ((bf16[16,16,256]{2,1,0:T(8,128)(2,1)}), bf16[16,16,256]{2,1,0:T(8,128)(2,1)S(1)}, u32[]{:S(2)}, u32[]{:S(2)}) async-start(bf16[16,16,256]{2,1,0:T(8,128)(2,1)} %scatter_fusion.1), calls=%async_computation.1 | async-start | bytes 262144 | tf_op jit(solution)/shard_map/all_to_all | solution.py:177
  114.4 0.4 fusion.83
  115.0 0.6 gather_fusion.4
  115.6 6.0 %all-to-all-done.1 = bf16[16,16,256]{2,1,0:T(8,128)(2,1)S(1)} async-done(((bf16[16,16,256]{2,1,0:T(8,128)(2,1)}), bf16[16,16,256]{2,1,0:T(8,128)(2,1)S(1)}, u32[]{:S(2)}, u32[]{:S(2)}) %all-to-all-start.1) | async-done | bytes 131104 | tf_op jit(solution)/shard_map/all_to_all | solution.py:177
  121.7 0.3 convolution_bitcast_fusion
  122.0 0.3 copy.201
  122.4 1.0 fusion.24
  124.3 0.5 fusion.29
  125.0 31.0 %all-gather.1 = f32[64,4,16]{2,0,1:T(8,128)S(1)} all-gather(f32[8,4,16]{2,0,1:T(8,128)S(1)} %fusion.41), channel_id=3, replica_groups=mesh['groups'=2,'section'=8,'tensor'=2] {'section'}, dimensions={0}, use_global_device_ids=true | all-gather | bytes 18432 | tf_op jit(solution)/shard_map/all_gather | solution.py:15
  156.1 30.8 %all_gather.18 = f32[8,8,4,16]{3,1,2,0:T(8,128)S(1)} all-gather(f32[1,8,4,16]{3,1,2,0:T(8,128)S(1)} %copy.155), channel_id=1, replica_groups=mesh['groups'=2,'section'=8,'tensor'=2] {'section'}, dimensions={0}, use_global_device_ids=true | all-gather | bytes 18432 | tf_op jit(solution)/shard_map/all_gather | solution.py:15
  186.9 1.0 slice.15
  188.0 12.8 %while.19 = (s32[]{:T(128)}, f32[8,4,2048]{2,1,0:T(4,128)S(1)}, f32[8,4,16]{2,1,0:T(4,128)S(1)}, f32[8,4,16]{2,1,0:T(4,128)S(1)}, f32[8,8,4,16]{3,1,2,0:T(8,128)...) while((s32[]{:T(128)}, f32[8,4,2048]{2,1,0:T(4,128)S(1)}, ...), condition=%wide.region_20.21_spmd, body=%wide.region_19.20_spmd.sunk | while | flops 199685 | bytes 3436699 | solution.py:20
  188.6 1.0 constant_dynamic-slice_fusion.10
  189.6 0.3 fusion.89
  190.4 1.0 constant_dynamic-slice_fusion.10
  191.4 0.3 fusion.89
  192.2 1.0 constant_dynamic-slice_fusion.10
  194.1 1.0 constant_dynamic-slice_fusion.10
  195.9 1.0 constant_dynamic-slice_fusion.10
  197.7 1.0 constant_dynamic-slice_fusion.10
  199.6 1.0 constant_dynamic-slice_fusion.10
  201.3 0.6 copy.146
  202.0 0.7 copy.226
  202.6 0.7 copy.227
  (151 shorter events, 10.2 us)
Async XLA Ops:
  7.2 116.8 %copy-start = (bf16[1,4,256]{2,1,0:T(4,128)(2,1)S(1)}, bf16[1,4,256]{2,1,0:T(4,128)(2,1)}, u32[]{:S(2)}) copy-start(bf16[1,4,256]{2,1,0:T(4,128)(2,1)} %param.27) | copy-start | bytes 6148
  7.2 39.2 %copy-start.2 = (bf16[256,4096]{1,0:T(8,128)(2,1)S(1)}, bf16[256,4096]{1,0:T(8,128)(2,1)}, u32[]{:S(2)}) copy-start(bf16[256,4096]{1,0:T(8,128)(2,1)} %param.15) | copy-start | bytes 6291460
  7.2 0.8 copy-start.5
  13.4 33.0 %all-to-all-start = ((bf16[8,16,4096]{2,1,0:T(8,128)(2,1)}), bf16[8,16,4096]{2,1,0:T(8,128)(2,1)S(1)}, u32[]{:S(2)}, u32[]{:S(2)}) async-start(bf16[8,16,4096]{2,1,0:T(8,128)(2,1)} %bitcast.141), calls=%async_computation | async-start | bytes 2097152 | tf_op jit(solution)/shard_map/all_to_all | solution.py:137
  20.6 66.7 %all-gather.5.cloned.1.call-start = ((), (), s32[]{:S(2)}) async-start(), calls=%async_computation.3 | async-start | bytes 6291456 | tf_op jit(solution)/shard_map/all_gather | solution.py:146
  46.4 4.5 %copy-start.10 = (s32[128,1]{0,1:T(1,128)S(1)}, s32[128,1]{0,1:T(1,128)}, u32[]{:S(2)}) copy-start(s32[128,1]{0,1:T(1,128)} %param.23) | copy-start | bytes 1540
  46.4 6.2 %copy-start.7 = (s32[8]{0:T(128)S(1)}, s32[8]{0:T(128)}, u32[]{:S(2)}) copy-start(s32[8]{0:T(128)} %param.21) | copy-start | bytes 100
  46.4 6.4 %copy-start.6 = (s32[8]{0:T(128)S(1)}, s32[8]{0:T(128)}, u32[]{:S(2)}) copy-start(s32[8]{0:T(128)} %param.22) | copy-start | bytes 100
  46.4 8.2 %copy-start.11 = (s32[8]{0:T(128)S(1)}, s32[8]{0:T(128)}, u32[]{:S(2)}) copy-start(s32[8]{0:T(128)} %param.24) | copy-start | bytes 100
  46.4 8.9 %copy-start.4 = (bf16[1,4,2048]{2,1,0:T(4,128)(2,1)S(1)}, bf16[1,4,2048]{2,1,0:T(4,128)(2,1)}, u32[]{:S(2)}) copy-start(bf16[1,4,2048]{2,1,0:T(4,128)(2,1)} %param.25) | copy-start | bytes 49156
  49.6 1.3 copy-start.1
  49.6 41.0 %copy-start.8 = (f32[8192]{0:T(1024)S(1)}, f32[8192]{0:T(1024)}, u32[]{:S(2)}) copy-start(f32[8192]{0:T(1024)} %param.18) | copy-start | bytes 98308
  87.3 3.5 %copy-start.3 = (bf16[256,8192]{1,0:T(8,128)(2,1)S(1)}, bf16[256,8192]{1,0:T(8,128)(2,1)}, u32[]{:S(2)}) copy-start(bf16[256,8192]{1,0:T(8,128)(2,1)} %all-gather.5.cloned.1.call-done) | copy-start | bytes 12582916
  97.1 11.2 %all-to-all-start.2 = ((bf16[16,16,256]{2,1,0:T(8,128)(2,1)}), bf16[16,16,256]{2,1,0:T(8,128)(2,1)S(1)}, u32[]{:S(2)}, u32[]{:S(2)}) async-start(bf16[16,16,256]{2,1,0:T(8,128)(2,1)} %scatter_fusion.2), calls=%async_computation.2 | async-start | bytes 262144 | tf_op jit(solution)/shard_map/all_to_all | solution.py:176
  105.4 18.0 %copy-start.9 = (bf16[1,4,256]{2,1,0:T(4,128)(2,1)S(1)}, bf16[1,4,256]{2,1,0:T(4,128)(2,1)}, u32[]{:S(2)}) copy-start(bf16[1,4,256]{2,1,0:T(4,128)(2,1)} %param.26) | copy-start | bytes 6148
  108.3 13.3 %all-to-all-start.1 = ((bf16[16,16,256]{2,1,0:T(8,128)(2,1)}), bf16[16,16,256]{2,1,0:T(8,128)(2,1)S(1)}, u32[]{:S(2)}, u32[]{:S(2)}) async-start(bf16[16,16,256]{2,1,0:T(8,128)(2,1)} %scatter_fusion.1), calls=%async_computation.1 | async-start | bytes 262144 | tf_op jit(solution)/shard_map/all_to_all | solution.py:177
  114.3 72.6 %all-gather.7.cloned.1.call-start = ((), (), s32[]{:S(2)}) async-start(), calls=%async_computation.4 | async-start | bytes 2359296 | tf_op jit(solution)/shard_map/all_gather | solution.py:15
Sparse Core Ops, SparseCore 0:
  51.1 12.6 all-gather.4
  123.5 48.4 all-gather.6
where the time goes:
time: 211 us; the launch traced here: 210 us
  blocking collectives  92.4 us (44%)
  local copies, waits for them, and re-layouts  32.9 us (16%)
  waiting for transfers between devices  31.2 us (15%)
  starting transfers between devices  16.8 us (8%)
  between operations  14.4 us (7%)
  other arithmetic  11.2 us (5%)
  matrix products  10.7 us (5%)
    all_gather x2, blocking collectives, joined(): gathered = jax.tree.map(lambda a: lax.all_gather(a, axis), part)  61.8 us
    all_gather x1, blocking collectives, body(): all_queries = lax.all_gather(dec_query, 'section', axis=0, tiled=True)  30.7 us
    all_to_all x1, waiting for transfers between devices, body(): lax.all_to_all(outgoing, 'section', split_axis=0, concat_axis=0, tiled=True)  25.1 us
    dynamic_slice x23, local copies, waits for them, and re-layouts, take(): lax.dynamic_index_in_dim(a, source, 0, False)  7.94 us
    all_to_all x1, starting transfers between devices, body(): lax.all_to_all(outgoing, 'section', split_axis=0, concat_axis=0, tiled=True)  7.28 us
    all_to_all x1, waiting for transfers between devices, body(): lax.all_to_all(value_out, 'section', split_axis=0, concat_axis=0, tiled=T...  6 us
    all_to_all x1, starting transfers between devices, body(): lax.all_to_all(value_out, 'section', split_axis=0, concat_axis=0, tiled=T...  5.99 us
    dot_general x1, matrix products, body(): jnp.dot(normed, w_value, preferred_element_type=jnp.float32)  4.78 us
  transfers between devices with their start and end apart: 5, of which 2 were waited for; matrix products, arithmetic and copies ran while one was open for 8% of the time, Pallas kernels for 0%

commit v1 on v0

v1 whole, which is shorter than its diff:
```python
import jax
import jax.numpy as jnp
from jax import lax
from jax.experimental import pallas as pl
from jax.experimental.pallas import tpu as pltpu
from jax.sharding import PartitionSpec as P

HD = 128
PAGE = 16
LOWEST = -1e30
EPS = 1e-06
STAT = 8
F32 = jnp.float32
BF16 = jnp.bfloat16
I32 = jnp.int32

VM = pl.BlockSpec(memory_space=pltpu.VMEM)
SM = pl.BlockSpec(memory_space=pltpu.SMEM)
MIB = 1 << 20


def call(kernel, out_shape, in_specs, out_specs, scratch=(), limit=16, flops=0, traffic=0):
    return pl.pallas_call(
        kernel,
        out_shape=out_shape,
        in_specs=in_specs,
        out_specs=out_specs,
        scratch_shapes=list(scratch),
        compiler_params=pltpu.CompilerParams(vmem_limit_bytes=limit * MIB),
        cost_estimate=pl.CostEstimate(flops=flops, bytes_accessed=traffic, transcendentals=0),
    )


def dot(a, b):
    return jnp.dot(a, b, preferred_element_type=F32)


def dot_t(a, b):
    return lax.dot_general(a, b, (((1,), (1,)), ((), ())), preferred_element_type=F32)


def diagonal(shape):
    return lax.broadcasted_iota(I32, shape, 0) == lax.broadcasted_iota(I32, shape, 1)


def column_to_row(column):
    rows = column.shape[0]
    return jnp.sum(jnp.where(diagonal((rows, rows)), column, 0.0), axis=0, keepdims=True)


def row_to_column(row):
    lanes = row.shape[1]
    return jnp.sum(jnp.where(diagonal((lanes, lanes)), row, 0.0), axis=1, keepdims=True)


def put_partial(out, kv_heads, numerators, tops, totals):
    rows = numerators[0].shape[0]
    for g in range(kv_heads):
        out[g * rows : (g + 1) * rows, :] = numerators[g]
    stats = column_to_row(jnp.concatenate(list(tops) + list(totals), axis=0))
    out[kv_heads * rows :, :] = jnp.broadcast_to(stats, (STAT, stats.shape[1]))


def meta_kernel(sizes, route, pages, count, tail, req, query, key, value, info, slots, fresh, starts):
    n, img, tok, blocks, cap, page_cap, kv_heads, steps = sizes
    pos = lax.axis_index("section")
    own = route[pl.ds(pos, 1), :]
    table = route[...]
    stations = lax.broadcasted_iota(I32, (n, img), 0)
    marks = own == stations
    ones = jnp.where(marks, 1.0, 0.0).astype(BF16)
    earlier = lax.broadcasted_iota(I32, (img, img), 0) < lax.broadcasted_iota(I32, (img, img), 1)
    prefix = dot(ones, jnp.where(earlier, 1.0, 0.0).astype(BF16))
    before = jnp.zeros((n, 1), I32)
    for e in range(n):
        here = jnp.sum((table[e : e + 1, :] == stations).astype(I32), axis=1, keepdims=True)
        before = before + jnp.where(e < pos, here, 0)
    local = jnp.sum(jnp.where(marks, prefix, 0.0), axis=0, keepdims=True).astype(I32)
    rank = local + jnp.sum(jnp.where(marks, before, 0), axis=0, keepdims=True)
    send = jnp.bitwise_xor(own, pos) * cap + local
    place = own * tok + rank
    arriving = jnp.sum((table == pos).astype(I32), axis=1, keepdims=True)
    lanes = lax.broadcasted_iota(I32, (n, n * cap), 1)
    source = jnp.bitwise_xor(lanes // cap, pos)
    number = lax.broadcasted_iota(I32, (n, n * cap), 0)
    fits = jnp.sum(jnp.where(number == source, arriving, 0), axis=0, keepdims=True)
    offset = jnp.sum(jnp.where(number < source, arriving, 0), axis=0, keepdims=True)
    inner = lanes[:1] % cap
    target = jnp.where(inner < fits, offset + inner, -1)
    replaced = jnp.sum(arriving, axis=0, keepdims=True)
    total = jnp.int32(0)
    for r in range(n):
        starts[r] = total
        total = total + count[r]
    inside = lax.broadcasted_iota(I32, (1, tok), 1)
    text = inside + pos * tok
    text_slot = jnp.full((1, tok), -1, I32)
    vis_slot = jnp.full((1, img), -1, I32)
    for b in range(n):
        r = req[b]
        first = starts[r] * PAGE
        last = first + (count[r] - 1) * PAGE + tail[r]
        text_slot = jnp.where((text >= first) & (text < last), b, text_slot)
        vis_slot = jnp.where((place >= first) & (place < last), b, vis_slot)
    text_slot = jnp.where(inside < replaced, -1, text_slot)
    info[0:1, :img] = send
    info[1:2, :img] = vis_slot
    info[2:3, :tok] = text_slot
    info[3:4, : n * cap] = target
    for g in range(blocks):
        holder = pages[pos * blocks + g]
        slot = jnp.bitwise_xor(holder, pos) * page_cap
        for e in range(g):
            slot = slot + (pages[pos * blocks + e] == holder).astype(I32)
        slots[g] = slot
    rows = query.shape[0] // kv_heads
    row = lax.broadcasted_iota(I32, (rows, steps), 0)
    causal = lax.broadcasted_iota(I32, (rows, steps), 1) <= row % steps
    parts = ([], [], [])
    for g in range(kv_heads):
        cols = slice(g * HD, (g + 1) * HD)
        scores = dot_t(query[g * rows : (g + 1) * rows, :], key[:, cols]) * HD**-0.5
        scores = jnp.where(causal, scores, LOWEST)
        top = jnp.max(scores, axis=1, keepdims=True)
        weights = jnp.where(causal, jnp.exp(scores - top), 0.0)
        numerator = dot(weights.astype(BF16), value[:, cols])
        for held, new in zip(parts, (numerator, top, jnp.sum(weights, axis=1, keepdims=True))):
            held.append(new)
    put_partial(fresh, kv_heads, *parts)


def project_kernel(sizes, text, text_far, vis, vis_far, gain, w_key, w_value, info, kv_text, kv_vis, *rest):
    n, cap, step = sizes
    packed, (total, ) = rest[:-1], rest[-1:]
    tok, half = text.shape
    img = vis.shape[0]
    kvw = w_key.shape[1]
    me = lax.axis_index("tensor")
    squares = [jnp.zeros((tok, 1), F32), jnp.zeros((img, 1), F32)]
    for number, pair in enumerate(((text, text_far), (vis, vis_far))):
        for half_rows in pair:
            for c in range(0, half, step):
                wide = half_rows[:, c : c + step].astype(F32)
                squares[number] += jnp.sum(wide * wide, axis=1, keepdims=True)
    scales = [lax.rsqrt(s / (2.0 * half) + EPS) for s in squares]
    for side in range(2):
        text_side, vis_side = (text, vis) if side == 0 else (text_far, vis_far)
        base = (me if side == 0 else 1 - me) * half
        for c in range(0, half, step):
            columns = pl.ds(pl.multiple_of(base + c, step), step)
            scaled = gain[:, columns]
            wk = w_key[columns, :]
            wv = w_value[columns, :]
            for scale, rows, lo in ((scales[0], text_side, 0), (scales[1], vis_side, tok)):
                size = rows.shape[0]
                normed = (rows[:, c : c + step].astype(F32) * scale * scaled).astype(BF16)
                for w, at in ((wk, 0), (wv, kvw)):
                    part = dot(normed, w)
                    if side == 0 and c == 0:
                        total[lo : lo + size, at : at + kvw] = part
                    else:
                        total[lo : lo + size, at : at + kvw] += part
    kv_text[...] = total[:tok, :].astype(BF16)
    own = total[tok : tok + img, :].astype(BF16)
    kv_vis[...] = own
    slot = lax.broadcasted_iota(I32, (n * cap, img), 0)
    chosen = jnp.where(slot == info[0:1, :img], 1.0, 0.0).astype(BF16)
    outgoing = dot(chosen, own).astype(BF16)
    for k in range(n):
        packed[k][...] = outgoing[k * cap : (k + 1) * cap, :]


def attend_kernel(n, kv_heads, query, kv_text, kv_vis, info, *out):
    pos = lax.axis_index("section")
    tok, img = kv_text.shape[0], kv_vis.shape[0]
    kvw = kv_heads * HD
    rows = query.shape[1] // kv_heads
    number = lax.broadcasted_iota(I32, (n * rows, 1), 0) // rows
    slot = jnp.bitwise_xor(number, pos)
    text_ok = slot == info[2:3, :tok]
    vis_ok = slot == info[1:2, :img]
    parts = []
    for g in range(kv_heads):
        q = query[:, g * rows : (g + 1) * rows, :].reshape(n * rows, HD)
        cols = slice(g * HD, (g + 1) * HD)
        vcols = slice(kvw + g * HD, kvw + (g + 1) * HD)
        s_text = jnp.where(text_ok, dot_t(q, kv_text[:, cols]) * HD**-0.5, LOWEST)
        s_vis = jnp.where(vis_ok, dot_t(q, kv_vis[:, cols]) * HD**-0.5, LOWEST)
        top = jnp.maximum(jnp.max(s_text, axis=1, keepdims=True), jnp.max(s_vis, axis=1, keepdims=True))
        w_text = jnp.where(text_ok, jnp.exp(s_text - top), 0.0)
        w_vis = jnp.where(vis_ok, jnp.exp(s_vis - top), 0.0)
        total = jnp.sum(w_text, axis=1, keepdims=True) + jnp.sum(w_vis, axis=1, keepdims=True)
        numerator = dot(w_text.astype(BF16), kv_text[:, vcols]) + dot(w_vis.astype(BF16), kv_vis[:, vcols])
        parts.append((numerator, top, total))
    for k in range(n):
        at = slice(k * rows, (k + 1) * rows)
        put_partial(out[k], kv_heads, *zip(*[tuple(x[at] for x in p) for p in parts]))


def pack_kernel(n, cap, page_cap, slots, info, kv_text, *rest):
    pieces, out, (incoming, staged) = rest[:n], rest[n : 2 * n], rest[2 * n :]
    tok = kv_text.shape[0]
    blocks = tok // PAGE
    for k in range(n):
        incoming[k * cap : (k + 1) * cap, :] = pieces[k][...]
    reach = min(tok, n * cap)
    hit = lax.broadcasted_iota(I32, (reach, n * cap), 0) == info[3:4, : n * cap]
    hot = jnp.where(hit, 1.0, 0.0)
    covered = jnp.sum(hot, axis=1, keepdims=True) > 0.0
    placed = dot(hot.astype(BF16), incoming[...])
    mixed = jnp.where(covered, placed, kv_text[:reach, :].astype(F32)).astype(BF16)
    staged[...] = jnp.zeros(staged.shape, BF16)
    for g in range(blocks):
        if (g + 1) * PAGE <= reach:
            rows = mixed[g * PAGE : (g + 1) * PAGE, :]
        else:
            rows = kv_text[g * PAGE : (g + 1) * PAGE, :]
        staged[slots[g]] = rows
    for k in range(n):
        out[k][...] = staged[k * page_cap : (k + 1) * page_cap]


def store_kernel(n, page_cap, *refs):
    pieces, (keys, values) = refs[:n], refs[n:]
    pos = lax.axis_index("section")
    kvw = keys.shape[2]
    for k in range(n):
        at = pl.ds(jnp.bitwise_xor(pos, k) * page_cap, page_cap)
        keys[at] = pieces[k][:, :, :kvw]
        values[at] = pieces[k][:, :, kvw:]


def join_kernel(kv_heads, steps, *refs):
    pieces, attended = refs[:-1], refs[-1]
    rows = pieces[0].shape[0] - STAT
    stats = [row_to_column(p[rows : rows + 1, :]) for p in pieces]
    tops = [s[:rows] for s in stats]
    highest = tops[0]
    for t in tops[1:]:
        highest = jnp.maximum(highest, t)
    numerator = jnp.zeros((rows, HD), F32)
    total = jnp.zeros((rows, 1), F32)
    for piece, s, t in zip(pieces, stats, tops):
        scale = jnp.exp(t - highest)
        numerator = numerator + piece[:rows, :] * scale
        total = total + s[rows:] * scale
    result = (numerator / total).astype(BF16)
    for h in range(rows // steps):
        attended[0, :, h * HD : (h + 1) * HD] = result[h * steps : (h + 1) * steps, :]


def body(
    text_rows,
    vis_rows,
    img_route,
    norm_gain,
    w_key,
    w_value,
    page_count,
    tail_len,
    page_dest,
    dec_req,
    dec_query,
    dec_key,
    dec_value,
):
    n = lax.axis_size("section")
    tok, half = text_rows.shape
    img = vis_rows.shape[0]
    kvw = w_key.shape[1]
    kv_heads = kvw // HD
    _, steps, q_width = dec_query.shape
    heads = q_width // HD
    q_rows = heads * steps
    blocks = tok // PAGE
    cap = max(2, (2 * img + n - 1) // n)
    page_cap = max(1, (blocks + n - 1) // n)

    def across(array):
        return lax.ppermute(array, "tensor", [(0, 1), (1, 0)])

    def swap(array, k):
        return lax.ppermute(array, "section", [(i, i ^ k) for i in range(n)])

    vis_far = across(vis_rows)
    text_far = across(text_rows)
    query = dec_query.reshape(steps, heads, HD).transpose(1, 0, 2).reshape(1, q_rows, HD)
    queries = query
    k = 1
    while k < n:
        queries = jnp.concatenate([queries, swap(queries, k)], axis=0)
        k *= 2

    width = max(tok, n * cap)
    info, slots, fresh = call(
        lambda *refs: meta_kernel((n, img, tok, blocks, cap, page_cap, kv_heads, steps), *refs),
        (
            jax.ShapeDtypeStruct((8, width), I32),
            jax.ShapeDtypeStruct((blocks,), I32),
            jax.ShapeDtypeStruct((q_rows + STAT, HD), F32),
        ),
        [VM, SM, SM, SM, SM, VM, VM, VM],
        (VM, SM, VM),
        [pltpu.SMEM((n,), I32)],
    )(
        img_route.reshape(n, img),
        page_dest.reshape(n * blocks),
        page_count,
        tail_len,
        dec_req,
        query[0],
        dec_key[0],
        dec_value[0],
    )

    kv_text, kv_vis, *packed = call(
        lambda *refs: project_kernel((n, cap, min(1024, half)), *refs),
        (
            jax.ShapeDtypeStruct((tok, 2 * kvw), BF16),
            jax.ShapeDtypeStruct((img, 2 * kvw), BF16),
            *[jax.ShapeDtypeStruct((cap, 2 * kvw), BF16)] * n,
        ),
        [VM] * 8,
        (VM,) * (2 + n),
        [pltpu.VMEM((tok + img, 2 * kvw), F32)],
        limit=32,
        flops=2 * (tok + img) * 2 * half * 2 * kvw,
        traffic=2 * (tok + img) * 2 * half + 8 * half * kvw,
    )(text_rows, text_far, vis_rows, vis_far, norm_gain.reshape(1, 2 * half), w_key, w_value, info)

    arrived = [packed[0]] + [swap(packed[k], k) for k in range(1, n)]

    partials = call(
        lambda *refs: attend_kernel(n, kv_heads, *refs),
        (jax.ShapeDtypeStruct((q_rows + STAT, HD), F32),) * n,
        [VM] * 4,
        (VM,) * n,
        limit=24,
        flops=4 * n * q_rows * (tok + img) * HD,
        traffic=n * (q_rows + STAT) * HD * 4,
    )(queries, kv_text, kv_vis, info)
    shares = [partials[0]] + [swap(partials[k], k) for k in range(1, n)]

    sent = call(
        lambda *refs: pack_kernel(n, cap, page_cap, *refs),
        (jax.ShapeDtypeStruct((page_cap, PAGE, 2 * kvw), BF16),) * n,
        [SM, VM, VM] + [VM] * n,
        (VM,) * n,
        [pltpu.VMEM((n * cap, 2 * kvw), BF16), pltpu.VMEM((n * page_cap, PAGE, 2 * kvw), BF16)],
        traffic=4 * tok * 2 * kvw,
    )(slots, info, kv_text, *arrived)
    stored = [sent[0]] + [swap(sent[k], k) for k in range(1, n)]

    attended = call(
        lambda *refs: join_kernel(kv_heads, steps, *refs),
        jax.ShapeDtypeStruct(dec_query.shape, BF16),
        [VM] * (n + 1),
        VM,
        traffic=(n + 1) * (q_rows + STAT) * HD * 4,
    )(*shares, fresh)

    cache_key, cache_value = call(
        lambda *refs: store_kernel(n, page_cap, *refs),
        (jax.ShapeDtypeStruct((n * page_cap, PAGE, kvw), BF16),) * 2,
        [VM] * n,
        (VM, VM),
        traffic=4 * tok * 2 * kvw,
    )(*stored)
    return (attended, cache_key, cache_value)


def solution(mesh):
    return jax.shard_map(
        body,
        mesh=mesh,
        in_specs=(
            P(("groups", "section"), "tensor"),
            P(("groups", "section"), "tensor"),
            P("groups", None),
            P(),
            P(None, "tensor"),
            P(None, "tensor"),
            P("groups"),
            P("groups"),
            P("groups", None),
            P("groups"),
            P(("groups", "section"), None, "tensor"),
            P(("groups", "section"), None, "tensor"),
            P(("groups", "section"), None, "tensor"),
        ),
        out_specs=(
            P(("groups", "section"), None, "tensor"),
            P(("groups", "section"), None, "tensor"),
            P(("groups", "section"), None, "tensor"),
        ),
        check_vma=False,
    )
```

time: 211 us -> 79 us (0.37)
  blocking collectives: 92.4 us -> 0 us
  starting transfers between devices: 16.8 us -> 37.6 us
  local copies, waits for them, and re-layouts: 32.9 us -> 13.1 us
  waiting for transfers between devices: 31.2 us -> 14.4 us
  between operations: 14.4 us -> 0.74 us
  matrix products: 10.7 us -> 0 us
  Pallas kernels: 0 us -> 10.6 us
  other arithmetic: 11.2 us -> 2.09 us
    all_gather x3 -> x0, blocking collectives: 92.4 us -> none  [the longest x2 61.8 us: joined(): gathered = jax.tree.map(lambda a: lax.all_gather(a, axis), part)]
    ppermute x0 -> x26, starting transfers between devices: none -> 37.6 us  [the longest x24 37 us: swap(): return lax.ppermute(array, 'section', [(i, i ^ k) for i in range(n)])]
    all_to_all x3 -> x0, waiting for transfers between devices: 31.1 us -> none  [the longest x1 25.1 us: body(): lax.all_to_all(outgoing, 'section', split_axis=0, concat_axis=0, tiled=True)]
    all_to_all x3 -> x0, starting transfers between devices: 16.8 us -> none  [the longest x1 7.28 us: body(): lax.all_to_all(outgoing, 'section', split_axis=0, concat_axis=0, tiled=True)]
    ppermute x0 -> x26, waiting for transfers between devices: none -> 14.4 us  [the longest x24 14.4 us: swap(): return lax.ppermute(array, 'section', [(i, i ^ k) for i in range(n)])]
    dot_general x8 -> x0, matrix products: 10.7 us -> none  [the longest x1 4.78 us: body(): jnp.dot(normed, w_value, preferred_element_type=jnp.float32)]
    pallas_call x0 -> x6, Pallas kernels: none -> 10.6 us  [the longest x1 5.1 us: body(): call(lambda *refs: project_kernel((n, cap, min(1024, half)), *refs), (jax...]
    scatter x4 -> x0, local copies, waits for them, and re-layouts: 10.5 us -> none  [the longest x1 3.13 us: body(): hidden = text_rows.at[places.reshape(-1)].set(incoming, mode='drop')]
  transfers between devices with their start and end apart: 5 -> 26, of which waited for: 2 -> 5; matrix products, arithmetic and copies ran while one was open for 8% -> 3% of each run, Pallas kernels for 0% -> 13%
where the time goes in v1:
time: 79 us; the launch traced here: 78.4 us
  starting transfers between devices  37.6 us (48%)
  waiting for transfers between devices  14.4 us (18%)
  local copies, waits for them, and re-layouts  13.1 us (17%)
  Pallas kernels  10.6 us (13%)
  other arithmetic  2.09 us (3%)
    ppermute x24, starting transfers between devices, swap(): return lax.ppermute(array, 'section', [(i, i ^ k) for i in range(n)])  37 us
    ppermute x24, waiting for transfers between devices, swap(): return lax.ppermute(array, 'section', [(i, i ^ k) for i in range(n)])  14.4 us
    unnamed x27, local copies, waits for them, and re-layouts  13 us
    pallas_call x1, Pallas kernels, body(): call(lambda *refs: project_kernel((n, cap, min(1024, half)), *refs), (jax...  5.1 us
    pallas_call x1, Pallas kernels, body(): call(lambda *refs: meta_kernel((n, img, tok, blocks, cap, page_cap, kv_he...  1.62 us
  transfers between devices with their start and end apart: 26, of which 5 were waited for; matrix products, arithmetic and copies ran while one was open for 3% of the time, Pallas kernels for 13%

profile of v1, /device:TPU:0, one launch (start us, length us, event | category | flops | bytes accessed | tf_op | source)
XLA Modules:
  0.0 78.4 jit_solution(2983669756056720815)
XLA Ops:
  0.6 0.5 collective-permute-start.3
  1.2 2.9 %collective-permute-start = (bf16[1,64,128]{2,1,0:T(8,128)(2,1)}, bf16[1,64,128]{2,1,0:T(8,128)(2,1)S(1)}, u32[]{:S(2)}, u32[]{:S(2)}) collective-permute-start(bf16[1,64,128]{2,1,0:T(8,128)(2,1)} %bitcast.12), channel_id=1, source_target_pairs={{0,2},{2,0},{4,6},{6,4},{8,10},{10,8},{12,14},{14,12},{1,3},{3,1},... | collective-permute-start | bytes 49160 | tf_op jit(solution)/shard_map/ppermute | solution.py:283
  4.2 1.9 %collective-permute-done = bf16[1,64,128]{2,1,0:T(8,128)(2,1)S(1)} collective-permute-done((bf16[1,64,128]{2,1,0:T(8,128)(2,1)}, bf16[1,64,128]{2,1,0:T(8,128)(2,1)S(1)}, u32[]{:S(2)}, u32[]{:S(2)}) %collective-permute-start) | collective-permute-done | bytes 16416 | tf_op jit(solution)/shard_map/ppermute | solution.py:283
  6.1 0.7 pad_maximum_fusion.2
  6.8 2.1 %collective-permute-start.1 = (bf16[2,64,128]{2,1,0:T(8,128)(2,1)S(1)}, bf16[2,64,128]{2,1,0:T(8,128)(2,1)S(1)}, u32[]{:S(2)}, u32[]{:S(2)}) collective-permute-start(bf16[2,64,128]{2,1,0:T(8,128)(2,1)S(1)} %pad_maximum_fusion.2), channel_id=1, source_target_pairs={{0,4},{2,6},{4,0},{6,2},{8,12},{10,14},{12,8},{14,10},{1,5},{3,7},... | collective-permute-start | bytes 98312 | tf_op jit(solution)/shard_map/ppermute | solution.py:283
  8.9 0.5 broadcast.3
  9.4 1.3 %reduce.3 = s32[512]{0:T(512)S(1)} reduce(s32[512,1]{0,1:T(1,128)} %param.15, s32[]{:T(128)} %broadcast.3), dimensions={1}, to_apply=%param.15.reduce_sub_computation.3 | reduce | bytes 4100 | tf_op args[2]
  10.8 0.7 copy-done.4
  11.6 0.7 copy-done.7
  12.2 0.7 copy-done.8
  12.9 0.7 copy-done.9
  13.6 0.7 copy-done.10
  14.2 0.7 copy-done.11
  14.9 0.7 copy-done.12
  15.5 1.6 %shard_map.148 = (s32[8,256]{1,0:T(8,128)S(1)}, s32[16]{0:T(128)S(1)}, f32[72,128]{1,0:T(8,128)S(1)}) custom-call(s32[8,64]{1,0:T(8,128)S(1)} %reshape.24.refs_0_, s32[128]{0:T(128)S(1)} %bitcast.20, s32[8]{0:T(128)S(1)} %copy-done.10, s32[8]{0:T(128)S(1)} %copy-done.11, s32[8]{0:T(128)S(1)} %copy-done.12, bf16[64,128]{1,0:T(8,128)(2,1)S(1)} %bitcast.14, ...), custom_call_target="tpu_custom_call" | custom-call | tf_op jit(solution)/shard_map/pallas_call | solution.py:295
  17.2 2.7 %collective-permute-start.2 = (bf16[4,64,128]{2,1,0:T(8,128)(2,1)S(1)}, bf16[4,64,128]{2,1,0:T(8,128)(2,1)S(1)}, u32[]{:S(2)}, u32[]{:S(2)}) collective-permute-start(bf16[4,64,128]{2,1,0:T(8,128)(2,1)S(1)} %pad_maximum_fusion.1), channel_id=1, source_target_pairs={{0,8},{2,10},{4,12},{6,14},{8,0},{10,2},{12,4},{14,6},{1,9},{3,11}... | collective-permute-start | bytes 196616 | tf_op jit(solution)/shard_map/ppermute | solution.py:283
  19.9 2.2 %copy-done = bf16[8192,256]{1,0:T(8,128)(2,1)S(1)} copy-done((bf16[8192,256]{1,0:T(8,128)(2,1)S(1)}, bf16[8192,256]{1,0:T(8,128)(2,1)}, u32[]{:S(2)}) %copy-start) | copy-done | bytes 4194328
  22.1 2.2 %copy-done.1 = bf16[8192,256]{1,0:T(8,128)(2,1)S(1)} copy-done((bf16[8192,256]{1,0:T(8,128)(2,1)S(1)}, bf16[8192,256]{1,0:T(8,128)(2,1)}, u32[]{:S(2)}) %copy-start.1) | copy-done | bytes 4194328
  24.2 1.6 %copy-done.2 = bf16[256,4096]{1,0:T(8,128)(2,1)S(1)} copy-done((bf16[256,4096]{1,0:T(8,128)(2,1)S(1)}, bf16[256,4096]{1,0:T(8,128)(2,1)}, u32[]{:S(2)}) %copy-start.2) | copy-done | bytes 2097176
  25.8 1.0 %copy-done.3 = bf16[64,4096]{1,0:T(8,128)(2,1)S(1)} copy-done((bf16[64,4096]{1,0:T(8,128)(2,1)S(1)}, bf16[64,4096]{1,0:T(8,128)(2,1)}, u32[]{:S(2)}) %copy-start.3) | copy-done | bytes 524312
  26.9 0.8 copy-done.6
  27.6 5.1 %shard_map.149 = (bf16[256,512]{1,0:T(8,128)(2,1)S(1)}, bf16[64,512]{1,0:T(8,128)(2,1)S(1)}, bf16[16,512]{1,0:T(8,128)(2,1)S(1)}, bf16[16,512]{1,0:T(8,128)(2,1)...) custom-call(bf16[256,4096]{1,0:T(8,128)(2,1)S(1)} %copy-done.2, ...), custom_call_target="tpu_custom_call" | custom-call | flops 2684354560 | bytes 13631488 | tf_op jit(solution)/shard_map/pallas_call | solution.py:316
  32.7 1.6 %collective-permute-start.12 = (bf16[16,512]{1,0:T(8,128)(2,1)S(1)}, bf16[16,512]{1,0:T(8,128)(2,1)S(1)}, u32[]{:S(2)}, u32[]{:S(2)}) collective-permute-start(bf16[16,512]{1,0:T(8,128)(2,1)S(1)} %get-tuple-element.48), channel_id=1, source_target_pairs={{0,2},{2,0},{4,6},{6,4},{8,10},{10,8},{12,14},{14,12},{1,3},{3,1},... | collective-permute-start | bytes 49160 | tf_op jit(solution)/shard_map/ppermute | solution.py:283
  34.3 0.5 collective-permute-start.13
  34.8 1.5 %collective-permute-start.14 = (bf16[16,512]{1,0:T(8,128)(2,1)S(1)}, bf16[16,512]{1,0:T(8,128)(2,1)S(1)}, u32[]{:S(2)}, u32[]{:S(2)}) collective-permute-start(bf16[16,512]{1,0:T(8,128)(2,1)S(1)} %get-tuple-element.50), channel_id=1, source_target_pairs={{0,6},{2,4},{4,2},{6,0},{8,14},{10,12},{12,10},{14,8},{1,7},{3,5},... | collective-permute-start | bytes 49160 | tf_op jit(solution)/shard_map/ppermute | solution.py:283
  36.3 0.3 collective-permute-start.15
  36.6 3.5 %collective-permute-start.16 = (bf16[16,512]{1,0:T(8,128)(2,1)S(1)}, bf16[16,512]{1,0:T(8,128)(2,1)S(1)}, u32[]{:S(2)}, u32[]{:S(2)}) collective-permute-start(bf16[16,512]{1,0:T(8,128)(2,1)S(1)} %get-tuple-element.52), channel_id=1, source_target_pairs={{0,10},{2,8},{4,14},{6,12},{8,2},{10,0},{12,6},{14,4},{1,11},{3,9}... | collective-permute-start | bytes 49160 | tf_op jit(solution)/shard_map/ppermute | solution.py:283
  40.2 1.5 %shard_map.150 = (f32[72,128]{1,0:T(8,128)S(1)}, f32[72,128]{1,0:T(8,128)S(1)}, f32[72,128]{1,0:T(8,128)S(1)}, f32[72,128]{1,0:T(8,128)S(1)}, f32[72,128]{1,0:T(...) custom-call(bf16[8,64,128]{2,1,0:T(8,128)(2,1)S(1)} %pad_maximum_fusion.refs_0_, ...), custom_call_target="tpu_custom_call" | custom-call | flops 83886080 | bytes 294912 | tf_op jit(solution)/shard_map/pallas_call | solution.py:333
  41.7 0.3 collective-permute-start.10
  42.0 3.5 %collective-permute-start.11 = (f32[72,128]{1,0:T(8,128)S(1)}, f32[72,128]{1,0:T(8,128)S(1)}, u32[]{:S(2)}, u32[]{:S(2)}) collective-permute-start(f32[72,128]{1,0:T(8,128)S(1)} %get-tuple-element.44), channel_id=1, source_target_pairs={{0,14},{2,12},{4,10},{6,8},{8,6},{10,4},{12,2},{14,0},{1,15},{3,13... | collective-permute-start | bytes 110600 | tf_op jit(solution)/shard_map/ppermute | solution.py:283
  45.7 1.6 %collective-permute-start.5 = (f32[72,128]{1,0:T(8,128)S(1)}, f32[72,128]{1,0:T(8,128)S(1)}, u32[]{:S(2)}, u32[]{:S(2)}) collective-permute-start(f32[72,128]{1,0:T(8,128)S(1)} %get-tuple-element.38), channel_id=1, source_target_pairs={{0,2},{2,0},{4,6},{6,4},{8,10},{10,8},{12,14},{14,12},{1,3},{3,1},... | collective-permute-start | bytes 110600 | tf_op jit(solution)/shard_map/ppermute | solution.py:283
  47.3 3.9 %collective-permute-done.17.refs_9_ = bf16[16,512]{1,0:T(8,128)(2,1)S(1)} collective-permute-done((bf16[16,512]{1,0:T(8,128)(2,1)S(1)}, bf16[16,512]{1,0:T(8,128)(2,1)S(1)}, u32[]{:S(2)}, u32[]{:S(2)}) %collective-permute-start.17) | collective-permute-done | bytes 16416 | tf_op jit(solution)/shard_map/ppermute | solution.py:283
  51.2 1.2 %collective-permute-start.18 = (bf16[16,512]{1,0:T(8,128)(2,1)S(1)}, bf16[16,512]{1,0:T(8,128)(2,1)S(1)}, u32[]{:S(2)}, u32[]{:S(2)}) collective-permute-start(bf16[16,512]{1,0:T(8,128)(2,1)S(1)} %get-tuple-element.54), channel_id=1, source_target_pairs={{0,14},{2,12},{4,10},{6,8},{8,6},{10,4},{12,2},{14,0},{1,15},{3,13... | collective-permute-start | bytes 49160 | tf_op jit(solution)/shard_map/ppermute | solution.py:283
  52.4 5.4 %collective-permute-done.18.refs_10_ = bf16[16,512]{1,0:T(8,128)(2,1)S(1)} collective-permute-done((bf16[16,512]{1,0:T(8,128)(2,1)S(1)}, bf16[16,512]{1,0:T(8,128)(2,1)S(1)}, u32[]{:S(2)}, u32[]{:S(2)}) %collective-permute-start.18) | collective-permute-done | bytes 16416 | tf_op jit(solution)/shard_map/ppermute | solution.py:283
  57.8 1.6 %collective-permute-start.8 = (f32[72,128]{1,0:T(8,128)S(1)}, f32[72,128]{1,0:T(8,128)S(1)}, u32[]{:S(2)}, u32[]{:S(2)}) collective-permute-start(f32[72,128]{1,0:T(8,128)S(1)} %get-tuple-element.41), channel_id=1, source_target_pairs={{0,8},{2,10},{4,12},{6,14},{8,0},{10,2},{12,4},{14,6},{1,9},{3,11}... | collective-permute-start | bytes 110600 | tf_op jit(solution)/shard_map/ppermute | solution.py:283
  59.5 2.0 %collective-permute-start.9 = (f32[72,128]{1,0:T(8,128)S(1)}, f32[72,128]{1,0:T(8,128)S(1)}, u32[]{:S(2)}, u32[]{:S(2)}) collective-permute-start(f32[72,128]{1,0:T(8,128)S(1)} %get-tuple-element.42), channel_id=1, source_target_pairs={{0,10},{2,8},{4,14},{6,12},{8,2},{10,0},{12,6},{14,4},{1,11},{3,9}... | collective-permute-start | bytes 110600 | tf_op jit(solution)/shard_map/ppermute | solution.py:283
  61.4 0.7 shard_map.152
  62.2 0.9 %collective-permute-start.19 = (bf16[2,16,512]{2,1,0:T(8,128)(2,1)S(1)}, bf16[2,16,512]{2,1,0:T(8,128)(2,1)S(1)}, u32[]{:S(2)}, u32[]{:S(2)}) collective-permute-start(bf16[2,16,512]{2,1,0:T(8,128)(2,1)S(1)} %get-tuple-element.56), channel_id=1, source_target_pairs={{0,2},{2,0},{4,6},{6,4},{8,10},{10,8},{12,14},{14,12},{1,3},{3,1},... | collective-permute-start | bytes 98312 | tf_op jit(solution)/shard_map/ppermute | solution.py:283
  63.0 2.7 %collective-permute-start.20 = (bf16[2,16,512]{2,1,0:T(8,128)(2,1)S(1)}, bf16[2,16,512]{2,1,0:T(8,128)(2,1)S(1)}, u32[]{:S(2)}, u32[]{:S(2)}) collective-permute-start(bf16[2,16,512]{2,1,0:T(8,128)(2,1)S(1)} %get-tuple-element.57), channel_id=1, source_target_pairs={{0,4},{2,6},{4,0},{6,2},{8,12},{10,14},{12,8},{14,10},{1,5},{3,7},... | collective-permute-start | bytes 98312 | tf_op jit(solution)/shard_map/ppermute | solution.py:283
  65.7 0.3 collective-permute-start.21
  66.0 0.8 %collective-permute-start.22 = (bf16[2,16,512]{2,1,0:T(8,128)(2,1)S(1)}, bf16[2,16,512]{2,1,0:T(8,128)(2,1)S(1)}, u32[]{:S(2)}, u32[]{:S(2)}) collective-permute-start(bf16[2,16,512]{2,1,0:T(8,128)(2,1)S(1)} %get-tuple-element.59), channel_id=1, source_target_pairs={{0,8},{2,10},{4,12},{6,14},{8,0},{10,2},{12,4},{14,6},{1,9},{3,11}... | collective-permute-start | bytes 98312 | tf_op jit(solution)/shard_map/ppermute | solution.py:283
  66.8 2.8 %collective-permute-start.23 = (bf16[2,16,512]{2,1,0:T(8,128)(2,1)S(1)}, bf16[2,16,512]{2,1,0:T(8,128)(2,1)S(1)}, u32[]{:S(2)}, u32[]{:S(2)}) collective-permute-start(bf16[2,16,512]{2,1,0:T(8,128)(2,1)S(1)} %get-tuple-element.60), channel_id=1, source_target_pairs={{0,10},{2,8},{4,14},{6,12},{8,2},{10,0},{12,6},{14,4},{1,11},{3,9}... | collective-permute-start | bytes 98312 | tf_op jit(solution)/shard_map/ppermute | solution.py:283
  69.6 1.5 %collective-permute-start.24 = (bf16[2,16,512]{2,1,0:T(8,128)(2,1)S(1)}, bf16[2,16,512]{2,1,0:T(8,128)(2,1)S(1)}, u32[]{:S(2)}, u32[]{:S(2)}) collective-permute-start(bf16[2,16,512]{2,1,0:T(8,128)(2,1)S(1)} %get-tuple-element.61), channel_id=1, source_target_pairs={{0,12},{2,14},{4,8},{6,10},{8,4},{10,6},{12,0},{14,2},{1,13},{3,15... | collective-permute-start | bytes 98312 | tf_op jit(solution)/shard_map/ppermute | solution.py:283
  71.1 2.6 %collective-permute-start.25 = (bf16[2,16,512]{2,1,0:T(8,128)(2,1)S(1)}, bf16[2,16,512]{2,1,0:T(8,128)(2,1)S(1)}, u32[]{:S(2)}, u32[]{:S(2)}) collective-permute-start(bf16[2,16,512]{2,1,0:T(8,128)(2,1)S(1)} %get-tuple-element.62), channel_id=1, source_target_pairs={{0,14},{2,12},{4,10},{6,8},{8,6},{10,4},{12,2},{14,0},{1,15},{3,13... | collective-permute-start | bytes 98312 | tf_op jit(solution)/shard_map/ppermute | solution.py:283
  73.7 0.9 %shard_map.151 = bf16[1,4,2048]{2,1,0:T(4,128)(2,1)} custom-call(f32[72,128]{1,0:T(8,128)S(1)} %get-tuple-element.37.refs_0_, f32[72,128]{1,0:T(8,128)S(1)} %collective-permute-done.5.refs_1_, f32[72,128]{1,0:T(8,128)S(1)} %collective-permute-done.6.refs_2_, f32[72,128]{1,0:T(8,128)S(1)} %collective-permute-done.7.refs_3_, ...), custom_call_target="tpu_custom_call" | custom-call | bytes 331776 | tf_op jit(solution)/shard_map/pallas_call | solution.py:354
  74.6 0.9 %collective-permute-done.24.refs_6_ = bf16[2,16,512]{2,1,0:T(8,128)(2,1)S(1)} collective-permute-done((bf16[2,16,512]{2,1,0:T(8,128)(2,1)S(1)}, bf16[2,16,512]{2,1,0:T(8,128)(2,1)S(1)}, u32[]{:S(2)}, u32[]{:S(2)}) %collective-permute-start.24) | collective-permute-done | bytes 32800 | tf_op jit(solution)/shard_map/ppermute | solution.py:283
  75.4 2.3 %collective-permute-done.25.refs_7_ = bf16[2,16,512]{2,1,0:T(8,128)(2,1)S(1)} collective-permute-done((bf16[2,16,512]{2,1,0:T(8,128)(2,1)S(1)}, bf16[2,16,512]{2,1,0:T(8,128)(2,1)S(1)}, u32[]{:S(2)}, u32[]{:S(2)}) %collective-permute-start.25) | collective-permute-done | bytes 32800 | tf_op jit(solution)/shard_map/ppermute | solution.py:283
  77.7 0.7 shard_map.153
  (42 shorter events, 0.4 us)
Async XLA Ops:
  0.6 19.2 %collective-permute-start.3 = (bf16[256,4096]{1,0:T(8,128)(2,1)}, bf16[256,4096]{1,0:T(8,128)(2,1)S(1)}, u32[]{:S(2)}, u32[]{:S(2)}) collective-permute-start(bf16[256,4096]{1,0:T(8,128)(2,1)} %refs_0_.1), channel_id=1, source_target_pairs={{0,1},{1,0},{2,3},{3,2},{4,5},{5,4},{6,7},{7,6},{8,9},{9,8},{10,11... | collective-permute-start | bytes 6291464 | tf_op jit(solution)/shard_map/ppermute | solution.py:280
  1.1 18.7 %collective-permute-start.4 = (bf16[64,4096]{1,0:T(8,128)(2,1)}, bf16[64,4096]{1,0:T(8,128)(2,1)S(1)}, u32[]{:S(2)}, u32[]{:S(2)}) collective-permute-start(bf16[64,4096]{1,0:T(8,128)(2,1)} %refs_2_.3), channel_id=1, source_target_pairs={{0,1},{1,0},{2,3},{3,2},{4,5},{5,4},{6,7},{7,6},{8,9},{9,8},{10,11... | collective-permute-start | bytes 1572872 | tf_op jit(solution)/shard_map/ppermute | solution.py:280
  1.2 4.9 %collective-permute-start = (bf16[1,64,128]{2,1,0:T(8,128)(2,1)}, bf16[1,64,128]{2,1,0:T(8,128)(2,1)S(1)}, u32[]{:S(2)}, u32[]{:S(2)}) collective-permute-start(bf16[1,64,128]{2,1,0:T(8,128)(2,1)} %bitcast.12), channel_id=1, source_target_pairs={{0,2},{2,0},{4,6},{6,4},{8,10},{10,8},{12,14},{14,12},{1,3},{3,1},... | collective-permute-start | bytes 49160 | tf_op jit(solution)/shard_map/ppermute | solution.py:283
  6.8 10.4 %collective-permute-start.1 = (bf16[2,64,128]{2,1,0:T(8,128)(2,1)S(1)}, bf16[2,64,128]{2,1,0:T(8,128)(2,1)S(1)}, u32[]{:S(2)}, u32[]{:S(2)}) collective-permute-start(bf16[2,64,128]{2,1,0:T(8,128)(2,1)S(1)} %pad_maximum_fusion.2), channel_id=1, source_target_pairs={{0,4},{2,6},{4,0},{6,2},{8,12},{10,14},{12,8},{14,10},{1,5},{3,7},... | collective-permute-start | bytes 98312 | tf_op jit(solution)/shard_map/ppermute | solution.py:283
  10.8 0.7 copy-start.4
  11.6 0.7 copy-start.7
  12.2 0.7 copy-start.8
  12.9 0.7 copy-start.9
  13.6 0.7 copy-start.10
  14.2 0.7 copy-start.11
  14.9 0.7 copy-start.12
  17.2 19.4 %collective-permute-start.2 = (bf16[4,64,128]{2,1,0:T(8,128)(2,1)S(1)}, bf16[4,64,128]{2,1,0:T(8,128)(2,1)S(1)}, u32[]{:S(2)}, u32[]{:S(2)}) collective-permute-start(bf16[4,64,128]{2,1,0:T(8,128)(2,1)S(1)} %pad_maximum_fusion.1), channel_id=1, source_target_pairs={{0,8},{2,10},{4,12},{6,14},{8,0},{10,2},{12,4},{14,6},{1,9},{3,11}... | collective-permute-start | bytes 196616 | tf_op jit(solution)/shard_map/ppermute | solution.py:283
  19.9 2.2 %copy-start = (bf16[8192,256]{1,0:T(8,128)(2,1)S(1)}, bf16[8192,256]{1,0:T(8,128)(2,1)}, u32[]{:S(2)}) copy-start(bf16[8192,256]{1,0:T(8,128)(2,1)} %refs_5_.1) | copy-start | bytes 12582916
  22.1 2.2 %copy-start.1 = (bf16[8192,256]{1,0:T(8,128)(2,1)S(1)}, bf16[8192,256]{1,0:T(8,128)(2,1)}, u32[]{:S(2)}) copy-start(bf16[8192,256]{1,0:T(8,128)(2,1)} %refs_6_.1) | copy-start | bytes 12582916
  24.2 1.6 %copy-start.2 = (bf16[256,4096]{1,0:T(8,128)(2,1)S(1)}, bf16[256,4096]{1,0:T(8,128)(2,1)}, u32[]{:S(2)}) copy-start(bf16[256,4096]{1,0:T(8,128)(2,1)} %refs_0_.1) | copy-start | bytes 6291460
  25.8 1.0 %copy-start.3 = (bf16[64,4096]{1,0:T(8,128)(2,1)S(1)}, bf16[64,4096]{1,0:T(8,128)(2,1)}, u32[]{:S(2)}) copy-start(bf16[64,4096]{1,0:T(8,128)(2,1)} %refs_2_.3) | copy-start | bytes 1572868
  26.9 0.8 copy-start.6
  27.6 12.5 %copy-start.5 = (bf16[1,4,2048]{2,1,0:T(4,128)(2,1)S(1)}, bf16[1,4,2048]{2,1,0:T(4,128)(2,1)}, u32[]{:S(2)}) copy-start(bf16[1,4,2048]{2,1,0:T(4,128)(2,1)} %param.23) | copy-start | bytes 49156
  32.7 9.0 %collective-permute-start.12 = (bf16[16,512]{1,0:T(8,128)(2,1)S(1)}, bf16[16,512]{1,0:T(8,128)(2,1)S(1)}, u32[]{:S(2)}, u32[]{:S(2)}) collective-permute-start(bf16[16,512]{1,0:T(8,128)(2,1)S(1)} %get-tuple-element.48), channel_id=1, source_target_pairs={{0,2},{2,0},{4,6},{6,4},{8,10},{10,8},{12,14},{14,12},{1,3},{3,1},... | collective-permute-start | bytes 49160 | tf_op jit(solution)/shard_map/ppermute | solution.py:283
  34.3 7.7 %collective-permute-start.13 = (bf16[16,512]{1,0:T(8,128)(2,1)S(1)}, bf16[16,512]{1,0:T(8,128)(2,1)S(1)}, u32[]{:S(2)}, u32[]{:S(2)}) collective-permute-start(bf16[16,512]{1,0:T(8,128)(2,1)S(1)} %get-tuple-element.49), channel_id=1, source_target_pairs={{0,4},{2,6},{4,0},{6,2},{8,12},{10,14},{12,8},{14,10},{1,5},{3,7},... | collective-permute-start | bytes 49160 | tf_op jit(solution)/shard_map/ppermute | solution.py:283
  34.8 10.8 %collective-permute-start.14 = (bf16[16,512]{1,0:T(8,128)(2,1)S(1)}, bf16[16,512]{1,0:T(8,128)(2,1)S(1)}, u32[]{:S(2)}, u32[]{:S(2)}) collective-permute-start(bf16[16,512]{1,0:T(8,128)(2,1)S(1)} %get-tuple-element.50), channel_id=1, source_target_pairs={{0,6},{2,4},{4,2},{6,0},{8,14},{10,12},{12,10},{14,8},{1,7},{3,5},... | collective-permute-start | bytes 49160 | tf_op jit(solution)/shard_map/ppermute | solution.py:283
  36.3 9.4 %collective-permute-start.15 = (bf16[16,512]{1,0:T(8,128)(2,1)S(1)}, bf16[16,512]{1,0:T(8,128)(2,1)S(1)}, u32[]{:S(2)}, u32[]{:S(2)}) collective-permute-start(bf16[16,512]{1,0:T(8,128)(2,1)S(1)} %get-tuple-element.51), channel_id=1, source_target_pairs={{0,8},{2,10},{4,12},{6,14},{8,0},{10,2},{12,4},{14,6},{1,9},{3,11}... | collective-permute-start | bytes 49160 | tf_op jit(solution)/shard_map/ppermute | solution.py:283
  36.6 10.7 %collective-permute-start.16 = (bf16[16,512]{1,0:T(8,128)(2,1)S(1)}, bf16[16,512]{1,0:T(8,128)(2,1)S(1)}, u32[]{:S(2)}, u32[]{:S(2)}) collective-permute-start(bf16[16,512]{1,0:T(8,128)(2,1)S(1)} %get-tuple-element.52), channel_id=1, source_target_pairs={{0,10},{2,8},{4,14},{6,12},{8,2},{10,0},{12,6},{14,4},{1,11},{3,9}... | collective-permute-start | bytes 49160 | tf_op jit(solution)/shard_map/ppermute | solution.py:283
  41.7 16.1 %collective-permute-start.10 = (f32[72,128]{1,0:T(8,128)S(1)}, f32[72,128]{1,0:T(8,128)S(1)}, u32[]{:S(2)}, u32[]{:S(2)}) collective-permute-start(f32[72,128]{1,0:T(8,128)S(1)} %get-tuple-element.43), channel_id=1, source_target_pairs={{0,12},{2,14},{4,8},{6,10},{8,4},{10,6},{12,0},{14,2},{1,13},{3,15... | collective-permute-start | bytes 110600 | tf_op jit(solution)/shard_map/ppermute | solution.py:283
  42.0 17.4 %collective-permute-start.11 = (f32[72,128]{1,0:T(8,128)S(1)}, f32[72,128]{1,0:T(8,128)S(1)}, u32[]{:S(2)}, u32[]{:S(2)}) collective-permute-start(f32[72,128]{1,0:T(8,128)S(1)} %get-tuple-element.44), channel_id=1, source_target_pairs={{0,14},{2,12},{4,10},{6,8},{8,6},{10,4},{12,2},{14,0},{1,15},{3,13... | collective-permute-start | bytes 110600 | tf_op jit(solution)/shard_map/ppermute | solution.py:283
  45.6 5.6 %collective-permute-start.17 = (bf16[16,512]{1,0:T(8,128)(2,1)S(1)}, bf16[16,512]{1,0:T(8,128)(2,1)S(1)}, u32[]{:S(2)}, u32[]{:S(2)}) collective-permute-start(bf16[16,512]{1,0:T(8,128)(2,1)S(1)} %get-tuple-element.53), channel_id=1, source_target_pairs={{0,12},{2,14},{4,8},{6,10},{8,4},{10,6},{12,0},{14,2},{1,13},{3,15... | collective-permute-start | bytes 49160 | tf_op jit(solution)/shard_map/ppermute | solution.py:283
  45.7 16.5 %collective-permute-start.5 = (f32[72,128]{1,0:T(8,128)S(1)}, f32[72,128]{1,0:T(8,128)S(1)}, u32[]{:S(2)}, u32[]{:S(2)}) collective-permute-start(f32[72,128]{1,0:T(8,128)S(1)} %get-tuple-element.38), channel_id=1, source_target_pairs={{0,2},{2,0},{4,6},{6,4},{8,10},{10,8},{12,14},{14,12},{1,3},{3,1},... | collective-permute-start | bytes 110600 | tf_op jit(solution)/shard_map/ppermute | solution.py:283
  47.3 15.7 %collective-permute-start.6 = (f32[72,128]{1,0:T(8,128)S(1)}, f32[72,128]{1,0:T(8,128)S(1)}, u32[]{:S(2)}, u32[]{:S(2)}) collective-permute-start(f32[72,128]{1,0:T(8,128)S(1)} %get-tuple-element.39), channel_id=1, source_target_pairs={{0,4},{2,6},{4,0},{6,2},{8,12},{10,14},{12,8},{14,10},{1,5},{3,7},... | collective-permute-start | bytes 110600 | tf_op jit(solution)/shard_map/ppermute | solution.py:283
  51.2 6.6 %collective-permute-start.18 = (bf16[16,512]{1,0:T(8,128)(2,1)S(1)}, bf16[16,512]{1,0:T(8,128)(2,1)S(1)}, u32[]{:S(2)}, u32[]{:S(2)}) collective-permute-start(bf16[16,512]{1,0:T(8,128)(2,1)S(1)} %get-tuple-element.54), channel_id=1, source_target_pairs={{0,14},{2,12},{4,10},{6,8},{8,6},{10,4},{12,2},{14,0},{1,15},{3,13... | collective-permute-start | bytes 49160 | tf_op jit(solution)/shard_map/ppermute | solution.py:283
  57.8 7.9 %collective-permute-start.7 = (f32[72,128]{1,0:T(8,128)S(1)}, f32[72,128]{1,0:T(8,128)S(1)}, u32[]{:S(2)}, u32[]{:S(2)}) collective-permute-start(f32[72,128]{1,0:T(8,128)S(1)} %get-tuple-element.40), channel_id=1, source_target_pairs={{0,6},{2,4},{4,2},{6,0},{8,14},{10,12},{12,10},{14,8},{1,7},{3,5},... | collective-permute-start | bytes 110600 | tf_op jit(solution)/shard_map/ppermute | solution.py:283
  57.8 8.2 %collective-permute-start.8 = (f32[72,128]{1,0:T(8,128)S(1)}, f32[72,128]{1,0:T(8,128)S(1)}, u32[]{:S(2)}, u32[]{:S(2)}) collective-permute-start(f32[72,128]{1,0:T(8,128)S(1)} %get-tuple-element.41), channel_id=1, source_target_pairs={{0,8},{2,10},{4,12},{6,14},{8,0},{10,2},{12,4},{14,6},{1,9},{3,11}... | collective-permute-start | bytes 110600 | tf_op jit(solution)/shard_map/ppermute | solution.py:283
  59.5 7.4 %collective-permute-start.9 = (f32[72,128]{1,0:T(8,128)S(1)}, f32[72,128]{1,0:T(8,128)S(1)}, u32[]{:S(2)}, u32[]{:S(2)}) collective-permute-start(f32[72,128]{1,0:T(8,128)S(1)} %get-tuple-element.42), channel_id=1, source_target_pairs={{0,10},{2,8},{4,14},{6,12},{8,2},{10,0},{12,6},{14,4},{1,11},{3,9}... | collective-permute-start | bytes 110600 | tf_op jit(solution)/shard_map/ppermute | solution.py:283
  62.2 7.5 %collective-permute-start.19 = (bf16[2,16,512]{2,1,0:T(8,128)(2,1)S(1)}, bf16[2,16,512]{2,1,0:T(8,128)(2,1)S(1)}, u32[]{:S(2)}, u32[]{:S(2)}) collective-permute-start(bf16[2,16,512]{2,1,0:T(8,128)(2,1)S(1)} %get-tuple-element.56), channel_id=1, source_target_pairs={{0,2},{2,0},{4,6},{6,4},{8,10},{10,8},{12,14},{14,12},{1,3},{3,1},... | collective-permute-start | bytes 98312 | tf_op jit(solution)/shard_map/ppermute | solution.py:283
  63.0 8.1 %collective-permute-start.20 = (bf16[2,16,512]{2,1,0:T(8,128)(2,1)S(1)}, bf16[2,16,512]{2,1,0:T(8,128)(2,1)S(1)}, u32[]{:S(2)}, u32[]{:S(2)}) collective-permute-start(bf16[2,16,512]{2,1,0:T(8,128)(2,1)S(1)} %get-tuple-element.57), channel_id=1, source_target_pairs={{0,4},{2,6},{4,0},{6,2},{8,12},{10,14},{12,8},{14,10},{1,5},{3,7},... | collective-permute-start | bytes 98312 | tf_op jit(solution)/shard_map/ppermute | solution.py:283
  65.7 8.8 %collective-permute-start.21 = (bf16[2,16,512]{2,1,0:T(8,128)(2,1)S(1)}, bf16[2,16,512]{2,1,0:T(8,128)(2,1)S(1)}, u32[]{:S(2)}, u32[]{:S(2)}) collective-permute-start(bf16[2,16,512]{2,1,0:T(8,128)(2,1)S(1)} %get-tuple-element.58), channel_id=1, source_target_pairs={{0,6},{2,4},{4,2},{6,0},{8,14},{10,12},{12,10},{14,8},{1,7},{3,5},... | collective-permute-start | bytes 98312 | tf_op jit(solution)/shard_map/ppermute | solution.py:283
  66.0 8.5 %collective-permute-start.22 = (bf16[2,16,512]{2,1,0:T(8,128)(2,1)S(1)}, bf16[2,16,512]{2,1,0:T(8,128)(2,1)S(1)}, u32[]{:S(2)}, u32[]{:S(2)}) collective-permute-start(bf16[2,16,512]{2,1,0:T(8,128)(2,1)S(1)} %get-tuple-element.59), channel_id=1, source_target_pairs={{0,8},{2,10},{4,12},{6,14},{8,0},{10,2},{12,4},{14,6},{1,9},{3,11}... | collective-permute-start | bytes 98312 | tf_op jit(solution)/shard_map/ppermute | solution.py:283
  66.8 7.8 %collective-permute-start.23 = (bf16[2,16,512]{2,1,0:T(8,128)(2,1)S(1)}, bf16[2,16,512]{2,1,0:T(8,128)(2,1)S(1)}, u32[]{:S(2)}, u32[]{:S(2)}) collective-permute-start(bf16[2,16,512]{2,1,0:T(8,128)(2,1)S(1)} %get-tuple-element.60), channel_id=1, source_target_pairs={{0,10},{2,8},{4,14},{6,12},{8,2},{10,0},{12,6},{14,4},{1,11},{3,9}... | collective-permute-start | bytes 98312 | tf_op jit(solution)/shard_map/ppermute | solution.py:283
  69.6 5.8 %collective-permute-start.24 = (bf16[2,16,512]{2,1,0:T(8,128)(2,1)S(1)}, bf16[2,16,512]{2,1,0:T(8,128)(2,1)S(1)}, u32[]{:S(2)}, u32[]{:S(2)}) collective-permute-start(bf16[2,16,512]{2,1,0:T(8,128)(2,1)S(1)} %get-tuple-element.61), channel_id=1, source_target_pairs={{0,12},{2,14},{4,8},{6,10},{8,4},{10,6},{12,0},{14,2},{1,13},{3,15... | collective-permute-start | bytes 98312 | tf_op jit(solution)/shard_map/ppermute | solution.py:283
  71.1 6.6 %collective-permute-start.25 = (bf16[2,16,512]{2,1,0:T(8,128)(2,1)S(1)}, bf16[2,16,512]{2,1,0:T(8,128)(2,1)S(1)}, u32[]{:S(2)}, u32[]{:S(2)}) collective-permute-start(bf16[2,16,512]{2,1,0:T(8,128)(2,1)S(1)} %get-tuple-element.62), channel_id=1, source_target_pairs={{0,14},{2,12},{4,10},{6,8},{8,6},{10,4},{12,2},{14,0},{1,15},{3,13... | collective-permute-start | bytes 98312 | tf_op jit(solution)/shard_map/ppermute | solution.py:283

commit v2 on v1

--- a/solution.py
+++ b/solution.py
@@ -16,6 +16,7 @@
 
 VM = pl.BlockSpec(memory_space=pltpu.VMEM)
 SM = pl.BlockSpec(memory_space=pltpu.SMEM)
+ANY = pl.BlockSpec(memory_space=pl.ANY)
 MIB = 1 << 20
 
 
@@ -61,46 +62,62 @@
     out[kv_heads * rows :, :] = jnp.broadcast_to(stats, (STAT, stats.shape[1]))
 
 
-def meta_kernel(sizes, route, pages, count, tail, req, query, key, value, info, slots, fresh, starts):
+def prepare_kernel(sizes, *refs):
     n, img, tok, blocks, cap, page_cap, kv_heads, steps = sizes
+    far, (info, slots, fresh, square), near, small, (starts, sems) = (
+        refs[:12],
+        refs[12:16],
+        refs[16:20],
+        refs[20:28],
+        refs[28:],
+    )
+    copies = [pltpu.make_async_copy(a, b, sems.at[i]) for i, (a, b) in enumerate(zip(far, small + near))]
+    for c in copies:
+        c.start()
+    route, pages, count, tail, req, query, key, value = small
+    text, vis, w_key, w_value = near
+    for c in copies[: len(small)]:
+        c.wait()
     pos = lax.axis_index("section")
-    own = route[pl.ds(pos, 1), :]
-    table = route[...]
+    table = [route[:, e * img : (e + 1) * img] for e in range(n)]
+    own = jnp.zeros((1, img), I32)
+    for e in range(n):
+        own = jnp.where(pos == e, table[e], own)
     stations = lax.broadcasted_iota(I32, (n, img), 0)
     marks = own == stations
     ones = jnp.where(marks, 1.0, 0.0).astype(BF16)
     earlier = lax.broadcasted_iota(I32, (img, img), 0) < lax.broadcasted_iota(I32, (img, img), 1)
     prefix = dot(ones, jnp.where(earlier, 1.0, 0.0).astype(BF16))
     before = jnp.zeros((n, 1), I32)
+    lanes = lax.broadcasted_iota(I32, (1, n * cap), 1)
+    source, inner = lanes // cap, lanes % cap
+    fits = jnp.zeros((1, n * cap), I32)
+    offset = jnp.zeros((1, n * cap), I32)
     for e in range(n):
-        here = jnp.sum((table[e : e + 1, :] == stations).astype(I32), axis=1, keepdims=True)
+        here = jnp.sum((table[e] == stations).astype(I32), axis=1, keepdims=True)
         before = before + jnp.where(e < pos, here, 0)
+        arriving = jnp.sum((table[e] == pos).astype(I32), axis=1, keepdims=True)
+        fits = fits + jnp.where(source == e, arriving, 0)
+        offset = offset + jnp.where(source > e, arriving, 0)
     local = jnp.sum(jnp.where(marks, prefix, 0.0), axis=0, keepdims=True).astype(I32)
     rank = local + jnp.sum(jnp.where(marks, before, 0), axis=0, keepdims=True)
-    send = jnp.bitwise_xor(own, pos) * cap + local
+    send = own * cap + local
     place = own * tok + rank
-    arriving = jnp.sum((table == pos).astype(I32), axis=1, keepdims=True)
-    lanes = lax.broadcasted_iota(I32, (n, n * cap), 1)
-    source = jnp.bitwise_xor(lanes // cap, pos)
-    number = lax.broadcasted_iota(I32, (n, n * cap), 0)
-    fits = jnp.sum(jnp.where(number == source, arriving, 0), axis=0, keepdims=True)
-    offset = jnp.sum(jnp.where(number < source, arriving, 0), axis=0, keepdims=True)
-    inner = lanes[:1] % cap
     target = jnp.where(inner < fits, offset + inner, -1)
-    replaced = jnp.sum(arriving, axis=0, keepdims=True)
+    replaced = jnp.sum(jnp.where(inner == 0, fits, 0), axis=1, keepdims=True)
     total = jnp.int32(0)
     for r in range(n):
         starts[r] = total
         total = total + count[r]
     inside = lax.broadcasted_iota(I32, (1, tok), 1)
-    text = inside + pos * tok
+    text_at = inside + pos * tok
     text_slot = jnp.full((1, tok), -1, I32)
     vis_slot = jnp.full((1, img), -1, I32)
     for b in range(n):
         r = req[b]
         first = starts[r] * PAGE
         last = first + (count[r] - 1) * PAGE + tail[r]
-        text_slot = jnp.where((text >= first) & (text < last), b, text_slot)
+        text_slot = jnp.where((text_at >= first) & (text_at < last), b, text_slot)
         vis_slot = jnp.where((place >= first) & (place < last), b, vis_slot)
     text_slot = jnp.where(inside < replaced, -1, text_slot)
     info[0:1, :img] = send
@@ -108,10 +125,10 @@
     info[2:3, :tok] = text_slot
     info[3:4, : n * cap] = target
     for g in range(blocks):
-        holder = pages[pos * blocks + g]
-        slot = jnp.bitwise_xor(holder, pos) * page_cap
+        holder = pages[0, pos * blocks + g]
+        slot = holder * page_cap
         for e in range(g):
-            slot = slot + (pages[pos * blocks + e] == holder).astype(I32)
+            slot = slot + (pages[0, pos * blocks + e] == holder).astype(I32)
         slots[g] = slot
     rows = query.shape[0] // kv_heads
     row = lax.broadcasted_iota(I32, (rows, steps), 0)
@@ -127,22 +144,33 @@
         for held, new in zip(parts, (numerator, top, jnp.sum(weights, axis=1, keepdims=True))):
             held.append(new)
     put_partial(fresh, kv_heads, *parts)
-
-
-def project_kernel(sizes, text, text_far, vis, vis_far, gain, w_key, w_value, info, kv_text, kv_vis, *rest):
+    for c in copies[len(small) : len(small) + 2]:
+        c.wait()
+    square[:tok, :] = squares_of(text)
+    square[tok:, :] = squares_of(vis)
+    for c in copies[len(small) + 2 :]:
+        c.wait()
+
+
+def squares_of(rows):
+    total = jnp.zeros((rows.shape[0], HD), F32)
+    for c in range(0, rows.shape[1], HD):
+        wide = rows[:, c : c + HD].astype(F32)
+        total = total + wide * wide
+    return total
+
+
+def project_kernel(sizes, text, text_far, vis, vis_far, gain, w_key, w_value, square, info, kv_text, kv_vis, packed, total):
     n, cap, step = sizes
-    packed, (total, ) = rest[:-1], rest[-1:]
     tok, half = text.shape
     img = vis.shape[0]
     kvw = w_key.shape[1]
     me = lax.axis_index("tensor")
-    squares = [jnp.zeros((tok, 1), F32), jnp.zeros((img, 1), F32)]
-    for number, pair in enumerate(((text, text_far), (vis, vis_far))):
-        for half_rows in pair:
-            for c in range(0, half, step):
-                wide = half_rows[:, c : c + step].astype(F32)
-                squares[number] += jnp.sum(wide * wide, axis=1, keepdims=True)
-    scales = [lax.rsqrt(s / (2.0 * half) + EPS) for s in squares]
+    scales = []
+    for far, lo in ((text_far, 0), (vis_far, tok)):
+        size = far.shape[0]
+        sums = jnp.sum(square[lo : lo + size, :] + squares_of(far), axis=1, keepdims=True)
+        scales.append(lax.rsqrt(sums / (2.0 * half) + EPS))
     for side in range(2):
         text_side, vis_side = (text, vis) if side == 0 else (text_far, vis_far)
         base = (me if side == 0 else 1 - me) * half
@@ -165,18 +193,14 @@
     kv_vis[...] = own
     slot = lax.broadcasted_iota(I32, (n * cap, img), 0)
     chosen = jnp.where(slot == info[0:1, :img], 1.0, 0.0).astype(BF16)
-    outgoing = dot(chosen, own).astype(BF16)
-    for k in range(n):
-        packed[k][...] = outgoing[k * cap : (k + 1) * cap, :]
-
-
-def attend_kernel(n, kv_heads, query, kv_text, kv_vis, info, *out):
-    pos = lax.axis_index("section")
+    packed[...] = dot(chosen, own).astype(BF16)
+
+
+def attend_kernel(n, kv_heads, query, kv_text, kv_vis, info, out):
     tok, img = kv_text.shape[0], kv_vis.shape[0]
     kvw = kv_heads * HD
     rows = query.shape[1] // kv_heads
-    number = lax.broadcasted_iota(I32, (n * rows, 1), 0) // rows
-    slot = jnp.bitwise_xor(number, pos)
+    slot = lax.broadcasted_iota(I32, (n * rows, 1), 0) // rows
     text_ok = slot == info[2:3, :tok]
     vis_ok = slot == info[1:2, :img]
     parts = []
@@ -194,45 +218,41 @@
         parts.append((numerator, top, total))
     for k in range(n):
         at = slice(k * rows, (k + 1) * rows)
-        put_partial(out[k], kv_heads, *zip(*[tuple(x[at] for x in p) for p in parts]))
-
-
-def pack_kernel(n, cap, page_cap, slots, info, kv_text, *rest):
-    pieces, out, (incoming, staged) = rest[:n], rest[n : 2 * n], rest[2 * n :]
+        put_partial(out.at[k], kv_heads, *zip(*[tuple(x[at] for x in p) for p in parts]))
+
+
+def pack_kernel(n, cap, page_cap, slots, info, kv_text, incoming, out):
     tok = kv_text.shape[0]
+    kvw = kv_text.shape[1] // 2
     blocks = tok // PAGE
-    for k in range(n):
-        incoming[k * cap : (k + 1) * cap, :] = pieces[k][...]
     reach = min(tok, n * cap)
     hit = lax.broadcasted_iota(I32, (reach, n * cap), 0) == info[3:4, : n * cap]
     hot = jnp.where(hit, 1.0, 0.0)
     covered = jnp.sum(hot, axis=1, keepdims=True) > 0.0
     placed = dot(hot.astype(BF16), incoming[...])
     mixed = jnp.where(covered, placed, kv_text[:reach, :].astype(F32)).astype(BF16)
-    staged[...] = jnp.zeros(staged.shape, BF16)
+    out[...] = jnp.zeros(out.shape, BF16)
     for g in range(blocks):
         if (g + 1) * PAGE <= reach:
             rows = mixed[g * PAGE : (g + 1) * PAGE, :]
         else:
             rows = kv_text[g * PAGE : (g + 1) * PAGE, :]
-        staged[slots[g]] = rows
-    for k in range(n):
-        out[k][...] = staged[k * page_cap : (k + 1) * page_cap]
-
-
-def store_kernel(n, page_cap, *refs):
-    pieces, (keys, values) = refs[:n], refs[n:]
-    pos = lax.axis_index("section")
-    kvw = keys.shape[2]
-    for k in range(n):
-        at = pl.ds(jnp.bitwise_xor(pos, k) * page_cap, page_cap)
-        keys[at] = pieces[k][:, :, :kvw]
-        values[at] = pieces[k][:, :, kvw:]
-
-
-def join_kernel(kv_heads, steps, *refs):
-    pieces, attended = refs[:-1], refs[-1]
-    rows = pieces[0].shape[0] - STAT
+        slot = slots[g]
+        out[slot // page_cap, 0, slot % page_cap] = rows[:, :kvw]
+        out[slot // page_cap, 1, slot % page_cap] = rows[:, kvw:]
+
+
+def store_kernel(pages, keys, values, sems):
+    copies = [pltpu.make_async_copy(pages.at[:, i], out, sems.at[i]) for i, out in enumerate((keys, values))]
+    for c in copies:
+        c.start()
+    for c in copies:
+        c.wait()
+
+
+def join_kernel(steps, shares, fresh, attended):
+    rows = fresh.shape[0] - STAT
+    pieces = [shares.at[k] for k in range(shares.shape[0])] + [fresh]
     stats = [row_to_column(p[rows : rows + 1, :]) for p in pieces]
     tops = [s[:rows] for s in stats]
     highest = tops[0]
@@ -279,94 +299,122 @@
     def across(array):
         return lax.ppermute(array, "tensor", [(0, 1), (1, 0)])
 
-    def swap(array, k):
-        return lax.ppermute(array, "section", [(i, i ^ k) for i in range(n)])
+    def exchange(array):
+        return lax.all_to_all(array, "section", split_axis=0, concat_axis=0, tiled=True)
+
+    def remote(array):
+        return pltpu.with_memory_space_constraint(array, pltpu.HBM)
+
+    def local(array):
+        return pltpu.with_memory_space_constraint(array, pltpu.VMEM)
 
     vis_far = across(vis_rows)
     text_far = across(text_rows)
     query = dec_query.reshape(steps, heads, HD).transpose(1, 0, 2).reshape(1, q_rows, HD)
-    queries = query
-    k = 1
-    while k < n:
-        queries = jnp.concatenate([queries, swap(queries, k)], axis=0)
-        k *= 2
+    queries = exchange(jnp.broadcast_to(query, (n, q_rows, HD)))
 
     width = max(tok, n * cap)
-    info, slots, fresh = call(
-        lambda *refs: meta_kernel((n, img, tok, blocks, cap, page_cap, kv_heads, steps), *refs),
-        (
-            jax.ShapeDtypeStruct((8, width), I32),
-            jax.ShapeDtypeStruct((blocks,), I32),
-            jax.ShapeDtypeStruct((q_rows + STAT, HD), F32),
-        ),
-        [VM, SM, SM, SM, SM, VM, VM, VM],
-        (VM, SM, VM),
-        [pltpu.SMEM((n,), I32)],
-    )(
-        img_route.reshape(n, img),
-        page_dest.reshape(n * blocks),
+    arguments = (
+        img_route.T,
+        page_dest.T,
         page_count,
         tail_len,
         dec_req,
         query[0],
         dec_key[0],
         dec_value[0],
-    )
-
-    kv_text, kv_vis, *packed = call(
+        text_rows,
+        vis_rows,
+        w_key,
+        w_value,
+    )
+    info, slots, fresh, square, *near = call(
+        lambda *refs: prepare_kernel((n, img, tok, blocks, cap, page_cap, kv_heads, steps), *refs),
+        (
+            jax.ShapeDtypeStruct((8, width), I32),
+            jax.ShapeDtypeStruct((blocks,), I32),
+            jax.ShapeDtypeStruct((q_rows + STAT, HD), F32),
+            jax.ShapeDtypeStruct((tok + img, HD), F32),
+            *[pltpu.VMEM(a.shape, a.dtype) for a in arguments[8:]],
+        ),
+        [ANY] * len(arguments),
+        (VM, SM, VM, VM) + (VM,) * 4,
+        [
+            *[(pltpu.SMEM if 1 <= i <= 4 else pltpu.VMEM)(a.shape, a.dtype) for i, a in enumerate(arguments[:8])],
+            pltpu.SMEM((n,), I32),
+            pltpu.SemaphoreType.DMA((len(arguments),)),
+        ],
+        flops=1 << 20,
+        traffic=2 * 2 * half * 2 * kvw * 2,
+    )(*[remote(a) for a in arguments])
+    text_near, vis_near, key_near, value_near = near
+
+    kv_text, kv_vis, packed = call(
         lambda *refs: project_kernel((n, cap, min(1024, half)), *refs),
         (
             jax.ShapeDtypeStruct((tok, 2 * kvw), BF16),
             jax.ShapeDtypeStruct((img, 2 * kvw), BF16),
-            *[jax.ShapeDtypeStruct((cap, 2 * kvw), BF16)] * n,
+            jax.ShapeDtypeStruct((n * cap, 2 * kvw), BF16),
         ),
-        [VM] * 8,
-        (VM,) * (2 + n),
+        [VM] * 9,
+        (VM,) * 3,
         [pltpu.VMEM((tok + img, 2 * kvw), F32)],
-        limit=32,
         flops=2 * (tok + img) * 2 * half * 2 * kvw,
         traffic=2 * (tok + img) * 2 * half + 8 * half * kvw,
-    )(text_rows, text_far, vis_rows, vis_far, norm_gain.reshape(1, 2 * half), w_key, w_value, info)
-
-    arrived = [packed[0]] + [swap(packed[k], k) for k in range(1, n)]
+    )(
+        local(text_near),
+        text_far,
+        local(vis_near),
+        vis_far,
+        remote(norm_gain.reshape(1, 2 * half)),
+        local(key_near),
+        local(value_near),
+        square,
+        info,
+    )
+    arrived = exchange(packed)
 
     partials = call(
         lambda *refs: attend_kernel(n, kv_heads, *refs),
-        (jax.ShapeDtypeStruct((q_rows + STAT, HD), F32),) * n,
+        jax.ShapeDtypeStruct((n, q_rows + STAT, HD), F32),
         [VM] * 4,
-        (VM,) * n,
-        limit=24,
+        VM,
         flops=4 * n * q_rows * (tok + img) * HD,
         traffic=n * (q_rows + STAT) * HD * 4,
     )(queries, kv_text, kv_vis, info)
-    shares = [partials[0]] + [swap(partials[k], k) for k in range(1, n)]
+    shares = exchange(partials)
 
     sent = call(
         lambda *refs: pack_kernel(n, cap, page_cap, *refs),
-        (jax.ShapeDtypeStruct((page_cap, PAGE, 2 * kvw), BF16),) * n,
-        [SM, VM, VM] + [VM] * n,
-        (VM,) * n,
-        [pltpu.VMEM((n * cap, 2 * kvw), BF16), pltpu.VMEM((n * page_cap, PAGE, 2 * kvw), BF16)],
+        jax.ShapeDtypeStruct((n, 2, page_cap, PAGE, kvw), BF16),
+        [SM, VM, VM, VM],
+        VM,
         traffic=4 * tok * 2 * kvw,
-    )(slots, info, kv_text, *arrived)
-    stored = [sent[0]] + [swap(sent[k], k) for k in range(1, n)]
+    )(slots, info, kv_text, arrived)
+    stored = exchange(sent)
 
     attended = call(
-        lambda *refs: join_kernel(kv_heads, steps, *refs),
+        lambda *refs: join_kernel(steps, *refs),
         jax.ShapeDtypeStruct(dec_query.shape, BF16),
-        [VM] * (n + 1),
+        [VM] * 2,
         VM,
         traffic=(n + 1) * (q_rows + STAT) * HD * 4,
-    )(*shares, fresh)
+    )(shares, fresh)
 
     cache_key, cache_value = call(
-        lambda *refs: store_kernel(n, page_cap, *refs),
-        (jax.ShapeDtypeStruct((n * page_cap, PAGE, kvw), BF16),) * 2,
-        [VM] * n,
-        (VM, VM),
+        store_kernel,
+        (jax.ShapeDtypeStruct((n, page_cap, PAGE, kvw), BF16),) * 2,
+        [ANY],
+        (ANY, ANY),
+        [pltpu.SemaphoreType.DMA((2,))],
         traffic=4 * tok * 2 * kvw,
-    )(*stored)
-    return (attended, cache_key, cache_value)
+    )(stored)
+    slots_here = n * page_cap
+    return (
+        attended,
+        cache_key.reshape(slots_here, PAGE, kvw),
+        cache_value.reshape(slots_here, PAGE, kvw),
+    )
 
 
 def solution(mesh):

time: 79 us -> 59 us (0.75)
  starting transfers between devices: 37.6 us -> 20.7 us
  local copies, waits for them, and re-layouts: 13.1 us -> 1.39 us
  Pallas kernels: 10.6 us -> 16.2 us
  waiting for transfers between devices: 14.4 us -> 19.4 us
  other arithmetic: 2.09 us -> 0 us
    ppermute x24 -> x0, starting transfers between devices: 37 us -> none  [swap(): return lax.ppermute(array, 'section', [(i, i ^ k) for i in range(n)])]
    all_to_all x0 -> x4, starting transfers between devices: none -> 20.1 us  [exchange(): lax.all_to_all(array, 'section', split_axis=0, concat_axis=0, tiled=True)]
    all_to_all x0 -> x4, waiting for transfers between devices: none -> 19.4 us  [exchange(): lax.all_to_all(array, 'section', split_axis=0, concat_axis=0, tiled=True)]
    ppermute x24 -> x0, waiting for transfers between devices: 14.4 us -> none  [swap(): return lax.ppermute(array, 'section', [(i, i ^ k) for i in range(n)])]
    unnamed x27 -> x0, local copies, waits for them, and re-layouts: 13 us -> none
    pallas_call x5, Pallas kernels: 5.45 us -> 10.2 us  [the longest x1 4.93 us: body(): call(lambda *refs: prepare_kernel((n, img, tok, blocks, cap, page_cap, kv...]
    broadcast_in_dim x0 -> x1, local copies, waits for them, and re-layouts: none -> 1.39 us  [body(): queries = exchange(jnp.broadcast_to(query, (n, q_rows, HD)))]
    unnamed x1 -> x0, other arithmetic: 1.34 us -> none
  transfers between devices with their start and end apart: 26 -> 6, of which waited for: 5 -> 3; matrix products, arithmetic and copies ran while one was open for 3% -> 2% of each run, Pallas kernels for 13% -> 27%
where the time goes in v2:
time: 59 us; the launch traced here: 58.4 us
  starting transfers between devices  20.7 us (35%)
  waiting for transfers between devices  19.4 us (33%)
  Pallas kernels  16.2 us (27%)
  local copies, waits for them, and re-layouts  1.39 us (2%)
  between operations  0.68 us (1%)
    all_to_all x4, starting transfers between devices, exchange(): lax.all_to_all(array, 'section', split_axis=0, concat_axis=0, tiled=True)  20.1 us
    all_to_all x4, waiting for transfers between devices, exchange(): lax.all_to_all(array, 'section', split_axis=0, concat_axis=0, tiled=True)  19.4 us
    pallas_call x1, Pallas kernels, body(): call(lambda *refs: project_kernel((n, cap, min(1024, half)), *refs), (jax...  6.07 us
    pallas_call x1, Pallas kernels, body(): call(lambda *refs: prepare_kernel((n, img, tok, blocks, cap, page_cap, kv...  4.93 us
    pallas_call x1, Pallas kernels, body(): call(lambda *refs: attend_kernel(n, kv_heads, *refs), jax.ShapeDtypeStruc...  2.22 us
    pallas_call x1, Pallas kernels, body(): call(lambda *refs: pack_kernel(n, cap, page_cap, *refs), jax.ShapeDtypeSt...  1.43 us
    broadcast_in_dim x1, local copies, waits for them, and re-layouts, body(): queries = exchange(jnp.broadcast_to(query, (n, q_rows, HD)))  1.39 us
  transfers between devices with their start and end apart: 6, of which 3 were waited for; matrix products, arithmetic and copies ran while one was open for 2% of the time, Pallas kernels for 27%

profile of v2, /device:TPU:0, one launch (start us, length us, event | category | flops | bytes accessed | tf_op | source)
XLA Modules:
  0.0 58.4 jit_solution(12931901227227647129)
XLA Ops:
  0.6 0.5 collective-permute-start
  1.1 0.1 collective-permute-start.1
  1.2 1.4 %broadcast_in_dim.8 = bf16[8,64,128]{2,1,0:T(8,128)(2,1)} broadcast(bf16[64,128]{1,0:T(8,128)(2,1)} %bitcast.15), dimensions={1,2} | broadcast | bytes 147456 | tf_op jit(solution)/shard_map/broadcast_in_dim | solution.py:314
  2.6 7.3 %all-to-all-start = ((bf16[8,64,128]{2,1,0:T(8,128)(2,1)}), bf16[8,64,128]{2,1,0:T(8,128)(2,1)S(1)}, u32[]{:S(2)}, u32[]{:S(2)}) async-start(bf16[8,64,128]{2,1,0:T(8,128)(2,1)} %broadcast_in_dim.8), calls=%async_computation | async-start | bytes 262144 | tf_op jit(solution)/shard_map/all_to_all | solution.py:303
  9.9 4.9 %shard_map.148 = (s32[8,256]{1,0:T(8,128)S(1)}, s32[16]{0:T(128)S(1)}, f32[72,128]{1,0:T(8,128)S(1)}, f32[320,128]{1,0:T(8,128)S(1)}, bf16[256,4096]{1,0:T(8,128...) custom-call(s32[1,512]{1,0:T(1,128)} %bitcast.18, ...), custom_call_target="tpu_custom_call" | custom-call | flops 1048576 | bytes 16777216 | tf_op jit(solution)/shard_map/pallas_call | solution.py:331
  14.8 0.0 collective-permute-done.1.refs_3_
  14.8 0.0 collective-permute-done.refs_1_
  14.8 6.1 %shard_map.149 = (bf16[256,512]{1,0:T(8,128)(2,1)S(1)}, bf16[64,512]{1,0:T(8,128)(2,1)S(1)}, bf16[128,512]{1,0:T(8,128)(2,1)}) custom-call(bf16[256,4096]{1,0:T(8,128)(2,1)S(1)} %get-tuple-element.16.refs_0_, bf16[256,4096]{1,0:T(8,128)(2,1)S(1)} %collective-permute-done.refs_1_, bf16[64,4096]{1,0:T(8,128)(2,1)S(1)} %get-tuple-element.17.refs_2_, ...), custom_call_target="tpu_custom_call" | custom-call | flops 2684354560 | bytes 13631488 | tf_op jit(solution)/shard_map/pallas_call | solution.py:352
  20.9 0.0 all-to-all-done.refs_0_
  20.9 6.0 %all-to-all-start.2 = ((bf16[8,16,512]{2,1,0:T(8,128)(2,1)}), bf16[8,16,512]{2,1,0:T(8,128)(2,1)S(1)}, u32[]{:S(2)}, u32[]{:S(2)}) async-start(bf16[8,16,512]{2,1,0:T(8,128)(2,1)} %bitcast.10), calls=%async_computation.2 | async-start | bytes 262144 | tf_op jit(solution)/shard_map/all_to_all | solution.py:303
  26.9 2.2 %shard_map.150 = f32[8,72,128]{2,1,0:T(8,128)} custom-call(bf16[8,64,128]{2,1,0:T(8,128)(2,1)S(1)} %all-to-all-done.refs_0_, bf16[256,512]{1,0:T(8,128)(2,1)S(1)} %get-tuple-element.22.refs_1_.refs_2_, bf16[64,512]{1,0:T(8,128)(2,1)S(1)} %get-tuple-element.23.refs_2_, s32[8,256]{1,0:T(8,128)S(1)} %get-tuple-element.21.refs_8_.refs_3_.refs_1_), custom_call_target="tpu_custom_call" | custom-call | flops 83886080 | bytes 294912 | tf_op jit(solution)/shard_map/pallas_call | solution.py:377
  29.1 5.1 %all-to-all-done.2 = bf16[8,16,512]{2,1,0:T(8,128)(2,1)S(1)} async-done(((bf16[8,16,512]{2,1,0:T(8,128)(2,1)}), bf16[8,16,512]{2,1,0:T(8,128)(2,1)S(1)}, u32[]{:S(2)}, u32[]{:S(2)}) %all-to-all-start.2) | async-done | bytes 131104 | tf_op jit(solution)/shard_map/all_to_all | solution.py:303
  34.3 3.4 %all-to-all-start.1 = ((f32[8,72,128]{2,1,0:T(8,128)}), f32[8,72,128]{2,1,0:T(8,128)S(1)}, u32[]{:S(2)}, u32[]{:S(2)}) async-start(f32[8,72,128]{2,1,0:T(8,128)} %shard_map.150), calls=%async_computation.1 | async-start | bytes 589824 | tf_op jit(solution)/shard_map/all_to_all | solution.py:303
  37.7 1.4 %shard_map.152 = bf16[8,2,2,16,256]{4,3,2,1,0:T(8,128)(2,1)} custom-call(s32[16]{0:T(128)S(1)} %get-tuple-element.25.refs_0_, s32[8,256]{1,0:T(8,128)S(1)} %get-tuple-element.21.refs_8_.refs_3_.refs_1_, bf16[256,512]{1,0:T(8,128)(2,1)S(1)} %get-tuple-element.22.refs_1_.refs_2_, bf16[128,512]{1,0:T(8,128)(2,1)S(1)} %bitcast.14), custom_call_target="tpu_custom_call" | custom-call | bytes 524288 | tf_op jit(solution)/shard_map/pallas_call | solution.py:387
  39.1 7.0 %all-to-all-done.1.refs_0_ = f32[8,72,128]{2,1,0:T(8,128)S(1)} async-done(((f32[8,72,128]{2,1,0:T(8,128)}), f32[8,72,128]{2,1,0:T(8,128)S(1)}, u32[]{:S(2)}, u32[]{:S(2)}) %all-to-all-start.1) | async-done | bytes 294944 | tf_op jit(solution)/shard_map/all_to_all | solution.py:303
  46.1 3.4 %all-to-all-start.3 = ((bf16[8,2,2,16,256]{4,3,2,1,0:T(8,128)(2,1)}), bf16[8,2,2,16,256]{4,3,2,1,0:T(8,128)(2,1)S(1)}, u32[]{:S(2)}, u32[]{:S(2)}) async-start(bf16[8,2,2,16,256]{4,3,2,1,0:T(8,128)(2,1)} %shard_map.152), calls=%async_computation.3 | async-start | bytes 524288 | tf_op jit(solution)/shard_map/all_to_all | solution.py:303
  49.5 0.9 %shard_map.151 = bf16[1,4,2048]{2,1,0:T(4,128)(2,1)} custom-call(f32[8,72,128]{2,1,0:T(8,128)S(1)} %all-to-all-done.1.refs_0_, f32[72,128]{1,0:T(8,128)S(1)} %get-tuple-element.24.refs_1_), custom_call_target="tpu_custom_call" | custom-call | bytes 331776 | tf_op jit(solution)/shard_map/pallas_call | solution.py:396
  50.4 7.3 %all-to-all-done.3.pages = bf16[8,2,2,16,256]{4,3,2,1,0:T(8,128)(2,1)S(1)} async-done(((bf16[8,2,2,16,256]{4,3,2,1,0:T(8,128)(2,1)}), bf16[8,2,2,16,256]{4,3,2,1,0:T(8,128)(2,1)S(1)}, u32[]{:S(2)}, u32[]{:S(2)}) %all-to-all-start.3) | async-done | bytes 262176 | tf_op jit(solution)/shard_map/all_to_all | solution.py:303
  57.6 0.7 %shard_map.153 = (bf16[8,2,16,256]{3,2,1,0:T(8,128)(2,1)}, bf16[8,2,16,256]{3,2,1,0:T(8,128)(2,1)}) custom-call(bf16[8,2,2,16,256]{4,3,2,1,0:T(8,128)(2,1)S(1)} %all-to-all-done.3.pages), custom_call_target="tpu_custom_call" | custom-call | bytes 524288 | tf_op jit(solution)/shard_map/pallas_call | solution.py:404
Async XLA Ops:
  0.6 14.2 %collective-permute-start = (bf16[256,4096]{1,0:T(8,128)(2,1)}, bf16[256,4096]{1,0:T(8,128)(2,1)S(1)}, u32[]{:S(2)}, u32[]{:S(2)}) collective-permute-start(bf16[256,4096]{1,0:T(8,128)(2,1)} %refs_8_.1), channel_id=1, source_target_pairs={{0,1},{1,0},{2,3},{3,2},{4,5},{5,4},{6,7},{7,6},{8,9},{9,8},{10,11... | collective-permute-start | bytes 6291464 | tf_op jit(solution)/shard_map/ppermute | solution.py:300
  1.1 13.7 %collective-permute-start.1 = (bf16[64,4096]{1,0:T(8,128)(2,1)}, bf16[64,4096]{1,0:T(8,128)(2,1)S(1)}, u32[]{:S(2)}, u32[]{:S(2)}) collective-permute-start(bf16[64,4096]{1,0:T(8,128)(2,1)} %refs_9_.1), channel_id=1, source_target_pairs={{0,1},{1,0},{2,3},{3,2},{4,5},{5,4},{6,7},{7,6},{8,9},{9,8},{10,11... | collective-permute-start | bytes 1572872 | tf_op jit(solution)/shard_map/ppermute | solution.py:300
  2.6 18.3 %all-to-all-start = ((bf16[8,64,128]{2,1,0:T(8,128)(2,1)}), bf16[8,64,128]{2,1,0:T(8,128)(2,1)S(1)}, u32[]{:S(2)}, u32[]{:S(2)}) async-start(bf16[8,64,128]{2,1,0:T(8,128)(2,1)} %broadcast_in_dim.8), calls=%async_computation | async-start | bytes 262144 | tf_op jit(solution)/shard_map/all_to_all | solution.py:303
  20.9 13.3 %all-to-all-start.2 = ((bf16[8,16,512]{2,1,0:T(8,128)(2,1)}), bf16[8,16,512]{2,1,0:T(8,128)(2,1)S(1)}, u32[]{:S(2)}, u32[]{:S(2)}) async-start(bf16[8,16,512]{2,1,0:T(8,128)(2,1)} %bitcast.10), calls=%async_computation.2 | async-start | bytes 262144 | tf_op jit(solution)/shard_map/all_to_all | solution.py:303
  34.3 11.8 %all-to-all-start.1 = ((f32[8,72,128]{2,1,0:T(8,128)}), f32[8,72,128]{2,1,0:T(8,128)S(1)}, u32[]{:S(2)}, u32[]{:S(2)}) async-start(f32[8,72,128]{2,1,0:T(8,128)} %shard_map.150), calls=%async_computation.1 | async-start | bytes 589824 | tf_op jit(solution)/shard_map/all_to_all | solution.py:303
  46.1 11.6 %all-to-all-start.3 = ((bf16[8,2,2,16,256]{4,3,2,1,0:T(8,128)(2,1)}), bf16[8,2,2,16,256]{4,3,2,1,0:T(8,128)(2,1)S(1)}, u32[]{:S(2)}, u32[]{:S(2)}) async-start(bf16[8,2,2,16,256]{4,3,2,1,0:T(8,128)(2,1)} %shard_map.152), calls=%async_computation.3 | async-start | bytes 524288 | tf_op jit(solution)/shard_map/all_to_all | solution.py:303

commit v3 on v2

v3 whole, which is shorter than its diff:
```python
import jax
import jax.numpy as jnp
from jax import lax
from jax.experimental import pallas as pl
from jax.experimental.pallas import tpu as pltpu
from jax.sharding import PartitionSpec as P

HD = 128
PAGE = 16
LOWEST = -1e30
EPS = 1e-06
STAT = 8
F32 = jnp.float32
BF16 = jnp.bfloat16
I32 = jnp.int32

VM = pl.BlockSpec(memory_space=pltpu.VMEM)
SM = pl.BlockSpec(memory_space=pltpu.SMEM)
ANY = pl.BlockSpec(memory_space=pl.ANY)
MIB = 1 << 20


def call(kernel, out_shape, in_specs, out_specs, scratch=(), limit=16, flops=0, traffic=0):
    return pl.pallas_call(
        kernel,
        out_shape=out_shape,
        in_specs=in_specs,
        out_specs=out_specs,
        scratch_shapes=list(scratch),
        compiler_params=pltpu.CompilerParams(vmem_limit_bytes=limit * MIB),
        cost_estimate=pl.CostEstimate(flops=flops, bytes_accessed=traffic, transcendentals=0),
    )


def dot(a, b):
    return jnp.dot(a, b, preferred_element_type=F32)


def dot_t(a, b):
    return lax.dot_general(a, b, (((1,), (1,)), ((), ())), preferred_element_type=F32)


def diagonal(shape):
    return lax.broadcasted_iota(I32, shape, 0) == lax.broadcasted_iota(I32, shape, 1)


def column_to_row(column):
    rows = column.shape[0]
    return jnp.sum(jnp.where(diagonal((rows, rows)), column, 0.0), axis=0, keepdims=True)


def row_to_column(row):
    lanes = row.shape[1]
    return jnp.sum(jnp.where(diagonal((lanes, lanes)), row, 0.0), axis=1, keepdims=True)


def squares_of(rows):
    total = jnp.zeros((rows.shape[0], HD), F32)
    for c in range(0, rows.shape[1], HD):
        wide = rows[:, c : c + HD].astype(F32)
        total = total + wide * wide
    return total


def split_three(values):
    high = values.astype(BF16).astype(F32)
    rest = values - high
    middle = rest.astype(BF16).astype(F32)
    return high, middle, rest - middle


def softmax_parts(query, key, value, usable):
    scores = jnp.where(usable, dot_t(query, key) * HD**-0.5, LOWEST)
    top = jnp.max(scores, axis=1, keepdims=True)
    weights = jnp.where(usable, jnp.exp(scores - top), 0.0)
    return dot(weights.astype(BF16), value), top, jnp.sum(weights, axis=1, keepdims=True)


def prepare_kernel(sizes, *refs):
    n, img, tok, blocks, cap, lot, page_cap, kv_heads, steps = sizes
    far, (info, slots, fresh), near, small, (starts, sems) = (
        refs[:12],
        refs[12:15],
        refs[15:19],
        refs[19:27],
        refs[27:],
    )
    copies = [pltpu.make_async_copy(a, b, sems.at[i]) for i, (a, b) in enumerate(zip(far, small + near))]
    for c in copies:
        c.start()
    route, pages, count, tail, req, query, key, value = small
    for c in copies[: len(small)]:
        c.wait()
    pos = lax.axis_index("section")
    table = [route[:, e * img : (e + 1) * img] for e in range(n)]
    own = jnp.zeros((1, img), I32)
    for e in range(n):
        own = jnp.where(pos == e, table[e], own)
    marks = own == lax.broadcasted_iota(I32, (n, img), 0)
    ones = jnp.where(marks, 1.0, 0.0).astype(BF16)
    earlier = lax.broadcasted_iota(I32, (img, img), 0) < lax.broadcasted_iota(I32, (img, img), 1)
    prefix = dot(ones, jnp.where(earlier, 1.0, 0.0).astype(BF16))
    local = jnp.sum(jnp.where(marks, prefix, 0.0), axis=0, keepdims=True).astype(I32)
    info[0:1, :img] = own * lot + local
    lanes = lax.broadcasted_iota(I32, (1, n * lot), 1)
    source, inner = lanes // lot, lanes % lot
    fits = jnp.zeros((1, n * lot), I32)
    offset = jnp.zeros((1, n * lot), I32)
    for e in range(n):
        arriving = jnp.sum((table[e] == pos).astype(I32), axis=1, keepdims=True)
        fits = fits + jnp.where(source == e, arriving, 0)
        offset = offset + jnp.where(source > e, arriving, 0)
    info[2:3, : n * lot] = jnp.where(inner < fits, offset + inner, -1)
    total = jnp.int32(0)
    for r in range(n):
        starts[r] = total
        total = total + count[r]
    token = lax.broadcasted_iota(I32, (1, tok), 1) + pos * tok
    token_slot = jnp.full((1, tok), -1, I32)
    for b in range(n):
        r = req[b]
        first = starts[r] * PAGE
        last = first + (count[r] - 1) * PAGE + tail[r]
        token_slot = jnp.where((token >= first) & (token < last), b, token_slot)
    info[1:2, :tok] = token_slot
    for g in range(blocks):
        holder = pages[0, pos * blocks + g]
        slot = holder * page_cap
        for e in range(g):
            slot = slot + (pages[0, pos * blocks + e] == holder).astype(I32)
        slots[g] = slot
    rows = query.shape[0] // kv_heads
    row = lax.broadcasted_iota(I32, (rows, steps), 0)
    causal = lax.broadcasted_iota(I32, (rows, steps), 1) <= row % steps
    tops, totals = [], []
    for g in range(kv_heads):
        cols = slice(g * HD, (g + 1) * HD)
        own_query = query[g * rows : (g + 1) * rows, :]
        numerator, top, weight = softmax_parts(own_query, key[:, cols], value[:, cols], causal)
        fresh[g * rows : (g + 1) * rows, :] = numerator
        tops.append(top)
        totals.append(weight)
    stats = column_to_row(jnp.concatenate(tops + totals, axis=0))
    fresh[kv_heads * rows :, :] = jnp.broadcast_to(stats, (STAT, stats.shape[1]))
    for c in copies[len(small) :]:
        c.wait()


def project(near, far, gain, w_key, w_value, total, step):
    half = near.shape[1]
    kvw = w_key.shape[1]
    me = lax.axis_index("tensor")
    sums = jnp.sum(squares_of(near) + squares_of(far), axis=1, keepdims=True)
    scale = lax.rsqrt(sums / (2.0 * half) + EPS)
    for rows, side in ((near, me), (far, 1 - me)):
        for c in range(0, half, step):
            columns = pl.ds(pl.multiple_of(side * half + c, step), step)
            normed = (rows[:, c : c + step].astype(F32) * scale * gain[:, columns]).astype(BF16)
            for w, at in ((w_key, 0), (w_value, kvw)):
                part = dot(normed, w[columns, :])
                if rows is near and c == 0:
                    total[:, at : at + kvw] = part
                else:
                    total[:, at : at + kvw] += part


def vis_kernel(n, lot, step, near, far, gain, w_key, w_value, info, query, out, total):
    project(near, far, gain, w_key, w_value, total, step)
    img = near.shape[0]
    slot = lax.broadcasted_iota(I32, (n * lot, img), 0)
    chosen = jnp.where(slot == info[0:1, :img], 1.0, 0.0).astype(BF16)
    packed = dot(chosen, total[...].astype(BF16)).astype(BF16)
    q_lots = out.shape[1] - lot
    for k in range(n):
        for j in range(query.shape[0] // q_lots):
            out[k, :q_lots, j * HD : (j + 1) * HD] = query[j * q_lots : (j + 1) * q_lots, :]
        out[k, q_lots:, :] = packed[k * lot : (k + 1) * lot, :]


def text_kernel(step, near, far, gain, w_key, w_value, out, total):
    project(near, far, gain, w_key, w_value, total, step)
    out[...] = total[...].astype(BF16)


def attend_kernel(n, cap, lot, page_cap, kv_heads, slots, info, kv_text, arrived, out, kv):
    tok = kv_text.shape[0]
    kvw = kv_heads * HD
    q_lots = arrived.shape[1] - lot
    reach = min(tok, n * cap)
    hit = lax.broadcasted_iota(I32, (reach, n * lot), 0) == info[2:3, : n * lot]
    hot = jnp.where(hit, 1.0, 0.0)
    covered = jnp.sum(hot, axis=1, keepdims=True) > 0.0
    incoming = jnp.concatenate([arrived[k, q_lots:, :] for k in range(n)], axis=0)
    placed = dot(hot.astype(BF16), incoming)
    kv[:reach, :] = jnp.where(covered, placed, kv_text[:reach, :].astype(F32)).astype(BF16)
    if reach < tok:
        kv[reach:, :] = kv_text[reach:, :]
    chunk = page_cap * PAGE
    halves = 2 * kv_heads
    pages = halves * chunk
    out[:, :pages, :] = jnp.zeros((n, pages, HD), BF16)
    for g in range(tok // PAGE):
        slot = slots[g]
        for h in range(halves):
            at = pl.ds(pl.multiple_of((slot % page_cap) * PAGE + h * chunk, PAGE), PAGE)
            out[slot // page_cap, at, :] = kv[g * PAGE : (g + 1) * PAGE, h * HD : (h + 1) * HD]
    groups = arrived.shape[2] // HD // kv_heads
    rows = groups * q_lots
    slot = lax.broadcasted_iota(I32, (n * rows, 1), 0) // rows
    usable = slot == info[1:2, :tok]
    tops, totals = [], []
    for g in range(kv_heads):
        query = jnp.concatenate(
            [
                arrived[k, :q_lots, (g * groups + j) * HD : (g * groups + j + 1) * HD]
                for k in range(n)
                for j in range(groups)
            ],
            axis=0,
        )
        key = kv[:, g * HD : (g + 1) * HD]
        value = kv[:, kvw + g * HD : kvw + (g + 1) * HD]
        numerator, top, weight = softmax_parts(query, key, value, usable)
        numerator = numerator.astype(BF16)
        for k in range(n):
            out[k, pages + g * rows : pages + (g + 1) * rows, :] = numerator[k * rows : (k + 1) * rows, :]
        tops.append(top)
        totals.append(weight)
    line = lax.broadcasted_iota(I32, (PAGE, HD), 0)
    for k in range(n):
        at = slice(k * rows, (k + 1) * rows)
        stats = column_to_row(jnp.concatenate([x[at] for x in tops + totals], axis=0))
        high, middle, low = split_three(stats)
        lines = jnp.where(line == 0, high, jnp.where(line == 1, middle, jnp.where(line == 2, low, 0.0)))
        out[k, pages + kv_heads * rows :, :] = lines.astype(BF16)


def finish_kernel(steps, page_cap, shares, fresh, attended, keys, values, sems):
    n = shares.shape[0]
    rows = fresh.shape[0] - STAT
    chunk = page_cap * PAGE
    copies = []
    for i, out in enumerate((keys, values)):
        for h in range(out.shape[2] // HD):
            at = len(copies)
            copies.append(
                pltpu.make_async_copy(
                    shares.at[:, at * chunk : (at + 1) * chunk, :],
                    out.at[:, :, h * HD : (h + 1) * HD],
                    sems.at[at],
                )
            )
    for c in copies:
        c.start()
    pages = len(copies) * chunk
    stats = [row_to_column(fresh[rows : rows + 1, :])]
    for k in range(n):
        lines = shares[k, pages + rows :, :].astype(F32)
        stats.append(row_to_column(lines[0:1] + lines[1:2] + lines[2:3]))
    highest = stats[0][:rows]
    for s in stats[1:]:
        highest = jnp.maximum(highest, s[:rows])
    scale = jnp.exp(stats[0][:rows] - highest)
    numerator = fresh[:rows, :] * scale
    total = stats[0][rows:] * scale
    for k in range(n):
        scale = jnp.exp(stats[k + 1][:rows] - highest)
        numerator = numerator + shares[k, pages : pages + rows, :].astype(F32) * scale
        total = total + stats[k + 1][rows:] * scale
    result = (numerator / total).astype(BF16)
    for h in range(rows // steps):
        attended[0, :, h * HD : (h + 1) * HD] = result[h * steps : (h + 1) * steps, :]
    for c in copies:
        c.wait()


def body(
    text_rows,
    vis_rows,
    img_route,
    norm_gain,
    w_key,
    w_value,
    page_count,
    tail_len,
    page_dest,
    dec_req,
    dec_query,
    dec_key,
    dec_value,
):
    n = lax.axis_size("section")
    tok, half = text_rows.shape
    img = vis_rows.shape[0]
    kvw = w_key.shape[1]
    kv_heads = kvw // HD
    _, steps, q_width = dec_query.shape
    heads = q_width // HD
    q_rows = heads * steps
    blocks = tok // PAGE
    cap = max(2, (2 * img + n - 1) // n)
    page_cap = max(1, (blocks + n - 1) // n)

    def across(array):
        return lax.ppermute(array, "tensor", [(0, 1), (1, 0)])

    def exchange(array):
        return lax.all_to_all(array, "section", split_axis=0, concat_axis=0, tiled=True)

    def remote(array):
        return pltpu.with_memory_space_constraint(array, pltpu.HBM)

    def local(array):
        return pltpu.with_memory_space_constraint(array, pltpu.VMEM)

    vis_far = across(vis_rows)
    text_far = across(text_rows)
    query = dec_query.reshape(steps, heads, HD).transpose(1, 0, 2).reshape(q_rows, HD)

    lot = -(-cap // PAGE) * PAGE
    q_lots = q_rows * HD // (2 * kvw)
    width = max(tok, n * lot)
    arguments = (
        img_route.T,
        page_dest.T,
        page_count,
        tail_len,
        dec_req,
        query,
        dec_key[0],
        dec_value[0],
        w_key,
        w_value,
        vis_rows,
        text_rows,
    )
    info, slots, fresh, key_near, value_near, vis_near, text_near = call(
        lambda *refs: prepare_kernel((n, img, tok, blocks, cap, lot, page_cap, kv_heads, steps), *refs),
        (
            jax.ShapeDtypeStruct((8, width), I32),
            jax.ShapeDtypeStruct((blocks,), I32),
            jax.ShapeDtypeStruct((q_rows + STAT, HD), F32),
            *[pltpu.VMEM(a.shape, a.dtype) for a in arguments[8:]],
        ),
        [ANY] * len(arguments),
        (VM, SM, VM) + (VM,) * 4,
        [
            *[(pltpu.SMEM if 1 <= i <= 4 else pltpu.VMEM)(a.shape, a.dtype) for i, a in enumerate(arguments[:8])],
            pltpu.SMEM((n,), I32),
            pltpu.SemaphoreType.DMA((len(arguments),)),
        ],
        flops=1 << 20,
        traffic=2 * 2 * half * 2 * kvw * 2,
    )(*[remote(a) for a in arguments])
    gain = remote(norm_gain.reshape(1, 2 * half))
    weights = (gain, local(key_near), local(value_near))

    step = min(1024, half)
    packed = call(
        lambda *refs: vis_kernel(n, lot, step, *refs),
        jax.ShapeDtypeStruct((n, q_lots + lot, 2 * kvw), BF16),
        [VM] * 7,
        VM,
        [pltpu.VMEM((img, 2 * kvw), F32)],
        flops=2 * img * 2 * half * 2 * kvw,
        traffic=2 * img * 2 * half + 8 * half * kvw,
    )(local(vis_near), vis_far, *weights, info, remote(query))
    arrived = exchange(packed)

    kv_text = call(
        lambda *refs: text_kernel(step, *refs),
        jax.ShapeDtypeStruct((tok, 2 * kvw), BF16),
        [VM] * 5,
        VM,
        [pltpu.VMEM((tok, 2 * kvw), F32)],
        flops=2 * tok * 2 * half * 2 * kvw,
        traffic=2 * tok * 2 * half + 8 * half * kvw,
    )(local(text_near), text_far, *weights)

    sent = call(
        lambda *refs: attend_kernel(n, cap, lot, page_cap, kv_heads, *refs),
        jax.ShapeDtypeStruct((n, page_cap * PAGE * 2 * kv_heads + q_rows + PAGE, HD), BF16),
        [SM, VM, VM, VM],
        VM,
        [pltpu.VMEM((tok, 2 * kvw), BF16)],
        flops=4 * n * q_rows * tok * HD,
        traffic=n * (q_rows + STAT) * HD * 4,
    )(slots, info, kv_text, arrived)
    shares = exchange(sent)

    slots_here = n * page_cap
    attended, cache_key, cache_value = call(
        lambda *refs: finish_kernel(steps, page_cap, *refs),
        (
            jax.ShapeDtypeStruct(dec_query.shape, BF16),
            jax.ShapeDtypeStruct((n, page_cap * PAGE, kvw), BF16),
            jax.ShapeDtypeStruct((n, page_cap * PAGE, kvw), BF16),
        ),
        [VM, VM],
        (VM, ANY, ANY),
        [pltpu.SemaphoreType.DMA((2 * kv_heads,))],
        traffic=4 * tok * 2 * kvw,
    )(shares, fresh)
    return (
        attended,
        cache_key.reshape(slots_here, PAGE, kvw),
        cache_value.reshape(slots_here, PAGE, kvw),
    )


def solution(mesh):
    return jax.shard_map(
        body,
        mesh=mesh,
        in_specs=(
            P(("groups", "section"), "tensor"),
            P(("groups", "section"), "tensor"),
            P("groups", None),
            P(),
            P(None, "tensor"),
            P(None, "tensor"),
            P("groups"),
            P("groups"),
            P("groups", None),
            P("groups"),
            P(("groups", "section"), None, "tensor"),
            P(("groups", "section"), None, "tensor"),
            P(("groups", "section"), None, "tensor"),
        ),
        out_specs=(
            P(("groups", "section"), None, "tensor"),
            P(("groups", "section"), None, "tensor"),
            P(("groups", "section"), None, "tensor"),
        ),
        check_vma=False,
    )
```

time: 59 us -> 54.2 us (0.919)
  waiting for transfers between devices: 19.4 us -> 0.01 us
  blocking collectives: 0 us -> 18.1 us
  starting transfers between devices: 20.7 us -> 7.85 us
  local copies, waits for them, and re-layouts: 1.39 us -> 11.2 us
    all_to_all x4 -> x1, waiting for transfers between devices: 19.4 us -> 0.01 us  [exchange(): lax.all_to_all(array, 'section', split_axis=0, concat_axis=0, tiled=True)]
    all_to_all x0 -> x1, blocking collectives: none -> 18.1 us  [exchange(): lax.all_to_all(array, 'section', split_axis=0, concat_axis=0, tiled=True)]
    all_to_all x4 -> x1, starting transfers between devices: 20.1 us -> 7.26 us  [exchange(): lax.all_to_all(array, 'section', split_axis=0, concat_axis=0, tiled=True)]
    unnamed x0 -> x12, local copies, waits for them, and re-layouts: none -> 11.2 us
    broadcast_in_dim x1 -> x0, local copies, waits for them, and re-layouts: 1.39 us -> none  [body(): queries = exchange(jnp.broadcast_to(query, (n, q_rows, HD)))]
    pallas_call x6 -> x5, Pallas kernels: 16.2 us -> 15.8 us  [the longest x1 4.96 us: body(): call(lambda *refs: prepare_kernel((n, img, tok, blocks, cap, lot, page_ca...]
  transfers between devices with their start and end apart: 6 -> 3, of which waited for: 3 -> 0; matrix products, arithmetic and copies ran while one was open for 2% -> 0% of each run, Pallas kernels for 27% -> 23%
where the time goes in v3:
time: 54.2 us; the launch traced here: 53.7 us
  blocking collectives  18.1 us (33%)
  Pallas kernels  15.8 us (29%)
  local copies, waits for them, and re-layouts  11.2 us (21%)
  starting transfers between devices  7.85 us (14%)
  between operations  0.69 us (1%)
    all_to_all x1, blocking collectives, exchange(): lax.all_to_all(array, 'section', split_axis=0, concat_axis=0, tiled=True)  18.1 us
    unnamed x12, local copies, waits for them, and re-layouts  11.2 us
    all_to_all x1, starting transfers between devices, exchange(): lax.all_to_all(array, 'section', split_axis=0, concat_axis=0, tiled=True)  7.26 us
    pallas_call x1, Pallas kernels, body(): call(lambda *refs: prepare_kernel((n, img, tok, blocks, cap, lot, page_ca...  4.96 us
    pallas_call x1, Pallas kernels, body(): call(lambda *refs: text_kernel(step, *refs), jax.ShapeDtypeStruct((tok, 2...  3.92 us
    pallas_call x1, Pallas kernels, body(): call(lambda *refs: vis_kernel(n, lot, step, *refs), jax.ShapeDtypeStruct(...  3.46 us
    pallas_call x1, Pallas kernels, body(): call(lambda *refs: attend_kernel(n, cap, lot, page_cap, kv_heads, *refs),...  2.12 us
    pallas_call x1, Pallas kernels, body(): call(lambda *refs: finish_kernel(steps, page_cap, *refs), (jax.ShapeDtype...  1.33 us
  transfers between devices with their start and end apart: 3, of which 0 were waited for; matrix products, arithmetic and copies ran while one was open for 0% of the time, Pallas kernels for 23%

profile of v3, /device:TPU:0, one launch (start us, length us, event | category | flops | bytes accessed | tf_op | source)
XLA Modules:
  0.0 53.7 jit_solution(9221632052759761465)
XLA Ops:
  0.6 0.5 collective-permute-start
  1.2 0.1 collective-permute-start.1
  1.2 5.0 %shard_map.148 = (s32[8,256]{1,0:T(8,128)S(1)}, s32[16]{0:T(128)S(1)}, f32[72,128]{1,0:T(8,128)S(1)}, bf16[8192,256]{1,0:T(8,128)(2,1)S(1)}, bf16[8192,256]{1,0:...) custom-call(s32[1,512]{1,0:T(1,128)} %bitcast.16, s32[1,128]{1,0:T(1,128)} %bitcast.19, ...), custom_call_target="tpu_custom_call" | custom-call | flops 1048576 | bytes 16777216 | tf_op jit(solution)/shard_map/pallas_call | solution.py:337
  6.2 0.0 copy-start.4
  6.2 1.4 %copy-done.4 = bf16[256,4096]{1,0:T(8,128)(2,1)} copy-done((bf16[256,4096]{1,0:T(8,128)(2,1)}, bf16[256,4096]{1,0:T(8,128)(2,1)S(1)}, u32[]{:S(2)}) %copy-start.4) | copy-done | bytes 2097176
  7.6 0.0 collective-permute-done.1.refs_1_
  7.6 3.5 %shard_map.150 = bf16[8,32,512]{2,1,0:T(8,128)(2,1)} custom-call(bf16[64,4096]{1,0:T(8,128)(2,1)S(1)} %get-tuple-element.18.refs_0_, bf16[64,4096]{1,0:T(8,128)(2,1)S(1)} %collective-permute-done.1.refs_1_, f32[1,8192]{1,0:T(1,128)} %bitcast.12, bf16[8192,256]{1,0:T(8,128)(2,1)S(1)} %get-tuple-element.16.refs_3_, ...), custom_call_target="tpu_custom_call" | custom-call | flops 536870912 | bytes 9437184 | tf_op jit(solution)/shard_map/pallas_call | solution.py:359
  11.0 0.0 copy-start
  11.0 2.0 %copy-done = bf16[8192,256]{1,0:T(8,128)(2,1)} copy-done((bf16[8192,256]{1,0:T(8,128)(2,1)}, bf16[8192,256]{1,0:T(8,128)(2,1)S(1)}, u32[]{:S(2)}) %copy-start) | copy-done | bytes 4194328
  13.0 0.0 copy-start.2
  13.0 2.0 %copy-done.2 = bf16[8192,256]{1,0:T(8,128)(2,1)} copy-done((bf16[8192,256]{1,0:T(8,128)(2,1)}, bf16[8192,256]{1,0:T(8,128)(2,1)S(1)}, u32[]{:S(2)}) %copy-start.2) | copy-done | bytes 4194328
  14.9 7.3 %all-to-all-start = ((bf16[8,32,512]{2,1,0:T(8,128)(2,1)}), bf16[8,32,512]{2,1,0:T(8,128)(2,1)S(1)}, u32[]{:S(2)}, u32[]{:S(2)}) async-start(bf16[8,32,512]{2,1,0:T(8,128)(2,1)} %shard_map.150), calls=%async_computation | async-start | bytes 524288 | tf_op jit(solution)/shard_map/all_to_all | solution.py:308
  22.2 0.0 collective-permute-done.refs_1_
  22.2 0.0 copy-start.1
  22.2 2.2 %copy-done.1 = bf16[8192,256]{1,0:T(8,128)(2,1)S(1)} copy-done((bf16[8192,256]{1,0:T(8,128)(2,1)S(1)}, bf16[8192,256]{1,0:T(8,128)(2,1)}, u32[]{:S(2)}) %copy-start.1) | copy-done | bytes 4194328
  24.4 0.0 copy-start.3
  24.4 2.2 %copy-done.3 = bf16[8192,256]{1,0:T(8,128)(2,1)S(1)} copy-done((bf16[8192,256]{1,0:T(8,128)(2,1)S(1)}, bf16[8192,256]{1,0:T(8,128)(2,1)}, u32[]{:S(2)}) %copy-start.3) | copy-done | bytes 4194328
  26.6 0.0 copy-start.5
  26.6 1.6 %copy-done.5 = bf16[256,4096]{1,0:T(8,128)(2,1)S(1)} copy-done((bf16[256,4096]{1,0:T(8,128)(2,1)S(1)}, bf16[256,4096]{1,0:T(8,128)(2,1)}, u32[]{:S(2)}) %copy-start.5) | copy-done | bytes 2097176
  28.2 3.9 %shard_map.149.refs_2_ = bf16[256,512]{1,0:T(8,128)(2,1)S(1)} custom-call(bf16[256,4096]{1,0:T(8,128)(2,1)S(1)} %copy-done.5, bf16[256,4096]{1,0:T(8,128)(2,1)S(1)} %collective-permute-done.refs_1_, f32[1,8192]{1,0:T(1,128)} %bitcast.13, bf16[8192,256]{1,0:T(8,128)(2,1)S(1)} %copy-done.1, bf16[8192,256]{1,0:T(8,128)(2,1)S(1)} %copy-done.3), custom_call_target="tpu_custom_call" | custom-call | flops 2147483648 | bytes 12582912 | tf_op jit(solution)/shard_map/pallas_call | solution.py:370
  32.1 0.0 all-to-all-done.refs_3_
  32.1 2.1 %shard_map.151 = bf16[8,208,128]{2,1,0:T(8,128)(2,1)S(1)} custom-call(s32[16]{0:T(128)S(1)} %get-tuple-element.13.refs_0_, s32[8,256]{1,0:T(8,128)S(1)} %get-tuple-element.14.refs_5_.refs_1_, bf16[256,512]{1,0:T(8,128)(2,1)S(1)} %shard_map.149.refs_2_, bf16[8,32,512]{2,1,0:T(8,128)(2,1)S(1)} %all-to-all-done.refs_3_), custom_call_target="tpu_custom_call" | custom-call | flops 67108864 | bytes 294912 | tf_op jit(solution)/shard_map/pallas_call | solution.py:380
  34.2 18.1 %all_to_all.10.refs_0_ = bf16[8,208,128]{2,1,0:T(8,128)(2,1)S(1)} all-to-all(bf16[8,208,128]{2,1,0:T(8,128)(2,1)S(1)} %shard_map.151), channel_id=1, replica_groups=mesh['groups'=2,'section'=8,'tensor'=2] {'section'}, dimensions={0} | all-to-all | bytes 851968 | tf_op jit(solution)/shard_map/all_to_all | solution.py:308
  52.4 1.3 %shard_map.152 = (bf16[1,4,2048]{2,1,0:T(4,128)(2,1)}, bf16[8,32,256]{2,1,0:T(8,128)(2,1)}, bf16[8,32,256]{2,1,0:T(8,128)(2,1)}) custom-call(bf16[8,208,128]{2,1,0:T(8,128)(2,1)S(1)} %all_to_all.10.refs_0_, f32[72,128]{1,0:T(8,128)S(1)} %get-tuple-element.19.refs_1_), custom_call_target="tpu_custom_call" | custom-call | bytes 524288 | tf_op jit(solution)/shard_map/pallas_call | solution.py:392
Async XLA Ops:
  0.6 21.6 %collective-permute-start = (bf16[256,4096]{1,0:T(8,128)(2,1)}, bf16[256,4096]{1,0:T(8,128)(2,1)S(1)}, u32[]{:S(2)}, u32[]{:S(2)}) collective-permute-start(bf16[256,4096]{1,0:T(8,128)(2,1)} %refs_11_.1), channel_id=1, source_target_pairs={{0,1},{1,0},{2,3},{3,2},{4,5},{5,4},{6,7},{7,6},{8,9},{9,8},{10,11... | collective-permute-start | bytes 6291464 | tf_op jit(solution)/shard_map/ppermute | solution.py:305
  1.2 6.4 %collective-permute-start.1 = (bf16[64,4096]{1,0:T(8,128)(2,1)}, bf16[64,4096]{1,0:T(8,128)(2,1)S(1)}, u32[]{:S(2)}, u32[]{:S(2)}) collective-permute-start(bf16[64,4096]{1,0:T(8,128)(2,1)} %refs_10_.1), channel_id=1, source_target_pairs={{0,1},{1,0},{2,3},{3,2},{4,5},{5,4},{6,7},{7,6},{8,9},{9,8},{10,11... | collective-permute-start | bytes 1572872 | tf_op jit(solution)/shard_map/ppermute | solution.py:305
  6.2 1.4 %copy-start.4 = (bf16[256,4096]{1,0:T(8,128)(2,1)}, bf16[256,4096]{1,0:T(8,128)(2,1)S(1)}, u32[]{:S(2)}) copy-start(bf16[256,4096]{1,0:T(8,128)(2,1)S(1)} %get-tuple-element.15.refs_0_) | copy-start | bytes 6291460
  11.0 2.0 %copy-start = (bf16[8192,256]{1,0:T(8,128)(2,1)}, bf16[8192,256]{1,0:T(8,128)(2,1)S(1)}, u32[]{:S(2)}) copy-start(bf16[8192,256]{1,0:T(8,128)(2,1)S(1)} %get-tuple-element.16.refs_3_) | copy-start | bytes 12582916
  13.0 2.0 %copy-start.2 = (bf16[8192,256]{1,0:T(8,128)(2,1)}, bf16[8192,256]{1,0:T(8,128)(2,1)S(1)}, u32[]{:S(2)}) copy-start(bf16[8192,256]{1,0:T(8,128)(2,1)S(1)} %get-tuple-element.17.refs_4_) | copy-start | bytes 12582916
  14.9 17.2 %all-to-all-start = ((bf16[8,32,512]{2,1,0:T(8,128)(2,1)}), bf16[8,32,512]{2,1,0:T(8,128)(2,1)S(1)}, u32[]{:S(2)}, u32[]{:S(2)}) async-start(bf16[8,32,512]{2,1,0:T(8,128)(2,1)} %shard_map.150), calls=%async_computation | async-start | bytes 524288 | tf_op jit(solution)/shard_map/all_to_all | solution.py:308
  22.2 2.2 %copy-start.1 = (bf16[8192,256]{1,0:T(8,128)(2,1)S(1)}, bf16[8192,256]{1,0:T(8,128)(2,1)}, u32[]{:S(2)}) copy-start(bf16[8192,256]{1,0:T(8,128)(2,1)} %copy-done) | copy-start | bytes 12582916
  24.4 2.2 %copy-start.3 = (bf16[8192,256]{1,0:T(8,128)(2,1)S(1)}, bf16[8192,256]{1,0:T(8,128)(2,1)}, u32[]{:S(2)}) copy-start(bf16[8192,256]{1,0:T(8,128)(2,1)} %copy-done.2) | copy-start | bytes 12582916
  26.6 1.6 %copy-start.5 = (bf16[256,4096]{1,0:T(8,128)(2,1)S(1)}, bf16[256,4096]{1,0:T(8,128)(2,1)}, u32[]{:S(2)}) copy-start(bf16[256,4096]{1,0:T(8,128)(2,1)} %copy-done.4) | copy-start | bytes 6291460

commit v4 on v3

--- a/solution.py
+++ b/solution.py
@@ -78,18 +78,12 @@
 
 def prepare_kernel(sizes, *refs):
     n, img, tok, blocks, cap, lot, page_cap, kv_heads, steps = sizes
-    far, (info, slots, fresh), near, small, (starts, sems) = (
-        refs[:12],
-        refs[12:15],
-        refs[15:19],
-        refs[19:27],
-        refs[27:],
-    )
-    copies = [pltpu.make_async_copy(a, b, sems.at[i]) for i, (a, b) in enumerate(zip(far, small + near))]
+    far, (info, slots, fresh), small, (starts, sems) = refs[:8], refs[8:11], refs[11:19], refs[19:]
+    copies = [pltpu.make_async_copy(a, b, sems.at[i]) for i, (a, b) in enumerate(zip(far, small))]
     for c in copies:
         c.start()
     route, pages, count, tail, req, query, key, value = small
-    for c in copies[: len(small)]:
+    for c in copies:
         c.wait()
     pos = lax.axis_index("section")
     table = [route[:, e * img : (e + 1) * img] for e in range(n)]
@@ -142,30 +136,46 @@
         totals.append(weight)
     stats = column_to_row(jnp.concatenate(tops + totals, axis=0))
     fresh[kv_heads * rows :, :] = jnp.broadcast_to(stats, (STAT, stats.shape[1]))
-    for c in copies[len(small) :]:
-        c.wait()
-
-
-def project(near, far, gain, w_key, w_value, total, step):
+
+
+def project(near_far, far, gain, w_key_far, w_value_far, near, w_key, w_value, total, sems, step):
     half = near.shape[1]
     kvw = w_key.shape[1]
     me = lax.axis_index("tensor")
-    sums = jnp.sum(squares_of(near) + squares_of(far), axis=1, keepdims=True)
+    first = pltpu.make_async_copy(near_far, near, sems.at[0])
+    first.start()
+    loads = []
+    for side in (me, 1 - me):
+        for c in range(0, half, step):
+            at = len(loads) * step
+            columns = pl.ds(pl.multiple_of(side * half + c, step), step)
+            pair = [
+                pltpu.make_async_copy(w.at[columns], held.at[at : at + step], sems.at[2 * len(loads) + i])
+                for i, (w, held) in enumerate(((w_key_far, w_key), (w_value_far, w_value)), 1)
+            ]
+            for copy in pair:
+                copy.start()
+            loads.append((columns, pair))
+    sums = squares_of(far)
+    first.wait()
+    sums = jnp.sum(squares_of(near) + sums, axis=1, keepdims=True)
     scale = lax.rsqrt(sums / (2.0 * half) + EPS)
-    for rows, side in ((near, me), (far, 1 - me)):
-        for c in range(0, half, step):
-            columns = pl.ds(pl.multiple_of(side * half + c, step), step)
-            normed = (rows[:, c : c + step].astype(F32) * scale * gain[:, columns]).astype(BF16)
-            for w, at in ((w_key, 0), (w_value, kvw)):
-                part = dot(normed, w[columns, :])
-                if rows is near and c == 0:
-                    total[:, at : at + kvw] = part
-                else:
-                    total[:, at : at + kvw] += part
-
-
-def vis_kernel(n, lot, step, near, far, gain, w_key, w_value, info, query, out, total):
-    project(near, far, gain, w_key, w_value, total, step)
+    for i, (columns, pair) in enumerate(loads):
+        rows = near if i * step < half else far
+        c = i * step % half
+        normed = (rows[:, c : c + step].astype(F32) * scale * gain[:, columns]).astype(BF16)
+        for copy, w, at in zip(pair, (w_key, w_value), (0, kvw)):
+            copy.wait()
+            part = dot(normed, w[i * step : (i + 1) * step, :])
+            if i == 0:
+                total[:, at : at + kvw] = part
+            else:
+                total[:, at : at + kvw] += part
+
+
+def vis_kernel(n, lot, step, near, far, gain, w_key, w_value, info, query, out, *scratch):
+    project(near, far, gain, w_key, w_value, *scratch, step)
+    total = scratch[3]
     img = near.shape[0]
     slot = lax.broadcasted_iota(I32, (n * lot, img), 0)
     chosen = jnp.where(slot == info[0:1, :img], 1.0, 0.0).astype(BF16)
@@ -177,9 +187,9 @@
         out[k, q_lots:, :] = packed[k * lot : (k + 1) * lot, :]
 
 
-def text_kernel(step, near, far, gain, w_key, w_value, out, total):
-    project(near, far, gain, w_key, w_value, total, step)
-    out[...] = total[...].astype(BF16)
+def text_kernel(step, near, far, gain, w_key, w_value, out, *scratch):
+    project(near, far, gain, w_key, w_value, *scratch, step)
+    out[...] = scratch[3][...].astype(BF16)
 
 
 def attend_kernel(n, cap, lot, page_cap, kv_heads, slots, info, kv_text, arrived, out, kv):
@@ -310,9 +320,6 @@
     def remote(array):
         return pltpu.with_memory_space_constraint(array, pltpu.HBM)
 
-    def local(array):
-        return pltpu.with_memory_space_constraint(array, pltpu.VMEM)
-
     vis_far = across(vis_rows)
     text_far = across(text_rows)
     query = dec_query.reshape(steps, heads, HD).transpose(1, 0, 2).reshape(q_rows, HD)
@@ -329,53 +336,57 @@
         query,
         dec_key[0],
         dec_value[0],
-        w_key,
-        w_value,
-        vis_rows,
-        text_rows,
     )
-    info, slots, fresh, key_near, value_near, vis_near, text_near = call(
+    info, slots, fresh = call(
         lambda *refs: prepare_kernel((n, img, tok, blocks, cap, lot, page_cap, kv_heads, steps), *refs),
         (
             jax.ShapeDtypeStruct((8, width), I32),
             jax.ShapeDtypeStruct((blocks,), I32),
             jax.ShapeDtypeStruct((q_rows + STAT, HD), F32),
-            *[pltpu.VMEM(a.shape, a.dtype) for a in arguments[8:]],
         ),
         [ANY] * len(arguments),
-        (VM, SM, VM) + (VM,) * 4,
+        (VM, SM, VM),
         [
-            *[(pltpu.SMEM if 1 <= i <= 4 else pltpu.VMEM)(a.shape, a.dtype) for i, a in enumerate(arguments[:8])],
+            *[(pltpu.SMEM if 1 <= i <= 4 else pltpu.VMEM)(a.shape, a.dtype) for i, a in enumerate(arguments)],
             pltpu.SMEM((n,), I32),
             pltpu.SemaphoreType.DMA((len(arguments),)),
         ],
         flops=1 << 20,
-        traffic=2 * 2 * half * 2 * kvw * 2,
+        traffic=1 << 22,
     )(*[remote(a) for a in arguments])
-    gain = remote(norm_gain.reshape(1, 2 * half))
-    weights = (gain, local(key_near), local(value_near))
 
     step = min(1024, half)
-    packed = call(
+    weights = (remote(norm_gain.reshape(1, 2 * half)), remote(w_key), remote(w_value))
+
+    def projection(kernel, out_shape, rows, others):
+        return call(
+            kernel,
+            out_shape,
+            [ANY, VM, VM, ANY, ANY] + [VM] * others,
+            VM,
+            [
+                pltpu.VMEM((rows, half), BF16),
+                pltpu.VMEM(w_key.shape, BF16),
+                pltpu.VMEM(w_value.shape, BF16),
+                pltpu.VMEM((rows, 2 * kvw), F32),
+                pltpu.SemaphoreType.DMA((1 + 4 * half // step,)),
+            ],
+            limit=24,
+            flops=2 * rows * 2 * half * 2 * kvw,
+            traffic=2 * rows * 2 * half + 8 * half * kvw,
+        )
+
+    packed = projection(
         lambda *refs: vis_kernel(n, lot, step, *refs),
         jax.ShapeDtypeStruct((n, q_lots + lot, 2 * kvw), BF16),
-        [VM] * 7,
-        VM,
-        [pltpu.VMEM((img, 2 * kvw), F32)],
-        flops=2 * img * 2 * half * 2 * kvw,
-        traffic=2 * img * 2 * half + 8 * half * kvw,
-    )(local(vis_near), vis_far, *weights, info, remote(query))
+        img,
+        2,
+    )(remote(vis_rows), vis_far, *weights, info, remote(query))
     arrived = exchange(packed)
 
-    kv_text = call(
-        lambda *refs: text_kernel(step, *refs),
-        jax.ShapeDtypeStruct((tok, 2 * kvw), BF16),
-        [VM] * 5,
-        VM,
-        [pltpu.VMEM((tok, 2 * kvw), F32)],
-        flops=2 * tok * 2 * half * 2 * kvw,
-        traffic=2 * tok * 2 * half + 8 * half * kvw,
-    )(local(text_near), text_far, *weights)
+    kv_text = projection(
+        lambda *refs: text_kernel(step, *refs), jax.ShapeDtypeStruct((tok, 2 * kvw), BF16), tok, 0
+    )(remote(text_rows), text_far, *weights)
 
     sent = call(
         lambda *refs: attend_kernel(n, cap, lot, page_cap, kv_heads, *refs),

time: 54.2 us -> 50.4 us (0.930)
  local copies, waits for them, and re-layouts: 11.2 us -> 0 us
  Pallas kernels: 15.8 us -> 21.2 us
  waiting for transfers between devices: 0.01 us -> 2.14 us
    unnamed x12 -> x0, local copies, waits for them, and re-layouts: 11.2 us -> none
    pallas_call x2, Pallas kernels: 7.37 us -> 15.2 us  [the longest x1 9.25 us: body(): projection(lambda *refs: text_kernel(step, *refs), jax.ShapeDtypeStruct((...]
    pallas_call x1, Pallas kernels: 4.96 us -> 2.52 us  [body(): call(lambda *refs: prepare_kernel((n, img, tok, blocks, cap, lot, page_ca...]
    ppermute x2, waiting for transfers between devices: 0.01 us -> 2.14 us  [across(): return lax.ppermute(array, 'tensor', [(0, 1), (1, 0)])]
  transfers between devices with their start and end apart: 3 -> 3, of which waited for: 0 -> 1; matrix products, arithmetic and copies ran while one was open for 0% -> 0% of each run, Pallas kernels for 23% -> 35%
where the time goes in v4:
time: 50.4 us; the launch traced here: 50 us
  Pallas kernels  21.2 us (42%)
  blocking collectives  18.2 us (36%)
  starting transfers between devices  7.82 us (16%)
  waiting for transfers between devices  2.14 us (4%)
  between operations  0.67 us (1%)
    all_to_all x1, blocking collectives, exchange(): lax.all_to_all(array, 'section', split_axis=0, concat_axis=0, tiled=True)  18.2 us
    pallas_call x1, Pallas kernels, body(): projection(lambda *refs: text_kernel(step, *refs), jax.ShapeDtypeStruct((...  9.25 us
    all_to_all x1, starting transfers between devices, exchange(): lax.all_to_all(array, 'section', split_axis=0, concat_axis=0, tiled=True)  7.22 us
    pallas_call x1, Pallas kernels, body(): projection(lambda *refs: vis_kernel(n, lot, step, *refs), jax.ShapeDtypeS...  5.94 us
    pallas_call x1, Pallas kernels, body(): call(lambda *refs: prepare_kernel((n, img, tok, blocks, cap, lot, page_ca...  2.52 us
    ppermute x2, waiting for transfers between devices, across(): return lax.ppermute(array, 'tensor', [(0, 1), (1, 0)])  2.14 us
    pallas_call x1, Pallas kernels, body(): call(lambda *refs: attend_kernel(n, cap, lot, page_cap, kv_heads, *refs),...  2.12 us
    pallas_call x1, Pallas kernels, body(): call(lambda *refs: finish_kernel(steps, page_cap, *refs), (jax.ShapeDtype...  1.33 us
  transfers between devices with their start and end apart: 3, of which 1 were waited for; matrix products, arithmetic and copies ran while one was open for 0% of the time, Pallas kernels for 35%

profile of v4, /device:TPU:0, one launch (start us, length us, event | category | flops | bytes accessed | tf_op | source)
XLA Modules:
  0.0 50.0 jit_solution(8306608927652906991)
XLA Ops:
  0.6 0.5 %collective-permute-start = (bf16[256,4096]{1,0:T(8,128)(2,1)}, bf16[256,4096]{1,0:T(8,128)(2,1)S(1)}, u32[]{:S(2)}, u32[]{:S(2)}) collective-permute-start(bf16[256,4096]{1,0:T(8,128)(2,1)} %refs_0_.2), channel_id=1, source_target_pairs={{0,1},{1,0},{2,3},{3,2},{4,5},{5,4},{6,7},{7,6},{8,9},{9,8},{10,11... | collective-permute-start | bytes 6291464 | tf_op jit(solution)/shard_map/ppermute | solution.py:315
  1.2 0.1 collective-permute-start.1
  1.2 2.5 %shard_map.148 = (s32[8,256]{1,0:T(8,128)S(1)}, s32[16]{0:T(128)S(1)}, f32[72,128]{1,0:T(8,128)S(1)}) custom-call(s32[1,512]{1,0:T(1,128)} %bitcast.16, s32[1,128]{1,0:T(1,128)} %bitcast.19, s32[8]{0:T(128)} %refs_2_.1, s32[8]{0:T(128)} %refs_3_.3, s32[8]{0:T(128)} %refs_4_.3, bf16[64,128]{1,0:T(8,128)(2,1)} %bitcast.14, bf16[4,256]{1,0:T(4,128)(2,1)} %bitcast.17, ...), custom_call_target="tpu_custom_call" | custom-call | flops 1048576 | bytes 4194304 | tf_op jit(solution)/shard_map/pallas_call | solution.py:340
  3.8 2.1 %collective-permute-done.1.refs_1_ = bf16[64,4096]{1,0:T(8,128)(2,1)S(1)} collective-permute-done((bf16[64,4096]{1,0:T(8,128)(2,1)}, bf16[64,4096]{1,0:T(8,128)(2,1)S(1)}, u32[]{:S(2)}, u32[]{:S(2)}) %collective-permute-start.1) | collective-permute-done | bytes 524320 | tf_op jit(solution)/shard_map/ppermute | solution.py:315
  5.9 5.9 %shard_map.150 = bf16[8,32,512]{2,1,0:T(8,128)(2,1)} custom-call(bf16[64,4096]{1,0:T(8,128)(2,1)} %refs_0_.3, bf16[64,4096]{1,0:T(8,128)(2,1)S(1)} %collective-permute-done.1.refs_1_, f32[1,8192]{1,0:T(1,128)} %bitcast.12, bf16[8192,256]{1,0:T(8,128)(2,1)} %refs_3_.5, bf16[8192,256]{1,0:T(8,128)(2,1)} %refs_4_.5, ...), custom_call_target="tpu_custom_call" | custom-call | flops 536870912 | bytes 9437184 | tf_op jit(solution)/shard_map/pallas_call | solution.py:379
  11.8 7.2 %all-to-all-start = ((bf16[8,32,512]{2,1,0:T(8,128)(2,1)}), bf16[8,32,512]{2,1,0:T(8,128)(2,1)S(1)}, u32[]{:S(2)}, u32[]{:S(2)}) async-start(bf16[8,32,512]{2,1,0:T(8,128)(2,1)} %shard_map.150), calls=%async_computation | async-start | bytes 524288 | tf_op jit(solution)/shard_map/all_to_all | solution.py:318
  19.1 0.0 collective-permute-done.refs_1_
  19.1 9.2 %shard_map.149.refs_2_ = bf16[256,512]{1,0:T(8,128)(2,1)S(1)} custom-call(bf16[256,4096]{1,0:T(8,128)(2,1)} %refs_0_.2, bf16[256,4096]{1,0:T(8,128)(2,1)S(1)} %collective-permute-done.refs_1_, f32[1,8192]{1,0:T(1,128)} %bitcast.13, bf16[8192,256]{1,0:T(8,128)(2,1)} %refs_3_.5, bf16[8192,256]{1,0:T(8,128)(2,1)} %refs_4_.5), custom_call_target="tpu_custom_call" | custom-call | flops 2147483648 | bytes 12582912 | tf_op jit(solution)/shard_map/pallas_call | solution.py:387
  28.3 0.0 all-to-all-done.refs_3_
  28.3 2.1 %shard_map.151 = bf16[8,208,128]{2,1,0:T(8,128)(2,1)S(1)} custom-call(s32[16]{0:T(128)S(1)} %get-tuple-element.9.refs_0_, s32[8,256]{1,0:T(8,128)S(1)} %get-tuple-element.10.refs_5_.refs_1_, bf16[256,512]{1,0:T(8,128)(2,1)S(1)} %shard_map.149.refs_2_, bf16[8,32,512]{2,1,0:T(8,128)(2,1)S(1)} %all-to-all-done.refs_3_), custom_call_target="tpu_custom_call" | custom-call | flops 67108864 | bytes 294912 | tf_op jit(solution)/shard_map/pallas_call | solution.py:391
  30.5 18.2 %all_to_all.10.refs_0_ = bf16[8,208,128]{2,1,0:T(8,128)(2,1)S(1)} all-to-all(bf16[8,208,128]{2,1,0:T(8,128)(2,1)S(1)} %shard_map.151), channel_id=1, replica_groups=mesh['groups'=2,'section'=8,'tensor'=2] {'section'}, dimensions={0} | all-to-all | bytes 851968 | tf_op jit(solution)/shard_map/all_to_all | solution.py:318
  48.7 1.3 %shard_map.152 = (bf16[1,4,2048]{2,1,0:T(4,128)(2,1)}, bf16[8,32,256]{2,1,0:T(8,128)(2,1)}, bf16[8,32,256]{2,1,0:T(8,128)(2,1)}) custom-call(bf16[8,208,128]{2,1,0:T(8,128)(2,1)S(1)} %all_to_all.10.refs_0_, f32[72,128]{1,0:T(8,128)S(1)} %get-tuple-element.11.refs_1_), custom_call_target="tpu_custom_call" | custom-call | bytes 524288 | tf_op jit(solution)/shard_map/pallas_call | solution.py:403
Async XLA Ops:
  0.6 18.4 %collective-permute-start = (bf16[256,4096]{1,0:T(8,128)(2,1)}, bf16[256,4096]{1,0:T(8,128)(2,1)S(1)}, u32[]{:S(2)}, u32[]{:S(2)}) collective-permute-start(bf16[256,4096]{1,0:T(8,128)(2,1)} %refs_0_.2), channel_id=1, source_target_pairs={{0,1},{1,0},{2,3},{3,2},{4,5},{5,4},{6,7},{7,6},{8,9},{9,8},{10,11... | collective-permute-start | bytes 6291464 | tf_op jit(solution)/shard_map/ppermute | solution.py:315
  1.2 4.7 %collective-permute-start.1 = (bf16[64,4096]{1,0:T(8,128)(2,1)}, bf16[64,4096]{1,0:T(8,128)(2,1)S(1)}, u32[]{:S(2)}, u32[]{:S(2)}) collective-permute-start(bf16[64,4096]{1,0:T(8,128)(2,1)} %refs_0_.3), channel_id=1, source_target_pairs={{0,1},{1,0},{2,3},{3,2},{4,5},{5,4},{6,7},{7,6},{8,9},{9,8},{10,11... | collective-permute-start | bytes 1572872 | tf_op jit(solution)/shard_map/ppermute | solution.py:315
  11.8 16.5 %all-to-all-start = ((bf16[8,32,512]{2,1,0:T(8,128)(2,1)}), bf16[8,32,512]{2,1,0:T(8,128)(2,1)S(1)}, u32[]{:S(2)}, u32[]{:S(2)}) async-start(bf16[8,32,512]{2,1,0:T(8,128)(2,1)} %shard_map.150), calls=%async_computation | async-start | bytes 524288 | tf_op jit(solution)/shard_map/all_to_all | solution.py:318

commit v5 on v3

--- a/solution.py
+++ b/solution.py
@@ -77,18 +77,12 @@
 
 
 def prepare_kernel(sizes, *refs):
-    n, img, tok, blocks, cap, lot, page_cap, kv_heads, steps = sizes
-    far, (info, slots, fresh), near, small, (starts, sems) = (
-        refs[:12],
-        refs[12:15],
-        refs[15:19],
-        refs[19:27],
-        refs[27:],
-    )
+    n, img, tok, blocks, lot, page_cap = sizes
+    far, (info, slots), near, small, (starts, sems) = refs[:8], refs[8:10], refs[10:13], refs[13:18], refs[18:]
     copies = [pltpu.make_async_copy(a, b, sems.at[i]) for i, (a, b) in enumerate(zip(far, small + near))]
     for c in copies:
         c.start()
-    route, pages, count, tail, req, query, key, value = small
+    route, pages, count, tail, req = small
     for c in copies[: len(small)]:
         c.wait()
     pos = lax.axis_index("section")
@@ -129,44 +123,39 @@
         for e in range(g):
             slot = slot + (pages[0, pos * blocks + e] == holder).astype(I32)
         slots[g] = slot
-    rows = query.shape[0] // kv_heads
-    row = lax.broadcasted_iota(I32, (rows, steps), 0)
-    causal = lax.broadcasted_iota(I32, (rows, steps), 1) <= row % steps
-    tops, totals = [], []
-    for g in range(kv_heads):
-        cols = slice(g * HD, (g + 1) * HD)
-        own_query = query[g * rows : (g + 1) * rows, :]
-        numerator, top, weight = softmax_parts(own_query, key[:, cols], value[:, cols], causal)
-        fresh[g * rows : (g + 1) * rows, :] = numerator
-        tops.append(top)
-        totals.append(weight)
-    stats = column_to_row(jnp.concatenate(tops + totals, axis=0))
-    fresh[kv_heads * rows :, :] = jnp.broadcast_to(stats, (STAT, stats.shape[1]))
     for c in copies[len(small) :]:
         c.wait()
 
 
-def project(near, far, gain, w_key, w_value, total, step):
-    half = near.shape[1]
+def scale_of(near, far):
+    sums = jnp.sum(squares_of(near) + squares_of(far), axis=1, keepdims=True)
+    return lax.rsqrt(sums / (2.0 * near.shape[1]) + EPS)
+
+
+def normed_rows(rows, c, step, scale, gain):
+    return (rows[:, c : c + step].astype(F32) * scale * gain).astype(BF16)
+
+
+def add_part(total, at, normed, w, begin):
+    part = dot(normed, w)
+    columns = slice(at, at + part.shape[1])
+    if begin:
+        total[:, columns] = part
+    else:
+        total[:, columns] += part
+
+
+def vis_kernel(n, lot, step, near, far, gain, w_key, w_value, info, query, out, total):
+    img, half = near.shape
     kvw = w_key.shape[1]
     me = lax.axis_index("tensor")
-    sums = jnp.sum(squares_of(near) + squares_of(far), axis=1, keepdims=True)
-    scale = lax.rsqrt(sums / (2.0 * half) + EPS)
+    scale = scale_of(near, far)
     for rows, side in ((near, me), (far, 1 - me)):
         for c in range(0, half, step):
             columns = pl.ds(pl.multiple_of(side * half + c, step), step)
-            normed = (rows[:, c : c + step].astype(F32) * scale * gain[:, columns]).astype(BF16)
+            normed = normed_rows(rows, c, step, scale, gain[:, columns])
             for w, at in ((w_key, 0), (w_value, kvw)):
-                part = dot(normed, w[columns, :])
-                if rows is near and c == 0:
-                    total[:, at : at + kvw] = part
-                else:
-                    total[:, at : at + kvw] += part
-
-
-def vis_kernel(n, lot, step, near, far, gain, w_key, w_value, info, query, out, total):
-    project(near, far, gain, w_key, w_value, total, step)
-    img = near.shape[0]
+                add_part(total, at, normed, w[columns, :], rows is near and c == 0)
     slot = lax.broadcasted_iota(I32, (n * lot, img), 0)
     chosen = jnp.where(slot == info[0:1, :img], 1.0, 0.0).astype(BF16)
     packed = dot(chosen, total[...].astype(BF16)).astype(BF16)
@@ -177,12 +166,43 @@
         out[k, q_lots:, :] = packed[k * lot : (k + 1) * lot, :]
 
 
-def text_kernel(step, near, far, gain, w_key, w_value, out, total):
-    project(near, far, gain, w_key, w_value, total, step)
+def text_kernel(load, step, near_far, far, gain, w_key_far, w_value_far, out, near, w_key, w_value, total, sems):
+    half = near.shape[1]
+    kvw = w_key.shape[1]
+    me = lax.axis_index("tensor")
+    first = pltpu.make_async_copy(near_far, near, sems.at[0])
+    first.start()
+    loads = []
+    for side in (me, 1 - me):
+        for c in range(0, half, load):
+            at = len(loads) * load
+            columns = pl.ds(pl.multiple_of(side * half + c, load), load)
+            pair = [
+                pltpu.make_async_copy(w.at[columns], held.at[at : at + load], sems.at[2 * len(loads) + i])
+                for i, (w, held) in enumerate(((w_key_far, w_key), (w_value_far, w_value)), 1)
+            ]
+            for copy in pair:
+                copy.start()
+            loads.append(pair)
+    sums = squares_of(far)
+    first.wait()
+    sums = jnp.sum(squares_of(near) + sums, axis=1, keepdims=True)
+    scale = lax.rsqrt(sums / (2.0 * half) + EPS)
+    for i, pair in enumerate(loads):
+        for copy in pair:
+            copy.wait()
+        for at in range(i * load, (i + 1) * load, step):
+            rows, side = (near, me) if at < half else (far, 1 - me)
+            c = at % half
+            columns = pl.ds(pl.multiple_of(side * half + c, step), step)
+            normed = normed_rows(rows, c, step, scale, gain[:, columns])
+            for w, col in ((w_key, 0), (w_value, kvw)):
+                add_part(total, col, normed, w[at : at + step, :], at == 0)
     out[...] = total[...].astype(BF16)
 
 
-def attend_kernel(n, cap, lot, page_cap, kv_heads, slots, info, kv_text, arrived, out, kv):
+def attend_kernel(n, cap, lot, page_cap, kv_heads, slots, info, kv_text, arrived, out, own, kv, held):
+    pos = lax.axis_index("section")
     tok = kv_text.shape[0]
     kvw = kv_heads * HD
     q_lots = arrived.shape[1] - lot
@@ -221,6 +241,8 @@
         key = kv[:, g * HD : (g + 1) * HD]
         value = kv[:, kvw + g * HD : kvw + (g + 1) * HD]
         numerator, top, weight = softmax_parts(query, key, value, usable)
+        held[g * n * rows : (g + 1) * n * rows, :] = numerator
+        own[g * rows : (g + 1) * rows, :] = held[pl.ds(pl.multiple_of((g * n + pos) * rows, rows), rows), :]
         numerator = numerator.astype(BF16)
         for k in range(n):
             out[k, pages + g * rows : pages + (g + 1) * rows, :] = numerator[k * rows : (k + 1) * rows, :]
@@ -230,14 +252,50 @@
     for k in range(n):
         at = slice(k * rows, (k + 1) * rows)
         stats = column_to_row(jnp.concatenate([x[at] for x in tops + totals], axis=0))
+
+        @pl.when(pos == k)
+        def _():
+            own[kv_heads * rows :, :] = jnp.broadcast_to(stats, (STAT, stats.shape[1]))
+
         high, middle, low = split_three(stats)
         lines = jnp.where(line == 0, high, jnp.where(line == 1, middle, jnp.where(line == 2, low, 0.0)))
         out[k, pages + kv_heads * rows :, :] = lines.astype(BF16)
 
 
-def finish_kernel(steps, page_cap, shares, fresh, attended, keys, values, sems):
+def combine(pieces, highest):
+    numerator, total = 0.0, 0.0
+    for rows, top, weight in pieces:
+        scale = jnp.exp(top - highest)
+        numerator = numerator + rows * scale
+        total = total + weight * scale
+    return numerator, total
+
+
+def fresh_kernel(kv_heads, steps, query, key, value, own, mine):
+    rows = query.shape[0] // kv_heads
+    every = kv_heads * rows
+    row = lax.broadcasted_iota(I32, (rows, steps), 0)
+    causal = lax.broadcasted_iota(I32, (rows, steps), 1) <= row % steps
+    stats = row_to_column(own[every : every + 1, :])
+    tops, totals = [], []
+    for g in range(kv_heads):
+        cols = slice(g * HD, (g + 1) * HD)
+        at = slice(g * rows, (g + 1) * rows)
+        fresh = softmax_parts(query[at, :], key[:, cols], value[:, cols], causal)
+        share = (own[at, :], stats[at], stats[every + g * rows : every + (g + 1) * rows])
+        highest = jnp.maximum(fresh[1], share[1])
+        numerator, total = combine((fresh, share), highest)
+        mine[at, :] = numerator
+        tops.append(highest)
+        totals.append(total)
+    line = column_to_row(jnp.concatenate(tops + totals, axis=0))
+    mine[every:, :] = jnp.broadcast_to(line, (STAT, line.shape[1]))
+
+
+def finish_kernel(steps, page_cap, shares, mine, attended, keys, values, sems):
     n = shares.shape[0]
-    rows = fresh.shape[0] - STAT
+    pos = lax.axis_index("section")
+    rows = mine.shape[0] - STAT
     chunk = page_cap * PAGE
     copies = []
     for i, out in enumerate((keys, values)):
@@ -253,20 +311,19 @@
     for c in copies:
         c.start()
     pages = len(copies) * chunk
-    stats = [row_to_column(fresh[rows : rows + 1, :])]
+    stats = row_to_column(mine[rows : rows + 1, :])
+    pieces = [(mine[:rows, :], stats[:rows], stats[rows:])]
     for k in range(n):
         lines = shares[k, pages + rows :, :].astype(F32)
-        stats.append(row_to_column(lines[0:1] + lines[1:2] + lines[2:3]))
-    highest = stats[0][:rows]
-    for s in stats[1:]:
-        highest = jnp.maximum(highest, s[:rows])
-    scale = jnp.exp(stats[0][:rows] - highest)
-    numerator = fresh[:rows, :] * scale
-    total = stats[0][rows:] * scale
-    for k in range(n):
-        scale = jnp.exp(stats[k + 1][:rows] - highest)
-        numerator = numerator + shares[k, pages : pages + rows, :].astype(F32) * scale
-        total = total + stats[k + 1][rows:] * scale
+        stats = row_to_column(lines[0:1] + lines[1:2] + lines[2:3])
+        away = pos != k
+        top = jnp.where(away, stats[:rows], LOWEST)
+        weight = jnp.where(away, stats[rows:], 0.0)
+        pieces.append((jnp.where(away, shares[k, pages : pages + rows, :].astype(F32), 0.0), top, weight))
+    highest = pieces[0][1]
+    for p in pieces[1:]:
+        highest = jnp.maximum(highest, p[1])
+    numerator, total = combine(pieces, highest)
     result = (numerator / total).astype(BF16)
     for h in range(rows // steps):
         attended[0, :, h * HD : (h + 1) * HD] = result[h * steps : (h + 1) * steps, :]
@@ -320,42 +377,29 @@
     lot = -(-cap // PAGE) * PAGE
     q_lots = q_rows * HD // (2 * kvw)
     width = max(tok, n * lot)
-    arguments = (
-        img_route.T,
-        page_dest.T,
-        page_count,
-        tail_len,
-        dec_req,
-        query,
-        dec_key[0],
-        dec_value[0],
-        w_key,
-        w_value,
-        vis_rows,
-        text_rows,
-    )
-    info, slots, fresh, key_near, value_near, vis_near, text_near = call(
-        lambda *refs: prepare_kernel((n, img, tok, blocks, cap, lot, page_cap, kv_heads, steps), *refs),
+    arguments = (img_route.T, page_dest.T, page_count, tail_len, dec_req, w_key, w_value, vis_rows)
+    info, slots, key_near, value_near, vis_near = call(
+        lambda *refs: prepare_kernel((n, img, tok, blocks, lot, page_cap), *refs),
         (
             jax.ShapeDtypeStruct((8, width), I32),
             jax.ShapeDtypeStruct((blocks,), I32),
-            jax.ShapeDtypeStruct((q_rows + STAT, HD), F32),
-            *[pltpu.VMEM(a.shape, a.dtype) for a in arguments[8:]],
+            *[pltpu.VMEM(a.shape, a.dtype) for a in arguments[5:]],
         ),
         [ANY] * len(arguments),
-        (VM, SM, VM) + (VM,) * 4,
+        (VM, SM) + (VM,) * 3,
         [
-            *[(pltpu.SMEM if 1 <= i <= 4 else pltpu.VMEM)(a.shape, a.dtype) for i, a in enumerate(arguments[:8])],
+            *[(pltpu.VMEM if i == 0 else pltpu.SMEM)(a.shape, a.dtype) for i, a in enumerate(arguments[:5])],
             pltpu.SMEM((n,), I32),
             pltpu.SemaphoreType.DMA((len(arguments),)),
         ],
         flops=1 << 20,
         traffic=2 * 2 * half * 2 * kvw * 2,
     )(*[remote(a) for a in arguments])
+
+    step = min(1024, half)
+    load = min(2048, half)
     gain = remote(norm_gain.reshape(1, 2 * half))
-    weights = (gain, local(key_near), local(value_near))
-
-    step = min(1024, half)
+
     packed = call(
         lambda *refs: vis_kernel(n, lot, step, *refs),
         jax.ShapeDtypeStruct((n, q_lots + lot, 2 * kvw), BF16),
@@ -364,29 +408,48 @@
         [pltpu.VMEM((img, 2 * kvw), F32)],
         flops=2 * img * 2 * half * 2 * kvw,
         traffic=2 * img * 2 * half + 8 * half * kvw,
-    )(local(vis_near), vis_far, *weights, info, remote(query))
+    )(local(vis_near), vis_far, gain, local(key_near), local(value_near), info, remote(query))
     arrived = exchange(packed)
 
     kv_text = call(
-        lambda *refs: text_kernel(step, *refs),
+        lambda *refs: text_kernel(load, step, *refs),
         jax.ShapeDtypeStruct((tok, 2 * kvw), BF16),
-        [VM] * 5,
+        [ANY, VM, VM, ANY, ANY],
         VM,
-        [pltpu.VMEM((tok, 2 * kvw), F32)],
+        [
+            pltpu.VMEM((tok, half), BF16),
+            pltpu.VMEM(w_key.shape, BF16),
+            pltpu.VMEM(w_value.shape, BF16),
+            pltpu.VMEM((tok, 2 * kvw), F32),
+            pltpu.SemaphoreType.DMA((1 + 4 * half // load,)),
+        ],
+        limit=24,
         flops=2 * tok * 2 * half * 2 * kvw,
         traffic=2 * tok * 2 * half + 8 * half * kvw,
-    )(local(text_near), text_far, *weights)
-
-    sent = call(
+    )(remote(text_rows), text_far, gain, remote(w_key), remote(w_value))
+
+    sent, own = call(
         lambda *refs: attend_kernel(n, cap, lot, page_cap, kv_heads, *refs),
-        jax.ShapeDtypeStruct((n, page_cap * PAGE * 2 * kv_heads + q_rows + PAGE, HD), BF16),
+        (
+            jax.ShapeDtypeStruct((n, page_cap * PAGE * 2 * kv_heads + q_rows + PAGE, HD), BF16),
+            jax.ShapeDtypeStruct((q_rows + STAT, HD), F32),
+        ),
         [SM, VM, VM, VM],
-        VM,
-        [pltpu.VMEM((tok, 2 * kvw), BF16)],
+        (VM, VM),
+        [pltpu.VMEM((tok, 2 * kvw), BF16), pltpu.VMEM((n * q_rows, HD), F32)],
         flops=4 * n * q_rows * tok * HD,
         traffic=n * (q_rows + STAT) * HD * 4,
     )(slots, info, kv_text, arrived)
     shares = exchange(sent)
+
+    mine = call(
+        lambda *refs: fresh_kernel(kv_heads, steps, *refs),
+        jax.ShapeDtypeStruct((q_rows + STAT, HD), F32),
+        [VM] * 4,
+        VM,
+        flops=1 << 20,
+        traffic=1 << 18,
+    )(remote(query), remote(dec_key[0]), remote(dec_value[0]), own)
 
     slots_here = n * page_cap
     attended, cache_key, cache_value = call(
@@ -400,7 +463,7 @@
         (VM, ANY, ANY),
         [pltpu.SemaphoreType.DMA((2 * kv_heads,))],
         traffic=4 * tok * 2 * kvw,
-    )(shares, fresh)
+    )(shares, mine)
     return (
         attended,
         cache_key.reshape(slots_here, PAGE, kvw),

time: 54.2 us -> 46.1 us (0.85)
  blocking collectives: 18.1 us -> 0 us
  waiting for transfers between devices: 0.01 us -> 14.9 us
  local copies, waits for them, and re-layouts: 11.2 us -> 0 us
  starting transfers between devices: 7.85 us -> 11.4 us
  Pallas kernels: 15.8 us -> 18.6 us
    all_to_all x1 -> x0, blocking collectives: 18.1 us -> none  [exchange(): lax.all_to_all(array, 'section', split_axis=0, concat_axis=0, tiled=True)]
    all_to_all x1 -> x2, waiting for transfers between devices: 0.01 us -> 14.4 us  [exchange(): lax.all_to_all(array, 'section', split_axis=0, concat_axis=0, tiled=True)]
    unnamed x12 -> x0, local copies, waits for them, and re-layouts: 11.2 us -> none
    all_to_all x1 -> x2, starting transfers between devices: 7.26 us -> 10.8 us  [exchange(): lax.all_to_all(array, 'section', split_axis=0, concat_axis=0, tiled=True)]
    pallas_call x2 -> x3, Pallas kernels: 8.87 us -> 11 us  [the longest x1 5.55 us: body(): call(lambda *refs: text_kernel(load, step, *refs), jax.ShapeDtypeStruct((...]
    pallas_call x1, Pallas kernels: 2.12 us -> 2.75 us  [body(): call(lambda *refs: attend_kernel(n, cap, lot, page_cap, kv_heads, *refs),...]
  transfers between devices with their start and end apart: 3 -> 4, of which waited for: 0 -> 3; matrix products, arithmetic and copies ran while one was open for 0% -> 0% of each run, Pallas kernels for 23% -> 32%
where the time goes in v5:
time: 46.1 us; the launch traced here: 45.5 us
  Pallas kernels  18.6 us (40%)
  waiting for transfers between devices  14.9 us (32%)
  starting transfers between devices  11.4 us (25%)
  between operations  0.66 us (1%)
    all_to_all x2, waiting for transfers between devices, exchange(): lax.all_to_all(array, 'section', split_axis=0, concat_axis=0, tiled=True)  14.4 us
    all_to_all x2, starting transfers between devices, exchange(): lax.all_to_all(array, 'section', split_axis=0, concat_axis=0, tiled=True)  10.8 us
    pallas_call x1, Pallas kernels, body(): call(lambda *refs: text_kernel(load, step, *refs), jax.ShapeDtypeStruct((...  5.55 us
    pallas_call x1, Pallas kernels, body(): call(lambda *refs: prepare_kernel((n, img, tok, blocks, lot, page_cap), *...  4.19 us
    pallas_call x1, Pallas kernels, body(): call(lambda *refs: vis_kernel(n, lot, step, *refs), jax.ShapeDtypeStruct(...  3.47 us
    pallas_call x1, Pallas kernels, body(): call(lambda *refs: attend_kernel(n, cap, lot, page_cap, kv_heads, *refs),...  2.75 us
    pallas_call x1, Pallas kernels, body(): call(lambda *refs: finish_kernel(steps, page_cap, *refs), (jax.ShapeDtype...  1.34 us
    pallas_call x1, Pallas kernels, body(): call(lambda *refs: fresh_kernel(kv_heads, steps, *refs), jax.ShapeDtypeSt...  1.3 us
  transfers between devices with their start and end apart: 4, of which 3 were waited for; matrix products, arithmetic and copies ran while one was open for 0% of the time, Pallas kernels for 32%

profile of v5, /device:TPU:0, one launch (start us, length us, event | category | flops | bytes accessed | tf_op | source)
XLA Modules:
  0.0 45.5 jit_solution(5577084151035057125)
XLA Ops:
  0.6 0.5 %collective-permute-start = (bf16[256,4096]{1,0:T(8,128)(2,1)}, bf16[256,4096]{1,0:T(8,128)(2,1)S(1)}, u32[]{:S(2)}, u32[]{:S(2)}) collective-permute-start(bf16[256,4096]{1,0:T(8,128)(2,1)} %refs_0_.1), channel_id=1, source_target_pairs={{0,1},{1,0},{2,3},{3,2},{4,5},{5,4},{6,7},{7,6},{8,9},{9,8},{10,11... | collective-permute-start | bytes 6291464 | tf_op jit(solution)/shard_map/ppermute | solution.py:362
  1.2 0.1 collective-permute-start.1
  1.2 4.2 %shard_map.148 = (s32[8,256]{1,0:T(8,128)S(1)}, s32[16]{0:T(128)S(1)}, bf16[8192,256]{1,0:T(8,128)(2,1)S(1)}, bf16[8192,256]{1,0:T(8,128)(2,1)S(1)}, bf16[64,4096]{1,0:T(8,128)(2,1)S(1)}) custom-call(s32[1,512]{1,0:T(1,128)} %bitcast.18, s32[1,128]{1,0:T(1,128)} %bitcast.19, s32[8]{0:T(128)} %refs_2_.1, s32[8]{0:T(128)} %refs_3_.2, s32[8]{0:T(128)} %refs_4_.2, ...), custom_call_target="tpu_custom_call" | custom-call | flops 1048576 | bytes 16777216 | tf_op jit(solution)/shard_map/pallas_call | solution.py:381
  5.4 0.5 %collective-permute-done.1.refs_1_ = bf16[64,4096]{1,0:T(8,128)(2,1)S(1)} collective-permute-done((bf16[64,4096]{1,0:T(8,128)(2,1)}, bf16[64,4096]{1,0:T(8,128)(2,1)S(1)}, u32[]{:S(2)}, u32[]{:S(2)}) %collective-permute-start.1) | collective-permute-done | bytes 524320 | tf_op jit(solution)/shard_map/ppermute | solution.py:362
  5.9 3.5 %shard_map.150 = bf16[8,32,512]{2,1,0:T(8,128)(2,1)} custom-call(bf16[64,4096]{1,0:T(8,128)(2,1)S(1)} %get-tuple-element.15.refs_0_, bf16[64,4096]{1,0:T(8,128)(2,1)S(1)} %collective-permute-done.1.refs_1_, f32[1,8192]{1,0:T(1,128)} %bitcast.12, bf16[8192,256]{1,0:T(8,128)(2,1)S(1)} %get-tuple-element.16.refs_3_, ...), custom_call_target="tpu_custom_call" | custom-call | flops 536870912 | bytes 9437184 | tf_op jit(solution)/shard_map/pallas_call | solution.py:403
  9.4 7.2 %all-to-all-start = ((bf16[8,32,512]{2,1,0:T(8,128)(2,1)}), bf16[8,32,512]{2,1,0:T(8,128)(2,1)S(1)}, u32[]{:S(2)}, u32[]{:S(2)}) async-start(bf16[8,32,512]{2,1,0:T(8,128)(2,1)} %shard_map.150), calls=%async_computation | async-start | bytes 524288 | tf_op jit(solution)/shard_map/all_to_all | solution.py:365
  16.6 0.0 collective-permute-done.refs_1_
  16.6 5.6 %shard_map.149.refs_2_ = bf16[256,512]{1,0:T(8,128)(2,1)S(1)} custom-call(bf16[256,4096]{1,0:T(8,128)(2,1)} %refs_0_.1, bf16[256,4096]{1,0:T(8,128)(2,1)S(1)} %collective-permute-done.refs_1_, f32[1,8192]{1,0:T(1,128)} %bitcast.13, bf16[8192,256]{1,0:T(8,128)(2,1)} %refs_3_.3, bf16[8192,256]{1,0:T(8,128)(2,1)} %refs_4_.3), custom_call_target="tpu_custom_call" | custom-call | flops 2147483648 | bytes 12582912 | tf_op jit(solution)/shard_map/pallas_call | solution.py:414
  22.1 3.7 %all-to-all-done.refs_3_ = bf16[8,32,512]{2,1,0:T(8,128)(2,1)S(1)} async-done(((bf16[8,32,512]{2,1,0:T(8,128)(2,1)}), bf16[8,32,512]{2,1,0:T(8,128)(2,1)S(1)}, u32[]{:S(2)}, u32[]{:S(2)}) %all-to-all-start) | async-done | bytes 262176 | tf_op jit(solution)/shard_map/all_to_all | solution.py:365
  25.8 2.8 %shard_map.151 = (bf16[8,208,128]{2,1,0:T(8,128)(2,1)}, f32[72,128]{1,0:T(8,128)S(1)}) custom-call(s32[16]{0:T(128)S(1)} %get-tuple-element.13.refs_0_, s32[8,256]{1,0:T(8,128)S(1)} %get-tuple-element.14.refs_5_.refs_1_, bf16[256,512]{1,0:T(8,128)(2,1)S(1)} %shard_map.149.refs_2_, bf16[8,32,512]{2,1,0:T(8,128)(2,1)S(1)} %all-to-all-done.refs_3_), custom_call_target="tpu_custom_call" | custom-call | flops 67108864 | bytes 294912 | tf_op jit(solution)/shard_map/pallas_call | solution.py:431
  28.5 3.6 %all-to-all-start.1 = ((bf16[8,208,128]{2,1,0:T(8,128)(2,1)}), bf16[8,208,128]{2,1,0:T(8,128)(2,1)S(1)}, u32[]{:S(2)}, u32[]{:S(2)}) async-start(bf16[8,208,128]{2,1,0:T(8,128)(2,1)} %get-tuple-element.18), calls=%async_computation.1 | async-start | bytes 851968 | tf_op jit(solution)/shard_map/all_to_all | solution.py:365
  32.1 1.3 %shard_map.152.refs_1_ = f32[72,128]{1,0:T(8,128)S(1)} custom-call(bf16[64,128]{1,0:T(8,128)(2,1)} %bitcast.15, bf16[4,256]{1,0:T(4,128)(2,1)} %bitcast.16, bf16[4,256]{1,0:T(4,128)(2,1)} %bitcast.17, f32[72,128]{1,0:T(8,128)S(1)} %get-tuple-element.19.refs_3_), custom_call_target="tpu_custom_call" | custom-call | flops 1048576 | bytes 262144 | tf_op jit(solution)/shard_map/pallas_call | solution.py:445
  33.4 10.8 %all-to-all-done.1.refs_0_ = bf16[8,208,128]{2,1,0:T(8,128)(2,1)S(1)} async-done(((bf16[8,208,128]{2,1,0:T(8,128)(2,1)}), bf16[8,208,128]{2,1,0:T(8,128)(2,1)S(1)}, u32[]{:S(2)}, u32[]{:S(2)}) %all-to-all-start.1) | async-done | bytes 426016 | tf_op jit(solution)/shard_map/all_to_all | solution.py:365
  44.2 1.3 %shard_map.153 = (bf16[1,4,2048]{2,1,0:T(4,128)(2,1)}, bf16[8,32,256]{2,1,0:T(8,128)(2,1)}, bf16[8,32,256]{2,1,0:T(8,128)(2,1)}) custom-call(bf16[8,208,128]{2,1,0:T(8,128)(2,1)S(1)} %all-to-all-done.1.refs_0_, f32[72,128]{1,0:T(8,128)S(1)} %shard_map.152.refs_1_), custom_call_target="tpu_custom_call" | custom-call | bytes 524288 | tf_op jit(solution)/shard_map/pallas_call | solution.py:455
Async XLA Ops:
  0.6 15.9 %collective-permute-start = (bf16[256,4096]{1,0:T(8,128)(2,1)}, bf16[256,4096]{1,0:T(8,128)(2,1)S(1)}, u32[]{:S(2)}, u32[]{:S(2)}) collective-permute-start(bf16[256,4096]{1,0:T(8,128)(2,1)} %refs_0_.1), channel_id=1, source_target_pairs={{0,1},{1,0},{2,3},{3,2},{4,5},{5,4},{6,7},{7,6},{8,9},{9,8},{10,11... | collective-permute-start | bytes 6291464 | tf_op jit(solution)/shard_map/ppermute | solution.py:362
  1.2 4.7 %collective-permute-start.1 = (bf16[64,4096]{1,0:T(8,128)(2,1)}, bf16[64,4096]{1,0:T(8,128)(2,1)S(1)}, u32[]{:S(2)}, u32[]{:S(2)}) collective-permute-start(bf16[64,4096]{1,0:T(8,128)(2,1)} %refs_7_.1), channel_id=1, source_target_pairs={{0,1},{1,0},{2,3},{3,2},{4,5},{5,4},{6,7},{7,6},{8,9},{9,8},{10,11... | collective-permute-start | bytes 1572872 | tf_op jit(solution)/shard_map/ppermute | solution.py:362
  9.4 16.4 %all-to-all-start = ((bf16[8,32,512]{2,1,0:T(8,128)(2,1)}), bf16[8,32,512]{2,1,0:T(8,128)(2,1)S(1)}, u32[]{:S(2)}, u32[]{:S(2)}) async-start(bf16[8,32,512]{2,1,0:T(8,128)(2,1)} %shard_map.150), calls=%async_computation | async-start | bytes 524288 | tf_op jit(solution)/shard_map/all_to_all | solution.py:365
  28.5 15.7 %all-to-all-start.1 = ((bf16[8,208,128]{2,1,0:T(8,128)(2,1)}), bf16[8,208,128]{2,1,0:T(8,128)(2,1)S(1)}, u32[]{:S(2)}, u32[]{:S(2)}) async-start(bf16[8,208,128]{2,1,0:T(8,128)(2,1)} %get-tuple-element.18), calls=%async_computation.1 | async-start | bytes 851968 | tf_op jit(solution)/shard_map/all_to_all | solution.py:365

commit v6 on v5

v6 whole, which is shorter than its diff:
```python
import jax
import jax.numpy as jnp
from jax import lax
from jax.experimental import pallas as pl
from jax.experimental.pallas import tpu as pltpu
from jax.sharding import PartitionSpec as P

HD = 128
PAGE = 16
LOWEST = -1e30
EPS = 1e-06
STAT = 8
F32 = jnp.float32
BF16 = jnp.bfloat16
I32 = jnp.int32

VM = pl.BlockSpec(memory_space=pltpu.VMEM)
SM = pl.BlockSpec(memory_space=pltpu.SMEM)
ANY = pl.BlockSpec(memory_space=pl.ANY)
MIB = 1 << 20


def call(kernel, out_shape, in_specs, out_specs, scratch=(), limit=16, flops=0, traffic=0):
    return pl.pallas_call(
        kernel,
        out_shape=out_shape,
        in_specs=in_specs,
        out_specs=out_specs,
        scratch_shapes=list(scratch),
        compiler_params=pltpu.CompilerParams(vmem_limit_bytes=limit * MIB),
        cost_estimate=pl.CostEstimate(flops=flops, bytes_accessed=traffic, transcendentals=0),
    )


def dot(a, b):
    return jnp.dot(a, b, preferred_element_type=F32)


def dot_t(a, b):
    return lax.dot_general(a, b, (((1,), (1,)), ((), ())), preferred_element_type=F32)


def diagonal(shape):
    return lax.broadcasted_iota(I32, shape, 0) == lax.broadcasted_iota(I32, shape, 1)


def column_to_row(column):
    rows = column.shape[0]
    return jnp.sum(jnp.where(diagonal((rows, rows)), column, 0.0), axis=0, keepdims=True)


def row_to_column(row):
    lanes = row.shape[1]
    return jnp.sum(jnp.where(diagonal((lanes, lanes)), row, 0.0), axis=1, keepdims=True)


def squares_of(rows):
    total = jnp.zeros((rows.shape[0], HD), F32)
    for c in range(0, rows.shape[1], HD):
        wide = rows[:, c : c + HD].astype(F32)
        total = total + wide * wide
    return total


def split_three(values):
    high = values.astype(BF16).astype(F32)
    rest = values - high
    middle = rest.astype(BF16).astype(F32)
    return high, middle, rest - middle


def softmax_parts(query, key, value, usable):
    scores = jnp.where(usable, dot_t(query, key) * HD**-0.5, LOWEST)
    top = jnp.max(scores, axis=1, keepdims=True)
    weights = jnp.where(usable, jnp.exp(scores - top), 0.0)
    return dot(weights.astype(BF16), value), top, jnp.sum(weights, axis=1, keepdims=True)


def prepare_kernel(sizes, *refs):
    n, img, tok, blocks, page_cap = sizes
    far, (info, places, slots, square, near), near_weights, rest = refs[:9], refs[9:14], refs[14:16], refs[16:]
    small, (starts, sems) = rest[:5], rest[5:]
    targets = (*small, near.at[:tok], near.at[tok:], *near_weights)
    copies = [pltpu.make_async_copy(a, b, sems.at[i]) for i, (a, b) in enumerate(zip(far, targets))]
    for c in copies:
        c.start()
    route, pages, count, tail, req = small
    for c in copies[: len(small)]:
        c.wait()
    pos = lax.axis_index("section")
    stations = lax.broadcasted_iota(I32, (n, img), 0)
    earlier = lax.broadcasted_iota(I32, (img, img), 0) < lax.broadcasted_iota(I32, (img, img), 1)
    earlier = jnp.where(earlier, 1.0, 0.0).astype(BF16)
    before = jnp.zeros((n, 1), F32)
    place = jnp.zeros((1, img), I32)
    for e in range(n):
        target = route[:, e * img : (e + 1) * img]
        marks = jnp.where(target == stations, 1.0, 0.0)
        prefix = dot(marks.astype(BF16), earlier) + before
        rank = jnp.sum(marks * prefix, axis=0, keepdims=True).astype(I32)
        here = target * tok + rank
        places[:, e * img : (e + 1) * img] = here
        place = jnp.where(pos == e, here, place)
        before = before + jnp.sum(marks, axis=1, keepdims=True)
    mine = lax.broadcasted_iota(I32, (n, 1), 0) == pos
    replaced = jnp.sum(jnp.where(mine, before, 0.0), axis=0, keepdims=True).astype(I32)
    total = jnp.int32(0)
    for r in range(n):
        starts[r] = total
        total = total + count[r]
    inside = lax.broadcasted_iota(I32, (1, tok), 1)
    token = inside + pos * tok
    text_slot = jnp.full((1, tok), -1, I32)
    vis_slot = jnp.full((1, img), -1, I32)
    for b in range(n):
        r = req[b]
        first = starts[r] * PAGE
        last = first + (count[r] - 1) * PAGE + tail[r]
        text_slot = jnp.where((token >= first) & (token < last), b, text_slot)
        vis_slot = jnp.where((place >= first) & (place < last), b, vis_slot)
    info[0:1, :tok] = jnp.where(inside < replaced, -1, text_slot)
    info[1:2, :img] = vis_slot
    for g in range(blocks):
        holder = pages[0, pos * blocks + g]
        slot = holder * page_cap
        for e in range(g):
            slot = slot + (pages[0, pos * blocks + e] == holder).astype(I32)
        slots[g] = slot
    for c in copies[len(small) : len(small) + 2]:
        c.wait()
    square[...] = squares_of(near)
    for c in copies[len(small) + 2 :]:
        c.wait()


def project_kernel(step, near, text_far, vis_far, gain, w_key, w_value, square, kv_text, kv_vis, total):
    tok, half = text_far.shape
    kvw = w_key.shape[1]
    me = lax.axis_index("tensor")
    far = (text_far, vis_far)
    sums = [jnp.sum(square[:tok, :] + squares_of(text_far), axis=1, keepdims=True)]
    sums.append(jnp.sum(square[tok:, :] + squares_of(vis_far), axis=1, keepdims=True))
    scales = [lax.rsqrt(x / (2.0 * half) + EPS) for x in sums]
    for nearby, side in ((True, me), (False, 1 - me)):
        rows = (near.at[:tok], near.at[tok:]) if nearby else far
        for c in range(0, half, step):
            columns = pl.ds(pl.multiple_of(side * half + c, step), step)
            scaled = gain[:, columns]
            normed = jnp.concatenate(
                [(x[:, c : c + step].astype(F32) * s * scaled).astype(BF16) for x, s in zip(rows, scales)], axis=0
            )
            for w, at in ((w_key, 0), (w_value, kvw)):
                part = dot(normed, w[columns, :])
                if nearby and c == 0:
                    total[:, at : at + kvw] = part
                else:
                    total[:, at : at + kvw] += part
    kv_text[...] = total[:tok, :].astype(BF16)
    kv_vis[...] = total[tok:, :].astype(BF16)


def attend_kernel(n, page_cap, kv_heads, slots, info, kv_text, kv_vis, queries, out, own, held):
    pos = lax.axis_index("section")
    tok, img = kv_text.shape[0], kv_vis.shape[0]
    kvw = kv_heads * HD
    chunk = page_cap * PAGE
    halves = 2 * kv_heads
    pages = halves * chunk
    out[:, :pages, :] = jnp.zeros((n, pages, HD), BF16)
    for g in range(tok // PAGE):
        slot = slots[g]
        for h in range(halves):
            at = pl.ds(pl.multiple_of((slot % page_cap) * PAGE + h * chunk, PAGE), PAGE)
            out[slot // page_cap, at, :] = kv_text[g * PAGE : (g + 1) * PAGE, h * HD : (h + 1) * HD]
    rows = queries.shape[0] // n // kv_heads
    slot = lax.broadcasted_iota(I32, (n * rows, 1), 0) // rows
    text_ok = slot == info[0:1, :tok]
    vis_ok = slot == info[1:2, :img]
    tops, totals = [], []
    for g in range(kv_heads):
        at = [(k * kv_heads + g) * rows for k in range(n)]
        query = jnp.concatenate([queries[x : x + rows, :HD] for x in at], axis=0)
        cols = slice(g * HD, (g + 1) * HD)
        vcols = slice(kvw + g * HD, kvw + (g + 1) * HD)
        s_text = jnp.where(text_ok, dot_t(query, kv_text[:, cols]) * HD**-0.5, LOWEST)
        s_vis = jnp.where(vis_ok, dot_t(query, kv_vis[:, cols]) * HD**-0.5, LOWEST)
        top = jnp.maximum(jnp.max(s_text, axis=1, keepdims=True), jnp.max(s_vis, axis=1, keepdims=True))
        w_text = jnp.where(text_ok, jnp.exp(s_text - top), 0.0)
        w_vis = jnp.where(vis_ok, jnp.exp(s_vis - top), 0.0)
        weight = jnp.sum(w_text, axis=1, keepdims=True) + jnp.sum(w_vis, axis=1, keepdims=True)
        numerator = dot(w_text.astype(BF16), kv_text[:, vcols]) + dot(w_vis.astype(BF16), kv_vis[:, vcols])
        held[g * n * rows : (g + 1) * n * rows, :] = numerator
        own[g * rows : (g + 1) * rows, :] = held[pl.ds(pl.multiple_of((g * n + pos) * rows, rows), rows), :]
        numerator = numerator.astype(BF16)
        for k in range(n):
            out[k, pages + g * rows : pages + (g + 1) * rows, :] = numerator[k * rows : (k + 1) * rows, :]
        tops.append(top)
        totals.append(weight)
    line = lax.broadcasted_iota(I32, (PAGE, HD), 0)
    for k in range(n):
        at = slice(k * rows, (k + 1) * rows)
        stats = column_to_row(jnp.concatenate([x[at] for x in tops + totals], axis=0))

        @pl.when(pos == k)
        def _():
            own[kv_heads * rows :, :] = jnp.broadcast_to(stats, (STAT, stats.shape[1]))

        high, middle, low = split_three(stats)
        lines = jnp.where(line == 0, high, jnp.where(line == 1, middle, jnp.where(line == 2, low, 0.0)))
        out[k, pages + kv_heads * rows :, :] = lines.astype(BF16)


def place_kernel(n, blocks, page_cap, pages, places, vis, token, placed):
    pos = lax.axis_index("section")
    lanes = n * blocks
    here = pages[...] == pos
    ones = jnp.where(here, 1.0, 0.0)
    first = lax.broadcasted_iota(I32, (lanes, lanes), 0)
    second = lax.broadcasted_iota(I32, (lanes, lanes), 1)
    earlier = (first < second) & (first // blocks == second // blocks)
    rank = dot(jnp.broadcast_to(ones, (STAT, lanes)).astype(BF16), jnp.where(earlier, 1.0, 0.0).astype(BF16))
    page = lax.broadcasted_iota(I32, (1, lanes), 1)
    slot = jnp.where(here, page // blocks * page_cap + rank[0:1].astype(I32), -1)
    rows = n * page_cap * PAGE
    row = lax.broadcasted_iota(I32, (rows, 1), 0)
    found = jnp.max(jnp.where(row // PAGE == slot, page, -1), axis=1, keepdims=True)
    at = jnp.where(found < 0, -1, found * PAGE + row % PAGE)
    hot = jnp.where(at == places[...], 1.0, 0.0)
    covered = jnp.sum(hot, axis=1, keepdims=True)
    token[...] = jnp.broadcast_to(covered, token.shape)
    placed[...] = dot(hot.astype(BF16), vis[...]).astype(BF16)


def combine(pieces, highest):
    numerator, total = 0.0, 0.0
    for rows, top, weight in pieces:
        scale = jnp.exp(top - highest)
        numerator = numerator + rows * scale
        total = total + weight * scale
    return numerator, total


def fresh_kernel(kv_heads, steps, query, key, value, own, mine):
    rows = query.shape[0] // kv_heads
    every = kv_heads * rows
    row = lax.broadcasted_iota(I32, (rows, steps), 0)
    causal = lax.broadcasted_iota(I32, (rows, steps), 1) <= row % steps
    stats = row_to_column(own[every : every + 1, :])
    tops, totals = [], []
    for g in range(kv_heads):
        cols = slice(g * HD, (g + 1) * HD)
        at = slice(g * rows, (g + 1) * rows)
        fresh = softmax_parts(query[at, :], key[:, cols], value[:, cols], causal)
        share = (own[at, :], stats[at], stats[every + g * rows : every + (g + 1) * rows])
        highest = jnp.maximum(fresh[1], share[1])
        numerator, total = combine((fresh, share), highest)
        mine[at, :] = numerator
        tops.append(highest)
        totals.append(total)
    line = column_to_row(jnp.concatenate(tops + totals, axis=0))
    mine[every:, :] = jnp.broadcast_to(line, (STAT, line.shape[1]))


def finish_kernel(steps, page_cap, shares, mine, covered, placed, attended, keys, values):
    n = shares.shape[0]
    pos = lax.axis_index("section")
    rows = mine.shape[0] - STAT
    chunk = page_cap * PAGE
    halves = keys.shape[2] // HD
    for k in range(n):
        at = slice(k * chunk, (k + 1) * chunk)
        inserted = covered[at, :] > 0.0
        for i, out in enumerate((keys, values)):
            for h in range(halves):
                part = i * halves + h
                text = shares[k, part * chunk : (part + 1) * chunk, :].astype(F32)
                image = placed[at, part * HD : (part + 1) * HD].astype(F32)
                out[k, :, h * HD : (h + 1) * HD] = jnp.where(inserted, image, text).astype(BF16)
    pages = 2 * halves * chunk
    stats = row_to_column(mine[rows : rows + 1, :])
    pieces = [(mine[:rows, :], stats[:rows], stats[rows:])]
    for k in range(n):
        lines = shares[k, pages + rows :, :].astype(F32)
        stats = row_to_column(lines[0:1] + lines[1:2] + lines[2:3])
        away = pos != k
        top = jnp.where(away, stats[:rows], LOWEST)
        weight = jnp.where(away, stats[rows:], 0.0)
        pieces.append((jnp.where(away, shares[k, pages : pages + rows, :].astype(F32), 0.0), top, weight))
    highest = pieces[0][1]
    for p in pieces[1:]:
        highest = jnp.maximum(highest, p[1])
    numerator, total = combine(pieces, highest)
    result = (numerator / total).astype(BF16)
    for h in range(rows // steps):
        attended[0, :, h * HD : (h + 1) * HD] = result[h * steps : (h + 1) * steps, :]


def body(
    text_rows,
    vis_rows,
    img_route,
    norm_gain,
    w_key,
    w_value,
    page_count,
    tail_len,
    page_dest,
    dec_req,
    dec_query,
    dec_key,
    dec_value,
):
    n = lax.axis_size("section")
    tok, half = text_rows.shape
    img = vis_rows.shape[0]
    kvw = w_key.shape[1]
    kv_heads = kvw // HD
    _, steps, q_width = dec_query.shape
    heads = q_width // HD
    q_rows = heads * steps
    blocks = tok // PAGE
    cap = max(2, (2 * img + n - 1) // n)
    page_cap = max(1, (blocks + n - 1) // n)

    def across(array):
        return lax.ppermute(array, "tensor", [(0, 1), (1, 0)])

    def exchange(array):
        return lax.all_to_all(array, "section", split_axis=0, concat_axis=0, tiled=True)

    def remote(array):
        return pltpu.with_memory_space_constraint(array, pltpu.HBM)

    def local(array):
        return pltpu.with_memory_space_constraint(array, pltpu.VMEM)

    vis_far = across(vis_rows)
    text_far = across(text_rows)
    query = dec_query.reshape(steps, heads, HD).transpose(1, 0, 2).reshape(q_rows, HD)

    def gathered(array):
        return lax.all_gather(array, "section", axis=0, tiled=True)

    queries = gathered(jnp.pad(query, ((0, 0), (0, 2 * kvw - HD))))
    routes, page_row = img_route.T, page_dest.T
    arguments = (routes, page_row, page_count, tail_len, dec_req, text_rows, vis_rows, w_key, w_value)
    info, places, slots, square, near, key_near, value_near = call(
        lambda *refs: prepare_kernel((n, img, tok, blocks, page_cap), *refs),
        (
            jax.ShapeDtypeStruct((8, max(tok, img)), I32),
            jax.ShapeDtypeStruct((1, n * img), I32),
            jax.ShapeDtypeStruct((blocks,), I32),
            jax.ShapeDtypeStruct((tok + img, HD), F32),
            pltpu.VMEM((tok + img, half), BF16),
            pltpu.VMEM(w_key.shape, BF16),
            pltpu.VMEM(w_value.shape, BF16),
        ),
        [ANY] * len(arguments),
        (VM, VM, SM) + (VM,) * 4,
        [
            *[(pltpu.VMEM if i == 0 else pltpu.SMEM)(a.shape, a.dtype) for i, a in enumerate(arguments[:5])],
            pltpu.SMEM((n,), I32),
            pltpu.SemaphoreType.DMA((len(arguments),)),
        ],
        flops=1 << 20,
        traffic=2 * 2 * half * 2 * kvw * 2,
    )(*[remote(a) for a in arguments])

    kv_text, kv_vis = call(
        lambda *refs: project_kernel(min(1024, half), *refs),
        (
            jax.ShapeDtypeStruct((tok, 2 * kvw), BF16),
            jax.ShapeDtypeStruct((img, 2 * kvw), BF16),
        ),
        [VM] * 7,
        (VM, VM),
        [pltpu.VMEM((tok + img, 2 * kvw), F32)],
        flops=2 * (tok + img) * 2 * half * 2 * kvw,
        traffic=2 * (tok + img) * 2 * half + 8 * half * kvw,
    )(
        local(near),
        text_far,
        vis_far,
        remote(norm_gain.reshape(1, 2 * half)),
        local(key_near),
        local(value_near),
        square,
    )
    vis_all = gathered(kv_vis)

    sent, own = call(
        lambda *refs: attend_kernel(n, page_cap, kv_heads, *refs),
        (
            jax.ShapeDtypeStruct((n, page_cap * PAGE * 2 * kv_heads + q_rows + PAGE, HD), BF16),
            jax.ShapeDtypeStruct((q_rows + STAT, HD), F32),
        ),
        [SM] + [VM] * 4,
        (VM, VM),
        [pltpu.VMEM((n * q_rows, HD), F32)],
        limit=24,
        flops=4 * n * q_rows * tok * HD,
        traffic=n * (q_rows + STAT) * HD * 4,
    )(slots, info, kv_text, kv_vis, queries)
    shares = exchange(sent)

    mine = call(
        lambda *refs: fresh_kernel(kv_heads, steps, *refs),
        jax.ShapeDtypeStruct((q_rows + STAT, HD), F32),
        [VM] * 4,
        VM,
        flops=1 << 20,
        traffic=1 << 18,
    )(remote(query), remote(dec_key[0]), remote(dec_value[0]), own)

    rows = n * page_cap * PAGE
    covered, placed = call(
        lambda *refs: place_kernel(n, blocks, page_cap, *refs),
        (jax.ShapeDtypeStruct((rows, HD), F32), jax.ShapeDtypeStruct((rows, 2 * kvw), BF16)),
        [VM] * 3,
        (VM, VM),
        limit=32,
        flops=2 * rows * n * img * 2 * kvw,
        traffic=2 * n * img * 2 * kvw,
    )(remote(page_row), places, vis_all)

    attended, cache_key, cache_value = call(
        lambda *refs: finish_kernel(steps, page_cap, *refs),
        (
            jax.ShapeDtypeStruct(dec_query.shape, BF16),
            jax.ShapeDtypeStruct((n, page_cap * PAGE, kvw), BF16),
            jax.ShapeDtypeStruct((n, page_cap * PAGE, kvw), BF16),
        ),
        [VM] * 4,
        (VM, VM, VM),
        traffic=4 * tok * 2 * kvw,
    )(shares, mine, covered, placed)
    slots_here = n * page_cap
    return (
        attended,
        cache_key.reshape(slots_here, PAGE, kvw),
        cache_value.reshape(slots_here, PAGE, kvw),
    )


def solution(mesh):
    return jax.shard_map(
        body,
        mesh=mesh,
        in_specs=(
            P(("groups", "section"), "tensor"),
            P(("groups", "section"), "tensor"),
            P("groups", None),
            P(),
            P(None, "tensor"),
            P(None, "tensor"),
            P("groups"),
            P("groups"),
            P("groups", None),
            P("groups"),
            P(("groups", "section"), None, "tensor"),
            P(("groups", "section"), None, "tensor"),
            P(("groups", "section"), None, "tensor"),
        ),
        out_specs=(
            P(("groups", "section"), None, "tensor"),
            P(("groups", "section"), None, "tensor"),
            P(("groups", "section"), None, "tensor"),
        ),
        check_vma=False,
    )
```

time: 46.1 us -> 90 us (1.95)
  blocking collectives: 0 us -> 66.6 us
  waiting for transfers between devices: 14.9 us -> 0.01 us
  starting transfers between devices: 11.4 us -> 6.16 us
  Pallas kernels: 18.6 us -> 15.4 us
    all_gather x0 -> x2, blocking collectives: none -> 66.6 us  [gathered(): return lax.all_gather(array, 'section', axis=0, tiled=True)]
    all_to_all x2 -> x1, waiting for transfers between devices: 14.4 us -> 0.01 us  [exchange(): lax.all_to_all(array, 'section', split_axis=0, concat_axis=0, tiled=True)]
    all_to_all x2 -> x1, starting transfers between devices: 10.8 us -> 5.56 us  [exchange(): lax.all_to_all(array, 'section', split_axis=0, concat_axis=0, tiled=True)]
    pallas_call x4, Pallas kernels: 16 us -> 13.1 us  [the longest x1 4.86 us: body(): call(lambda *refs: prepare_kernel((n, img, tok, blocks, page_cap), *refs)...]
  transfers between devices with their start and end apart: 4 -> 3, of which waited for: 3 -> 0; matrix products, arithmetic and copies ran while one was open for 0% -> 1% of each run, Pallas kernels for 32% -> 8%
where the time goes in v6:
time: 90 us; the launch traced here: 89.6 us
  blocking collectives  66.6 us (74%)
  Pallas kernels  15.4 us (17%)
  starting transfers between devices  6.16 us (7%)
    all_gather x2, blocking collectives, gathered(): return lax.all_gather(array, 'section', axis=0, tiled=True)  66.6 us
    all_to_all x1, starting transfers between devices, exchange(): lax.all_to_all(array, 'section', split_axis=0, concat_axis=0, tiled=True)  5.56 us
    pallas_call x1, Pallas kernels, body(): call(lambda *refs: prepare_kernel((n, img, tok, blocks, page_cap), *refs)...  4.86 us
    pallas_call x1, Pallas kernels, body(): call(lambda *refs: project_kernel(min(1024, half), *refs), (jax.ShapeDtyp...  4.15 us
    pallas_call x1, Pallas kernels, body(): call(lambda *refs: attend_kernel(n, page_cap, kv_heads, *refs), (jax.Shap...  2.85 us
  transfers between devices with their start and end apart: 3, of which 0 were waited for; matrix products, arithmetic and copies ran while one was open for 1% of the time, Pallas kernels for 8%

profile of v6, /device:TPU:0, one launch (start us, length us, event | category | flops | bytes accessed | tf_op | source)
XLA Modules:
  0.0 89.6 jit_solution(10148306788906820672)
XLA Ops:
  0.6 0.5 collective-permute-start
  1.1 0.1 collective-permute-start.1
  1.2 0.7 pad.4
  2.0 4.9 %shard_map.148 = (s32[8,256]{1,0:T(8,128)S(1)}, s32[1,512]{1,0:T(1,128)S(1)}, s32[16]{0:T(128)S(1)}, f32[320,128]{1,0:T(8,128)S(1)}, bf16[320,4096]{1,0:T(8,128)...) custom-call(s32[1,512]{1,0:T(1,128)} %bitcast.15, s32[1,128]{1,0:T(1,128)} %bitcast.16, ...), custom_call_target="tpu_custom_call" | custom-call | flops 1048576 | bytes 16777216 | tf_op jit(solution)/shard_map/pallas_call | solution.py:347
  6.8 33.1 %all_gather.6.refs_4_ = bf16[512,512]{1,0:T(8,128)(2,1)S(1)} all-gather(bf16[64,512]{1,0:T(8,128)(2,1)S(1)} %pad.4), channel_id=1, replica_groups=mesh['groups'=2,'section'=8,'tensor'=2] {'section'}, dimensions={0}, use_global_device_ids=true | all-gather | bytes 589824 | tf_op jit(solution)/shard_map/all_gather | solution.py:342
  40.0 0.0 collective-permute-done.1.refs_2_
  40.0 0.0 collective-permute-done.refs_1_
  40.0 4.1 %shard_map.149 = (bf16[256,512]{1,0:T(8,128)(2,1)S(1)}, bf16[64,512]{1,0:T(8,128)(2,1)S(1)}) custom-call(bf16[320,4096]{1,0:T(8,128)(2,1)S(1)} %get-tuple-element.21.refs_0_, bf16[256,4096]{1,0:T(8,128)(2,1)S(1)} %collective-permute-done.refs_1_, bf16[64,4096]{1,0:T(8,128)(2,1)S(1)} %collective-permute-done.1.refs_2_, f32[1,8192]{1,0:T(1,128)} %bitcast.14, ...), custom_call_target="tpu_custom_call" | custom-call | flops 2684354560 | bytes 13631488 | tf_op jit(solution)/shard_map/pallas_call | solution.py:369
  44.1 2.8 %shard_map.150 = (bf16[8,208,128]{2,1,0:T(8,128)(2,1)}, f32[72,128]{1,0:T(8,128)S(1)}) custom-call(s32[16]{0:T(128)S(1)} %get-tuple-element.19.refs_0_, s32[8,256]{1,0:T(8,128)S(1)} %get-tuple-element.20.refs_1_, bf16[256,512]{1,0:T(8,128)(2,1)S(1)} %get-tuple-element.25.refs_2_, bf16[64,512]{1,0:T(8,128)(2,1)S(1)} %get-tuple-element.26.refs_3_, ...), custom_call_target="tpu_custom_call" | custom-call | flops 67108864 | bytes 294912 | tf_op jit(solution)/shard_map/pallas_call | solution.py:391
  47.0 5.6 %all-to-all-start = ((bf16[8,208,128]{2,1,0:T(8,128)(2,1)}), bf16[8,208,128]{2,1,0:T(8,128)(2,1)S(1)}, u32[]{:S(2)}, u32[]{:S(2)}) async-start(bf16[8,208,128]{2,1,0:T(8,128)(2,1)} %get-tuple-element.27), calls=%async_computation | async-start | bytes 851968 | tf_op jit(solution)/shard_map/all_to_all | solution.py:329
  52.5 1.3 %shard_map.151.refs_1_ = f32[72,128]{1,0:T(8,128)S(1)} custom-call(bf16[64,128]{1,0:T(8,128)(2,1)} %bitcast.13, bf16[4,256]{1,0:T(4,128)(2,1)} %bitcast.18, bf16[4,256]{1,0:T(4,128)(2,1)} %bitcast.19, f32[72,128]{1,0:T(8,128)S(1)} %get-tuple-element.28.refs_3_), custom_call_target="tpu_custom_call" | custom-call | flops 1048576 | bytes 262144 | tf_op jit(solution)/shard_map/pallas_call | solution.py:406
  53.8 33.5 %all_gather.7.refs_2_ = bf16[512,512]{1,0:T(8,128)(2,1)S(1)} all-gather(bf16[64,512]{1,0:T(8,128)(2,1)S(1)} %get-tuple-element.26.refs_3_), channel_id=1, replica_groups=mesh['groups'=2,'section'=8,'tensor'=2] {'section'}, dimensions={0}, use_global_device_ids=true | all-gather | bytes 589824 | tf_op jit(solution)/shard_map/all_gather | solution.py:342
  87.3 1.3 %shard_map.152 = (f32[256,128]{1,0:T(8,128)S(1)}, bf16[256,512]{1,0:T(8,128)(2,1)S(1)}) custom-call(s32[1,128]{1,0:T(1,128)} %bitcast.17, s32[1,512]{1,0:T(1,128)S(1)} %get-tuple-element.29.refs_1_, bf16[512,512]{1,0:T(8,128)(2,1)S(1)} %all_gather.7.refs_2_), custom_call_target="tpu_custom_call" | custom-call | flops 134217728 | bytes 524288 | tf_op jit(solution)/shard_map/pallas_call | solution.py:416
  88.6 0.0 all-to-all-done.refs_0_
  88.6 1.0 %shard_map.153 = (bf16[1,4,2048]{2,1,0:T(4,128)(2,1)}, bf16[8,32,256]{2,1,0:T(8,128)(2,1)}, bf16[8,32,256]{2,1,0:T(8,128)(2,1)}) custom-call(bf16[8,208,128]{2,1,0:T(8,128)(2,1)S(1)} %all-to-all-done.refs_0_, f32[72,128]{1,0:T(8,128)S(1)} %shard_map.151.refs_1_, f32[256,128]{1,0:T(8,128)S(1)} %get-tuple-element.30.refs_2_, ...), custom_call_target="tpu_custom_call" | custom-call | bytes 524288 | tf_op jit(solution)/shard_map/pallas_call | solution.py:426
Async XLA Ops:
  0.6 39.3 %collective-permute-start = (bf16[256,4096]{1,0:T(8,128)(2,1)}, bf16[256,4096]{1,0:T(8,128)(2,1)S(1)}, u32[]{:S(2)}, u32[]{:S(2)}) collective-permute-start(bf16[256,4096]{1,0:T(8,128)(2,1)} %refs_5_.1), channel_id=1, source_target_pairs={{0,1},{1,0},{2,3},{3,2},{4,5},{5,4},{6,7},{7,6},{8,9},{9,8},{10,11... | collective-permute-start | bytes 6291464 | tf_op jit(solution)/shard_map/ppermute | solution.py:326
  1.1 38.8 %collective-permute-start.1 = (bf16[64,4096]{1,0:T(8,128)(2,1)}, bf16[64,4096]{1,0:T(8,128)(2,1)S(1)}, u32[]{:S(2)}, u32[]{:S(2)}) collective-permute-start(bf16[64,4096]{1,0:T(8,128)(2,1)} %refs_6_.1), channel_id=1, source_target_pairs={{0,1},{1,0},{2,3},{3,2},{4,5},{5,4},{6,7},{7,6},{8,9},{9,8},{10,11... | collective-permute-start | bytes 1572872 | tf_op jit(solution)/shard_map/ppermute | solution.py:326
  47.0 41.6 %all-to-all-start = ((bf16[8,208,128]{2,1,0:T(8,128)(2,1)}), bf16[8,208,128]{2,1,0:T(8,128)(2,1)S(1)}, u32[]{:S(2)}, u32[]{:S(2)}) async-start(bf16[8,208,128]{2,1,0:T(8,128)(2,1)} %get-tuple-element.27), calls=%async_computation | async-start | bytes 851968 | tf_op jit(solution)/shard_map/all_to_all | solution.py:329

commit v7 on v5

--- a/solution.py
+++ b/solution.py
@@ -79,7 +79,10 @@
 def prepare_kernel(sizes, *refs):
     n, img, tok, blocks, lot, page_cap = sizes
     far, (info, slots), near, small, (starts, sems) = refs[:8], refs[8:10], refs[10:13], refs[13:18], refs[18:]
-    copies = [pltpu.make_async_copy(a, b, sems.at[i]) for i, (a, b) in enumerate(zip(far, small + near))]
+    half = near[0].shape[0]
+    mine = pl.ds(pl.multiple_of(lax.axis_index("tensor") * half, half), half)
+    sources = (*far[:5], far[5].at[mine], far[6].at[mine], far[7])
+    copies = [pltpu.make_async_copy(a, b, sems.at[i]) for i, (a, b) in enumerate(zip(sources, small + near))]
     for c in copies:
         c.start()
     route, pages, count, tail, req = small
@@ -145,17 +148,26 @@
         total[:, columns] += part
 
 
-def vis_kernel(n, lot, step, near, far, gain, w_key, w_value, info, query, out, total):
+def vis_kernel(n, lot, step, *refs):
+    near, far, gain, key_near, value_near, w_key, w_value, info, query, out, key_far, value_far, total, sems = refs
     img, half = near.shape
     kvw = w_key.shape[1]
     me = lax.axis_index("tensor")
+    other = pl.ds(pl.multiple_of((1 - me) * half, half), half)
+    pairs = ((w_key, key_far), (w_value, value_far))
+    copies = [pltpu.make_async_copy(w.at[other], held, sems.at[i]) for i, (w, held) in enumerate(pairs)]
+    for c in copies:
+        c.start()
     scale = scale_of(near, far)
-    for rows, side in ((near, me), (far, 1 - me)):
+    for rows, side, weights in ((near, me, (key_near, value_near)), (far, 1 - me, (key_far, value_far))):
+        if rows is far:
+            for c in copies:
+                c.wait()
         for c in range(0, half, step):
             columns = pl.ds(pl.multiple_of(side * half + c, step), step)
             normed = normed_rows(rows, c, step, scale, gain[:, columns])
-            for w, at in ((w_key, 0), (w_value, kvw)):
-                add_part(total, at, normed, w[columns, :], rows is near and c == 0)
+            for w, at in zip(weights, (0, kvw)):
+                add_part(total, at, normed, w[c : c + step, :], rows is near and c == 0)
     slot = lax.broadcasted_iota(I32, (n * lot, img), 0)
     chosen = jnp.where(slot == info[0:1, :img], 1.0, 0.0).astype(BF16)
     packed = dot(chosen, total[...].astype(BF16)).astype(BF16)
@@ -166,7 +178,15 @@
         out[k, q_lots:, :] = packed[k * lot : (k + 1) * lot, :]
 
 
-def text_kernel(load, step, near_far, far, gain, w_key_far, w_value_far, out, near, w_key, w_value, total, sems):
+def put_page(out, page_cap, slot, rows):
+    chunk = page_cap * PAGE
+    for h in range(rows.shape[1] // HD):
+        at = pl.ds(pl.multiple_of((slot % page_cap) * PAGE + h * chunk, PAGE), PAGE)
+        out[slot // page_cap, at, :] = rows[:, h * HD : (h + 1) * HD]
+
+
+def text_kernel(load, step, page_cap, q_rows, *refs):
+    near_far, far, gain, w_key_far, w_value_far, info, slots, out, bias, base, near, w_key, w_value, total, sems = refs
     half = near.shape[1]
     kvw = w_key.shape[1]
     me = lax.axis_index("tensor")
@@ -199,9 +219,16 @@
             for w, col in ((w_key, 0), (w_value, kvw)):
                 add_part(total, col, normed, w[at : at + step, :], at == 0)
     out[...] = total[...].astype(BF16)
-
-
-def attend_kernel(n, cap, lot, page_cap, kv_heads, slots, info, kv_text, arrived, out, own, kv, held):
+    base[...] = jnp.zeros(base.shape, BF16)
+    tok = near.shape[0]
+    for g in range(tok // PAGE):
+        put_page(base, page_cap, slots[g], out[g * PAGE : (g + 1) * PAGE, :])
+    token_slot = row_to_column(info[1:2, :tok].astype(F32))
+    lanes = lax.broadcasted_iota(I32, bias.shape, 1) // q_rows
+    bias[...] = jnp.where(token_slot == lanes.astype(F32), 0.0, LOWEST)
+
+
+def attend_kernel(n, cap, lot, page_cap, kv_heads, slots, info, kv_text, arrived, bias, base, out, own, mixed, held, rows_held):
     pos = lax.axis_index("section")
     tok = kv_text.shape[0]
     kvw = kv_heads * HD
@@ -212,23 +239,13 @@
     covered = jnp.sum(hot, axis=1, keepdims=True) > 0.0
     incoming = jnp.concatenate([arrived[k, q_lots:, :] for k in range(n)], axis=0)
     placed = dot(hot.astype(BF16), incoming)
-    kv[:reach, :] = jnp.where(covered, placed, kv_text[:reach, :].astype(F32)).astype(BF16)
-    if reach < tok:
-        kv[reach:, :] = kv_text[reach:, :]
-    chunk = page_cap * PAGE
-    halves = 2 * kv_heads
-    pages = halves * chunk
-    out[:, :pages, :] = jnp.zeros((n, pages, HD), BF16)
-    for g in range(tok // PAGE):
-        slot = slots[g]
-        for h in range(halves):
-            at = pl.ds(pl.multiple_of((slot % page_cap) * PAGE + h * chunk, PAGE), PAGE)
-            out[slot // page_cap, at, :] = kv[g * PAGE : (g + 1) * PAGE, h * HD : (h + 1) * HD]
+    mixed[...] = jnp.where(covered, placed, kv_text[:reach, :].astype(F32)).astype(BF16)
     groups = arrived.shape[2] // HD // kv_heads
     rows = groups * q_lots
-    slot = lax.broadcasted_iota(I32, (n * rows, 1), 0) // rows
-    usable = slot == info[1:2, :tok]
-    tops, totals = [], []
+    pages = base.shape[1]
+    out[:, :pages, :] = base[...]
+    for g in range(reach // PAGE):
+        put_page(out, page_cap, slots[g], mixed[g * PAGE : (g + 1) * PAGE, :])
     for g in range(kv_heads):
         query = jnp.concatenate(
             [
@@ -238,28 +255,39 @@
             ],
             axis=0,
         )
-        key = kv[:, g * HD : (g + 1) * HD]
-        value = kv[:, kvw + g * HD : kvw + (g + 1) * HD]
-        numerator, top, weight = softmax_parts(query, key, value, usable)
+        cols = slice(g * HD, (g + 1) * HD)
+        vcols = slice(kvw + g * HD, kvw + (g + 1) * HD)
+        key = jnp.concatenate([mixed[:, cols], kv_text[reach:, cols]], axis=0)
+        value = jnp.concatenate([mixed[:, vcols], kv_text[reach:, vcols]], axis=0)
+        scores = dot_t(key, query) * HD**-0.5 + bias[...]
+        top = jnp.max(scores, axis=0, keepdims=True)
+        weights = jnp.exp(scores - top)
+        rows_held[g : g + 1, :] = top
+        rows_held[kv_heads + g : kv_heads + g + 1, :] = jnp.sum(weights, axis=0, keepdims=True)
+        numerator = lax.dot_general(
+            weights.astype(BF16), value, (((0,), (0,)), ((), ())), preferred_element_type=F32
+        )
         held[g * n * rows : (g + 1) * n * rows, :] = numerator
         own[g * rows : (g + 1) * rows, :] = held[pl.ds(pl.multiple_of((g * n + pos) * rows, rows), rows), :]
         numerator = numerator.astype(BF16)
         for k in range(n):
             out[k, pages + g * rows : pages + (g + 1) * rows, :] = numerator[k * rows : (k + 1) * rows, :]
-        tops.append(top)
-        totals.append(weight)
-    line = lax.broadcasted_iota(I32, (PAGE, HD), 0)
-    for k in range(n):
-        at = slice(k * rows, (k + 1) * rows)
-        stats = column_to_row(jnp.concatenate([x[at] for x in tops + totals], axis=0))
-
-        @pl.when(pos == k)
-        def _():
-            own[kv_heads * rows :, :] = jnp.broadcast_to(stats, (STAT, stats.shape[1]))
-
-        high, middle, low = split_three(stats)
-        lines = jnp.where(line == 0, high, jnp.where(line == 1, middle, jnp.where(line == 2, low, 0.0)))
-        out[k, pages + kv_heads * rows :, :] = lines.astype(BF16)
+    stat_rows = 2 * kv_heads
+    share = HD // rows
+    window = pl.ds(pl.multiple_of(pos // share * HD, HD), HD)
+    own[kv_heads * rows : kv_heads * rows + stat_rows, :] = rows_held[:stat_rows, window]
+    blank = jnp.zeros((PAGE - 3 * stat_rows, HD), F32)
+    for w in range(-(-n // share)):
+        stats = rows_held[:stat_rows, w * HD : (w + 1) * HD]
+        lines = jnp.concatenate([*split_three(stats), blank], axis=0).astype(BF16)
+        for k in range(w * share, min(n, (w + 1) * share)):
+            out[k, pages + kv_heads * rows :, :] = lines
+
+
+def pick_column(row, rows, start):
+    shape = (rows, HD)
+    chosen = lax.broadcasted_iota(I32, shape, 1) == lax.broadcasted_iota(I32, shape, 0) + start
+    return jnp.sum(jnp.where(chosen, row, 0.0), axis=1, keepdims=True)
 
 
 def combine(pieces, highest):
@@ -274,15 +302,19 @@
 def fresh_kernel(kv_heads, steps, query, key, value, own, mine):
     rows = query.shape[0] // kv_heads
     every = kv_heads * rows
+    start = lax.axis_index("section") % (HD // rows) * rows
     row = lax.broadcasted_iota(I32, (rows, steps), 0)
     causal = lax.broadcasted_iota(I32, (rows, steps), 1) <= row % steps
-    stats = row_to_column(own[every : every + 1, :])
     tops, totals = [], []
     for g in range(kv_heads):
         cols = slice(g * HD, (g + 1) * HD)
         at = slice(g * rows, (g + 1) * rows)
         fresh = softmax_parts(query[at, :], key[:, cols], value[:, cols], causal)
-        share = (own[at, :], stats[at], stats[every + g * rows : every + (g + 1) * rows])
+        share = (
+            own[at, :],
+            pick_column(own[every + g : every + g + 1, :], rows, start),
+            pick_column(own[every + kv_heads + g : every + kv_heads + g + 1, :], rows, start),
+        )
         highest = jnp.maximum(fresh[1], share[1])
         numerator, total = combine((fresh, share), highest)
         mine[at, :] = numerator
@@ -292,43 +324,43 @@
     mine[every:, :] = jnp.broadcast_to(line, (STAT, line.shape[1]))
 
 
-def finish_kernel(steps, page_cap, shares, mine, attended, keys, values, sems):
+def finish_kernel(kv_heads, steps, page_cap, shares, mine, attended, keys, values):
     n = shares.shape[0]
     pos = lax.axis_index("section")
-    rows = mine.shape[0] - STAT
+    every = mine.shape[0] - STAT
+    rows = every // kv_heads
+    start = pos % (HD // rows) * rows
     chunk = page_cap * PAGE
-    copies = []
-    for i, out in enumerate((keys, values)):
-        for h in range(out.shape[2] // HD):
-            at = len(copies)
-            copies.append(
-                pltpu.make_async_copy(
-                    shares.at[:, at * chunk : (at + 1) * chunk, :],
-                    out.at[:, :, h * HD : (h + 1) * HD],
-                    sems.at[at],
-                )
-            )
-    for c in copies:
-        c.start()
-    pages = len(copies) * chunk
-    stats = row_to_column(mine[rows : rows + 1, :])
-    pieces = [(mine[:rows, :], stats[:rows], stats[rows:])]
+    halves = keys.shape[2] // HD
     for k in range(n):
-        lines = shares[k, pages + rows :, :].astype(F32)
-        stats = row_to_column(lines[0:1] + lines[1:2] + lines[2:3])
-        away = pos != k
-        top = jnp.where(away, stats[:rows], LOWEST)
-        weight = jnp.where(away, stats[rows:], 0.0)
-        pieces.append((jnp.where(away, shares[k, pages : pages + rows, :].astype(F32), 0.0), top, weight))
-    highest = pieces[0][1]
-    for p in pieces[1:]:
-        highest = jnp.maximum(highest, p[1])
-    numerator, total = combine(pieces, highest)
-    result = (numerator / total).astype(BF16)
-    for h in range(rows // steps):
-        attended[0, :, h * HD : (h + 1) * HD] = result[h * steps : (h + 1) * steps, :]
-    for c in copies:
-        c.wait()
+        for i, out in enumerate((keys, values)):
+            for h in range(halves):
+                part = i * halves + h
+                out[k, :, h * HD : (h + 1) * HD] = shares[k, part * chunk : (part + 1) * chunk, :]
+    pages = 2 * halves * chunk
+    stats = row_to_column(mine[every : every + 1, :])
+    lines = []
+    for k in range(n):
+        three = shares[k, pages + every :, :].astype(F32)
+        size = 2 * kv_heads
+        lines.append(three[:size] + three[size : 2 * size] + three[2 * size : 3 * size])
+    for g in range(kv_heads):
+        at = slice(g * rows, (g + 1) * rows)
+        pieces = [(mine[at, :], stats[at], stats[every + g * rows : every + (g + 1) * rows])]
+        for k in range(n):
+            away = pos != k
+            top = jnp.where(away, pick_column(lines[k][g : g + 1], rows, start), LOWEST)
+            weight = jnp.where(away, pick_column(lines[k][kv_heads + g : kv_heads + g + 1], rows, start), 0.0)
+            share = shares[k, pages + g * rows : pages + (g + 1) * rows, :].astype(F32)
+            pieces.append((share, top, weight))
+        highest = pieces[0][1]
+        for p in pieces[1:]:
+            highest = jnp.maximum(highest, p[1])
+        numerator, total = combine(pieces, highest)
+        result = (numerator / total).astype(BF16)
+        for h in range(rows // steps):
+            to = (g * rows // steps + h) * HD
+            attended[0, :, to : to + HD] = result[h * steps : (h + 1) * steps, :]
 
 
 def body(
@@ -383,7 +415,9 @@
         (
             jax.ShapeDtypeStruct((8, width), I32),
             jax.ShapeDtypeStruct((blocks,), I32),
-            *[pltpu.VMEM(a.shape, a.dtype) for a in arguments[5:]],
+            pltpu.VMEM((half, kvw), BF16),
+            pltpu.VMEM((half, kvw), BF16),
+            pltpu.VMEM(vis_rows.shape, BF16),
         ),
         [ANY] * len(arguments),
         (VM, SM) + (VM,) * 3,
@@ -403,19 +437,39 @@
     packed = call(
         lambda *refs: vis_kernel(n, lot, step, *refs),
         jax.ShapeDtypeStruct((n, q_lots + lot, 2 * kvw), BF16),
-        [VM] * 7,
+        [VM] * 5 + [ANY] * 2 + [VM] * 2,
         VM,
-        [pltpu.VMEM((img, 2 * kvw), F32)],
-        flops=2 * img * 2 * half * 2 * kvw,
+        [
+            pltpu.VMEM((half, kvw), BF16),
+            pltpu.VMEM((half, kvw), BF16),
+            pltpu.VMEM((img, 2 * kvw), F32),
+            pltpu.SemaphoreType.DMA((2,)),
+        ],
+        flops=64 * img * 2 * half * 2 * kvw,
         traffic=2 * img * 2 * half + 8 * half * kvw,
-    )(local(vis_near), vis_far, gain, local(key_near), local(value_near), info, remote(query))
+    )(
+        local(vis_near),
+        vis_far,
+        gain,
+        local(key_near),
+        local(value_near),
+        remote(w_key),
+        remote(w_value),
+        info,
+        remote(query),
+    )
     arrived = exchange(packed)
 
-    kv_text = call(
-        lambda *refs: text_kernel(load, step, *refs),
-        jax.ShapeDtypeStruct((tok, 2 * kvw), BF16),
-        [ANY, VM, VM, ANY, ANY],
-        VM,
+    block = page_cap * PAGE * 2 * kv_heads + q_rows + PAGE
+    kv_text, bias, base = call(
+        lambda *refs: text_kernel(load, step, page_cap, q_rows // kv_heads, *refs),
+        (
+            jax.ShapeDtypeStruct((tok, 2 * kvw), BF16),
+            jax.ShapeDtypeStruct((tok, n * q_rows // kv_heads), F32),
+            jax.ShapeDtypeStruct((n, block - q_rows - PAGE, HD), BF16),
+        ),
+        [ANY, VM, VM, ANY, ANY, VM, SM],
+        (VM, VM, VM),
         [
             pltpu.VMEM((tok, half), BF16),
             pltpu.VMEM(w_key.shape, BF16),
@@ -426,20 +480,24 @@
         limit=24,
         flops=2 * tok * 2 * half * 2 * kvw,
         traffic=2 * tok * 2 * half + 8 * half * kvw,
-    )(remote(text_rows), text_far, gain, remote(w_key), remote(w_value))
+    )(remote(text_rows), text_far, gain, remote(w_key), remote(w_value), info, slots)
 
     sent, own = call(
         lambda *refs: attend_kernel(n, cap, lot, page_cap, kv_heads, *refs),
         (
-            jax.ShapeDtypeStruct((n, page_cap * PAGE * 2 * kv_heads + q_rows + PAGE, HD), BF16),
+            jax.ShapeDtypeStruct((n, block, HD), BF16),
             jax.ShapeDtypeStruct((q_rows + STAT, HD), F32),
         ),
-        [SM, VM, VM, VM],
+        [SM] + [VM] * 5,
         (VM, VM),
-        [pltpu.VMEM((tok, 2 * kvw), BF16), pltpu.VMEM((n * q_rows, HD), F32)],
+        [
+            pltpu.VMEM((min(tok, n * cap), 2 * kvw), BF16),
+            pltpu.VMEM((n * q_rows, HD), F32),
+            pltpu.VMEM((STAT, n * q_rows // kv_heads), F32),
+        ],
         flops=4 * n * q_rows * tok * HD,
         traffic=n * (q_rows + STAT) * HD * 4,
-    )(slots, info, kv_text, arrived)
+    )(slots, info, kv_text, arrived, bias, base)
     shares = exchange(sent)
 
     mine = call(
@@ -453,15 +511,14 @@
 
     slots_here = n * page_cap
     attended, cache_key, cache_value = call(
-        lambda *refs: finish_kernel(steps, page_cap, *refs),
+        lambda *refs: finish_kernel(kv_heads, steps, page_cap, *refs),
         (
             jax.ShapeDtypeStruct(dec_query.shape, BF16),
             jax.ShapeDtypeStruct((n, page_cap * PAGE, kvw), BF16),
             jax.ShapeDtypeStruct((n, page_cap * PAGE, kvw), BF16),
         ),
         [VM, VM],
-        (VM, ANY, ANY),
-        [pltpu.SemaphoreType.DMA((2 * kv_heads,))],
+        (VM, VM, VM),
         traffic=4 * tok * 2 * kvw,
     )(shares, mine)
     return (

time: 46.1 us -> 44.7 us (0.970)
  Pallas kernels: 18.6 us -> 17.6 us
  waiting for transfers between devices: 14.9 us -> 14.4 us
    pallas_call x1, Pallas kernels: 3.47 us -> 4.84 us  [body(): call(lambda *refs: vis_kernel(n, lot, step, *refs), jax.ShapeDtypeStruct(...]
    pallas_call x1, Pallas kernels: 4.19 us -> 2.98 us  [body(): call(lambda *refs: prepare_kernel((n, img, tok, blocks, lot, page_cap), *...]
    pallas_call x1, Pallas kernels: 2.75 us -> 1.98 us  [body(): call(lambda *refs: attend_kernel(n, cap, lot, page_cap, kv_heads, *refs),...]
    ppermute x2, waiting for transfers between devices: 0.47 us -> 0.01 us  [across(): return lax.ppermute(array, 'tensor', [(0, 1), (1, 0)])]
  transfers between devices with their start and end apart: 4 -> 4, of which waited for: 3 -> 2; matrix products, arithmetic and copies ran while one was open for 0% -> 0% of each run, Pallas kernels for 32% -> 33%
where the time goes in v7:
time: 44.7 us; the launch traced here: 44.1 us
  Pallas kernels  17.6 us (39%)
  waiting for transfers between devices  14.4 us (32%)
  starting transfers between devices  11.5 us (26%)
  between operations  0.68 us (2%)
    all_to_all x2, waiting for transfers between devices, exchange(): lax.all_to_all(array, 'section', split_axis=0, concat_axis=0, tiled=True)  14.4 us
    all_to_all x2, starting transfers between devices, exchange(): lax.all_to_all(array, 'section', split_axis=0, concat_axis=0, tiled=True)  10.9 us
    pallas_call x1, Pallas kernels, body(): call(lambda *refs: text_kernel(load, step, page_cap, q_rows // kv_heads,...  5.58 us
    pallas_call x1, Pallas kernels, body(): call(lambda *refs: vis_kernel(n, lot, step, *refs), jax.ShapeDtypeStruct(...  4.84 us
    pallas_call x1, Pallas kernels, body(): call(lambda *refs: prepare_kernel((n, img, tok, blocks, lot, page_cap), *...  2.98 us
    pallas_call x1, Pallas kernels, body(): call(lambda *refs: attend_kernel(n, cap, lot, page_cap, kv_heads, *refs),...  1.98 us
    pallas_call x1, Pallas kernels, body(): call(lambda *refs: fresh_kernel(kv_heads, steps, *refs), jax.ShapeDtypeSt...  1.3 us
    pallas_call x1, Pallas kernels, body(): call(lambda *refs: finish_kernel(kv_heads, steps, page_cap, *refs), (jax....  0.93 us
  transfers between devices with their start and end apart: 4, of which 2 were waited for; matrix products, arithmetic and copies ran while one was open for 0% of the time, Pallas kernels for 33%

profile of v7, /device:TPU:0, one launch (start us, length us, event | category | flops | bytes accessed | tf_op | source)
XLA Modules:
  0.0 44.1 jit_solution(15489431244938871544)
XLA Ops:
  0.6 0.5 %collective-permute-start.1 = (bf16[64,4096]{1,0:T(8,128)(2,1)}, bf16[64,4096]{1,0:T(8,128)(2,1)S(1)}, u32[]{:S(2)}, u32[]{:S(2)}) collective-permute-start(bf16[64,4096]{1,0:T(8,128)(2,1)} %refs_7_.1), channel_id=1, source_target_pairs={{0,1},{1,0},{2,3},{3,2},{4,5},{5,4},{6,7},{7,6},{8,9},{9,8},{10,11... | collective-permute-start | bytes 1572872 | tf_op jit(solution)/shard_map/ppermute | solution.py:394
  1.2 0.1 collective-permute-start
  1.2 3.0 %shard_map.148 = (s32[8,256]{1,0:T(8,128)S(1)}, s32[16]{0:T(128)S(1)}, bf16[4096,256]{1,0:T(8,128)(2,1)S(1)}, bf16[4096,256]{1,0:T(8,128)(2,1)S(1)}, bf16[64,4096]{1,0:T(8,128)(2,1)S(1)}) custom-call(s32[1,512]{1,0:T(1,128)} %bitcast.18, s32[1,128]{1,0:T(1,128)} %bitcast.19, s32[8]{0:T(128)} %refs_2_.1, s32[8]{0:T(128)} %refs_3_.2, s32[8]{0:T(128)} %refs_4_.2, ...), custom_call_target="tpu_custom_call" | custom-call | flops 1048576 | bytes 16777216 | tf_op jit(solution)/shard_map/pallas_call | solution.py:413
  4.2 0.0 collective-permute-done.1.refs_1_
  4.2 4.8 %shard_map.150 = bf16[8,32,512]{2,1,0:T(8,128)(2,1)} custom-call(bf16[64,4096]{1,0:T(8,128)(2,1)S(1)} %get-tuple-element.19.refs_0_, bf16[64,4096]{1,0:T(8,128)(2,1)S(1)} %collective-permute-done.1.refs_1_, f32[1,8192]{1,0:T(1,128)} %bitcast.12, bf16[4096,256]{1,0:T(8,128)(2,1)S(1)} %get-tuple-element.20.refs_3_, ...), custom_call_target="tpu_custom_call" | custom-call | flops 17179869184 | bytes 9437184 | tf_op jit(solution)/shard_map/pallas_call | solution.py:437
  9.1 7.3 %all-to-all-start = ((bf16[8,32,512]{2,1,0:T(8,128)(2,1)}), bf16[8,32,512]{2,1,0:T(8,128)(2,1)S(1)}, u32[]{:S(2)}, u32[]{:S(2)}) async-start(bf16[8,32,512]{2,1,0:T(8,128)(2,1)} %shard_map.150), calls=%async_computation | async-start | bytes 524288 | tf_op jit(solution)/shard_map/all_to_all | solution.py:397
  16.3 0.0 collective-permute-done.refs_1_
  16.4 5.6 %shard_map.149 = (bf16[256,512]{1,0:T(8,128)(2,1)S(1)}, f32[256,256]{1,0:T(8,128)S(1)}, bf16[8,128,128]{2,1,0:T(8,128)(2,1)S(1)}) custom-call(bf16[256,4096]{1,0:T(8,128)(2,1)} %refs_0_.1, bf16[256,4096]{1,0:T(8,128)(2,1)S(1)} %collective-permute-done.refs_1_, f32[1,8192]{1,0:T(1,128)} %bitcast.13, bf16[8192,256]{1,0:T(8,128)(2,1)} %refs_5_.3, ...), custom_call_target="tpu_custom_call" | custom-call | flops 2147483648 | bytes 12582912 | tf_op jit(solution)/shard_map/pallas_call | solution.py:464
  21.9 3.6 %all-to-all-done.refs_3_ = bf16[8,32,512]{2,1,0:T(8,128)(2,1)S(1)} async-done(((bf16[8,32,512]{2,1,0:T(8,128)(2,1)}), bf16[8,32,512]{2,1,0:T(8,128)(2,1)S(1)}, u32[]{:S(2)}, u32[]{:S(2)}) %all-to-all-start) | async-done | bytes 262176 | tf_op jit(solution)/shard_map/all_to_all | solution.py:397
  25.6 2.0 %shard_map.151 = (bf16[8,208,128]{2,1,0:T(8,128)(2,1)}, f32[72,128]{1,0:T(8,128)S(1)}) custom-call(s32[16]{0:T(128)S(1)} %get-tuple-element.16.refs_6_.refs_0_, s32[8,256]{1,0:T(8,128)S(1)} %get-tuple-element.17.refs_5_.refs_7_.refs_1_, bf16[256,512]{1,0:T(8,128)(2,1)S(1)} %get-tuple-element.18.refs_2_, bf16[8,32,512]{2,1,0:T(8,128)(2,1)S(1)} %all-to-all-done.refs_3_, ...), custom_call_target="tpu_custom_call" | custom-call | flops 67108864 | bytes 294912 | tf_op jit(solution)/shard_map/pallas_call | solution.py:485
  27.6 3.6 %all-to-all-start.1 = ((bf16[8,208,128]{2,1,0:T(8,128)(2,1)}), bf16[8,208,128]{2,1,0:T(8,128)(2,1)S(1)}, u32[]{:S(2)}, u32[]{:S(2)}) async-start(bf16[8,208,128]{2,1,0:T(8,128)(2,1)} %get-tuple-element.24), calls=%async_computation.1 | async-start | bytes 851968 | tf_op jit(solution)/shard_map/all_to_all | solution.py:397
  31.1 1.3 %shard_map.152.refs_1_ = f32[72,128]{1,0:T(8,128)S(1)} custom-call(bf16[64,128]{1,0:T(8,128)(2,1)} %bitcast.15, bf16[4,256]{1,0:T(4,128)(2,1)} %bitcast.16, bf16[4,256]{1,0:T(4,128)(2,1)} %bitcast.17, f32[72,128]{1,0:T(8,128)S(1)} %get-tuple-element.25.refs_3_), custom_call_target="tpu_custom_call" | custom-call | flops 1048576 | bytes 262144 | tf_op jit(solution)/shard_map/pallas_call | solution.py:503
  32.5 10.8 %all-to-all-done.1.refs_0_ = bf16[8,208,128]{2,1,0:T(8,128)(2,1)S(1)} async-done(((bf16[8,208,128]{2,1,0:T(8,128)(2,1)}), bf16[8,208,128]{2,1,0:T(8,128)(2,1)S(1)}, u32[]{:S(2)}, u32[]{:S(2)}) %all-to-all-start.1) | async-done | bytes 426016 | tf_op jit(solution)/shard_map/all_to_all | solution.py:397
  43.2 0.9 %shard_map.153 = (bf16[1,4,2048]{2,1,0:T(4,128)(2,1)}, bf16[8,32,256]{2,1,0:T(8,128)(2,1)}, bf16[8,32,256]{2,1,0:T(8,128)(2,1)}) custom-call(bf16[8,208,128]{2,1,0:T(8,128)(2,1)S(1)} %all-to-all-done.1.refs_0_, f32[72,128]{1,0:T(8,128)S(1)} %shard_map.152.refs_1_), custom_call_target="tpu_custom_call" | custom-call | bytes 524288 | tf_op jit(solution)/shard_map/pallas_call | solution.py:513
Async XLA Ops:
  0.6 3.6 %collective-permute-start.1 = (bf16[64,4096]{1,0:T(8,128)(2,1)}, bf16[64,4096]{1,0:T(8,128)(2,1)S(1)}, u32[]{:S(2)}, u32[]{:S(2)}) collective-permute-start(bf16[64,4096]{1,0:T(8,128)(2,1)} %refs_7_.1), channel_id=1, source_target_pairs={{0,1},{1,0},{2,3},{3,2},{4,5},{5,4},{6,7},{7,6},{8,9},{9,8},{10,11... | collective-permute-start | bytes 1572872 | tf_op jit(solution)/shard_map/ppermute | solution.py:394
  1.2 15.2 %collective-permute-start = (bf16[256,4096]{1,0:T(8,128)(2,1)}, bf16[256,4096]{1,0:T(8,128)(2,1)S(1)}, u32[]{:S(2)}, u32[]{:S(2)}) collective-permute-start(bf16[256,4096]{1,0:T(8,128)(2,1)} %refs_0_.1), channel_id=1, source_target_pairs={{0,1},{1,0},{2,3},{3,2},{4,5},{5,4},{6,7},{7,6},{8,9},{9,8},{10,11... | collective-permute-start | bytes 6291464 | tf_op jit(solution)/shard_map/ppermute | solution.py:394
  9.1 16.5 %all-to-all-start = ((bf16[8,32,512]{2,1,0:T(8,128)(2,1)}), bf16[8,32,512]{2,1,0:T(8,128)(2,1)S(1)}, u32[]{:S(2)}, u32[]{:S(2)}) async-start(bf16[8,32,512]{2,1,0:T(8,128)(2,1)} %shard_map.150), calls=%async_computation | async-start | bytes 524288 | tf_op jit(solution)/shard_map/all_to_all | solution.py:397
  27.6 15.7 %all-to-all-start.1 = ((bf16[8,208,128]{2,1,0:T(8,128)(2,1)}), bf16[8,208,128]{2,1,0:T(8,128)(2,1)S(1)}, u32[]{:S(2)}, u32[]{:S(2)}) async-start(bf16[8,208,128]{2,1,0:T(8,128)(2,1)} %get-tuple-element.24), calls=%async_computation.1 | async-start | bytes 851968 | tf_op jit(solution)/shard_map/all_to_all | solution.py:397

commit v8 on v7

v8 whole, which is shorter than its diff:
```python
import jax
import jax.numpy as jnp
from jax import lax
from jax.experimental import pallas as pl
from jax.experimental.pallas import tpu as pltpu
from jax.sharding import PartitionSpec as P

HD = 128
PAGE = 16
LOWEST = -1e30
EPS = 1e-06
STAT = 8
F32 = jnp.float32
BF16 = jnp.bfloat16
I32 = jnp.int32

VM = pl.BlockSpec(memory_space=pltpu.VMEM)
SM = pl.BlockSpec(memory_space=pltpu.SMEM)
ANY = pl.BlockSpec(memory_space=pl.ANY)
MIB = 1 << 20


def call(kernel, out_shape, in_specs, out_specs, scratch=(), limit=16, flops=0, traffic=0):
    return pl.pallas_call(
        kernel,
        out_shape=out_shape,
        in_specs=in_specs,
        out_specs=out_specs,
        scratch_shapes=list(scratch),
        compiler_params=pltpu.CompilerParams(vmem_limit_bytes=limit * MIB),
        cost_estimate=pl.CostEstimate(flops=flops, bytes_accessed=traffic, transcendentals=0),
    )


def dot(a, b):
    return jnp.dot(a, b, preferred_element_type=F32)


def dot_t(a, b):
    return lax.dot_general(a, b, (((1,), (1,)), ((), ())), preferred_element_type=F32)


def diagonal(shape):
    return lax.broadcasted_iota(I32, shape, 0) == lax.broadcasted_iota(I32, shape, 1)


def column_to_row(column):
    rows = column.shape[0]
    return jnp.sum(jnp.where(diagonal((rows, rows)), column, 0.0), axis=0, keepdims=True)


def row_to_column(row):
    lanes = row.shape[1]
    return jnp.sum(jnp.where(diagonal((lanes, lanes)), row, 0.0), axis=1, keepdims=True)


def squares_of(rows):
    total = jnp.zeros((rows.shape[0], HD), F32)
    for c in range(0, rows.shape[1], HD):
        wide = rows[:, c : c + HD].astype(F32)
        total = total + wide * wide
    return total


def split_three(values):
    high = values.astype(BF16).astype(F32)
    rest = values - high
    middle = rest.astype(BF16).astype(F32)
    return high, middle, rest - middle


def softmax_parts(query, key, value, usable):
    scores = jnp.where(usable, dot_t(query, key) * HD**-0.5, LOWEST)
    top = jnp.max(scores, axis=1, keepdims=True)
    weights = jnp.where(usable, jnp.exp(scores - top), 0.0)
    return dot(weights.astype(BF16), value), top, jnp.sum(weights, axis=1, keepdims=True)


def prepare_kernel(sizes, *refs):
    n, img, tok, blocks, lot, page_cap, q_rows = sizes
    far, (info, slots, bias, square, near), more, rest = refs[:11], refs[11:16], refs[16:20], refs[20:]
    small, (starts, sems) = rest[:5], rest[5:]
    targets = (*small, near.at[:tok], near.at[tok:], *more)
    copies = [pltpu.make_async_copy(a, b, sems.at[i]) for i, (a, b) in enumerate(zip(far, targets))]
    for c in copies:
        c.start()
    route, pages, count, tail, req = small
    for c in copies[: len(small)]:
        c.wait()
    pos = lax.axis_index("section")
    table = [route[:, e * img : (e + 1) * img] for e in range(n)]
    own = jnp.zeros((1, img), I32)
    for e in range(n):
        own = jnp.where(pos == e, table[e], own)
    marks = own == lax.broadcasted_iota(I32, (n, img), 0)
    ones = jnp.where(marks, 1.0, 0.0).astype(BF16)
    earlier = lax.broadcasted_iota(I32, (img, img), 0) < lax.broadcasted_iota(I32, (img, img), 1)
    prefix = dot(ones, jnp.where(earlier, 1.0, 0.0).astype(BF16))
    local = jnp.sum(jnp.where(marks, prefix, 0.0), axis=0, keepdims=True).astype(I32)
    info[0:1, :img] = jnp.bitwise_xor(own, pos) * lot + local
    lanes = lax.broadcasted_iota(I32, (1, n * lot), 1)
    source, inner = jnp.bitwise_xor(lanes // lot, pos), lanes % lot
    fits = jnp.zeros((1, n * lot), I32)
    offset = jnp.zeros((1, n * lot), I32)
    for e in range(n):
        arriving = jnp.sum((table[e] == pos).astype(I32), axis=1, keepdims=True)
        fits = fits + jnp.where(source == e, arriving, 0)
        offset = offset + jnp.where(source > e, arriving, 0)
    info[1:2, : n * lot] = jnp.where(inner < fits, offset + inner, -1)
    total = jnp.int32(0)
    for r in range(n):
        starts[r] = total
        total = total + count[r]
    token = lax.broadcasted_iota(I32, (1, tok), 1) + pos * tok
    token_slot = jnp.full((1, tok), -1, I32)
    for b in range(n):
        r = req[b]
        first = starts[r] * PAGE
        last = first + (count[r] - 1) * PAGE + tail[r]
        token_slot = jnp.where((token >= first) & (token < last), b, token_slot)
    column = row_to_column(token_slot.astype(F32))
    member = jnp.bitwise_xor(lax.broadcasted_iota(I32, (1, bias.shape[1]), 1) // q_rows, pos)
    bias[...] = jnp.where(column == member.astype(F32), 0.0, LOWEST)
    for g in range(blocks):
        holder = pages[0, pos * blocks + g]
        slot = holder * page_cap
        for e in range(g):
            slot = slot + (pages[0, pos * blocks + e] == holder).astype(I32)
        slots[g] = slot
    for c in copies[len(small) : len(small) + 2]:
        c.wait()
    square[...] = squares_of(near)
    for c in copies[len(small) + 2 :]:
        c.wait()


def project_kernel(n, lot, step, near, text_far, vis_far, w_key, w_value, gain, query, square, info, kv_text, *rest):
    packed, total = rest[:-1], rest[-1]
    tok, half = text_far.shape
    img = vis_far.shape[0]
    kvw = w_key.shape[1]
    me = lax.axis_index("tensor")
    far = (text_far, vis_far)
    sums = [jnp.sum(square[:tok, :] + squares_of(text_far), axis=1, keepdims=True)]
    sums.append(jnp.sum(square[tok:, :] + squares_of(vis_far), axis=1, keepdims=True))
    scales = [lax.rsqrt(x / (2.0 * half) + EPS) for x in sums]
    for nearby, side in ((True, me), (False, 1 - me)):
        rows = (near.at[:tok], near.at[tok:]) if nearby else far
        for c in range(0, half, step):
            columns = pl.ds(pl.multiple_of(side * half + c, step), step)
            scaled = gain[:, columns]
            normed = jnp.concatenate(
                [(x[:, c : c + step].astype(F32) * s * scaled).astype(BF16) for x, s in zip(rows, scales)], axis=0
            )
            for w, at in ((w_key, 0), (w_value, kvw)):
                part = dot(normed, w[columns, :])
                if nearby and c == 0:
                    total[:, at : at + kvw] = part
                else:
                    total[:, at : at + kvw] += part
    kv_text[...] = total[:tok, :].astype(BF16)
    slot = lax.broadcasted_iota(I32, (n * lot, img), 0)
    chosen = jnp.where(slot == info[0:1, :img], 1.0, 0.0).astype(BF16)
    images = dot(chosen, total[tok:, :].astype(BF16)).astype(BF16)
    q_lots = packed[0].shape[0] - lot
    for k in range(n):
        for j in range(query.shape[0] // q_lots):
            packed[k][:q_lots, j * HD : (j + 1) * HD] = query[j * q_lots : (j + 1) * q_lots, :]
        packed[k][q_lots:, :] = images[k * lot : (k + 1) * lot, :]


def put_page(out, page_cap, slot, rows):
    chunk = page_cap * PAGE
    for h in range(rows.shape[1] // HD):
        at = pl.ds(pl.multiple_of((slot % page_cap) * PAGE + h * chunk, PAGE), PAGE)
        out[slot // page_cap, at, :] = rows[:, h * HD : (h + 1) * HD]


def attend_kernel(n, cap, lot, page_cap, kv_heads, slots, info, kv_text, bias, *rest):
    arrived, (out, own, mixed, held) = rest[:n], rest[n:]
    pos = lax.axis_index("section")
    tok = kv_text.shape[0]
    kvw = kv_heads * HD
    q_lots = arrived[0].shape[0] - lot
    reach = min(tok, n * cap)
    hit = lax.broadcasted_iota(I32, (reach, n * lot), 0) == info[1:2, : n * lot]
    hot = jnp.where(hit, 1.0, 0.0)
    covered = jnp.sum(hot, axis=1, keepdims=True) > 0.0
    incoming = jnp.concatenate([x[q_lots:, :] for x in arrived], axis=0)
    placed = dot(hot.astype(BF16), incoming)
    mixed[...] = jnp.where(covered, placed, kv_text[:reach, :].astype(F32)).astype(BF16)
    groups = arrived[0].shape[1] // HD // kv_heads
    rows = groups * q_lots
    pages = page_cap * PAGE * 2 * kv_heads
    out[:, :pages, :] = jnp.zeros((n, pages, HD), BF16)
    for g in range(tok // PAGE):
        at = slice(g * PAGE, (g + 1) * PAGE)
        put_page(out, page_cap, slots[g], mixed[at, :] if (g + 1) * PAGE <= reach else kv_text[at, :])
    for g in range(kv_heads):
        query = jnp.concatenate(
            [x[:q_lots, (g * groups + j) * HD : (g * groups + j + 1) * HD] for x in arrived for j in range(groups)],
            axis=0,
        )
        cols = slice(g * HD, (g + 1) * HD)
        vcols = slice(kvw + g * HD, kvw + (g + 1) * HD)
        key = jnp.concatenate([mixed[:, cols], kv_text[reach:, cols]], axis=0)
        value = jnp.concatenate([mixed[:, vcols], kv_text[reach:, vcols]], axis=0)
        scores = dot_t(key, query) * HD**-0.5 + bias[...]
        top = jnp.max(scores, axis=0, keepdims=True)
        weights = jnp.exp(scores - top)
        held[g : g + 1, :] = top
        held[kv_heads + g : kv_heads + g + 1, :] = jnp.sum(weights, axis=0, keepdims=True)
        numerator = lax.dot_general(
            weights.astype(BF16), value, (((0,), (0,)), ((), ())), preferred_element_type=F32
        )
        own[g * rows : (g + 1) * rows, :] = numerator[:rows, :]
        numerator = numerator.astype(BF16)
        for k in range(n):
            to = jnp.bitwise_xor(pos, k)
            out[to, pages + g * rows : pages + (g + 1) * rows, :] = numerator[k * rows : (k + 1) * rows, :]
    stat_rows = 2 * kv_heads
    share = HD // rows
    own[kv_heads * rows : kv_heads * rows + stat_rows, :] = held[:stat_rows, :HD]
    blank = jnp.zeros((PAGE - 3 * stat_rows, HD), F32)
    for w in range(-(-n // share)):
        stats = held[:stat_rows, w * HD : (w + 1) * HD]
        lines = jnp.concatenate([*split_three(stats), blank], axis=0).astype(BF16)
        for k in range(w * share, min(n, (w + 1) * share)):
            out[jnp.bitwise_xor(pos, k), pages + kv_heads * rows :, :] = lines


def pick_column(row, rows, start):
    shape = (rows, HD)
    chosen = lax.broadcasted_iota(I32, shape, 1) == lax.broadcasted_iota(I32, shape, 0) + start
    return jnp.sum(jnp.where(chosen, row, 0.0), axis=1, keepdims=True)


def combine(pieces, highest):
    numerator, total = 0.0, 0.0
    for rows, top, weight in pieces:
        scale = jnp.exp(top - highest)
        numerator = numerator + rows * scale
        total = total + weight * scale
    return numerator, total


def fresh_kernel(kv_heads, steps, query, key, value, own, mine):
    rows = query.shape[0] // kv_heads
    every = kv_heads * rows
    row = lax.broadcasted_iota(I32, (rows, steps), 0)
    causal = lax.broadcasted_iota(I32, (rows, steps), 1) <= row % steps
    tops, totals = [], []
    for g in range(kv_heads):
        cols = slice(g * HD, (g + 1) * HD)
        at = slice(g * rows, (g + 1) * rows)
        fresh = softmax_parts(query[at, :], key[:, cols], value[:, cols], causal)
        share = (
            own[at, :],
            pick_column(own[every + g : every + g + 1, :], rows, 0),
            pick_column(own[every + kv_heads + g : every + kv_heads + g + 1, :], rows, 0),
        )
        highest = jnp.maximum(fresh[1], share[1])
        numerator, total = combine((fresh, share), highest)
        mine[at, :] = numerator
        tops.append(highest)
        totals.append(total)
    line = column_to_row(jnp.concatenate(tops + totals, axis=0))
    mine[every:, :] = jnp.broadcast_to(line, (STAT, line.shape[1]))


def finish_kernel(kv_heads, steps, page_cap, shares, mine, attended, keys, values):
    n = shares.shape[0]
    pos = lax.axis_index("section")
    every = mine.shape[0] - STAT
    rows = every // kv_heads
    chunk = page_cap * PAGE
    halves = keys.shape[2] // HD
    for k in range(n):
        for i, out in enumerate((keys, values)):
            for h in range(halves):
                part = i * halves + h
                out[k, :, h * HD : (h + 1) * HD] = shares[k, part * chunk : (part + 1) * chunk, :]
    pages = 2 * halves * chunk
    stats = row_to_column(mine[every : every + 1, :])
    lines = []
    for k in range(n):
        three = shares[k, pages + every :, :].astype(F32)
        size = 2 * kv_heads
        lines.append(three[:size] + three[size : 2 * size] + three[2 * size : 3 * size])
    for g in range(kv_heads):
        at = slice(g * rows, (g + 1) * rows)
        pieces = [(mine[at, :], stats[at], stats[every + g * rows : every + (g + 1) * rows])]
        for k in range(n):
            away = pos != k
            start = jnp.bitwise_xor(pos, k) % (HD // rows) * rows
            top = jnp.where(away, pick_column(lines[k][g : g + 1], rows, start), LOWEST)
            weight = jnp.where(away, pick_column(lines[k][kv_heads + g : kv_heads + g + 1], rows, start), 0.0)
            share = shares[k, pages + g * rows : pages + (g + 1) * rows, :].astype(F32)
            pieces.append((share, top, weight))
        highest = pieces[0][1]
        for p in pieces[1:]:
            highest = jnp.maximum(highest, p[1])
        numerator, total = combine(pieces, highest)
        result = (numerator / total).astype(BF16)
        for h in range(rows // steps):
            to = (g * rows // steps + h) * HD
            attended[0, :, to : to + HD] = result[h * steps : (h + 1) * steps, :]


def body(
    text_rows,
    vis_rows,
    img_route,
    norm_gain,
    w_key,
    w_value,
    page_count,
    tail_len,
    page_dest,
    dec_req,
    dec_query,
    dec_key,
    dec_value,
):
    n = lax.axis_size("section")
    tok, half = text_rows.shape
    img = vis_rows.shape[0]
    kvw = w_key.shape[1]
    kv_heads = kvw // HD
    _, steps, q_width = dec_query.shape
    heads = q_width // HD
    q_rows = heads * steps
    blocks = tok // PAGE
    cap = max(2, (2 * img + n - 1) // n)
    page_cap = max(1, (blocks + n - 1) // n)

    def across(array):
        return lax.ppermute(array, "tensor", [(0, 1), (1, 0)])

    def swap(array, k):
        return lax.ppermute(array, "section", [(i, i ^ k) for i in range(n)])

    def exchange(array):
        return lax.all_to_all(array, "section", split_axis=0, concat_axis=0, tiled=True)

    def remote(array):
        return pltpu.with_memory_space_constraint(array, pltpu.HBM)

    def local(array):
        return pltpu.with_memory_space_constraint(array, pltpu.VMEM)

    vis_far = across(vis_rows)
    text_far = across(text_rows)
    query = dec_query.reshape(steps, heads, HD).transpose(1, 0, 2).reshape(q_rows, HD)

    lot = -(-cap // PAGE) * PAGE
    q_lots = q_rows * HD // (2 * kvw)
    width = max(tok, n * lot)
    arguments = (
        img_route.T,
        page_dest.T,
        page_count,
        tail_len,
        dec_req,
        text_rows,
        vis_rows,
        w_key,
        w_value,
        norm_gain.reshape(1, 2 * half),
        query,
    )
    info, slots, bias, square, near, *more = call(
        lambda *refs: prepare_kernel((n, img, tok, blocks, lot, page_cap, q_rows // kv_heads), *refs),
        (
            jax.ShapeDtypeStruct((8, width), I32),
            jax.ShapeDtypeStruct((blocks,), I32),
            jax.ShapeDtypeStruct((tok, n * q_rows // kv_heads), F32),
            jax.ShapeDtypeStruct((tok + img, HD), F32),
            pltpu.VMEM((tok + img, half), BF16),
            *[pltpu.VMEM(a.shape, a.dtype) for a in arguments[7:]],
        ),
        [ANY] * len(arguments),
        (VM, SM) + (VM,) * 7,
        [
            *[(pltpu.VMEM if i == 0 else pltpu.SMEM)(a.shape, a.dtype) for i, a in enumerate(arguments[:5])],
            pltpu.SMEM((n,), I32),
            pltpu.SemaphoreType.DMA((len(arguments),)),
        ],
        flops=1 << 20,
        traffic=2 * 2 * half * 2 * kvw * 2,
    )(*[remote(a) for a in arguments])

    kv_text, *packed = call(
        lambda *refs: project_kernel(n, lot, min(1024, half), *refs),
        (
            jax.ShapeDtypeStruct((tok, 2 * kvw), BF16),
            *[jax.ShapeDtypeStruct((q_lots + lot, 2 * kvw), BF16)] * n,
        ),
        [VM] * 9,
        (VM,) * (1 + n),
        [pltpu.VMEM((tok + img, 2 * kvw), F32)],
        flops=2 * (tok + img) * 2 * half * 2 * kvw,
        traffic=2 * (tok + img) * 2 * half + 8 * half * kvw,
    )(local(near), text_far, vis_far, *[local(a) for a in more], square, info)
    arrived = [packed[0]] + [swap(packed[k], k) for k in range(1, n)]

    block = page_cap * PAGE * 2 * kv_heads + q_rows + PAGE
    sent, own = call(
        lambda *refs: attend_kernel(n, cap, lot, page_cap, kv_heads, *refs),
        (
            jax.ShapeDtypeStruct((n, block, HD), BF16),
            jax.ShapeDtypeStruct((q_rows + STAT, HD), F32),
        ),
        [SM] + [VM] * (3 + n),
        (VM, VM),
        [
            pltpu.VMEM((min(tok, n * cap), 2 * kvw), BF16),
            pltpu.VMEM((STAT, n * q_rows // kv_heads), F32),
        ],
        flops=4 * n * q_rows * tok * HD,
        traffic=n * (q_rows + STAT) * HD * 4,
    )(slots, info, kv_text, bias, *arrived)
    shares = exchange(sent)

    mine = call(
        lambda *refs: fresh_kernel(kv_heads, steps, *refs),
        jax.ShapeDtypeStruct((q_rows + STAT, HD), F32),
        [VM] * 4,
        VM,
        flops=1 << 20,
        traffic=1 << 18,
    )(remote(query), remote(dec_key[0]), remote(dec_value[0]), own)

    slots_here = n * page_cap
    attended, cache_key, cache_value = call(
        lambda *refs: finish_kernel(kv_heads, steps, page_cap, *refs),
        (
            jax.ShapeDtypeStruct(dec_query.shape, BF16),
            jax.ShapeDtypeStruct((n, page_cap * PAGE, kvw), BF16),
            jax.ShapeDtypeStruct((n, page_cap * PAGE, kvw), BF16),
        ),
        [VM, VM],
        (VM, VM, VM),
        traffic=4 * tok * 2 * kvw,
    )(shares, mine)
    return (
        attended,
        cache_key.reshape(slots_here, PAGE, kvw),
        cache_value.reshape(slots_here, PAGE, kvw),
    )


def solution(mesh):
    return jax.shard_map(
        body,
        mesh=mesh,
        in_specs=(
            P(("groups", "section"), "tensor"),
            P(("groups", "section"), "tensor"),
            P("groups", None),
            P(),
            P(None, "tensor"),
            P(None, "tensor"),
            P("groups"),
            P("groups"),
            P("groups", None),
            P("groups"),
            P(("groups", "section"), None, "tensor"),
            P(("groups", "section"), None, "tensor"),
            P(("groups", "section"), None, "tensor"),
        ),
        out_specs=(
            P(("groups", "section"), None, "tensor"),
            P(("groups", "section"), None, "tensor"),
            P(("groups", "section"), None, "tensor"),
        ),
        check_vma=False,
    )
```

time: 44.7 us -> 45.6 us (1.020)
  starting transfers between devices: 11.5 us -> 16.5 us
  Pallas kernels: 17.6 us -> 12.7 us
  waiting for transfers between devices: 14.4 us -> 15.4 us
    ppermute x0 -> x7, starting transfers between devices: none -> 12.5 us  [swap(): return lax.ppermute(array, 'section', [(i, i ^ k) for i in range(n)])]
    all_to_all x2 -> x1, starting transfers between devices: 10.9 us -> 3.46 us  [exchange(): lax.all_to_all(array, 'section', split_axis=0, concat_axis=0, tiled=True)]
    ppermute x0 -> x7, waiting for transfers between devices: none -> 6.6 us  [swap(): return lax.ppermute(array, 'section', [(i, i ^ k) for i in range(n)])]
    all_to_all x2 -> x1, waiting for transfers between devices: 14.4 us -> 8.78 us  [exchange(): lax.all_to_all(array, 'section', split_axis=0, concat_axis=0, tiled=True)]
    pallas_call x3 -> x2, Pallas kernels: 13.4 us -> 8.5 us  [the longest x1 4.88 us: body(): call(lambda *refs: prepare_kernel((n, img, tok, blocks, lot, page_cap, q_...]
  transfers between devices with their start and end apart: 4 -> 10, of which waited for: 2 -> 4; matrix products, arithmetic and copies ran while one was open for 0% -> 0% of each run, Pallas kernels for 33% -> 14%
where the time goes in v8:
time: 45.6 us; the launch traced here: 45.3 us
  starting transfers between devices  16.5 us (36%)
  waiting for transfers between devices  15.4 us (34%)
  Pallas kernels  12.7 us (28%)
  between operations  0.68 us (1%)
    ppermute x7, starting transfers between devices, swap(): return lax.ppermute(array, 'section', [(i, i ^ k) for i in range(n)])  12.5 us
    all_to_all x1, waiting for transfers between devices, exchange(): lax.all_to_all(array, 'section', split_axis=0, concat_axis=0, tiled=True)  8.78 us
    ppermute x7, waiting for transfers between devices, swap(): return lax.ppermute(array, 'section', [(i, i ^ k) for i in range(n)])  6.6 us
    pallas_call x1, Pallas kernels, body(): call(lambda *refs: prepare_kernel((n, img, tok, blocks, lot, page_cap, q_...  4.88 us
    pallas_call x1, Pallas kernels, body(): call(lambda *refs: project_kernel(n, lot, min(1024, half), *refs), (jax.S...  3.61 us
    all_to_all x1, starting transfers between devices, exchange(): lax.all_to_all(array, 'section', split_axis=0, concat_axis=0, tiled=True)  3.46 us
    pallas_call x1, Pallas kernels, body(): call(lambda *refs: attend_kernel(n, cap, lot, page_cap, kv_heads, *refs),...  2.02 us
    pallas_call x1, Pallas kernels, body(): call(lambda *refs: fresh_kernel(kv_heads, steps, *refs), jax.ShapeDtypeSt...  1.3 us
  transfers between devices with their start and end apart: 10, of which 4 were waited for; matrix products, arithmetic and copies ran while one was open for 0% of the time, Pallas kernels for 14%

profile of v8, /device:TPU:0, one launch (start us, length us, event | category | flops | bytes accessed | tf_op | source)
XLA Modules:
  0.0 45.3 jit_solution(7529398172737898639)
XLA Ops:
  0.6 0.5 %collective-permute-start = (bf16[256,4096]{1,0:T(8,128)(2,1)}, bf16[256,4096]{1,0:T(8,128)(2,1)S(1)}, u32[]{:S(2)}, u32[]{:S(2)}) collective-permute-start(bf16[256,4096]{1,0:T(8,128)(2,1)} %refs_5_.1), channel_id=1, source_target_pairs={{0,1},{1,0},{2,3},{3,2},{4,5},{5,4},{6,7},{7,6},{8,9},{9,8},{10,11... | collective-permute-start | bytes 6291464 | tf_op jit(solution)/shard_map/ppermute | solution.py:338
  1.2 0.1 collective-permute-start.1
  1.2 4.9 %shard_map.148 = (s32[8,256]{1,0:T(8,128)S(1)}, s32[16]{0:T(128)S(1)}, f32[256,256]{1,0:T(8,128)S(1)}, f32[320,128]{1,0:T(8,128)S(1)}, bf16[320,4096]{1,0:T(8,12...) custom-call(s32[1,512]{1,0:T(1,128)} %bitcast.15, ...), custom_call_target="tpu_custom_call" | custom-call | flops 1048576 | bytes 16777216 | tf_op jit(solution)/shard_map/pallas_call | solution.py:372
  6.1 0.0 collective-permute-done.1.refs_2_
  6.1 0.0 collective-permute-done.refs_1_
  6.1 3.6 %shard_map.149 = (bf16[256,512]{1,0:T(8,128)(2,1)S(1)}, bf16[32,512]{1,0:T(8,128)(2,1)S(1)}, bf16[32,512]{1,0:T(8,128)(2,1)S(1)}, bf16[32,512]{1,0:T(8,128)(2,1)...) custom-call(bf16[320,4096]{1,0:T(8,128)(2,1)S(1)} %get-tuple-element, ...), custom_call_target="tpu_custom_call" | custom-call | flops 2684354560 | bytes 13631488 | tf_op jit(solution)/shard_map/pallas_call | solution.py:393
  9.8 3.0 %collective-permute-start.2 = (bf16[32,512]{1,0:T(8,128)(2,1)S(1)}, bf16[32,512]{1,0:T(8,128)(2,1)S(1)}, u32[]{:S(2)}, u32[]{:S(2)}) collective-permute-start(bf16[32,512]{1,0:T(8,128)(2,1)S(1)} %get-tuple-element.37), channel_id=1, source_target_pairs={{0,2},{2,0},{4,6},{6,4},{8,10},{10,8},{12,14},{14,12},{1,3},{3,1},... | collective-permute-start | bytes 98312 | tf_op jit(solution)/shard_map/ppermute | solution.py:341
  12.8 1.6 %collective-permute-start.3 = (bf16[32,512]{1,0:T(8,128)(2,1)S(1)}, bf16[32,512]{1,0:T(8,128)(2,1)S(1)}, u32[]{:S(2)}, u32[]{:S(2)}) collective-permute-start(bf16[32,512]{1,0:T(8,128)(2,1)S(1)} %get-tuple-element.38), channel_id=1, source_target_pairs={{0,4},{2,6},{4,0},{6,2},{8,12},{10,14},{12,8},{14,10},{1,5},{3,7},... | collective-permute-start | bytes 98312 | tf_op jit(solution)/shard_map/ppermute | solution.py:341
  14.3 0.0 collective-permute-start.4
  14.4 3.0 %collective-permute-start.5 = (bf16[32,512]{1,0:T(8,128)(2,1)S(1)}, bf16[32,512]{1,0:T(8,128)(2,1)S(1)}, u32[]{:S(2)}, u32[]{:S(2)}) collective-permute-start(bf16[32,512]{1,0:T(8,128)(2,1)S(1)} %get-tuple-element.40), channel_id=1, source_target_pairs={{0,8},{2,10},{4,12},{6,14},{8,0},{10,2},{12,4},{14,6},{1,9},{3,11}... | collective-permute-start | bytes 98312 | tf_op jit(solution)/shard_map/ppermute | solution.py:341
  17.3 1.3 %collective-permute-start.6 = (bf16[32,512]{1,0:T(8,128)(2,1)S(1)}, bf16[32,512]{1,0:T(8,128)(2,1)S(1)}, u32[]{:S(2)}, u32[]{:S(2)}) collective-permute-start(bf16[32,512]{1,0:T(8,128)(2,1)S(1)} %get-tuple-element.41), channel_id=1, source_target_pairs={{0,10},{2,8},{4,14},{6,12},{8,2},{10,0},{12,6},{14,4},{1,11},{3,9}... | collective-permute-start | bytes 98312 | tf_op jit(solution)/shard_map/ppermute | solution.py:341
  18.6 0.0 collective-permute-done.2.refs_5_
  18.6 3.6 %collective-permute-start.7 = (bf16[32,512]{1,0:T(8,128)(2,1)S(1)}, bf16[32,512]{1,0:T(8,128)(2,1)S(1)}, u32[]{:S(2)}, u32[]{:S(2)}) collective-permute-start(bf16[32,512]{1,0:T(8,128)(2,1)S(1)} %get-tuple-element.42), channel_id=1, source_target_pairs={{0,12},{2,14},{4,8},{6,10},{8,4},{10,6},{12,0},{14,2},{1,13},{3,15... | collective-permute-start | bytes 98312 | tf_op jit(solution)/shard_map/ppermute | solution.py:341
  22.2 0.0 collective-permute-done.3.refs_6_
  22.2 0.0 collective-permute-start.8
  22.2 0.0 collective-permute-done.4.refs_7_
  22.3 0.0 collective-permute-done.5.refs_8_
  22.3 0.8 %collective-permute-done.6.refs_9_ = bf16[32,512]{1,0:T(8,128)(2,1)S(1)} collective-permute-done((bf16[32,512]{1,0:T(8,128)(2,1)S(1)}, bf16[32,512]{1,0:T(8,128)(2,1)S(1)}, u32[]{:S(2)}, u32[]{:S(2)}) %collective-permute-start.6) | collective-permute-done | bytes 32800 | tf_op jit(solution)/shard_map/ppermute | solution.py:341
  23.0 1.4 %collective-permute-done.7.refs_10_ = bf16[32,512]{1,0:T(8,128)(2,1)S(1)} collective-permute-done((bf16[32,512]{1,0:T(8,128)(2,1)S(1)}, bf16[32,512]{1,0:T(8,128)(2,1)S(1)}, u32[]{:S(2)}, u32[]{:S(2)}) %collective-permute-start.7) | collective-permute-done | bytes 32800 | tf_op jit(solution)/shard_map/ppermute | solution.py:341
  24.5 4.4 %collective-permute-done.8.refs_11_ = bf16[32,512]{1,0:T(8,128)(2,1)S(1)} collective-permute-done((bf16[32,512]{1,0:T(8,128)(2,1)S(1)}, bf16[32,512]{1,0:T(8,128)(2,1)S(1)}, u32[]{:S(2)}, u32[]{:S(2)}) %collective-permute-start.8) | collective-permute-done | bytes 32800 | tf_op jit(solution)/shard_map/ppermute | solution.py:341
  28.8 2.0 %shard_map.150 = (bf16[8,208,128]{2,1,0:T(8,128)(2,1)}, f32[72,128]{1,0:T(8,128)S(1)}) custom-call(s32[16]{0:T(128)S(1)} %get-tuple-element.26.refs_0_, s32[8,256]{1,0:T(8,128)S(1)} %get-tuple-element.27.refs_8_.refs_1_, bf16[256,512]{1,0:T(8,128)(2,1)S(1)} %get-tuple-element.34.refs_2_, f32[256,256]{1,0:T(8,128)S(1)} %get-tuple-element.35.refs_3_, ...), custom_call_target="tpu_custom_call" | custom-call | flops 67108864 | bytes 294912 | tf_op jit(solution)/shard_map/pallas_call | solution.py:408
  30.9 3.5 %all-to-all-start = ((bf16[8,208,128]{2,1,0:T(8,128)(2,1)}), bf16[8,208,128]{2,1,0:T(8,128)(2,1)S(1)}, u32[]{:S(2)}, u32[]{:S(2)}) async-start(bf16[8,208,128]{2,1,0:T(8,128)(2,1)} %get-tuple-element.44), calls=%async_computation | async-start | bytes 851968 | tf_op jit(solution)/shard_map/all_to_all | solution.py:344
  34.3 1.3 %shard_map.151.refs_1_ = f32[72,128]{1,0:T(8,128)S(1)} custom-call(bf16[64,128]{1,0:T(8,128)(2,1)} %bitcast.13, bf16[4,256]{1,0:T(4,128)(2,1)} %bitcast.16, bf16[4,256]{1,0:T(4,128)(2,1)} %bitcast.17, f32[72,128]{1,0:T(8,128)S(1)} %get-tuple-element.45.refs_3_), custom_call_target="tpu_custom_call" | custom-call | flops 1048576 | bytes 262144 | tf_op jit(solution)/shard_map/pallas_call | solution.py:425
  35.6 8.8 %all-to-all-done.refs_0_ = bf16[8,208,128]{2,1,0:T(8,128)(2,1)S(1)} async-done(((bf16[8,208,128]{2,1,0:T(8,128)(2,1)}), bf16[8,208,128]{2,1,0:T(8,128)(2,1)S(1)}, u32[]{:S(2)}, u32[]{:S(2)}) %all-to-all-start) | async-done | bytes 426016 | tf_op jit(solution)/shard_map/all_to_all | solution.py:344
  44.4 0.9 %shard_map.152 = (bf16[1,4,2048]{2,1,0:T(4,128)(2,1)}, bf16[8,32,256]{2,1,0:T(8,128)(2,1)}, bf16[8,32,256]{2,1,0:T(8,128)(2,1)}) custom-call(bf16[8,208,128]{2,1,0:T(8,128)(2,1)S(1)} %all-to-all-done.refs_0_, f32[72,128]{1,0:T(8,128)S(1)} %shard_map.151.refs_1_), custom_call_target="tpu_custom_call" | custom-call | bytes 524288 | tf_op jit(solution)/shard_map/pallas_call | solution.py:435
Async XLA Ops:
  0.6 5.5 %collective-permute-start = (bf16[256,4096]{1,0:T(8,128)(2,1)}, bf16[256,4096]{1,0:T(8,128)(2,1)S(1)}, u32[]{:S(2)}, u32[]{:S(2)}) collective-permute-start(bf16[256,4096]{1,0:T(8,128)(2,1)} %refs_5_.1), channel_id=1, source_target_pairs={{0,1},{1,0},{2,3},{3,2},{4,5},{5,4},{6,7},{7,6},{8,9},{9,8},{10,11... | collective-permute-start | bytes 6291464 | tf_op jit(solution)/shard_map/ppermute | solution.py:338
  1.2 5.0 %collective-permute-start.1 = (bf16[64,4096]{1,0:T(8,128)(2,1)}, bf16[64,4096]{1,0:T(8,128)(2,1)S(1)}, u32[]{:S(2)}, u32[]{:S(2)}) collective-permute-start(bf16[64,4096]{1,0:T(8,128)(2,1)} %refs_6_.1), channel_id=1, source_target_pairs={{0,1},{1,0},{2,3},{3,2},{4,5},{5,4},{6,7},{7,6},{8,9},{9,8},{10,11... | collective-permute-start | bytes 1572872 | tf_op jit(solution)/shard_map/ppermute | solution.py:338
  9.8 8.9 %collective-permute-start.2 = (bf16[32,512]{1,0:T(8,128)(2,1)S(1)}, bf16[32,512]{1,0:T(8,128)(2,1)S(1)}, u32[]{:S(2)}, u32[]{:S(2)}) collective-permute-start(bf16[32,512]{1,0:T(8,128)(2,1)S(1)} %get-tuple-element.37), channel_id=1, source_target_pairs={{0,2},{2,0},{4,6},{6,4},{8,10},{10,8},{12,14},{14,12},{1,3},{3,1},... | collective-permute-start | bytes 98312 | tf_op jit(solution)/shard_map/ppermute | solution.py:341
  12.8 9.5 %collective-permute-start.3 = (bf16[32,512]{1,0:T(8,128)(2,1)S(1)}, bf16[32,512]{1,0:T(8,128)(2,1)S(1)}, u32[]{:S(2)}, u32[]{:S(2)}) collective-permute-start(bf16[32,512]{1,0:T(8,128)(2,1)S(1)} %get-tuple-element.38), channel_id=1, source_target_pairs={{0,4},{2,6},{4,0},{6,2},{8,12},{10,14},{12,8},{14,10},{1,5},{3,7},... | collective-permute-start | bytes 98312 | tf_op jit(solution)/shard_map/ppermute | solution.py:341
  14.3 7.9 %collective-permute-start.4 = (bf16[32,512]{1,0:T(8,128)(2,1)S(1)}, bf16[32,512]{1,0:T(8,128)(2,1)S(1)}, u32[]{:S(2)}, u32[]{:S(2)}) collective-permute-start(bf16[32,512]{1,0:T(8,128)(2,1)S(1)} %get-tuple-element.39), channel_id=1, source_target_pairs={{0,6},{2,4},{4,2},{6,0},{8,14},{10,12},{12,10},{14,8},{1,7},{3,5},... | collective-permute-start | bytes 98312 | tf_op jit(solution)/shard_map/ppermute | solution.py:341
  14.4 7.9 %collective-permute-start.5 = (bf16[32,512]{1,0:T(8,128)(2,1)S(1)}, bf16[32,512]{1,0:T(8,128)(2,1)S(1)}, u32[]{:S(2)}, u32[]{:S(2)}) collective-permute-start(bf16[32,512]{1,0:T(8,128)(2,1)S(1)} %get-tuple-element.40), channel_id=1, source_target_pairs={{0,8},{2,10},{4,12},{6,14},{8,0},{10,2},{12,4},{14,6},{1,9},{3,11}... | collective-permute-start | bytes 98312 | tf_op jit(solution)/shard_map/ppermute | solution.py:341
  17.3 5.7 %collective-permute-start.6 = (bf16[32,512]{1,0:T(8,128)(2,1)S(1)}, bf16[32,512]{1,0:T(8,128)(2,1)S(1)}, u32[]{:S(2)}, u32[]{:S(2)}) collective-permute-start(bf16[32,512]{1,0:T(8,128)(2,1)S(1)} %get-tuple-element.41), channel_id=1, source_target_pairs={{0,10},{2,8},{4,14},{6,12},{8,2},{10,0},{12,6},{14,4},{1,11},{3,9}... | collective-permute-start | bytes 98312 | tf_op jit(solution)/shard_map/ppermute | solution.py:341
  18.6 5.9 %collective-permute-start.7 = (bf16[32,512]{1,0:T(8,128)(2,1)S(1)}, bf16[32,512]{1,0:T(8,128)(2,1)S(1)}, u32[]{:S(2)}, u32[]{:S(2)}) collective-permute-start(bf16[32,512]{1,0:T(8,128)(2,1)S(1)} %get-tuple-element.42), channel_id=1, source_target_pairs={{0,12},{2,14},{4,8},{6,10},{8,4},{10,6},{12,0},{14,2},{1,13},{3,15... | collective-permute-start | bytes 98312 | tf_op jit(solution)/shard_map/ppermute | solution.py:341
  22.2 6.6 %collective-permute-start.8 = (bf16[32,512]{1,0:T(8,128)(2,1)S(1)}, bf16[32,512]{1,0:T(8,128)(2,1)S(1)}, u32[]{:S(2)}, u32[]{:S(2)}) collective-permute-start(bf16[32,512]{1,0:T(8,128)(2,1)S(1)} %get-tuple-element.43), channel_id=1, source_target_pairs={{0,14},{2,12},{4,10},{6,8},{8,6},{10,4},{12,2},{14,0},{1,15},{3,13... | collective-permute-start | bytes 98312 | tf_op jit(solution)/shard_map/ppermute | solution.py:341
  30.9 13.6 %all-to-all-start = ((bf16[8,208,128]{2,1,0:T(8,128)(2,1)}), bf16[8,208,128]{2,1,0:T(8,128)(2,1)S(1)}, u32[]{:S(2)}, u32[]{:S(2)}) async-start(bf16[8,208,128]{2,1,0:T(8,128)(2,1)} %get-tuple-element.44), calls=%async_computation | async-start | bytes 851968 | tf_op jit(solution)/shard_map/all_to_all | solution.py:344

commit v9 on v7

--- a/solution.py
+++ b/solution.py
@@ -78,11 +78,16 @@
 
 def prepare_kernel(sizes, *refs):
     n, img, tok, blocks, lot, page_cap = sizes
-    far, (info, slots), near, small, (starts, sems) = refs[:8], refs[8:10], refs[10:13], refs[13:18], refs[18:]
-    half = near[0].shape[0]
-    mine = pl.ds(pl.multiple_of(lax.axis_index("tensor") * half, half), half)
-    sources = (*far[:5], far[5].at[mine], far[6].at[mine], far[7])
-    copies = [pltpu.make_async_copy(a, b, sems.at[i]) for i, (a, b) in enumerate(zip(sources, small + near))]
+    far, (info, slots), near, small, (starts, sems) = refs[:10], refs[10:12], refs[12:17], refs[17:22], refs[22:]
+    held = near[0].shape[0]
+    half = near[2].shape[1]
+    me = lax.axis_index("tensor")
+    pairs = list(zip(far[:5], small)) + list(zip(far[7:], near[2:]))
+    for w, kept in zip(far[5:7], near[:2]):
+        for start, at, size in ((me * half, 0, half), ((1 - me) * half, half, held - half)):
+            source = pl.ds(pl.multiple_of(start, held - half), size)
+            pairs.append((w.at[source], kept.at[at : at + size]))
+    copies = [pltpu.make_async_copy(a, b, sems.at[i]) for i, (a, b) in enumerate(pairs)]
     for c in copies:
         c.start()
     route, pages, count, tail, req = small
@@ -149,25 +154,28 @@
 
 
 def vis_kernel(n, lot, step, *refs):
-    near, far, gain, key_near, value_near, w_key, w_value, info, query, out, key_far, value_far, total, sems = refs
+    near, far, gain, query, key_held, value_held, w_key, w_value, info, out, key_rest, value_rest, total, sems = refs
     img, half = near.shape
     kvw = w_key.shape[1]
     me = lax.axis_index("tensor")
-    other = pl.ds(pl.multiple_of((1 - me) * half, half), half)
-    pairs = ((w_key, key_far), (w_value, value_far))
-    copies = [pltpu.make_async_copy(w.at[other], held, sems.at[i]) for i, (w, held) in enumerate(pairs)]
+    held, size = key_held.shape[0], key_rest.shape[0]
+    last = pl.ds(pl.multiple_of((1 - me) * half + held - half, size), size)
+    pairs = ((w_key, key_rest), (w_value, value_rest))
+    copies = [pltpu.make_async_copy(w.at[last], kept, sems.at[i]) for i, (w, kept) in enumerate(pairs)]
     for c in copies:
         c.start()
     scale = scale_of(near, far)
-    for rows, side, weights in ((near, me, (key_near, value_near)), (far, 1 - me, (key_far, value_far))):
-        if rows is far:
+    for at in range(0, 2 * half, step):
+        if at == held:
             for c in copies:
                 c.wait()
-        for c in range(0, half, step):
-            columns = pl.ds(pl.multiple_of(side * half + c, step), step)
-            normed = normed_rows(rows, c, step, scale, gain[:, columns])
-            for w, at in zip(weights, (0, kvw)):
-                add_part(total, at, normed, w[c : c + step, :], rows is near and c == 0)
+        rows, side = (near, me) if at < half else (far, 1 - me)
+        weights, w_at = ((key_held, value_held), at) if at < held else ((key_rest, value_rest), at - held)
+        c = at % half
+        columns = pl.ds(pl.multiple_of(side * half + c, step), step)
+        normed = normed_rows(rows, c, step, scale, gain[:, columns])
+        for w, col in zip(weights, (0, kvw)):
+            add_part(total, col, normed, w[w_at : w_at + step, :], at == 0)
     slot = lax.broadcasted_iota(I32, (n * lot, img), 0)
     chosen = jnp.where(slot == info[0:1, :img], 1.0, 0.0).astype(BF16)
     packed = dot(chosen, total[...].astype(BF16)).astype(BF16)
@@ -409,22 +417,35 @@
     lot = -(-cap // PAGE) * PAGE
     q_lots = q_rows * HD // (2 * kvw)
     width = max(tok, n * lot)
-    arguments = (img_route.T, page_dest.T, page_count, tail_len, dec_req, w_key, w_value, vis_rows)
-    info, slots, key_near, value_near, vis_near = call(
+    gain = norm_gain.reshape(1, 2 * half)
+    held = half + half // 2
+    arguments = (
+        img_route.T,
+        page_dest.T,
+        page_count,
+        tail_len,
+        dec_req,
+        w_key,
+        w_value,
+        vis_rows,
+        gain,
+        query,
+    )
+    info, slots, key_held, value_held, vis_near, gain_near, query_near = call(
         lambda *refs: prepare_kernel((n, img, tok, blocks, lot, page_cap), *refs),
         (
             jax.ShapeDtypeStruct((8, width), I32),
             jax.ShapeDtypeStruct((blocks,), I32),
-            pltpu.VMEM((half, kvw), BF16),
-            pltpu.VMEM((half, kvw), BF16),
-            pltpu.VMEM(vis_rows.shape, BF16),
+            pltpu.VMEM((held, kvw), BF16),
+            pltpu.VMEM((held, kvw), BF16),
+            *[pltpu.VMEM(a.shape, a.dtype) for a in arguments[7:]],
         ),
         [ANY] * len(arguments),
-        (VM, SM) + (VM,) * 3,
+        (VM, SM) + (VM,) * 5,
         [
             *[(pltpu.VMEM if i == 0 else pltpu.SMEM)(a.shape, a.dtype) for i, a in enumerate(arguments[:5])],
             pltpu.SMEM((n,), I32),
-            pltpu.SemaphoreType.DMA((len(arguments),)),
+            pltpu.SemaphoreType.DMA((len(arguments) + 2,)),
         ],
         flops=1 << 20,
         traffic=2 * 2 * half * 2 * kvw * 2,
@@ -432,16 +453,15 @@
 
     step = min(1024, half)
     load = min(2048, half)
-    gain = remote(norm_gain.reshape(1, 2 * half))
 
     packed = call(
         lambda *refs: vis_kernel(n, lot, step, *refs),
-        jax.ShapeDtypeStruct((n, q_lots + lot, 2 * kvw), BF16),
-        [VM] * 5 + [ANY] * 2 + [VM] * 2,
+        pltpu.VMEM((n, q_lots + lot, 2 * kvw), BF16),
+        [VM] * 6 + [ANY] * 2 + [VM],
         VM,
         [
-            pltpu.VMEM((half, kvw), BF16),
-            pltpu.VMEM((half, kvw), BF16),
+            pltpu.VMEM((2 * half - held, kvw), BF16),
+            pltpu.VMEM((2 * half - held, kvw), BF16),
             pltpu.VMEM((img, 2 * kvw), F32),
             pltpu.SemaphoreType.DMA((2,)),
         ],
@@ -450,13 +470,13 @@
     )(
         local(vis_near),
         vis_far,
-        gain,
-        local(key_near),
-        local(value_near),
+        local(gain_near),
+        local(query_near),
+        local(key_held),
+        local(value_held),
         remote(w_key),
         remote(w_value),
         info,
-        remote(query),
     )
     arrived = exchange(packed)
 
@@ -480,12 +500,12 @@
         limit=24,
         flops=2 * tok * 2 * half * 2 * kvw,
         traffic=2 * tok * 2 * half + 8 * half * kvw,
-    )(remote(text_rows), text_far, gain, remote(w_key), remote(w_value), info, slots)
+    )(remote(text_rows), text_far, remote(gain), remote(w_key), remote(w_value), info, slots)
 
     sent, own = call(
         lambda *refs: attend_kernel(n, cap, lot, page_cap, kv_heads, *refs),
         (
-            jax.ShapeDtypeStruct((n, block, HD), BF16),
+            pltpu.VMEM((n, block, HD), BF16),
             jax.ShapeDtypeStruct((q_rows + STAT, HD), F32),
         ),
         [SM] + [VM] * 5,

time: 44.7 us -> 43.8 us (0.980)
  Pallas kernels: 17.6 us -> 16.9 us
    pallas_call x1, Pallas kernels: 4.84 us -> 3.41 us  [body(): call(lambda *refs: vis_kernel(n, lot, step, *refs), pltpu.VMEM((n, q_lots...]
    pallas_call x1, Pallas kernels: 2.98 us -> 3.7 us  [body(): call(lambda *refs: prepare_kernel((n, img, tok, blocks, lot, page_cap), *...]
  transfers between devices with their start and end apart: 4 -> 4, of which waited for: 2 -> 2; matrix products, arithmetic and copies ran while one was open for 0% -> 0% of each run, Pallas kernels for 33% -> 32%
where the time goes in v9:
time: 43.8 us; the launch traced here: 43.4 us
  Pallas kernels  16.9 us (39%)
  waiting for transfers between devices  14.3 us (33%)
  starting transfers between devices  11.5 us (26%)
  between operations  0.68 us (2%)
    all_to_all x2, waiting for transfers between devices, exchange(): lax.all_to_all(array, 'section', split_axis=0, concat_axis=0, tiled=True)  14.3 us
    all_to_all x2, starting transfers between devices, exchange(): lax.all_to_all(array, 'section', split_axis=0, concat_axis=0, tiled=True)  10.9 us
    pallas_call x1, Pallas kernels, body(): call(lambda *refs: text_kernel(load, step, page_cap, q_rows // kv_heads,...  5.58 us
    pallas_call x1, Pallas kernels, body(): call(lambda *refs: prepare_kernel((n, img, tok, blocks, lot, page_cap), *...  3.7 us
    pallas_call x1, Pallas kernels, body(): call(lambda *refs: vis_kernel(n, lot, step, *refs), pltpu.VMEM((n, q_lots...  3.41 us
    pallas_call x1, Pallas kernels, body(): call(lambda *refs: attend_kernel(n, cap, lot, page_cap, kv_heads, *refs),...  1.98 us
    pallas_call x1, Pallas kernels, body(): call(lambda *refs: fresh_kernel(kv_heads, steps, *refs), jax.ShapeDtypeSt...  1.3 us
    pallas_call x1, Pallas kernels, body(): call(lambda *refs: finish_kernel(kv_heads, steps, page_cap, *refs), (jax....  0.93 us
  transfers between devices with their start and end apart: 4, of which 2 were waited for; matrix products, arithmetic and copies ran while one was open for 0% of the time, Pallas kernels for 32%

profile of v9, /device:TPU:0, one launch (start us, length us, event | category | flops | bytes accessed | tf_op | source)
XLA Modules:
  0.0 43.4 jit_solution(14832822812603217179)
XLA Ops:
  0.6 0.5 %collective-permute-start.1 = (bf16[64,4096]{1,0:T(8,128)(2,1)}, bf16[64,4096]{1,0:T(8,128)(2,1)S(1)}, u32[]{:S(2)}, u32[]{:S(2)}) collective-permute-start(bf16[64,4096]{1,0:T(8,128)(2,1)} %refs_7_.2), channel_id=1, source_target_pairs={{0,1},{1,0},{2,3},{3,2},{4,5},{5,4},{6,7},{7,6},{8,9},{9,8},{10,11... | collective-permute-start | bytes 1572872 | tf_op jit(solution)/shard_map/ppermute | solution.py:402
  1.2 0.1 collective-permute-start
  1.2 3.7 %shard_map.148 = (s32[8,256]{1,0:T(8,128)S(1)}, s32[16]{0:T(128)S(1)}, bf16[6144,256]{1,0:T(8,128)(2,1)S(1)}, bf16[6144,256]{1,0:T(8,128)(2,1)S(1)}, bf16[64,409...) custom-call(s32[1,512]{1,0:T(1,128)} %bitcast.18, s32[1,128]{1,0:T(1,128)} %bitcast.19, ...), custom_call_target="tpu_custom_call" | custom-call | flops 1048576 | bytes 16777216 | tf_op jit(solution)/shard_map/pallas_call | solution.py:434
  4.9 0.0 collective-permute-done.1.refs_1_
  4.9 3.4 %shard_map.150 = bf16[8,32,512]{2,1,0:T(8,128)(2,1)} custom-call(bf16[64,4096]{1,0:T(8,128)(2,1)S(1)} %get-tuple-element.21.refs_0_, bf16[64,4096]{1,0:T(8,128)(2,1)S(1)} %collective-permute-done.1.refs_1_, f32[1,8192]{1,0:T(1,128)S(1)} %get-tuple-element.22.refs_2_, bf16[64,128]{1,0:T(8,128)(2,1)S(1)} %get-tuple-element.23.refs_3_, ...), custom_call_target="tpu_custom_call" | custom-call | flops 17179869184 | bytes 9437184 | tf_op jit(solution)/shard_map/pallas_call | solution.py:457
  8.4 7.3 %all-to-all-start = ((bf16[8,32,512]{2,1,0:T(8,128)(2,1)}), bf16[8,32,512]{2,1,0:T(8,128)(2,1)S(1)}, u32[]{:S(2)}, u32[]{:S(2)}) async-start(bf16[8,32,512]{2,1,0:T(8,128)(2,1)} %shard_map.150), calls=%async_computation | async-start | bytes 524288 | tf_op jit(solution)/shard_map/all_to_all | solution.py:405
  15.6 0.0 collective-permute-done.refs_1_
  15.6 5.6 %shard_map.149 = (bf16[256,512]{1,0:T(8,128)(2,1)S(1)}, f32[256,256]{1,0:T(8,128)S(1)}, bf16[8,128,128]{2,1,0:T(8,128)(2,1)S(1)}) custom-call(bf16[256,4096]{1,0:T(8,128)(2,1)} %refs_0_.1, bf16[256,4096]{1,0:T(8,128)(2,1)S(1)} %collective-permute-done.refs_1_, f32[1,8192]{1,0:T(1,128)} %bitcast.13, bf16[8192,256]{1,0:T(8,128)(2,1)} %refs_6_.3, ...), custom_call_target="tpu_custom_call" | custom-call | flops 2147483648 | bytes 12582912 | tf_op jit(solution)/shard_map/pallas_call | solution.py:484
  21.2 3.6 %all-to-all-done.refs_3_ = bf16[8,32,512]{2,1,0:T(8,128)(2,1)S(1)} async-done(((bf16[8,32,512]{2,1,0:T(8,128)(2,1)}), bf16[8,32,512]{2,1,0:T(8,128)(2,1)S(1)}, u32[]{:S(2)}, u32[]{:S(2)}) %all-to-all-start) | async-done | bytes 262176 | tf_op jit(solution)/shard_map/all_to_all | solution.py:405
  24.8 2.0 %shard_map.151 = (bf16[8,208,128]{2,1,0:T(8,128)(2,1)}, f32[72,128]{1,0:T(8,128)S(1)}) custom-call(s32[16]{0:T(128)S(1)} %get-tuple-element.18.refs_6_.refs_0_, s32[8,256]{1,0:T(8,128)S(1)} %get-tuple-element.19.refs_5_.refs_8_.refs_1_, bf16[256,512]{1,0:T(8,128)(2,1)S(1)} %get-tuple-element.20.refs_2_, bf16[8,32,512]{2,1,0:T(8,128)(2,1)S(1)} %all-to-all-done.refs_3_, ...), custom_call_target="tpu_custom_call" | custom-call | flops 67108864 | bytes 294912 | tf_op jit(solution)/shard_map/pallas_call | solution.py:505
  26.8 3.6 %all-to-all-start.1 = ((bf16[8,208,128]{2,1,0:T(8,128)(2,1)}), bf16[8,208,128]{2,1,0:T(8,128)(2,1)S(1)}, u32[]{:S(2)}, u32[]{:S(2)}) async-start(bf16[8,208,128]{2,1,0:T(8,128)(2,1)} %get-tuple-element.28), calls=%async_computation.1 | async-start | bytes 851968 | tf_op jit(solution)/shard_map/all_to_all | solution.py:405
  30.4 1.3 %shard_map.152.refs_1_ = f32[72,128]{1,0:T(8,128)S(1)} custom-call(bf16[64,128]{1,0:T(8,128)(2,1)} %bitcast.15, bf16[4,256]{1,0:T(4,128)(2,1)} %bitcast.16, bf16[4,256]{1,0:T(4,128)(2,1)} %bitcast.17, f32[72,128]{1,0:T(8,128)S(1)} %get-tuple-element.29.refs_3_), custom_call_target="tpu_custom_call" | custom-call | flops 1048576 | bytes 262144 | tf_op jit(solution)/shard_map/pallas_call | solution.py:523
  31.7 10.8 %all-to-all-done.1.refs_0_ = bf16[8,208,128]{2,1,0:T(8,128)(2,1)S(1)} async-done(((bf16[8,208,128]{2,1,0:T(8,128)(2,1)}), bf16[8,208,128]{2,1,0:T(8,128)(2,1)S(1)}, u32[]{:S(2)}, u32[]{:S(2)}) %all-to-all-start.1) | async-done | bytes 426016 | tf_op jit(solution)/shard_map/all_to_all | solution.py:405
  42.4 0.9 %shard_map.153 = (bf16[1,4,2048]{2,1,0:T(4,128)(2,1)}, bf16[8,32,256]{2,1,0:T(8,128)(2,1)}, bf16[8,32,256]{2,1,0:T(8,128)(2,1)}) custom-call(bf16[8,208,128]{2,1,0:T(8,128)(2,1)S(1)} %all-to-all-done.1.refs_0_, f32[72,128]{1,0:T(8,128)S(1)} %shard_map.152.refs_1_), custom_call_target="tpu_custom_call" | custom-call | bytes 524288 | tf_op jit(solution)/shard_map/pallas_call | solution.py:533
Async XLA Ops:
  0.6 4.3 %collective-permute-start.1 = (bf16[64,4096]{1,0:T(8,128)(2,1)}, bf16[64,4096]{1,0:T(8,128)(2,1)S(1)}, u32[]{:S(2)}, u32[]{:S(2)}) collective-permute-start(bf16[64,4096]{1,0:T(8,128)(2,1)} %refs_7_.2), channel_id=1, source_target_pairs={{0,1},{1,0},{2,3},{3,2},{4,5},{5,4},{6,7},{7,6},{8,9},{9,8},{10,11... | collective-permute-start | bytes 1572872 | tf_op jit(solution)/shard_map/ppermute | solution.py:402
  1.2 14.5 %collective-permute-start = (bf16[256,4096]{1,0:T(8,128)(2,1)}, bf16[256,4096]{1,0:T(8,128)(2,1)S(1)}, u32[]{:S(2)}, u32[]{:S(2)}) collective-permute-start(bf16[256,4096]{1,0:T(8,128)(2,1)} %refs_0_.1), channel_id=1, source_target_pairs={{0,1},{1,0},{2,3},{3,2},{4,5},{5,4},{6,7},{7,6},{8,9},{9,8},{10,11... | collective-permute-start | bytes 6291464 | tf_op jit(solution)/shard_map/ppermute | solution.py:402
  8.4 16.4 %all-to-all-start = ((bf16[8,32,512]{2,1,0:T(8,128)(2,1)}), bf16[8,32,512]{2,1,0:T(8,128)(2,1)S(1)}, u32[]{:S(2)}, u32[]{:S(2)}) async-start(bf16[8,32,512]{2,1,0:T(8,128)(2,1)} %shard_map.150), calls=%async_computation | async-start | bytes 524288 | tf_op jit(solution)/shard_map/all_to_all | solution.py:405
  26.8 15.7 %all-to-all-start.1 = ((bf16[8,208,128]{2,1,0:T(8,128)(2,1)}), bf16[8,208,128]{2,1,0:T(8,128)(2,1)S(1)}, u32[]{:S(2)}, u32[]{:S(2)}) async-start(bf16[8,208,128]{2,1,0:T(8,128)(2,1)} %get-tuple-element.28), calls=%async_computation.1 | async-start | bytes 851968 | tf_op jit(solution)/shard_map/all_to_all | solution.py:405

commit v10 on v9

--- a/solution.py
+++ b/solution.py
@@ -30,6 +30,14 @@
         compiler_params=pltpu.CompilerParams(vmem_limit_bytes=limit * MIB),
         cost_estimate=pl.CostEstimate(flops=flops, bytes_accessed=traffic, transcendentals=0),
     )
+
+
+def rank_of(section, n):
+    return jnp.where(section < n // 2, n - 2 - 2 * section, 2 * section - n + 1)
+
+
+def section_of(rank, n):
+    return n // 2 - 1 - rank // 2 + rank % 2 * (rank // 2 * 2 + 1)
 
 
 def dot(a, b):
@@ -103,9 +111,9 @@
     earlier = lax.broadcasted_iota(I32, (img, img), 0) < lax.broadcasted_iota(I32, (img, img), 1)
     prefix = dot(ones, jnp.where(earlier, 1.0, 0.0).astype(BF16))
     local = jnp.sum(jnp.where(marks, prefix, 0.0), axis=0, keepdims=True).astype(I32)
-    info[0:1, :img] = own * lot + local
+    info[0:1, :img] = rank_of(own, n) * lot + local
     lanes = lax.broadcasted_iota(I32, (1, n * lot), 1)
-    source, inner = lanes // lot, lanes % lot
+    source, inner = section_of(lanes // lot, n), lanes % lot
     fits = jnp.zeros((1, n * lot), I32)
     offset = jnp.zeros((1, n * lot), I32)
     for e in range(n):
@@ -127,7 +135,7 @@
     info[1:2, :tok] = token_slot
     for g in range(blocks):
         holder = pages[0, pos * blocks + g]
-        slot = holder * page_cap
+        slot = rank_of(holder, n) * page_cap
         for e in range(g):
             slot = slot + (pages[0, pos * blocks + e] == holder).astype(I32)
         slots[g] = slot
@@ -232,12 +240,12 @@
     for g in range(tok // PAGE):
         put_page(base, page_cap, slots[g], out[g * PAGE : (g + 1) * PAGE, :])
     token_slot = row_to_column(info[1:2, :tok].astype(F32))
-    lanes = lax.broadcasted_iota(I32, bias.shape, 1) // q_rows
+    lanes = section_of(lax.broadcasted_iota(I32, bias.shape, 1) // q_rows, bias.shape[1] // q_rows)
     bias[...] = jnp.where(token_slot == lanes.astype(F32), 0.0, LOWEST)
 
 
 def attend_kernel(n, cap, lot, page_cap, kv_heads, slots, info, kv_text, arrived, bias, base, out, own, mixed, held, rows_held):
-    pos = lax.axis_index("section")
+    rank = rank_of(lax.axis_index("section"), n)
     tok = kv_text.shape[0]
     kvw = kv_heads * HD
     q_lots = arrived.shape[1] - lot
@@ -276,13 +284,13 @@
             weights.astype(BF16), value, (((0,), (0,)), ((), ())), preferred_element_type=F32
         )
         held[g * n * rows : (g + 1) * n * rows, :] = numerator
-        own[g * rows : (g + 1) * rows, :] = held[pl.ds(pl.multiple_of((g * n + pos) * rows, rows), rows), :]
+        own[g * rows : (g + 1) * rows, :] = held[pl.ds(pl.multiple_of((g * n + rank) * rows, rows), rows), :]
         numerator = numerator.astype(BF16)
         for k in range(n):
             out[k, pages + g * rows : pages + (g + 1) * rows, :] = numerator[k * rows : (k + 1) * rows, :]
     stat_rows = 2 * kv_heads
     share = HD // rows
-    window = pl.ds(pl.multiple_of(pos // share * HD, HD), HD)
+    window = pl.ds(pl.multiple_of(rank // share * HD, HD), HD)
     own[kv_heads * rows : kv_heads * rows + stat_rows, :] = rows_held[:stat_rows, window]
     blank = jnp.zeros((PAGE - 3 * stat_rows, HD), F32)
     for w in range(-(-n // share)):
@@ -307,10 +315,10 @@
     return numerator, total
 
 
-def fresh_kernel(kv_heads, steps, query, key, value, own, mine):
+def fresh_kernel(n, kv_heads, steps, query, key, value, own, mine):
     rows = query.shape[0] // kv_heads
     every = kv_heads * rows
-    start = lax.axis_index("section") % (HD // rows) * rows
+    start = rank_of(lax.axis_index("section"), n) % (HD // rows) * rows
     row = lax.broadcasted_iota(I32, (rows, steps), 0)
     causal = lax.broadcasted_iota(I32, (rows, steps), 1) <= row % steps
     tops, totals = [], []
@@ -337,14 +345,14 @@
     pos = lax.axis_index("section")
     every = mine.shape[0] - STAT
     rows = every // kv_heads
-    start = pos % (HD // rows) * rows
+    start = rank_of(pos, n) % (HD // rows) * rows
     chunk = page_cap * PAGE
     halves = keys.shape[2] // HD
     for k in range(n):
         for i, out in enumerate((keys, values)):
             for h in range(halves):
                 part = i * halves + h
-                out[k, :, h * HD : (h + 1) * HD] = shares[k, part * chunk : (part + 1) * chunk, :]
+                out[section_of(k, n), :, h * HD : (h + 1) * HD] = shares[k, part * chunk : (part + 1) * chunk, :]
     pages = 2 * halves * chunk
     stats = row_to_column(mine[every : every + 1, :])
     lines = []
@@ -356,7 +364,7 @@
         at = slice(g * rows, (g + 1) * rows)
         pieces = [(mine[at, :], stats[at], stats[every + g * rows : every + (g + 1) * rows])]
         for k in range(n):
-            away = pos != k
+            away = pos != section_of(k, n)
             top = jnp.where(away, pick_column(lines[k][g : g + 1], rows, start), LOWEST)
             weight = jnp.where(away, pick_column(lines[k][kv_heads + g : kv_heads + g + 1], rows, start), 0.0)
             share = shares[k, pages + g * rows : pages + (g + 1) * rows, :].astype(F32)
@@ -402,7 +410,8 @@
         return lax.ppermute(array, "tensor", [(0, 1), (1, 0)])
 
     def exchange(array):
-        return lax.all_to_all(array, "section", split_axis=0, concat_axis=0, tiled=True)
+        order = [[section_of(rank, n) for rank in range(n)]]
+        return lax.all_to_all(array, "section", split_axis=0, concat_axis=0, tiled=True, axis_index_groups=order)
 
     def remote(array):
         return pltpu.with_memory_space_constraint(array, pltpu.HBM)
@@ -521,7 +530,7 @@
     shares = exchange(sent)
 
     mine = call(
-        lambda *refs: fresh_kernel(kv_heads, steps, *refs),
+        lambda *refs: fresh_kernel(n, kv_heads, steps, *refs),
         jax.ShapeDtypeStruct((q_rows + STAT, HD), F32),
         [VM] * 4,
         VM,

time: 43.8 us -> 40.3 us (0.920)
  waiting for transfers between devices: 14.3 us -> 9.64 us
  starting transfers between devices: 11.5 us -> 12.6 us
    all_to_all x2, waiting for transfers between devices: 14.3 us -> 9.63 us  [exchange(): lax.all_to_all(array, 'section', split_axis=0, concat_axis=0, tiled=True,...]
    all_to_all x2, starting transfers between devices: 10.9 us -> 12 us  [exchange(): lax.all_to_all(array, 'section', split_axis=0, concat_axis=0, tiled=True,...]
  transfers between devices with their start and end apart: 4 -> 4, of which waited for: 2 -> 2; matrix products, arithmetic and copies ran while one was open for 0% -> 0% of each run, Pallas kernels for 32% -> 35%
where the time goes in v10:
time: 40.3 us; the launch traced here: 39.8 us
  Pallas kernels  16.9 us (42%)
  starting transfers between devices  12.6 us (31%)
  waiting for transfers between devices  9.64 us (24%)
  between operations  0.68 us (2%)
    all_to_all x2, starting transfers between devices, exchange(): lax.all_to_all(array, 'section', split_axis=0, concat_axis=0, tiled=True,...  12 us
    all_to_all x2, waiting for transfers between devices, exchange(): lax.all_to_all(array, 'section', split_axis=0, concat_axis=0, tiled=True,...  9.63 us
    pallas_call x1, Pallas kernels, body(): call(lambda *refs: text_kernel(load, step, page_cap, q_rows // kv_heads,...  5.56 us
    pallas_call x1, Pallas kernels, body(): call(lambda *refs: prepare_kernel((n, img, tok, blocks, lot, page_cap), *...  3.7 us
    pallas_call x1, Pallas kernels, body(): call(lambda *refs: vis_kernel(n, lot, step, *refs), pltpu.VMEM((n, q_lots...  3.41 us
    pallas_call x1, Pallas kernels, body(): call(lambda *refs: attend_kernel(n, cap, lot, page_cap, kv_heads, *refs),...  1.98 us
    pallas_call x1, Pallas kernels, body(): call(lambda *refs: fresh_kernel(n, kv_heads, steps, *refs), jax.ShapeDtyp...  1.3 us
    pallas_call x1, Pallas kernels, body(): call(lambda *refs: finish_kernel(kv_heads, steps, page_cap, *refs), (jax....  0.93 us
  transfers between devices with their start and end apart: 4, of which 2 were waited for; matrix products, arithmetic and copies ran while one was open for 0% of the time, Pallas kernels for 35%

profile of v10, /device:TPU:0, one launch (start us, length us, event | category | flops | bytes accessed | tf_op | source)
XLA Modules:
  0.0 39.8 jit_solution(5538156278911767965)
XLA Ops:
  0.6 0.5 %collective-permute-start.1 = (bf16[64,4096]{1,0:T(8,128)(2,1)}, bf16[64,4096]{1,0:T(8,128)(2,1)S(1)}, u32[]{:S(2)}, u32[]{:S(2)}) collective-permute-start(bf16[64,4096]{1,0:T(8,128)(2,1)} %refs_7_.2), channel_id=1, source_target_pairs={{0,1},{1,0},{2,3},{3,2},{4,5},{5,4},{6,7},{7,6},{8,9},{9,8},{10,11... | collective-permute-start | bytes 1572872 | tf_op jit(solution)/shard_map/ppermute | solution.py:410
  1.2 0.1 collective-permute-start
  1.2 3.7 %shard_map.148 = (s32[8,256]{1,0:T(8,128)S(1)}, s32[16]{0:T(128)S(1)}, bf16[6144,256]{1,0:T(8,128)(2,1)S(1)}, bf16[6144,256]{1,0:T(8,128)(2,1)S(1)}, bf16[64,409...) custom-call(s32[1,512]{1,0:T(1,128)} %bitcast.18, s32[1,128]{1,0:T(1,128)} %bitcast.19, ...), custom_call_target="tpu_custom_call" | custom-call | flops 1048576 | bytes 16777216 | tf_op jit(solution)/shard_map/pallas_call | solution.py:443
  4.9 0.0 collective-permute-done.1.refs_1_
  4.9 3.4 %shard_map.150 = bf16[8,32,512]{2,1,0:T(8,128)(2,1)} custom-call(bf16[64,4096]{1,0:T(8,128)(2,1)S(1)} %get-tuple-element.21.refs_0_, bf16[64,4096]{1,0:T(8,128)(2,1)S(1)} %collective-permute-done.1.refs_1_, f32[1,8192]{1,0:T(1,128)S(1)} %get-tuple-element.22.refs_2_, bf16[64,128]{1,0:T(8,128)(2,1)S(1)} %get-tuple-element.23.refs_3_, ...), custom_call_target="tpu_custom_call" | custom-call | flops 17179869184 | bytes 9437184 | tf_op jit(solution)/shard_map/pallas_call | solution.py:466
  8.4 7.8 %all-to-all-start = ((bf16[8,32,512]{2,1,0:T(8,128)(2,1)}), bf16[8,32,512]{2,1,0:T(8,128)(2,1)S(1)}, u32[]{:S(2)}, u32[]{:S(2)}) async-start(bf16[8,32,512]{2,1,0:T(8,128)(2,1)} %shard_map.150), calls=%async_computation | async-start | bytes 524288 | tf_op jit(solution)/shard_map/all_to_all | solution.py:414
  16.2 0.0 collective-permute-done.refs_1_
  16.2 5.6 %shard_map.149 = (bf16[256,512]{1,0:T(8,128)(2,1)S(1)}, f32[256,256]{1,0:T(8,128)S(1)}, bf16[8,128,128]{2,1,0:T(8,128)(2,1)S(1)}) custom-call(bf16[256,4096]{1,0:T(8,128)(2,1)} %refs_0_.1, bf16[256,4096]{1,0:T(8,128)(2,1)S(1)} %collective-permute-done.refs_1_, f32[1,8192]{1,0:T(1,128)} %bitcast.13, bf16[8192,256]{1,0:T(8,128)(2,1)} %refs_6_.3, ...), custom_call_target="tpu_custom_call" | custom-call | flops 2147483648 | bytes 12582912 | tf_op jit(solution)/shard_map/pallas_call | solution.py:493
  21.8 1.8 %all-to-all-done.refs_3_ = bf16[8,32,512]{2,1,0:T(8,128)(2,1)S(1)} async-done(((bf16[8,32,512]{2,1,0:T(8,128)(2,1)}), bf16[8,32,512]{2,1,0:T(8,128)(2,1)S(1)}, u32[]{:S(2)}, u32[]{:S(2)}) %all-to-all-start) | async-done | bytes 262176 | tf_op jit(solution)/shard_map/all_to_all | solution.py:414
  23.5 2.0 %shard_map.151 = (bf16[8,208,128]{2,1,0:T(8,128)(2,1)}, f32[72,128]{1,0:T(8,128)S(1)}) custom-call(s32[16]{0:T(128)S(1)} %get-tuple-element.18.refs_6_.refs_0_, s32[8,256]{1,0:T(8,128)S(1)} %get-tuple-element.19.refs_5_.refs_8_.refs_1_, bf16[256,512]{1,0:T(8,128)(2,1)S(1)} %get-tuple-element.20.refs_2_, bf16[8,32,512]{2,1,0:T(8,128)(2,1)S(1)} %all-to-all-done.refs_3_, ...), custom_call_target="tpu_custom_call" | custom-call | flops 67108864 | bytes 294912 | tf_op jit(solution)/shard_map/pallas_call | solution.py:514
  25.5 4.2 %all-to-all-start.1 = ((bf16[8,208,128]{2,1,0:T(8,128)(2,1)}), bf16[8,208,128]{2,1,0:T(8,128)(2,1)S(1)}, u32[]{:S(2)}, u32[]{:S(2)}) async-start(bf16[8,208,128]{2,1,0:T(8,128)(2,1)} %get-tuple-element.28), calls=%async_computation.1 | async-start | bytes 851968 | tf_op jit(solution)/shard_map/all_to_all | solution.py:414
  29.7 1.3 %shard_map.152.refs_1_ = f32[72,128]{1,0:T(8,128)S(1)} custom-call(bf16[64,128]{1,0:T(8,128)(2,1)} %bitcast.15, bf16[4,256]{1,0:T(4,128)(2,1)} %bitcast.16, bf16[4,256]{1,0:T(4,128)(2,1)} %bitcast.17, f32[72,128]{1,0:T(8,128)S(1)} %get-tuple-element.29.refs_3_), custom_call_target="tpu_custom_call" | custom-call | flops 1048576 | bytes 262144 | tf_op jit(solution)/shard_map/pallas_call | solution.py:532
  31.0 7.9 %all-to-all-done.1.refs_0_ = bf16[8,208,128]{2,1,0:T(8,128)(2,1)S(1)} async-done(((bf16[8,208,128]{2,1,0:T(8,128)(2,1)}), bf16[8,208,128]{2,1,0:T(8,128)(2,1)S(1)}, u32[]{:S(2)}, u32[]{:S(2)}) %all-to-all-start.1) | async-done | bytes 426016 | tf_op jit(solution)/shard_map/all_to_all | solution.py:414
  38.9 0.9 %shard_map.153 = (bf16[1,4,2048]{2,1,0:T(4,128)(2,1)}, bf16[8,32,256]{2,1,0:T(8,128)(2,1)}, bf16[8,32,256]{2,1,0:T(8,128)(2,1)}) custom-call(bf16[8,208,128]{2,1,0:T(8,128)(2,1)S(1)} %all-to-all-done.1.refs_0_, f32[72,128]{1,0:T(8,128)S(1)} %shard_map.152.refs_1_), custom_call_target="tpu_custom_call" | custom-call | bytes 524288 | tf_op jit(solution)/shard_map/pallas_call | solution.py:542
Async XLA Ops:
  0.6 4.3 %collective-permute-start.1 = (bf16[64,4096]{1,0:T(8,128)(2,1)}, bf16[64,4096]{1,0:T(8,128)(2,1)S(1)}, u32[]{:S(2)}, u32[]{:S(2)}) collective-permute-start(bf16[64,4096]{1,0:T(8,128)(2,1)} %refs_7_.2), channel_id=1, source_target_pairs={{0,1},{1,0},{2,3},{3,2},{4,5},{5,4},{6,7},{7,6},{8,9},{9,8},{10,11... | collective-permute-start | bytes 1572872 | tf_op jit(solution)/shard_map/ppermute | solution.py:410
  1.2 15.0 %collective-permute-start = (bf16[256,4096]{1,0:T(8,128)(2,1)}, bf16[256,4096]{1,0:T(8,128)(2,1)S(1)}, u32[]{:S(2)}, u32[]{:S(2)}) collective-permute-start(bf16[256,4096]{1,0:T(8,128)(2,1)} %refs_0_.1), channel_id=1, source_target_pairs={{0,1},{1,0},{2,3},{3,2},{4,5},{5,4},{6,7},{7,6},{8,9},{9,8},{10,11... | collective-permute-start | bytes 6291464 | tf_op jit(solution)/shard_map/ppermute | solution.py:410
  8.4 15.2 %all-to-all-start = ((bf16[8,32,512]{2,1,0:T(8,128)(2,1)}), bf16[8,32,512]{2,1,0:T(8,128)(2,1)S(1)}, u32[]{:S(2)}, u32[]{:S(2)}) async-start(bf16[8,32,512]{2,1,0:T(8,128)(2,1)} %shard_map.150), calls=%async_computation | async-start | bytes 524288 | tf_op jit(solution)/shard_map/all_to_all | solution.py:414
  25.5 13.4 %all-to-all-start.1 = ((bf16[8,208,128]{2,1,0:T(8,128)(2,1)}), bf16[8,208,128]{2,1,0:T(8,128)(2,1)S(1)}, u32[]{:S(2)}, u32[]{:S(2)}) async-start(bf16[8,208,128]{2,1,0:T(8,128)(2,1)} %get-tuple-element.28), calls=%async_computation.1 | async-start | bytes 851968 | tf_op jit(solution)/shard_map/all_to_all | solution.py:414

commit v11 on v10

--- a/solution.py
+++ b/solution.py
@@ -33,11 +33,14 @@
 
 
 def rank_of(section, n):
-    return jnp.where(section < n // 2, n - 2 - 2 * section, 2 * section - n + 1)
+    lower = section < n // 2
+    z, y = section // 2, section % 2
+    return jnp.where(lower, n // 4 - 1 - z, z - n // 4) * 4 + (1 - y) * 2 + jnp.where(lower, 0, 1)
 
 
 def section_of(rank, n):
-    return n // 2 - 1 - rank // 2 + rank % 2 * (rank // 2 * 2 + 1)
+    away, side = rank // 4, rank % 2
+    return 2 * (n // 4 - 1 - away + side * (2 * away + 1)) + 1 - rank // 2 % 2
 
 
 def dot(a, b):

time: 40.3 us -> 40.3 us (level)
  starting transfers between devices: 12.6 us -> 13.3 us
  waiting for transfers between devices: 9.64 us -> 9.02 us
    all_to_all x2, starting transfers between devices: 12 us -> 12.7 us  [exchange(): lax.all_to_all(array, 'section', split_axis=0, concat_axis=0, tiled=True,...]
    all_to_all x2, waiting for transfers between devices: 9.63 us -> 9.01 us  [exchange(): lax.all_to_all(array, 'section', split_axis=0, concat_axis=0, tiled=True,...]
where the time goes in v11:
time: 40.3 us; the launch traced here: 39.9 us
  Pallas kernels  16.9 us (42%)
  starting transfers between devices  13.3 us (33%)
  waiting for transfers between devices  9.02 us (22%)
  between operations  0.68 us (2%)
    all_to_all x2, starting transfers between devices, exchange(): lax.all_to_all(array, 'section', split_axis=0, concat_axis=0, tiled=True,...  12.7 us
    all_to_all x2, waiting for transfers between devices, exchange(): lax.all_to_all(array, 'section', split_axis=0, concat_axis=0, tiled=True,...  9.01 us
    pallas_call x1, Pallas kernels, body(): call(lambda *refs: text_kernel(load, step, page_cap, q_rows // kv_heads,...  5.56 us
    pallas_call x1, Pallas kernels, body(): call(lambda *refs: prepare_kernel((n, img, tok, blocks, lot, page_cap), *...  3.7 us
    pallas_call x1, Pallas kernels, body(): call(lambda *refs: vis_kernel(n, lot, step, *refs), pltpu.VMEM((n, q_lots...  3.41 us
    pallas_call x1, Pallas kernels, body(): call(lambda *refs: attend_kernel(n, cap, lot, page_cap, kv_heads, *refs),...  1.98 us
    pallas_call x1, Pallas kernels, body(): call(lambda *refs: fresh_kernel(n, kv_heads, steps, *refs), jax.ShapeDtyp...  1.3 us
    pallas_call x1, Pallas kernels, body(): call(lambda *refs: finish_kernel(kv_heads, steps, page_cap, *refs), (jax....  0.93 us
  transfers between devices with their start and end apart: 4, of which 2 were waited for; matrix products, arithmetic and copies ran while one was open for 0% of the time, Pallas kernels for 35%

profile of v11, /device:TPU:0, one launch (start us, length us, event | category | flops | bytes accessed | tf_op | source)
XLA Modules:
  0.0 39.9 jit_solution(7609544586497616204)
XLA Ops:
  0.6 0.5 %collective-permute-start.1 = (bf16[64,4096]{1,0:T(8,128)(2,1)}, bf16[64,4096]{1,0:T(8,128)(2,1)S(1)}, u32[]{:S(2)}, u32[]{:S(2)}) collective-permute-start(bf16[64,4096]{1,0:T(8,128)(2,1)} %refs_7_.2), channel_id=1, source_target_pairs={{0,1},{1,0},{2,3},{3,2},{4,5},{5,4},{6,7},{7,6},{8,9},{9,8},{10,11... | collective-permute-start | bytes 1572872 | tf_op jit(solution)/shard_map/ppermute | solution.py:413
  1.2 0.1 collective-permute-start
  1.2 3.7 %shard_map.148 = (s32[8,256]{1,0:T(8,128)S(1)}, s32[16]{0:T(128)S(1)}, bf16[6144,256]{1,0:T(8,128)(2,1)S(1)}, bf16[6144,256]{1,0:T(8,128)(2,1)S(1)}, bf16[64,409...) custom-call(s32[1,512]{1,0:T(1,128)} %bitcast.18, s32[1,128]{1,0:T(1,128)} %bitcast.19, ...), custom_call_target="tpu_custom_call" | custom-call | flops 1048576 | bytes 16777216 | tf_op jit(solution)/shard_map/pallas_call | solution.py:446
  4.9 0.0 collective-permute-done.1.refs_1_
  4.9 3.4 %shard_map.150 = bf16[8,32,512]{2,1,0:T(8,128)(2,1)} custom-call(bf16[64,4096]{1,0:T(8,128)(2,1)S(1)} %get-tuple-element.21.refs_0_, bf16[64,4096]{1,0:T(8,128)(2,1)S(1)} %collective-permute-done.1.refs_1_, f32[1,8192]{1,0:T(1,128)S(1)} %get-tuple-element.22.refs_2_, bf16[64,128]{1,0:T(8,128)(2,1)S(1)} %get-tuple-element.23.refs_3_, ...), custom_call_target="tpu_custom_call" | custom-call | flops 17179869184 | bytes 9437184 | tf_op jit(solution)/shard_map/pallas_call | solution.py:469
  8.4 7.8 %all-to-all-start = ((bf16[8,32,512]{2,1,0:T(8,128)(2,1)}), bf16[8,32,512]{2,1,0:T(8,128)(2,1)S(1)}, u32[]{:S(2)}, u32[]{:S(2)}) async-start(bf16[8,32,512]{2,1,0:T(8,128)(2,1)} %shard_map.150), calls=%async_computation | async-start | bytes 524288 | tf_op jit(solution)/shard_map/all_to_all | solution.py:417
  16.2 0.0 collective-permute-done.refs_1_
  16.2 5.6 %shard_map.149 = (bf16[256,512]{1,0:T(8,128)(2,1)S(1)}, f32[256,256]{1,0:T(8,128)S(1)}, bf16[8,128,128]{2,1,0:T(8,128)(2,1)S(1)}) custom-call(bf16[256,4096]{1,0:T(8,128)(2,1)} %refs_0_.1, bf16[256,4096]{1,0:T(8,128)(2,1)S(1)} %collective-permute-done.refs_1_, f32[1,8192]{1,0:T(1,128)} %bitcast.13, bf16[8192,256]{1,0:T(8,128)(2,1)} %refs_6_.3, ...), custom_call_target="tpu_custom_call" | custom-call | flops 2147483648 | bytes 12582912 | tf_op jit(solution)/shard_map/pallas_call | solution.py:496
  21.8 1.7 %all-to-all-done.refs_3_ = bf16[8,32,512]{2,1,0:T(8,128)(2,1)S(1)} async-done(((bf16[8,32,512]{2,1,0:T(8,128)(2,1)}), bf16[8,32,512]{2,1,0:T(8,128)(2,1)S(1)}, u32[]{:S(2)}, u32[]{:S(2)}) %all-to-all-start) | async-done | bytes 262176 | tf_op jit(solution)/shard_map/all_to_all | solution.py:417
  23.5 2.0 %shard_map.151 = (bf16[8,208,128]{2,1,0:T(8,128)(2,1)}, f32[72,128]{1,0:T(8,128)S(1)}) custom-call(s32[16]{0:T(128)S(1)} %get-tuple-element.18.refs_6_.refs_0_, s32[8,256]{1,0:T(8,128)S(1)} %get-tuple-element.19.refs_5_.refs_8_.refs_1_, bf16[256,512]{1,0:T(8,128)(2,1)S(1)} %get-tuple-element.20.refs_2_, bf16[8,32,512]{2,1,0:T(8,128)(2,1)S(1)} %all-to-all-done.refs_3_, ...), custom_call_target="tpu_custom_call" | custom-call | flops 67108864 | bytes 294912 | tf_op jit(solution)/shard_map/pallas_call | solution.py:517
  25.5 4.9 %all-to-all-start.1 = ((bf16[8,208,128]{2,1,0:T(8,128)(2,1)}), bf16[8,208,128]{2,1,0:T(8,128)(2,1)S(1)}, u32[]{:S(2)}, u32[]{:S(2)}) async-start(bf16[8,208,128]{2,1,0:T(8,128)(2,1)} %get-tuple-element.28), calls=%async_computation.1 | async-start | bytes 851968 | tf_op jit(solution)/shard_map/all_to_all | solution.py:417
  30.3 1.3 %shard_map.152.refs_1_ = f32[72,128]{1,0:T(8,128)S(1)} custom-call(bf16[64,128]{1,0:T(8,128)(2,1)} %bitcast.15, bf16[4,256]{1,0:T(4,128)(2,1)} %bitcast.16, bf16[4,256]{1,0:T(4,128)(2,1)} %bitcast.17, f32[72,128]{1,0:T(8,128)S(1)} %get-tuple-element.29.refs_3_), custom_call_target="tpu_custom_call" | custom-call | flops 1048576 | bytes 262144 | tf_op jit(solution)/shard_map/pallas_call | solution.py:535
  31.6 7.3 %all-to-all-done.1.refs_0_ = bf16[8,208,128]{2,1,0:T(8,128)(2,1)S(1)} async-done(((bf16[8,208,128]{2,1,0:T(8,128)(2,1)}), bf16[8,208,128]{2,1,0:T(8,128)(2,1)S(1)}, u32[]{:S(2)}, u32[]{:S(2)}) %all-to-all-start.1) | async-done | bytes 426016 | tf_op jit(solution)/shard_map/all_to_all | solution.py:417
  38.9 0.9 %shard_map.153 = (bf16[1,4,2048]{2,1,0:T(4,128)(2,1)}, bf16[8,32,256]{2,1,0:T(8,128)(2,1)}, bf16[8,32,256]{2,1,0:T(8,128)(2,1)}) custom-call(bf16[8,208,128]{2,1,0:T(8,128)(2,1)S(1)} %all-to-all-done.1.refs_0_, f32[72,128]{1,0:T(8,128)S(1)} %shard_map.152.refs_1_), custom_call_target="tpu_custom_call" | custom-call | bytes 524288 | tf_op jit(solution)/shard_map/pallas_call | solution.py:545
Async XLA Ops:
  0.6 4.3 %collective-permute-start.1 = (bf16[64,4096]{1,0:T(8,128)(2,1)}, bf16[64,4096]{1,0:T(8,128)(2,1)S(1)}, u32[]{:S(2)}, u32[]{:S(2)}) collective-permute-start(bf16[64,4096]{1,0:T(8,128)(2,1)} %refs_7_.2), channel_id=1, source_target_pairs={{0,1},{1,0},{2,3},{3,2},{4,5},{5,4},{6,7},{7,6},{8,9},{9,8},{10,11... | collective-permute-start | bytes 1572872 | tf_op jit(solution)/shard_map/ppermute | solution.py:413
  1.2 15.0 %collective-permute-start = (bf16[256,4096]{1,0:T(8,128)(2,1)}, bf16[256,4096]{1,0:T(8,128)(2,1)S(1)}, u32[]{:S(2)}, u32[]{:S(2)}) collective-permute-start(bf16[256,4096]{1,0:T(8,128)(2,1)} %refs_0_.1), channel_id=1, source_target_pairs={{0,1},{1,0},{2,3},{3,2},{4,5},{5,4},{6,7},{7,6},{8,9},{9,8},{10,11... | collective-permute-start | bytes 6291464 | tf_op jit(solution)/shard_map/ppermute | solution.py:413
  8.4 15.1 %all-to-all-start = ((bf16[8,32,512]{2,1,0:T(8,128)(2,1)}), bf16[8,32,512]{2,1,0:T(8,128)(2,1)S(1)}, u32[]{:S(2)}, u32[]{:S(2)}) async-start(bf16[8,32,512]{2,1,0:T(8,128)(2,1)} %shard_map.150), calls=%async_computation | async-start | bytes 524288 | tf_op jit(solution)/shard_map/all_to_all | solution.py:417
  25.5 13.4 %all-to-all-start.1 = ((bf16[8,208,128]{2,1,0:T(8,128)(2,1)}), bf16[8,208,128]{2,1,0:T(8,128)(2,1)S(1)}, u32[]{:S(2)}, u32[]{:S(2)}) async-start(bf16[8,208,128]{2,1,0:T(8,128)(2,1)} %get-tuple-element.28), calls=%async_computation.1 | async-start | bytes 851968 | tf_op jit(solution)/shard_map/all_to_all | solution.py:417

commit v12 on v11

--- a/solution.py
+++ b/solution.py
@@ -33,12 +33,20 @@
 
 
 def rank_of(section, n):
+    return jnp.where(section < n // 2, n - 2 - 2 * section, 2 * section - n + 1)
+
+
+def section_of(rank, n):
+    return n // 2 - 1 - rank // 2 + rank % 2 * (rank // 2 * 2 + 1)
+
+
+def page_rank_of(section, n):
     lower = section < n // 2
     z, y = section // 2, section % 2
     return jnp.where(lower, n // 4 - 1 - z, z - n // 4) * 4 + (1 - y) * 2 + jnp.where(lower, 0, 1)
 
 
-def section_of(rank, n):
+def page_section_of(rank, n):
     away, side = rank // 4, rank % 2
     return 2 * (n // 4 - 1 - away + side * (2 * away + 1)) + 1 - rank // 2 % 2
 
@@ -90,14 +98,11 @@
 def prepare_kernel(sizes, *refs):
     n, img, tok, blocks, lot, page_cap = sizes
     far, (info, slots), near, small, (starts, sems) = refs[:10], refs[10:12], refs[12:17], refs[17:22], refs[22:]
-    held = near[0].shape[0]
-    half = near[2].shape[1]
+    half = near[0].shape[0]
     me = lax.axis_index("tensor")
     pairs = list(zip(far[:5], small)) + list(zip(far[7:], near[2:]))
-    for w, kept in zip(far[5:7], near[:2]):
-        for start, at, size in ((me * half, 0, half), ((1 - me) * half, half, held - half)):
-            source = pl.ds(pl.multiple_of(start, held - half), size)
-            pairs.append((w.at[source], kept.at[at : at + size]))
+    mine = pl.ds(pl.multiple_of(me * half, half), half)
+    pairs += [(w.at[mine], kept) for w, kept in zip(far[5:7], near[:2])]
     copies = [pltpu.make_async_copy(a, b, sems.at[i]) for i, (a, b) in enumerate(pairs)]
     for c in copies:
         c.start()
@@ -138,7 +143,7 @@
     info[1:2, :tok] = token_slot
     for g in range(blocks):
         holder = pages[0, pos * blocks + g]
-        slot = rank_of(holder, n) * page_cap
+        slot = page_rank_of(holder, n) * page_cap
         for e in range(g):
             slot = slot + (pages[0, pos * blocks + e] == holder).astype(I32)
         slots[g] = slot
@@ -164,29 +169,33 @@
         total[:, columns] += part
 
 
-def vis_kernel(n, lot, step, *refs):
+def vis_kernel(n, lot, load, step, *refs):
     near, far, gain, query, key_held, value_held, w_key, w_value, info, out, key_rest, value_rest, total, sems = refs
     img, half = near.shape
     kvw = w_key.shape[1]
     me = lax.axis_index("tensor")
-    held, size = key_held.shape[0], key_rest.shape[0]
-    last = pl.ds(pl.multiple_of((1 - me) * half + held - half, size), size)
-    pairs = ((w_key, key_rest), (w_value, value_rest))
-    copies = [pltpu.make_async_copy(w.at[last], kept, sems.at[i]) for i, (w, kept) in enumerate(pairs)]
-    for c in copies:
-        c.start()
+    loads = []
+    for c in range(0, half, load):
+        source = pl.ds(pl.multiple_of((1 - me) * half + c, load), load)
+        at = len(loads) * 2
+        loads.append(
+            [
+                pltpu.make_async_copy(w.at[source], kept.at[c : c + load], sems.at[at + i])
+                for i, (w, kept) in enumerate(((w_key, key_rest), (w_value, value_rest)))
+            ]
+        )
+        for copy in loads[-1]:
+            copy.start()
     scale = scale_of(near, far)
-    for at in range(0, 2 * half, step):
-        if at == held:
-            for c in copies:
-                c.wait()
-        rows, side = (near, me) if at < half else (far, 1 - me)
-        weights, w_at = ((key_held, value_held), at) if at < held else ((key_rest, value_rest), at - held)
-        c = at % half
-        columns = pl.ds(pl.multiple_of(side * half + c, step), step)
-        normed = normed_rows(rows, c, step, scale, gain[:, columns])
-        for w, col in zip(weights, (0, kvw)):
-            add_part(total, col, normed, w[w_at : w_at + step, :], at == 0)
+    for rows, side, weights in ((near, me, (key_held, value_held)), (far, 1 - me, (key_rest, value_rest))):
+        for c in range(0, half, step):
+            if rows is far and c % load == 0:
+                for copy in loads[c // load]:
+                    copy.wait()
+            columns = pl.ds(pl.multiple_of(side * half + c, step), step)
+            normed = normed_rows(rows, c, step, scale, gain[:, columns])
+            for w, col in zip(weights, (0, kvw)):
+                add_part(total, col, normed, w[c : c + step, :], rows is near and c == 0)
     slot = lax.broadcasted_iota(I32, (n * lot, img), 0)
     chosen = jnp.where(slot == info[0:1, :img], 1.0, 0.0).astype(BF16)
     packed = dot(chosen, total[...].astype(BF16)).astype(BF16)
@@ -247,7 +256,9 @@
     bias[...] = jnp.where(token_slot == lanes.astype(F32), 0.0, LOWEST)
 
 
-def attend_kernel(n, cap, lot, page_cap, kv_heads, slots, info, kv_text, arrived, bias, base, out, own, mixed, held, rows_held):
+def attend_kernel(n, cap, lot, page_cap, kv_heads, slots, info, kv_text, arrived, bias, base, sent, own, *scratch):
+    out, mixed, held, rows_held, sems = scratch
+    order = [page_section_of(k, n) for k in range(n)]
     rank = rank_of(lax.axis_index("section"), n)
     tok = kv_text.shape[0]
     kvw = kv_heads * HD
@@ -265,6 +276,8 @@
     out[:, :pages, :] = base[...]
     for g in range(reach // PAGE):
         put_page(out, page_cap, slots[g], mixed[g * PAGE : (g + 1) * PAGE, :])
+    first = pltpu.make_async_copy(out.at[:, :pages, :], sent.at[:, :pages, :], sems.at[0])
+    first.start()
     for g in range(kv_heads):
         query = jnp.concatenate(
             [
@@ -290,7 +303,8 @@
         own[g * rows : (g + 1) * rows, :] = held[pl.ds(pl.multiple_of((g * n + rank) * rows, rows), rows), :]
         numerator = numerator.astype(BF16)
         for k in range(n):
-            out[k, pages + g * rows : pages + (g + 1) * rows, :] = numerator[k * rows : (k + 1) * rows, :]
+            to = order.index(section_of(k, n))
+            out[to, pages + g * rows : pages + (g + 1) * rows, :] = numerator[k * rows : (k + 1) * rows, :]
     stat_rows = 2 * kv_heads
     share = HD // rows
     window = pl.ds(pl.multiple_of(rank // share * HD, HD), HD)
@@ -300,7 +314,11 @@
         stats = rows_held[:stat_rows, w * HD : (w + 1) * HD]
         lines = jnp.concatenate([*split_three(stats), blank], axis=0).astype(BF16)
         for k in range(w * share, min(n, (w + 1) * share)):
-            out[k, pages + kv_heads * rows :, :] = lines
+            out[order.index(section_of(k, n)), pages + kv_heads * rows :, :] = lines
+    last = pltpu.make_async_copy(out.at[:, pages:, :], sent.at[:, pages:, :], sems.at[1])
+    last.start()
+    first.wait()
+    last.wait()
 
 
 def pick_column(row, rows, start):
@@ -355,7 +373,7 @@
         for i, out in enumerate((keys, values)):
             for h in range(halves):
                 part = i * halves + h
-                out[section_of(k, n), :, h * HD : (h + 1) * HD] = shares[k, part * chunk : (part + 1) * chunk, :]
+                out[page_section_of(k, n), :, h * HD : (h + 1) * HD] = shares[k, part * chunk : (part + 1) * chunk, :]
     pages = 2 * halves * chunk
     stats = row_to_column(mine[every : every + 1, :])
     lines = []
@@ -367,7 +385,7 @@
         at = slice(g * rows, (g + 1) * rows)
         pieces = [(mine[at, :], stats[at], stats[every + g * rows : every + (g + 1) * rows])]
         for k in range(n):
-            away = pos != section_of(k, n)
+            away = pos != page_section_of(k, n)
             top = jnp.where(away, pick_column(lines[k][g : g + 1], rows, start), LOWEST)
             weight = jnp.where(away, pick_column(lines[k][kv_heads + g : kv_heads + g + 1], rows, start), 0.0)
             share = shares[k, pages + g * rows : pages + (g + 1) * rows, :].astype(F32)
@@ -412,8 +430,8 @@
     def across(array):
         return lax.ppermute(array, "tensor", [(0, 1), (1, 0)])
 
-    def exchange(array):
-        order = [[section_of(rank, n) for rank in range(n)]]
+    def exchange(array, section_at):
+        order = [[section_at(rank, n) for rank in range(n)]]
         return lax.all_to_all(array, "section", split_axis=0, concat_axis=0, tiled=True, axis_index_groups=order)
 
     def remote(array):
@@ -430,7 +448,6 @@
     q_lots = q_rows * HD // (2 * kvw)
     width = max(tok, n * lot)
     gain = norm_gain.reshape(1, 2 * half)
-    held = half + half // 2
     arguments = (
         img_route.T,
         page_dest.T,
@@ -448,8 +465,8 @@
         (
             jax.ShapeDtypeStruct((8, width), I32),
             jax.ShapeDtypeStruct((blocks,), I32),
-            pltpu.VMEM((held, kvw), BF16),
-            pltpu.VMEM((held, kvw), BF16),
+            pltpu.VMEM((half, kvw), BF16),
+            pltpu.VMEM((half, kvw), BF16),
             *[pltpu.VMEM(a.shape, a.dtype) for a in arguments[7:]],
         ),
         [ANY] * len(arguments),
@@ -457,7 +474,7 @@
         [
             *[(pltpu.VMEM if i == 0 else pltpu.SMEM)(a.shape, a.dtype) for i, a in enumerate(arguments[:5])],
             pltpu.SMEM((n,), I32),
-            pltpu.SemaphoreType.DMA((len(arguments) + 2,)),
+            pltpu.SemaphoreType.DMA((len(arguments),)),
         ],
         flops=1 << 20,
         traffic=2 * 2 * half * 2 * kvw * 2,
@@ -467,15 +484,15 @@
     load = min(2048, half)
 
     packed = call(
-        lambda *refs: vis_kernel(n, lot, step, *refs),
+        lambda *refs: vis_kernel(n, lot, load, step, *refs),
         pltpu.VMEM((n, q_lots + lot, 2 * kvw), BF16),
         [VM] * 6 + [ANY] * 2 + [VM],
         VM,
         [
-            pltpu.VMEM((2 * half - held, kvw), BF16),
-            pltpu.VMEM((2 * half - held, kvw), BF16),
+            pltpu.VMEM((half, kvw), BF16),
+            pltpu.VMEM((half, kvw), BF16),
             pltpu.VMEM((img, 2 * kvw), F32),
-            pltpu.SemaphoreType.DMA((2,)),
+            pltpu.SemaphoreType.DMA((2 * half // load,)),
         ],
         flops=64 * img * 2 * half * 2 * kvw,
         traffic=2 * img * 2 * half + 8 * half * kvw,
@@ -490,7 +507,7 @@
         remote(w_value),
         info,
     )
-    arrived = exchange(packed)
+    arrived = exchange(packed, section_of)
 
     block = page_cap * PAGE * 2 * kv_heads + q_rows + PAGE
     kv_text, bias, base = call(
@@ -517,20 +534,22 @@
     sent, own = call(
         lambda *refs: attend_kernel(n, cap, lot, page_cap, kv_heads, *refs),
         (
-            pltpu.VMEM((n, block, HD), BF16),
+            jax.ShapeDtypeStruct((n, block, HD), BF16),
             jax.ShapeDtypeStruct((q_rows + STAT, HD), F32),
         ),
         [SM] + [VM] * 5,
-        (VM, VM),
+        (ANY, VM),
         [
+            pltpu.VMEM((n, block, HD), BF16),
             pltpu.VMEM((min(tok, n * cap), 2 * kvw), BF16),
             pltpu.VMEM((n * q_rows, HD), F32),
             pltpu.VMEM((STAT, n * q_rows // kv_heads), F32),
+            pltpu.SemaphoreType.DMA((2,)),
         ],
         flops=4 * n * q_rows * tok * HD,
         traffic=n * (q_rows + STAT) * HD * 4,
     )(slots, info, kv_text, arrived, bias, base)
-    shares = exchange(sent)
+    shares = exchange(sent, page_section_of)
 
     mine = call(
         lambda *refs: fresh_kernel(n, kv_heads, steps, *refs),

time: 40.3 us -> 40.2 us (level)
  starting transfers between devices: 13.3 us -> 12.6 us
  waiting for transfers between devices: 9.02 us -> 9.64 us
    all_to_all x2, starting transfers between devices: 12.7 us -> 12 us  [exchange(): lax.all_to_all(array, 'section', split_axis=0, concat_axis=0, tiled=True,...]
    all_to_all x2, waiting for transfers between devices: 9.01 us -> 9.63 us  [exchange(): lax.all_to_all(array, 'section', split_axis=0, concat_axis=0, tiled=True,...]
    pallas_call x1, Pallas kernels: 3.7 us -> 3.13 us  [body(): call(lambda *refs: prepare_kernel((n, img, tok, blocks, lot, page_cap), *...]
    pallas_call x1, Pallas kernels: 3.41 us -> 3.93 us  [body(): call(lambda *refs: vis_kernel(n, lot, load, step, *refs), pltpu.VMEM((n,...]
where the time goes in v12:
time: 40.2 us; the launch traced here: 39.7 us
  Pallas kernels  16.7 us (42%)
  starting transfers between devices  12.6 us (31%)
  waiting for transfers between devices  9.64 us (24%)
  between operations  0.68 us (2%)
    all_to_all x2, starting transfers between devices, exchange(): lax.all_to_all(array, 'section', split_axis=0, concat_axis=0, tiled=True,...  12 us
    all_to_all x2, waiting for transfers between devices, exchange(): lax.all_to_all(array, 'section', split_axis=0, concat_axis=0, tiled=True,...  9.63 us
    pallas_call x1, Pallas kernels, body(): call(lambda *refs: text_kernel(load, step, page_cap, q_rows // kv_heads,...  5.56 us
    pallas_call x1, Pallas kernels, body(): call(lambda *refs: vis_kernel(n, lot, load, step, *refs), pltpu.VMEM((n,...  3.93 us
    pallas_call x1, Pallas kernels, body(): call(lambda *refs: prepare_kernel((n, img, tok, blocks, lot, page_cap), *...  3.13 us
    pallas_call x1, Pallas kernels, body(): call(lambda *refs: attend_kernel(n, cap, lot, page_cap, kv_heads, *refs),...  1.91 us
    pallas_call x1, Pallas kernels, body(): call(lambda *refs: fresh_kernel(n, kv_heads, steps, *refs), jax.ShapeDtyp...  1.3 us
    pallas_call x1, Pallas kernels, body(): call(lambda *refs: finish_kernel(kv_heads, steps, page_cap, *refs), (jax....  0.93 us
  transfers between devices with their start and end apart: 4, of which 2 were waited for; matrix products, arithmetic and copies ran while one was open for 0% of the time, Pallas kernels for 35%

profile of v12, /device:TPU:0, one launch (start us, length us, event | category | flops | bytes accessed | tf_op | source)
XLA Modules:
  0.0 39.7 jit_solution(10961591789539298035)
XLA Ops:
  0.6 0.5 %collective-permute-start.1 = (bf16[64,4096]{1,0:T(8,128)(2,1)}, bf16[64,4096]{1,0:T(8,128)(2,1)S(1)}, u32[]{:S(2)}, u32[]{:S(2)}) collective-permute-start(bf16[64,4096]{1,0:T(8,128)(2,1)} %refs_7_.2), channel_id=1, source_target_pairs={{0,1},{1,0},{2,3},{3,2},{4,5},{5,4},{6,7},{7,6},{8,9},{9,8},{10,11... | collective-permute-start | bytes 1572872 | tf_op jit(solution)/shard_map/ppermute | solution.py:431
  1.2 0.1 collective-permute-start
  1.2 3.1 %shard_map.148 = (s32[8,256]{1,0:T(8,128)S(1)}, s32[16]{0:T(128)S(1)}, bf16[4096,256]{1,0:T(8,128)(2,1)S(1)}, bf16[4096,256]{1,0:T(8,128)(2,1)S(1)}, bf16[64,409...) custom-call(s32[1,512]{1,0:T(1,128)} %bitcast.18, s32[1,128]{1,0:T(1,128)} %bitcast.19, ...), custom_call_target="tpu_custom_call" | custom-call | flops 1048576 | bytes 16777216 | tf_op jit(solution)/shard_map/pallas_call | solution.py:463
  4.4 0.0 collective-permute-done.1.refs_1_
  4.4 3.9 %shard_map.150 = bf16[8,32,512]{2,1,0:T(8,128)(2,1)} custom-call(bf16[64,4096]{1,0:T(8,128)(2,1)S(1)} %get-tuple-element.21.refs_0_, bf16[64,4096]{1,0:T(8,128)(2,1)S(1)} %collective-permute-done.1.refs_1_, f32[1,8192]{1,0:T(1,128)S(1)} %get-tuple-element.22.refs_2_, bf16[64,128]{1,0:T(8,128)(2,1)S(1)} %get-tuple-element.23.refs_3_, ...), custom_call_target="tpu_custom_call" | custom-call | flops 17179869184 | bytes 9437184 | tf_op jit(solution)/shard_map/pallas_call | solution.py:486
  8.3 7.8 %all-to-all-start = ((bf16[8,32,512]{2,1,0:T(8,128)(2,1)}), bf16[8,32,512]{2,1,0:T(8,128)(2,1)S(1)}, u32[]{:S(2)}, u32[]{:S(2)}) async-start(bf16[8,32,512]{2,1,0:T(8,128)(2,1)} %shard_map.150), calls=%async_computation | async-start | bytes 524288 | tf_op jit(solution)/shard_map/all_to_all | solution.py:435
  16.1 0.0 collective-permute-done.refs_1_
  16.1 5.6 %shard_map.149 = (bf16[256,512]{1,0:T(8,128)(2,1)S(1)}, f32[256,256]{1,0:T(8,128)S(1)}, bf16[8,128,128]{2,1,0:T(8,128)(2,1)S(1)}) custom-call(bf16[256,4096]{1,0:T(8,128)(2,1)} %refs_0_.1, bf16[256,4096]{1,0:T(8,128)(2,1)S(1)} %collective-permute-done.refs_1_, f32[1,8192]{1,0:T(1,128)} %bitcast.13, bf16[8192,256]{1,0:T(8,128)(2,1)} %refs_6_.3, ...), custom_call_target="tpu_custom_call" | custom-call | flops 2147483648 | bytes 12582912 | tf_op jit(solution)/shard_map/pallas_call | solution.py:513
  21.7 1.8 %all-to-all-done.refs_3_ = bf16[8,32,512]{2,1,0:T(8,128)(2,1)S(1)} async-done(((bf16[8,32,512]{2,1,0:T(8,128)(2,1)}), bf16[8,32,512]{2,1,0:T(8,128)(2,1)S(1)}, u32[]{:S(2)}, u32[]{:S(2)}) %all-to-all-start) | async-done | bytes 262176 | tf_op jit(solution)/shard_map/all_to_all | solution.py:435
  23.5 1.9 %shard_map.151 = (bf16[8,208,128]{2,1,0:T(8,128)(2,1)}, f32[72,128]{1,0:T(8,128)S(1)}) custom-call(s32[16]{0:T(128)S(1)} %get-tuple-element.18.refs_6_.refs_0_, s32[8,256]{1,0:T(8,128)S(1)} %get-tuple-element.19.refs_5_.refs_8_.refs_1_, bf16[256,512]{1,0:T(8,128)(2,1)S(1)} %get-tuple-element.20.refs_2_, bf16[8,32,512]{2,1,0:T(8,128)(2,1)S(1)} %all-to-all-done.refs_3_, ...), custom_call_target="tpu_custom_call" | custom-call | flops 67108864 | bytes 294912 | tf_op jit(solution)/shard_map/pallas_call | solution.py:534
  25.4 4.2 %all-to-all-start.1 = ((bf16[8,208,128]{2,1,0:T(8,128)(2,1)}), bf16[8,208,128]{2,1,0:T(8,128)(2,1)S(1)}, u32[]{:S(2)}, u32[]{:S(2)}) async-start(bf16[8,208,128]{2,1,0:T(8,128)(2,1)} %get-tuple-element.28), calls=%async_computation.1 | async-start | bytes 851968 | tf_op jit(solution)/shard_map/all_to_all | solution.py:435
  29.6 1.3 %shard_map.152.refs_1_ = f32[72,128]{1,0:T(8,128)S(1)} custom-call(bf16[64,128]{1,0:T(8,128)(2,1)} %bitcast.15, bf16[4,256]{1,0:T(4,128)(2,1)} %bitcast.16, bf16[4,256]{1,0:T(4,128)(2,1)} %bitcast.17, f32[72,128]{1,0:T(8,128)S(1)} %get-tuple-element.29.refs_3_), custom_call_target="tpu_custom_call" | custom-call | flops 1048576 | bytes 262144 | tf_op jit(solution)/shard_map/pallas_call | solution.py:554
  30.9 7.9 %all-to-all-done.1.refs_0_ = bf16[8,208,128]{2,1,0:T(8,128)(2,1)S(1)} async-done(((bf16[8,208,128]{2,1,0:T(8,128)(2,1)}), bf16[8,208,128]{2,1,0:T(8,128)(2,1)S(1)}, u32[]{:S(2)}, u32[]{:S(2)}) %all-to-all-start.1) | async-done | bytes 426016 | tf_op jit(solution)/shard_map/all_to_all | solution.py:435
  38.8 0.9 %shard_map.153 = (bf16[1,4,2048]{2,1,0:T(4,128)(2,1)}, bf16[8,32,256]{2,1,0:T(8,128)(2,1)}, bf16[8,32,256]{2,1,0:T(8,128)(2,1)}) custom-call(bf16[8,208,128]{2,1,0:T(8,128)(2,1)S(1)} %all-to-all-done.1.refs_0_, f32[72,128]{1,0:T(8,128)S(1)} %shard_map.152.refs_1_), custom_call_target="tpu_custom_call" | custom-call | bytes 524288 | tf_op jit(solution)/shard_map/pallas_call | solution.py:564
Async XLA Ops:
  0.6 3.7 %collective-permute-start.1 = (bf16[64,4096]{1,0:T(8,128)(2,1)}, bf16[64,4096]{1,0:T(8,128)(2,1)S(1)}, u32[]{:S(2)}, u32[]{:S(2)}) collective-permute-start(bf16[64,4096]{1,0:T(8,128)(2,1)} %refs_7_.2), channel_id=1, source_target_pairs={{0,1},{1,0},{2,3},{3,2},{4,5},{5,4},{6,7},{7,6},{8,9},{9,8},{10,11... | collective-permute-start | bytes 1572872 | tf_op jit(solution)/shard_map/ppermute | solution.py:431
  1.2 15.0 %collective-permute-start = (bf16[256,4096]{1,0:T(8,128)(2,1)}, bf16[256,4096]{1,0:T(8,128)(2,1)S(1)}, u32[]{:S(2)}, u32[]{:S(2)}) collective-permute-start(bf16[256,4096]{1,0:T(8,128)(2,1)} %refs_0_.1), channel_id=1, source_target_pairs={{0,1},{1,0},{2,3},{3,2},{4,5},{5,4},{6,7},{7,6},{8,9},{9,8},{10,11... | collective-permute-start | bytes 6291464 | tf_op jit(solution)/shard_map/ppermute | solution.py:431
  8.3 15.2 %all-to-all-start = ((bf16[8,32,512]{2,1,0:T(8,128)(2,1)}), bf16[8,32,512]{2,1,0:T(8,128)(2,1)S(1)}, u32[]{:S(2)}, u32[]{:S(2)}) async-start(bf16[8,32,512]{2,1,0:T(8,128)(2,1)} %shard_map.150), calls=%async_computation | async-start | bytes 524288 | tf_op jit(solution)/shard_map/all_to_all | solution.py:435
  25.4 13.4 %all-to-all-start.1 = ((bf16[8,208,128]{2,1,0:T(8,128)(2,1)}), bf16[8,208,128]{2,1,0:T(8,128)(2,1)S(1)}, u32[]{:S(2)}, u32[]{:S(2)}) async-start(bf16[8,208,128]{2,1,0:T(8,128)(2,1)} %get-tuple-element.28), calls=%async_computation.1 | async-start | bytes 851968 | tf_op jit(solution)/shard_map/all_to_all | solution.py:435

commit v13 on v10

--- a/solution.py
+++ b/solution.py
@@ -84,43 +84,44 @@
     return dot(weights.astype(BF16), value), top, jnp.sum(weights, axis=1, keepdims=True)
 
 
-def prepare_kernel(sizes, *refs):
-    n, img, tok, blocks, lot, page_cap = sizes
-    far, (info, slots), near, small, (starts, sems) = refs[:10], refs[10:12], refs[12:17], refs[17:22], refs[22:]
-    held = near[0].shape[0]
-    half = near[2].shape[1]
-    me = lax.axis_index("tensor")
-    pairs = list(zip(far[:5], small)) + list(zip(far[7:], near[2:]))
-    for w, kept in zip(far[5:7], near[:2]):
-        for start, at, size in ((me * half, 0, half), ((1 - me) * half, half, held - half)):
-            source = pl.ds(pl.multiple_of(start, held - half), size)
-            pairs.append((w.at[source], kept.at[at : at + size]))
-    copies = [pltpu.make_async_copy(a, b, sems.at[i]) for i, (a, b) in enumerate(pairs)]
+def prepare_kernel(n, lot, *refs):
+    far, info, near, (route, sems) = refs[:6], refs[6], refs[7:12], refs[12:]
+    img, half = near[2].shape
+    first = pl.ds(pl.multiple_of(lax.axis_index("tensor") * half, half), near[0].shape[0])
+    sources = (far[0], far[1].at[first], far[2].at[first], *far[3:])
+    copies = [pltpu.make_async_copy(a, b, sems.at[i]) for i, (a, b) in enumerate(zip(sources, (route, *near)))]
     for c in copies:
         c.start()
-    route, pages, count, tail, req = small
-    for c in copies[: len(small)]:
-        c.wait()
+    copies[0].wait()
     pos = lax.axis_index("section")
-    table = [route[:, e * img : (e + 1) * img] for e in range(n)]
     own = jnp.zeros((1, img), I32)
     for e in range(n):
-        own = jnp.where(pos == e, table[e], own)
+        own = jnp.where(pos == e, route[:, e * img : (e + 1) * img], own)
     marks = own == lax.broadcasted_iota(I32, (n, img), 0)
     ones = jnp.where(marks, 1.0, 0.0).astype(BF16)
     earlier = lax.broadcasted_iota(I32, (img, img), 0) < lax.broadcasted_iota(I32, (img, img), 1)
     prefix = dot(ones, jnp.where(earlier, 1.0, 0.0).astype(BF16))
     local = jnp.sum(jnp.where(marks, prefix, 0.0), axis=0, keepdims=True).astype(I32)
-    info[0:1, :img] = rank_of(own, n) * lot + local
+    info[...] = jnp.broadcast_to(rank_of(own, n) * lot + local, info.shape)
+    for c in copies[1:]:
+        c.wait()
+
+
+def plan_tokens(n, img, lot, page_cap, small, info, slots, bias, starts):
+    route, pages, count, tail, req = small
+    pos = lax.axis_index("section")
+    tok, width = bias.shape
+    blocks = tok // PAGE
     lanes = lax.broadcasted_iota(I32, (1, n * lot), 1)
     source, inner = section_of(lanes // lot, n), lanes % lot
     fits = jnp.zeros((1, n * lot), I32)
     offset = jnp.zeros((1, n * lot), I32)
     for e in range(n):
-        arriving = jnp.sum((table[e] == pos).astype(I32), axis=1, keepdims=True)
+        here = (route[:, e * img : (e + 1) * img] == pos).astype(I32)
+        arriving = jnp.sum(here, axis=1, keepdims=True)
         fits = fits + jnp.where(source == e, arriving, 0)
         offset = offset + jnp.where(source > e, arriving, 0)
-    info[2:3, : n * lot] = jnp.where(inner < fits, offset + inner, -1)
+    info[...] = jnp.broadcast_to(jnp.where(inner < fits, offset + inner, -1), info.shape)
     total = jnp.int32(0)
     for r in range(n):
         starts[r] = total
@@ -132,15 +133,14 @@
         first = starts[r] * PAGE
         last = first + (count[r] - 1) * PAGE + tail[r]
         token_slot = jnp.where((token >= first) & (token < last), b, token_slot)
-    info[1:2, :tok] = token_slot
+    member = section_of(lax.broadcasted_iota(I32, (1, width), 1) // (width // n), n)
+    bias[...] = jnp.where(row_to_column(token_slot.astype(F32)) == member.astype(F32), 0.0, LOWEST)
     for g in range(blocks):
         holder = pages[0, pos * blocks + g]
         slot = rank_of(holder, n) * page_cap
         for e in range(g):
             slot = slot + (pages[0, pos * blocks + e] == holder).astype(I32)
         slots[g] = slot
-    for c in copies[len(small) :]:
-        c.wait()
 
 
 def scale_of(near, far):
@@ -161,22 +161,29 @@
         total[:, columns] += part
 
 
-def vis_kernel(n, lot, step, *refs):
+def vis_kernel(n, lot, sizes, step, *refs):
     near, far, gain, query, key_held, value_held, w_key, w_value, info, out, key_rest, value_rest, total, sems = refs
     img, half = near.shape
     kvw = w_key.shape[1]
     me = lax.axis_index("tensor")
-    held, size = key_held.shape[0], key_rest.shape[0]
-    last = pl.ds(pl.multiple_of((1 - me) * half + held - half, size), size)
-    pairs = ((w_key, key_rest), (w_value, value_rest))
-    copies = [pltpu.make_async_copy(w.at[last], kept, sems.at[i]) for i, (w, kept) in enumerate(pairs)]
-    for c in copies:
-        c.start()
+    held = key_held.shape[0]
+    loads = {}
+    at = held
+    for size in sizes:
+        side = me if at < half else 1 - me
+        source = pl.ds(pl.multiple_of(side * half + at % half, size), size)
+        number = 2 * len(loads)
+        loads[at] = [
+            pltpu.make_async_copy(w.at[source], kept.at[at - held : at - held + size], sems.at[number + i])
+            for i, (w, kept) in enumerate(((w_key, key_rest), (w_value, value_rest)))
+        ]
+        for copy in loads[at]:
+            copy.start()
+        at += size
     scale = scale_of(near, far)
     for at in range(0, 2 * half, step):
-        if at == held:
-            for c in copies:
-                c.wait()
+        for copy in loads.get(at, ()):
+            copy.wait()
         rows, side = (near, me) if at < half else (far, 1 - me)
         weights, w_at = ((key_held, value_held), at) if at < held else ((key_rest, value_rest), at - held)
         c = at % half
@@ -201,13 +208,18 @@
         out[slot // page_cap, at, :] = rows[:, h * HD : (h + 1) * HD]
 
 
-def text_kernel(load, step, page_cap, q_rows, *refs):
-    near_far, far, gain, w_key_far, w_value_far, info, slots, out, bias, base, near, w_key, w_value, total, sems = refs
+def text_kernel(n, img, lot, load, step, page_cap, *refs):
+    (near_far, far, gain, w_key_far, w_value_far), small_far, refs = refs[:5], refs[5:10], refs[10:]
+    (out, bias, base, info, slots), (near, w_key, w_value, total, starts, sems), small = refs[:5], refs[5:11], refs[11:]
     half = near.shape[1]
     kvw = w_key.shape[1]
     me = lax.axis_index("tensor")
     first = pltpu.make_async_copy(near_far, near, sems.at[0])
     first.start()
+    used = sems.shape[0] - len(small)
+    lists = [pltpu.make_async_copy(a, b, sems.at[used + i]) for i, (a, b) in enumerate(zip(small_far, small))]
+    for copy in lists:
+        copy.start()
     loads = []
     for side in (me, 1 - me):
         for c in range(0, half, load):
@@ -221,6 +233,9 @@
                 copy.start()
             loads.append(pair)
     sums = squares_of(far)
+    for copy in lists:
+        copy.wait()
+    plan_tokens(n, img, lot, page_cap, small, info, slots, bias, starts)
     first.wait()
     sums = jnp.sum(squares_of(near) + sums, axis=1, keepdims=True)
     scale = lax.rsqrt(sums / (2.0 * half) + EPS)
@@ -239,18 +254,16 @@
     tok = near.shape[0]
     for g in range(tok // PAGE):
         put_page(base, page_cap, slots[g], out[g * PAGE : (g + 1) * PAGE, :])
-    token_slot = row_to_column(info[1:2, :tok].astype(F32))
-    lanes = section_of(lax.broadcasted_iota(I32, bias.shape, 1) // q_rows, bias.shape[1] // q_rows)
-    bias[...] = jnp.where(token_slot == lanes.astype(F32), 0.0, LOWEST)
-
-
-def attend_kernel(n, cap, lot, page_cap, kv_heads, slots, info, kv_text, arrived, bias, base, out, own, mixed, held, rows_held):
+
+
+def attend_kernel(n, cap, lot, page_cap, kv_heads, slots, info, kv_text, arrived, bias, base, sent, own, *scratch):
+    out, mixed, held, rows_held, sems = scratch
     rank = rank_of(lax.axis_index("section"), n)
     tok = kv_text.shape[0]
     kvw = kv_heads * HD
     q_lots = arrived.shape[1] - lot
     reach = min(tok, n * cap)
-    hit = lax.broadcasted_iota(I32, (reach, n * lot), 0) == info[2:3, : n * lot]
+    hit = lax.broadcasted_iota(I32, (reach, n * lot), 0) == info[0:1, :]
     hot = jnp.where(hit, 1.0, 0.0)
     covered = jnp.sum(hot, axis=1, keepdims=True) > 0.0
     incoming = jnp.concatenate([arrived[k, q_lots:, :] for k in range(n)], axis=0)
@@ -262,6 +275,8 @@
     out[:, :pages, :] = base[...]
     for g in range(reach // PAGE):
         put_page(out, page_cap, slots[g], mixed[g * PAGE : (g + 1) * PAGE, :])
+    first = pltpu.make_async_copy(out.at[:, :pages, :], sent.at[:, :pages, :], sems.at[0])
+    first.start()
     for g in range(kv_heads):
         query = jnp.concatenate(
             [
@@ -298,6 +313,10 @@
         lines = jnp.concatenate([*split_three(stats), blank], axis=0).astype(BF16)
         for k in range(w * share, min(n, (w + 1) * share)):
             out[k, pages + kv_heads * rows :, :] = lines
+    last = pltpu.make_async_copy(out.at[:, pages:, :], sent.at[:, pages:, :], sems.at[1])
+    last.start()
+    first.wait()
+    last.wait()
 
 
 def pick_column(row, rows, start):
@@ -425,54 +444,38 @@
 
     lot = -(-cap // PAGE) * PAGE
     q_lots = q_rows * HD // (2 * kvw)
-    width = max(tok, n * lot)
     gain = norm_gain.reshape(1, 2 * half)
-    held = half + half // 2
-    arguments = (
-        img_route.T,
-        page_dest.T,
-        page_count,
-        tail_len,
-        dec_req,
-        w_key,
-        w_value,
-        vis_rows,
-        gain,
-        query,
-    )
-    info, slots, key_held, value_held, vis_near, gain_near, query_near = call(
-        lambda *refs: prepare_kernel((n, img, tok, blocks, lot, page_cap), *refs),
+    load = min(2048, half)
+    step = min(1024, load)
+    kept = load
+    arguments = (img_route.T, w_key, w_value, vis_rows, gain, query)
+    info, key_held, value_held, vis_near, gain_near, query_near = call(
+        lambda *refs: prepare_kernel(n, lot, *refs),
         (
-            jax.ShapeDtypeStruct((8, width), I32),
-            jax.ShapeDtypeStruct((blocks,), I32),
-            pltpu.VMEM((held, kvw), BF16),
-            pltpu.VMEM((held, kvw), BF16),
-            *[pltpu.VMEM(a.shape, a.dtype) for a in arguments[7:]],
+            jax.ShapeDtypeStruct((STAT, img), I32),
+            pltpu.VMEM((kept, kvw), BF16),
+            pltpu.VMEM((kept, kvw), BF16),
+            *[pltpu.VMEM(a.shape, a.dtype) for a in arguments[3:]],
         ),
         [ANY] * len(arguments),
-        (VM, SM) + (VM,) * 5,
-        [
-            *[(pltpu.VMEM if i == 0 else pltpu.SMEM)(a.shape, a.dtype) for i, a in enumerate(arguments[:5])],
-            pltpu.SMEM((n,), I32),
-            pltpu.SemaphoreType.DMA((len(arguments) + 2,)),
-        ],
+        (VM,) * 6,
+        [pltpu.VMEM((1, n * img), I32), pltpu.SemaphoreType.DMA((len(arguments),))],
         flops=1 << 20,
         traffic=2 * 2 * half * 2 * kvw * 2,
     )(*[remote(a) for a in arguments])
 
-    step = min(1024, half)
-    load = min(2048, half)
-
+    left = 2 * half - kept
+    sizes = [load] * (left // load - 1) + [step] * (load // step)
     packed = call(
-        lambda *refs: vis_kernel(n, lot, step, *refs),
+        lambda *refs: vis_kernel(n, lot, sizes, step, *refs),
         pltpu.VMEM((n, q_lots + lot, 2 * kvw), BF16),
         [VM] * 6 + [ANY] * 2 + [VM],
         VM,
         [
-            pltpu.VMEM((2 * half - held, kvw), BF16),
-            pltpu.VMEM((2 * half - held, kvw), BF16),
+            pltpu.VMEM((left, kvw), BF16),
+            pltpu.VMEM((left, kvw), BF16),
             pltpu.VMEM((img, 2 * kvw), F32),
-            pltpu.SemaphoreType.DMA((2,)),
+            pltpu.SemaphoreType.DMA((2 * len(sizes),)),
         ],
         flops=64 * img * 2 * half * 2 * kvw,
         traffic=2 * img * 2 * half + 8 * half * kvw,
@@ -490,39 +493,46 @@
     arrived = exchange(packed)
 
     block = page_cap * PAGE * 2 * kv_heads + q_rows + PAGE
-    kv_text, bias, base = call(
-        lambda *refs: text_kernel(load, step, page_cap, q_rows // kv_heads, *refs),
+    lists = (img_route.T, page_dest.T, page_count, tail_len, dec_req)
+    kv_text, bias, base, info, slots = call(
+        lambda *refs: text_kernel(n, img, lot, load, step, page_cap, *refs),
         (
             jax.ShapeDtypeStruct((tok, 2 * kvw), BF16),
             jax.ShapeDtypeStruct((tok, n * q_rows // kv_heads), F32),
             jax.ShapeDtypeStruct((n, block - q_rows - PAGE, HD), BF16),
+            jax.ShapeDtypeStruct((STAT, n * lot), I32),
+            jax.ShapeDtypeStruct((blocks,), I32),
         ),
-        [ANY, VM, VM, ANY, ANY, VM, SM],
-        (VM, VM, VM),
+        [ANY, VM, VM] + [ANY] * 7,
+        (VM, VM, VM, VM, SM),
         [
             pltpu.VMEM((tok, half), BF16),
             pltpu.VMEM(w_key.shape, BF16),
             pltpu.VMEM(w_value.shape, BF16),
             pltpu.VMEM((tok, 2 * kvw), F32),
-            pltpu.SemaphoreType.DMA((1 + 4 * half // load,)),
+            pltpu.SMEM((n,), I32),
+            pltpu.SemaphoreType.DMA((1 + 4 * half // load + len(lists),)),
+            *[(pltpu.VMEM if i == 0 else pltpu.SMEM)(a.shape, a.dtype) for i, a in enumerate(lists)],
         ],
         limit=24,
         flops=2 * tok * 2 * half * 2 * kvw,
         traffic=2 * tok * 2 * half + 8 * half * kvw,
-    )(remote(text_rows), text_far, remote(gain), remote(w_key), remote(w_value), info, slots)
+    )(remote(text_rows), text_far, remote(gain), remote(w_key), remote(w_value), *[remote(a) for a in lists])
 
     sent, own = call(
         lambda *refs: attend_kernel(n, cap, lot, page_cap, kv_heads, *refs),
         (
-            pltpu.VMEM((n, block, HD), BF16),
+            jax.ShapeDtypeStruct((n, block, HD), BF16),
             jax.ShapeDtypeStruct((q_rows + STAT, HD), F32),
         ),
         [SM] + [VM] * 5,
-        (VM, VM),
+        (ANY, VM),
         [
+            pltpu.VMEM((n, block, HD), BF16),
             pltpu.VMEM((min(tok, n * cap), 2 * kvw), BF16),
             pltpu.VMEM((n * q_rows, HD), F32),
             pltpu.VMEM((STAT, n * q_rows // kv_heads), F32),
+            pltpu.SemaphoreType.DMA((2,)),
         ],
         flops=4 * n * q_rows * tok * HD,
         traffic=n * (q_rows + STAT) * HD * 4,

time: 40.3 us -> 39.7 us (0.985)
  Pallas kernels: 16.9 us -> 16.2 us
    pallas_call x3, Pallas kernels: 12.7 us -> 12.1 us  [the longest x1 6.14 us: body(): call(lambda *refs: text_kernel(n, img, lot, load, step, page_cap, *refs),...]
  transfers between devices with their start and end apart: 4 -> 4, of which waited for: 2 -> 2; matrix products, arithmetic and copies ran while one was open for 0% -> 0% of each run, Pallas kernels for 35% -> 34%
where the time goes in v13:
time: 39.7 us; the launch traced here: 39.2 us
  Pallas kernels  16.2 us (41%)
  starting transfers between devices  12.6 us (32%)
  waiting for transfers between devices  9.63 us (24%)
  between operations  0.68 us (2%)
    all_to_all x2, starting transfers between devices, exchange(): lax.all_to_all(array, 'section', split_axis=0, concat_axis=0, tiled=True,...  12 us
    all_to_all x2, waiting for transfers between devices, exchange(): lax.all_to_all(array, 'section', split_axis=0, concat_axis=0, tiled=True,...  9.63 us
    pallas_call x1, Pallas kernels, body(): call(lambda *refs: text_kernel(n, img, lot, load, step, page_cap, *refs),...  6.14 us
    pallas_call x1, Pallas kernels, body(): call(lambda *refs: vis_kernel(n, lot, sizes, step, *refs), pltpu.VMEM((n,...  4.21 us
    pallas_call x1, Pallas kernels, body(): call(lambda *refs: attend_kernel(n, cap, lot, page_cap, kv_heads, *refs),...  1.91 us
    pallas_call x1, Pallas kernels, body(): call(lambda *refs: prepare_kernel(n, lot, *refs), (jax.ShapeDtypeStruct((...  1.74 us
    pallas_call x1, Pallas kernels, body(): call(lambda *refs: fresh_kernel(n, kv_heads, steps, *refs), jax.ShapeDtyp...  1.3 us
    pallas_call x1, Pallas kernels, body(): call(lambda *refs: finish_kernel(kv_heads, steps, page_cap, *refs), (jax....  0.93 us
  transfers between devices with their start and end apart: 4, of which 2 were waited for; matrix products, arithmetic and copies ran while one was open for 0% of the time, Pallas kernels for 34%

profile of v13, /device:TPU:0, one launch (start us, length us, event | category | flops | bytes accessed | tf_op | source)
XLA Modules:
  0.0 39.2 jit_solution(12830975679142557996)
XLA Ops:
  0.6 0.5 %collective-permute-start.1 = (bf16[64,4096]{1,0:T(8,128)(2,1)}, bf16[64,4096]{1,0:T(8,128)(2,1)S(1)}, u32[]{:S(2)}, u32[]{:S(2)}) collective-permute-start(bf16[64,4096]{1,0:T(8,128)(2,1)} %refs_3_.3), channel_id=1, source_target_pairs={{0,1},{1,0},{2,3},{3,2},{4,5},{5,4},{6,7},{7,6},{8,9},{9,8},{10,11... | collective-permute-start | bytes 1572872 | tf_op jit(solution)/shard_map/ppermute | solution.py:429
  1.1 0.1 collective-permute-start
  1.2 1.7 %shard_map.149 = (s32[8,64]{1,0:T(8,128)S(1)}, bf16[2048,256]{1,0:T(8,128)(2,1)S(1)}, bf16[2048,256]{1,0:T(8,128)(2,1)S(1)}, bf16[64,4096]{1,0:T(8,128)(2,1)S(1)...) custom-call(s32[1,512]{1,0:T(1,128)} %bitcast.16, bf16[8192,256]{1,0:T(8,128)(2,1)} %refs_6_.1, ...), custom_call_target="tpu_custom_call" | custom-call | flops 1048576 | bytes 16777216 | tf_op jit(solution)/shard_map/pallas_call | solution.py:452
  3.0 0.0 collective-permute-done.1.refs_1_
  3.0 4.2 %shard_map.150 = bf16[8,32,512]{2,1,0:T(8,128)(2,1)} custom-call(bf16[64,4096]{1,0:T(8,128)(2,1)S(1)} %get-tuple-element.22.refs_0_, bf16[64,4096]{1,0:T(8,128)(2,1)S(1)} %collective-permute-done.1.refs_1_, f32[1,8192]{1,0:T(1,128)S(1)} %get-tuple-element.23.refs_2_, bf16[64,128]{1,0:T(8,128)(2,1)S(1)} %get-tuple-element.24.refs_3_, ...), custom_call_target="tpu_custom_call" | custom-call | flops 17179869184 | bytes 9437184 | tf_op jit(solution)/shard_map/pallas_call | solution.py:469
  7.2 7.8 %all-to-all-start = ((bf16[8,32,512]{2,1,0:T(8,128)(2,1)}), bf16[8,32,512]{2,1,0:T(8,128)(2,1)S(1)}, u32[]{:S(2)}, u32[]{:S(2)}) async-start(bf16[8,32,512]{2,1,0:T(8,128)(2,1)} %shard_map.150), calls=%async_computation | async-start | bytes 524288 | tf_op jit(solution)/shard_map/all_to_all | solution.py:433
  15.0 0.0 collective-permute-done.refs_1_
  15.0 6.1 %shard_map.148 = (bf16[256,512]{1,0:T(8,128)(2,1)S(1)}, f32[256,256]{1,0:T(8,128)S(1)}, bf16[8,128,128]{2,1,0:T(8,128)(2,1)S(1)}, s32[8,128]{1,0:T(8,128)S(1)}, s32[16]{0:T(128)S(1)}) custom-call(bf16[256,4096]{1,0:T(8,128)(2,1)} %refs_0_.1, bf16[256,4096]{1,0:T(8,128)(2,1)S(1)} %collective-permute-done.refs_1_, f32[1,8192]{1,0:T(1,128)} %bitcast.13, ...), custom_call_target="tpu_custom_call" | custom-call | flops 2147483648 | bytes 12582912 | tf_op jit(solution)/shard_map/pallas_call | solution.py:497
  21.2 1.2 %all-to-all-done.refs_3_ = bf16[8,32,512]{2,1,0:T(8,128)(2,1)S(1)} async-done(((bf16[8,32,512]{2,1,0:T(8,128)(2,1)}), bf16[8,32,512]{2,1,0:T(8,128)(2,1)S(1)}, u32[]{:S(2)}, u32[]{:S(2)}) %all-to-all-start) | async-done | bytes 262176 | tf_op jit(solution)/shard_map/all_to_all | solution.py:433
  22.4 1.9 %shard_map.151 = (bf16[8,208,128]{2,1,0:T(8,128)(2,1)}, f32[72,128]{1,0:T(8,128)S(1)}) custom-call(s32[16]{0:T(128)S(1)} %get-tuple-element.19.refs_0_, s32[8,128]{1,0:T(8,128)S(1)} %get-tuple-element.20.refs_1_, bf16[256,512]{1,0:T(8,128)(2,1)S(1)} %get-tuple-element.21.refs_2_, bf16[8,32,512]{2,1,0:T(8,128)(2,1)S(1)} %all-to-all-done.refs_3_, ...), custom_call_target="tpu_custom_call" | custom-call | flops 67108864 | bytes 294912 | tf_op jit(solution)/shard_map/pallas_call | solution.py:522
  24.3 4.2 %all-to-all-start.1 = ((bf16[8,208,128]{2,1,0:T(8,128)(2,1)}), bf16[8,208,128]{2,1,0:T(8,128)(2,1)S(1)}, u32[]{:S(2)}, u32[]{:S(2)}) async-start(bf16[8,208,128]{2,1,0:T(8,128)(2,1)} %get-tuple-element.30), calls=%async_computation.1 | async-start | bytes 851968 | tf_op jit(solution)/shard_map/all_to_all | solution.py:433
  28.5 1.3 %shard_map.152.refs_1_ = f32[72,128]{1,0:T(8,128)S(1)} custom-call(bf16[64,128]{1,0:T(8,128)(2,1)} %bitcast.15, bf16[4,256]{1,0:T(4,128)(2,1)} %bitcast.18, bf16[4,256]{1,0:T(4,128)(2,1)} %bitcast.19, f32[72,128]{1,0:T(8,128)S(1)} %get-tuple-element.31.refs_3_), custom_call_target="tpu_custom_call" | custom-call | flops 1048576 | bytes 262144 | tf_op jit(solution)/shard_map/pallas_call | solution.py:542
  29.8 8.4 %all-to-all-done.1.refs_0_ = bf16[8,208,128]{2,1,0:T(8,128)(2,1)S(1)} async-done(((bf16[8,208,128]{2,1,0:T(8,128)(2,1)}), bf16[8,208,128]{2,1,0:T(8,128)(2,1)S(1)}, u32[]{:S(2)}, u32[]{:S(2)}) %all-to-all-start.1) | async-done | bytes 426016 | tf_op jit(solution)/shard_map/all_to_all | solution.py:433
  38.2 0.9 %shard_map.153 = (bf16[1,4,2048]{2,1,0:T(4,128)(2,1)}, bf16[8,32,256]{2,1,0:T(8,128)(2,1)}, bf16[8,32,256]{2,1,0:T(8,128)(2,1)}) custom-call(bf16[8,208,128]{2,1,0:T(8,128)(2,1)S(1)} %all-to-all-done.1.refs_0_, f32[72,128]{1,0:T(8,128)S(1)} %shard_map.152.refs_1_), custom_call_target="tpu_custom_call" | custom-call | bytes 524288 | tf_op jit(solution)/shard_map/pallas_call | solution.py:552
Async XLA Ops:
  0.6 2.4 %collective-permute-start.1 = (bf16[64,4096]{1,0:T(8,128)(2,1)}, bf16[64,4096]{1,0:T(8,128)(2,1)S(1)}, u32[]{:S(2)}, u32[]{:S(2)}) collective-permute-start(bf16[64,4096]{1,0:T(8,128)(2,1)} %refs_3_.3), channel_id=1, source_target_pairs={{0,1},{1,0},{2,3},{3,2},{4,5},{5,4},{6,7},{7,6},{8,9},{9,8},{10,11... | collective-permute-start | bytes 1572872 | tf_op jit(solution)/shard_map/ppermute | solution.py:429
  1.1 13.9 %collective-permute-start = (bf16[256,4096]{1,0:T(8,128)(2,1)}, bf16[256,4096]{1,0:T(8,128)(2,1)S(1)}, u32[]{:S(2)}, u32[]{:S(2)}) collective-permute-start(bf16[256,4096]{1,0:T(8,128)(2,1)} %refs_0_.1), channel_id=1, source_target_pairs={{0,1},{1,0},{2,3},{3,2},{4,5},{5,4},{6,7},{7,6},{8,9},{9,8},{10,11... | collective-permute-start | bytes 6291464 | tf_op jit(solution)/shard_map/ppermute | solution.py:429
  7.2 15.2 %all-to-all-start = ((bf16[8,32,512]{2,1,0:T(8,128)(2,1)}), bf16[8,32,512]{2,1,0:T(8,128)(2,1)S(1)}, u32[]{:S(2)}, u32[]{:S(2)}) async-start(bf16[8,32,512]{2,1,0:T(8,128)(2,1)} %shard_map.150), calls=%async_computation | async-start | bytes 524288 | tf_op jit(solution)/shard_map/all_to_all | solution.py:433
  24.3 14.0 %all-to-all-start.1 = ((bf16[8,208,128]{2,1,0:T(8,128)(2,1)}), bf16[8,208,128]{2,1,0:T(8,128)(2,1)S(1)}, u32[]{:S(2)}, u32[]{:S(2)}) async-start(bf16[8,208,128]{2,1,0:T(8,128)(2,1)} %get-tuple-element.30), calls=%async_computation.1 | async-start | bytes 851968 | tf_op jit(solution)/shard_map/all_to_all | solution.py:433

commit v14 on v13

--- a/solution.py
+++ b/solution.py
@@ -33,11 +33,13 @@
 
 
 def rank_of(section, n):
-    return jnp.where(section < n // 2, n - 2 - 2 * section, 2 * section - n + 1)
+    z, y, length = section // 2, section % 2, n // 2
+    return (1 - y) * length + (z + length - n // 4 + 1) % length
 
 
 def section_of(rank, n):
-    return n // 2 - 1 - rank // 2 + rank % 2 * (rank // 2 * 2 + 1)
+    length = n // 2
+    return 2 * ((rank % length + n // 4 - 1) % length) + 1 - rank // length
 
 
 def dot(a, b):

time: 39.7 us -> 40.3 us (1.015)
  waiting for transfers between devices: 9.63 us -> 10.2 us
    all_to_all x2, waiting for transfers between devices: 9.63 us -> 10.2 us  [exchange(): lax.all_to_all(array, 'section', split_axis=0, concat_axis=0, tiled=True,...]
where the time goes in v14:
time: 40.3 us; the launch traced here: 39.9 us
  Pallas kernels  16.3 us (40%)
  starting transfers between devices  12.6 us (31%)
  waiting for transfers between devices  10.2 us (25%)
  between operations  0.68 us (2%)
    all_to_all x2, starting transfers between devices, exchange(): lax.all_to_all(array, 'section', split_axis=0, concat_axis=0, tiled=True,...  12 us
    all_to_all x2, waiting for transfers between devices, exchange(): lax.all_to_all(array, 'section', split_axis=0, concat_axis=0, tiled=True,...  10.2 us
    pallas_call x1, Pallas kernels, body(): call(lambda *refs: text_kernel(n, img, lot, load, step, page_cap, *refs),...  6.25 us
    pallas_call x1, Pallas kernels, body(): call(lambda *refs: vis_kernel(n, lot, sizes, step, *refs), pltpu.VMEM((n,...  4.21 us
    pallas_call x1, Pallas kernels, body(): call(lambda *refs: attend_kernel(n, cap, lot, page_cap, kv_heads, *refs),...  1.91 us
    pallas_call x1, Pallas kernels, body(): call(lambda *refs: prepare_kernel(n, lot, *refs), (jax.ShapeDtypeStruct((...  1.74 us
    pallas_call x1, Pallas kernels, body(): call(lambda *refs: fresh_kernel(n, kv_heads, steps, *refs), jax.ShapeDtyp...  1.3 us
    pallas_call x1, Pallas kernels, body(): call(lambda *refs: finish_kernel(kv_heads, steps, page_cap, *refs), (jax....  0.93 us
  transfers between devices with their start and end apart: 4, of which 2 were waited for; matrix products, arithmetic and copies ran while one was open for 0% of the time, Pallas kernels for 34%

profile of v14, /device:TPU:0, one launch (start us, length us, event | category | flops | bytes accessed | tf_op | source)
XLA Modules:
  0.0 39.9 jit_solution(646170843259393173)
XLA Ops:
  0.6 0.5 %collective-permute-start.1 = (bf16[64,4096]{1,0:T(8,128)(2,1)}, bf16[64,4096]{1,0:T(8,128)(2,1)S(1)}, u32[]{:S(2)}, u32[]{:S(2)}) collective-permute-start(bf16[64,4096]{1,0:T(8,128)(2,1)} %refs_3_.3), channel_id=1, source_target_pairs={{0,1},{1,0},{2,3},{3,2},{4,5},{5,4},{6,7},{7,6},{8,9},{9,8},{10,11... | collective-permute-start | bytes 1572872 | tf_op jit(solution)/shard_map/ppermute | solution.py:431
  1.1 0.1 collective-permute-start
  1.2 1.7 %shard_map.149 = (s32[8,64]{1,0:T(8,128)S(1)}, bf16[2048,256]{1,0:T(8,128)(2,1)S(1)}, bf16[2048,256]{1,0:T(8,128)(2,1)S(1)}, bf16[64,4096]{1,0:T(8,128)(2,1)S(1)...) custom-call(s32[1,512]{1,0:T(1,128)} %bitcast.16, bf16[8192,256]{1,0:T(8,128)(2,1)} %refs_6_.1, ...), custom_call_target="tpu_custom_call" | custom-call | flops 1048576 | bytes 16777216 | tf_op jit(solution)/shard_map/pallas_call | solution.py:454
  3.0 0.0 collective-permute-done.1.refs_1_
  3.0 4.2 %shard_map.150 = bf16[8,32,512]{2,1,0:T(8,128)(2,1)} custom-call(bf16[64,4096]{1,0:T(8,128)(2,1)S(1)} %get-tuple-element.22.refs_0_, bf16[64,4096]{1,0:T(8,128)(2,1)S(1)} %collective-permute-done.1.refs_1_, f32[1,8192]{1,0:T(1,128)S(1)} %get-tuple-element.23.refs_2_, bf16[64,128]{1,0:T(8,128)(2,1)S(1)} %get-tuple-element.24.refs_3_, ...), custom_call_target="tpu_custom_call" | custom-call | flops 17179869184 | bytes 9437184 | tf_op jit(solution)/shard_map/pallas_call | solution.py:471
  7.2 7.8 %all-to-all-start = ((bf16[8,32,512]{2,1,0:T(8,128)(2,1)}), bf16[8,32,512]{2,1,0:T(8,128)(2,1)S(1)}, u32[]{:S(2)}, u32[]{:S(2)}) async-start(bf16[8,32,512]{2,1,0:T(8,128)(2,1)} %shard_map.150), calls=%async_computation | async-start | bytes 524288 | tf_op jit(solution)/shard_map/all_to_all | solution.py:435
  15.0 0.0 collective-permute-done.refs_1_
  15.0 6.2 %shard_map.148 = (bf16[256,512]{1,0:T(8,128)(2,1)S(1)}, f32[256,256]{1,0:T(8,128)S(1)}, bf16[8,128,128]{2,1,0:T(8,128)(2,1)S(1)}, s32[8,128]{1,0:T(8,128)S(1)}, s32[16]{0:T(128)S(1)}) custom-call(bf16[256,4096]{1,0:T(8,128)(2,1)} %refs_0_.1, bf16[256,4096]{1,0:T(8,128)(2,1)S(1)} %collective-permute-done.refs_1_, f32[1,8192]{1,0:T(1,128)} %bitcast.13, ...), custom_call_target="tpu_custom_call" | custom-call | flops 2147483648 | bytes 12582912 | tf_op jit(solution)/shard_map/pallas_call | solution.py:499
  21.3 1.4 %all-to-all-done.refs_3_ = bf16[8,32,512]{2,1,0:T(8,128)(2,1)S(1)} async-done(((bf16[8,32,512]{2,1,0:T(8,128)(2,1)}), bf16[8,32,512]{2,1,0:T(8,128)(2,1)S(1)}, u32[]{:S(2)}, u32[]{:S(2)}) %all-to-all-start) | async-done | bytes 262176 | tf_op jit(solution)/shard_map/all_to_all | solution.py:435
  22.7 1.9 %shard_map.151 = (bf16[8,208,128]{2,1,0:T(8,128)(2,1)}, f32[72,128]{1,0:T(8,128)S(1)}) custom-call(s32[16]{0:T(128)S(1)} %get-tuple-element.19.refs_0_, s32[8,128]{1,0:T(8,128)S(1)} %get-tuple-element.20.refs_1_, bf16[256,512]{1,0:T(8,128)(2,1)S(1)} %get-tuple-element.21.refs_2_, bf16[8,32,512]{2,1,0:T(8,128)(2,1)S(1)} %all-to-all-done.refs_3_, ...), custom_call_target="tpu_custom_call" | custom-call | flops 67108864 | bytes 294912 | tf_op jit(solution)/shard_map/pallas_call | solution.py:524
  24.6 4.2 %all-to-all-start.1 = ((bf16[8,208,128]{2,1,0:T(8,128)(2,1)}), bf16[8,208,128]{2,1,0:T(8,128)(2,1)S(1)}, u32[]{:S(2)}, u32[]{:S(2)}) async-start(bf16[8,208,128]{2,1,0:T(8,128)(2,1)} %get-tuple-element.30), calls=%async_computation.1 | async-start | bytes 851968 | tf_op jit(solution)/shard_map/all_to_all | solution.py:435
  28.8 1.3 %shard_map.152.refs_1_ = f32[72,128]{1,0:T(8,128)S(1)} custom-call(bf16[64,128]{1,0:T(8,128)(2,1)} %bitcast.15, bf16[4,256]{1,0:T(4,128)(2,1)} %bitcast.18, bf16[4,256]{1,0:T(4,128)(2,1)} %bitcast.19, f32[72,128]{1,0:T(8,128)S(1)} %get-tuple-element.31.refs_3_), custom_call_target="tpu_custom_call" | custom-call | flops 1048576 | bytes 262144 | tf_op jit(solution)/shard_map/pallas_call | solution.py:544
  30.1 8.8 %all-to-all-done.1.refs_0_ = bf16[8,208,128]{2,1,0:T(8,128)(2,1)S(1)} async-done(((bf16[8,208,128]{2,1,0:T(8,128)(2,1)}), bf16[8,208,128]{2,1,0:T(8,128)(2,1)S(1)}, u32[]{:S(2)}, u32[]{:S(2)}) %all-to-all-start.1) | async-done | bytes 426016 | tf_op jit(solution)/shard_map/all_to_all | solution.py:435
  38.9 0.9 %shard_map.153 = (bf16[1,4,2048]{2,1,0:T(4,128)(2,1)}, bf16[8,32,256]{2,1,0:T(8,128)(2,1)}, bf16[8,32,256]{2,1,0:T(8,128)(2,1)}) custom-call(bf16[8,208,128]{2,1,0:T(8,128)(2,1)S(1)} %all-to-all-done.1.refs_0_, f32[72,128]{1,0:T(8,128)S(1)} %shard_map.152.refs_1_), custom_call_target="tpu_custom_call" | custom-call | bytes 524288 | tf_op jit(solution)/shard_map/pallas_call | solution.py:554
Async XLA Ops:
  0.6 2.4 %collective-permute-start.1 = (bf16[64,4096]{1,0:T(8,128)(2,1)}, bf16[64,4096]{1,0:T(8,128)(2,1)S(1)}, u32[]{:S(2)}, u32[]{:S(2)}) collective-permute-start(bf16[64,4096]{1,0:T(8,128)(2,1)} %refs_3_.3), channel_id=1, source_target_pairs={{0,1},{1,0},{2,3},{3,2},{4,5},{5,4},{6,7},{7,6},{8,9},{9,8},{10,11... | collective-permute-start | bytes 1572872 | tf_op jit(solution)/shard_map/ppermute | solution.py:431
  1.1 13.9 %collective-permute-start = (bf16[256,4096]{1,0:T(8,128)(2,1)}, bf16[256,4096]{1,0:T(8,128)(2,1)S(1)}, u32[]{:S(2)}, u32[]{:S(2)}) collective-permute-start(bf16[256,4096]{1,0:T(8,128)(2,1)} %refs_0_.1), channel_id=1, source_target_pairs={{0,1},{1,0},{2,3},{3,2},{4,5},{5,4},{6,7},{7,6},{8,9},{9,8},{10,11... | collective-permute-start | bytes 6291464 | tf_op jit(solution)/shard_map/ppermute | solution.py:431
  7.2 15.5 %all-to-all-start = ((bf16[8,32,512]{2,1,0:T(8,128)(2,1)}), bf16[8,32,512]{2,1,0:T(8,128)(2,1)S(1)}, u32[]{:S(2)}, u32[]{:S(2)}) async-start(bf16[8,32,512]{2,1,0:T(8,128)(2,1)} %shard_map.150), calls=%async_computation | async-start | bytes 524288 | tf_op jit(solution)/shard_map/all_to_all | solution.py:435
  24.6 14.3 %all-to-all-start.1 = ((bf16[8,208,128]{2,1,0:T(8,128)(2,1)}), bf16[8,208,128]{2,1,0:T(8,128)(2,1)S(1)}, u32[]{:S(2)}, u32[]{:S(2)}) async-start(bf16[8,208,128]{2,1,0:T(8,128)(2,1)} %get-tuple-element.30), calls=%async_computation.1 | async-start | bytes 851968 | tf_op jit(solution)/shard_map/all_to_all | solution.py:435

commit v15 on v14

--- a/solution.py
+++ b/solution.py
@@ -34,12 +34,12 @@
 
 def rank_of(section, n):
     z, y, length = section // 2, section % 2, n // 2
-    return (1 - y) * length + (z + length - n // 4 + 1) % length
+    return (1 - y) * length + (2 * length - z - n // 4) % length
 
 
 def section_of(rank, n):
     length = n // 2
-    return 2 * ((rank % length + n // 4 - 1) % length) + 1 - rank // length
+    return 2 * (length - 1 - (rank % length + n // 4 - 1) % length) + 1 - rank // length
 
 
 def dot(a, b):

time: 40.3 us -> 39 us (0.968)
  waiting for transfers between devices: 10.2 us -> 6.79 us
  starting transfers between devices: 12.6 us -> 14.7 us
    all_to_all x2, waiting for transfers between devices: 10.2 us -> 6.79 us  [exchange(): lax.all_to_all(array, 'section', split_axis=0, concat_axis=0, tiled=True,...]
    all_to_all x2, starting transfers between devices: 12 us -> 14.1 us  [exchange(): lax.all_to_all(array, 'section', split_axis=0, concat_axis=0, tiled=True,...]
  transfers between devices with their start and end apart: 4 -> 4, of which waited for: 2 -> 2; matrix products, arithmetic and copies ran while one was open for 0% -> 0% of each run, Pallas kernels for 34% -> 35%
where the time goes in v15:
time: 39 us; the launch traced here: 38.6 us
  Pallas kernels  16.3 us (42%)
  starting transfers between devices  14.7 us (38%)
  waiting for transfers between devices  6.79 us (17%)
  between operations  0.68 us (2%)
    all_to_all x2, starting transfers between devices, exchange(): lax.all_to_all(array, 'section', split_axis=0, concat_axis=0, tiled=True,...  14.1 us
    all_to_all x2, waiting for transfers between devices, exchange(): lax.all_to_all(array, 'section', split_axis=0, concat_axis=0, tiled=True,...  6.79 us
    pallas_call x1, Pallas kernels, body(): call(lambda *refs: text_kernel(n, img, lot, load, step, page_cap, *refs),...  6.25 us
    pallas_call x1, Pallas kernels, body(): call(lambda *refs: vis_kernel(n, lot, sizes, step, *refs), pltpu.VMEM((n,...  4.21 us
    pallas_call x1, Pallas kernels, body(): call(lambda *refs: attend_kernel(n, cap, lot, page_cap, kv_heads, *refs),...  1.91 us
    pallas_call x1, Pallas kernels, body(): call(lambda *refs: prepare_kernel(n, lot, *refs), (jax.ShapeDtypeStruct((...  1.74 us
    pallas_call x1, Pallas kernels, body(): call(lambda *refs: fresh_kernel(n, kv_heads, steps, *refs), jax.ShapeDtyp...  1.3 us
    pallas_call x1, Pallas kernels, body(): call(lambda *refs: finish_kernel(kv_heads, steps, page_cap, *refs), (jax....  0.93 us
  transfers between devices with their start and end apart: 4, of which 2 were waited for; matrix products, arithmetic and copies ran while one was open for 0% of the time, Pallas kernels for 35%

profile of v15, /device:TPU:0, one launch (start us, length us, event | category | flops | bytes accessed | tf_op | source)
XLA Modules:
  0.0 38.6 jit_solution(17983273122629361853)
XLA Ops:
  0.6 0.5 %collective-permute-start.1 = (bf16[64,4096]{1,0:T(8,128)(2,1)}, bf16[64,4096]{1,0:T(8,128)(2,1)S(1)}, u32[]{:S(2)}, u32[]{:S(2)}) collective-permute-start(bf16[64,4096]{1,0:T(8,128)(2,1)} %refs_3_.3), channel_id=1, source_target_pairs={{0,1},{1,0},{2,3},{3,2},{4,5},{5,4},{6,7},{7,6},{8,9},{9,8},{10,11... | collective-permute-start | bytes 1572872 | tf_op jit(solution)/shard_map/ppermute | solution.py:431
  1.1 0.1 collective-permute-start
  1.2 1.7 %shard_map.149 = (s32[8,64]{1,0:T(8,128)S(1)}, bf16[2048,256]{1,0:T(8,128)(2,1)S(1)}, bf16[2048,256]{1,0:T(8,128)(2,1)S(1)}, bf16[64,4096]{1,0:T(8,128)(2,1)S(1)...) custom-call(s32[1,512]{1,0:T(1,128)} %bitcast.16, bf16[8192,256]{1,0:T(8,128)(2,1)} %refs_6_.1, ...), custom_call_target="tpu_custom_call" | custom-call | flops 1048576 | bytes 16777216 | tf_op jit(solution)/shard_map/pallas_call | solution.py:454
  3.0 0.0 collective-permute-done.1.refs_1_
  3.0 4.2 %shard_map.150 = bf16[8,32,512]{2,1,0:T(8,128)(2,1)} custom-call(bf16[64,4096]{1,0:T(8,128)(2,1)S(1)} %get-tuple-element.22.refs_0_, bf16[64,4096]{1,0:T(8,128)(2,1)S(1)} %collective-permute-done.1.refs_1_, f32[1,8192]{1,0:T(1,128)S(1)} %get-tuple-element.23.refs_2_, bf16[64,128]{1,0:T(8,128)(2,1)S(1)} %get-tuple-element.24.refs_3_, ...), custom_call_target="tpu_custom_call" | custom-call | flops 17179869184 | bytes 9437184 | tf_op jit(solution)/shard_map/pallas_call | solution.py:471
  7.2 8.3 %all-to-all-start = ((bf16[8,32,512]{2,1,0:T(8,128)(2,1)}), bf16[8,32,512]{2,1,0:T(8,128)(2,1)S(1)}, u32[]{:S(2)}, u32[]{:S(2)}) async-start(bf16[8,32,512]{2,1,0:T(8,128)(2,1)} %shard_map.150), calls=%async_computation | async-start | bytes 524288 | tf_op jit(solution)/shard_map/all_to_all | solution.py:435
  15.5 0.0 collective-permute-done.refs_1_
  15.5 6.2 %shard_map.148 = (bf16[256,512]{1,0:T(8,128)(2,1)S(1)}, f32[256,256]{1,0:T(8,128)S(1)}, bf16[8,128,128]{2,1,0:T(8,128)(2,1)S(1)}, s32[8,128]{1,0:T(8,128)S(1)}, s32[16]{0:T(128)S(1)}) custom-call(bf16[256,4096]{1,0:T(8,128)(2,1)} %refs_0_.1, bf16[256,4096]{1,0:T(8,128)(2,1)S(1)} %collective-permute-done.refs_1_, f32[1,8192]{1,0:T(1,128)} %bitcast.13, ...), custom_call_target="tpu_custom_call" | custom-call | flops 2147483648 | bytes 12582912 | tf_op jit(solution)/shard_map/pallas_call | solution.py:499
  21.8 0.1 all-to-all-done.refs_3_
  21.8 1.9 %shard_map.151 = (bf16[8,208,128]{2,1,0:T(8,128)(2,1)}, f32[72,128]{1,0:T(8,128)S(1)}) custom-call(s32[16]{0:T(128)S(1)} %get-tuple-element.19.refs_0_, s32[8,128]{1,0:T(8,128)S(1)} %get-tuple-element.20.refs_1_, bf16[256,512]{1,0:T(8,128)(2,1)S(1)} %get-tuple-element.21.refs_2_, bf16[8,32,512]{2,1,0:T(8,128)(2,1)S(1)} %all-to-all-done.refs_3_, ...), custom_call_target="tpu_custom_call" | custom-call | flops 67108864 | bytes 294912 | tf_op jit(solution)/shard_map/pallas_call | solution.py:524
  23.8 5.8 %all-to-all-start.1 = ((bf16[8,208,128]{2,1,0:T(8,128)(2,1)}), bf16[8,208,128]{2,1,0:T(8,128)(2,1)S(1)}, u32[]{:S(2)}, u32[]{:S(2)}) async-start(bf16[8,208,128]{2,1,0:T(8,128)(2,1)} %get-tuple-element.30), calls=%async_computation.1 | async-start | bytes 851968 | tf_op jit(solution)/shard_map/all_to_all | solution.py:435
  29.6 1.3 %shard_map.152.refs_1_ = f32[72,128]{1,0:T(8,128)S(1)} custom-call(bf16[64,128]{1,0:T(8,128)(2,1)} %bitcast.15, bf16[4,256]{1,0:T(4,128)(2,1)} %bitcast.18, bf16[4,256]{1,0:T(4,128)(2,1)} %bitcast.19, f32[72,128]{1,0:T(8,128)S(1)} %get-tuple-element.31.refs_3_), custom_call_target="tpu_custom_call" | custom-call | flops 1048576 | bytes 262144 | tf_op jit(solution)/shard_map/pallas_call | solution.py:544
  30.9 6.7 %all-to-all-done.1.refs_0_ = bf16[8,208,128]{2,1,0:T(8,128)(2,1)S(1)} async-done(((bf16[8,208,128]{2,1,0:T(8,128)(2,1)}), bf16[8,208,128]{2,1,0:T(8,128)(2,1)S(1)}, u32[]{:S(2)}, u32[]{:S(2)}) %all-to-all-start.1) | async-done | bytes 426016 | tf_op jit(solution)/shard_map/all_to_all | solution.py:435
  37.6 0.9 %shard_map.153 = (bf16[1,4,2048]{2,1,0:T(4,128)(2,1)}, bf16[8,32,256]{2,1,0:T(8,128)(2,1)}, bf16[8,32,256]{2,1,0:T(8,128)(2,1)}) custom-call(bf16[8,208,128]{2,1,0:T(8,128)(2,1)S(1)} %all-to-all-done.1.refs_0_, f32[72,128]{1,0:T(8,128)S(1)} %shard_map.152.refs_1_), custom_call_target="tpu_custom_call" | custom-call | bytes 524288 | tf_op jit(solution)/shard_map/pallas_call | solution.py:554
Async XLA Ops:
  0.6 2.4 %collective-permute-start.1 = (bf16[64,4096]{1,0:T(8,128)(2,1)}, bf16[64,4096]{1,0:T(8,128)(2,1)S(1)}, u32[]{:S(2)}, u32[]{:S(2)}) collective-permute-start(bf16[64,4096]{1,0:T(8,128)(2,1)} %refs_3_.3), channel_id=1, source_target_pairs={{0,1},{1,0},{2,3},{3,2},{4,5},{5,4},{6,7},{7,6},{8,9},{9,8},{10,11... | collective-permute-start | bytes 1572872 | tf_op jit(solution)/shard_map/ppermute | solution.py:431
  1.1 14.4 %collective-permute-start = (bf16[256,4096]{1,0:T(8,128)(2,1)}, bf16[256,4096]{1,0:T(8,128)(2,1)S(1)}, u32[]{:S(2)}, u32[]{:S(2)}) collective-permute-start(bf16[256,4096]{1,0:T(8,128)(2,1)} %refs_0_.1), channel_id=1, source_target_pairs={{0,1},{1,0},{2,3},{3,2},{4,5},{5,4},{6,7},{7,6},{8,9},{9,8},{10,11... | collective-permute-start | bytes 6291464 | tf_op jit(solution)/shard_map/ppermute | solution.py:431
  7.2 14.6 %all-to-all-start = ((bf16[8,32,512]{2,1,0:T(8,128)(2,1)}), bf16[8,32,512]{2,1,0:T(8,128)(2,1)S(1)}, u32[]{:S(2)}, u32[]{:S(2)}) async-start(bf16[8,32,512]{2,1,0:T(8,128)(2,1)} %shard_map.150), calls=%async_computation | async-start | bytes 524288 | tf_op jit(solution)/shard_map/all_to_all | solution.py:435
  23.8 13.9 %all-to-all-start.1 = ((bf16[8,208,128]{2,1,0:T(8,128)(2,1)}), bf16[8,208,128]{2,1,0:T(8,128)(2,1)S(1)}, u32[]{:S(2)}, u32[]{:S(2)}) async-start(bf16[8,208,128]{2,1,0:T(8,128)(2,1)} %get-tuple-element.30), calls=%async_computation.1 | async-start | bytes 851968 | tf_op jit(solution)/shard_map/all_to_all | solution.py:435

commit v16 on v15

--- a/solution.py
+++ b/solution.py
@@ -33,11 +33,19 @@
 
 
 def rank_of(section, n):
+    return jnp.where(section < n // 2, n - 2 - 2 * section, 2 * section - n + 1)
+
+
+def section_of(rank, n):
+    return n // 2 - 1 - rank // 2 + rank % 2 * (rank // 2 * 2 + 1)
+
+
+def page_rank_of(section, n):
     z, y, length = section // 2, section % 2, n // 2
     return (1 - y) * length + (2 * length - z - n // 4) % length
 
 
-def section_of(rank, n):
+def page_section_of(rank, n):
     length = n // 2
     return 2 * (length - 1 - (rank % length + n // 4 - 1) % length) + 1 - rank // length
 
@@ -139,7 +147,7 @@
     bias[...] = jnp.where(row_to_column(token_slot.astype(F32)) == member.astype(F32), 0.0, LOWEST)
     for g in range(blocks):
         holder = pages[0, pos * blocks + g]
-        slot = rank_of(holder, n) * page_cap
+        slot = page_rank_of(holder, n) * page_cap
         for e in range(g):
             slot = slot + (pages[0, pos * blocks + e] == holder).astype(I32)
         slots[g] = slot
@@ -260,6 +268,7 @@
 
 def attend_kernel(n, cap, lot, page_cap, kv_heads, slots, info, kv_text, arrived, bias, base, sent, own, *scratch):
     out, mixed, held, rows_held, sems = scratch
+    order = [page_section_of(k, n) for k in range(n)]
     rank = rank_of(lax.axis_index("section"), n)
     tok = kv_text.shape[0]
     kvw = kv_heads * HD
@@ -304,7 +313,8 @@
         own[g * rows : (g + 1) * rows, :] = held[pl.ds(pl.multiple_of((g * n + rank) * rows, rows), rows), :]
         numerator = numerator.astype(BF16)
         for k in range(n):
-            out[k, pages + g * rows : pages + (g + 1) * rows, :] = numerator[k * rows : (k + 1) * rows, :]
+            to = order.index(section_of(k, n))
+            out[to, pages + g * rows : pages + (g + 1) * rows, :] = numerator[k * rows : (k + 1) * rows, :]
     stat_rows = 2 * kv_heads
     share = HD // rows
     window = pl.ds(pl.multiple_of(rank // share * HD, HD), HD)
@@ -314,7 +324,7 @@
         stats = rows_held[:stat_rows, w * HD : (w + 1) * HD]
         lines = jnp.concatenate([*split_three(stats), blank], axis=0).astype(BF16)
         for k in range(w * share, min(n, (w + 1) * share)):
-            out[k, pages + kv_heads * rows :, :] = lines
+            out[order.index(section_of(k, n)), pages + kv_heads * rows :, :] = lines
     last = pltpu.make_async_copy(out.at[:, pages:, :], sent.at[:, pages:, :], sems.at[1])
     last.start()
     first.wait()
@@ -361,7 +371,7 @@
     mine[every:, :] = jnp.broadcast_to(line, (STAT, line.shape[1]))
 
 
-def finish_kernel(kv_heads, steps, page_cap, shares, mine, attended, keys, values):
+def finish_kernel(kv_heads, steps, page_cap, shares, mine, attended, keys, values, *scratch):
     n = shares.shape[0]
     pos = lax.axis_index("section")
     every = mine.shape[0] - STAT
@@ -369,11 +379,15 @@
     start = rank_of(pos, n) % (HD // rows) * rows
     chunk = page_cap * PAGE
     halves = keys.shape[2] // HD
+    held, sems = scratch[:2], scratch[2]
     for k in range(n):
-        for i, out in enumerate((keys, values)):
+        for i, out in enumerate(held):
             for h in range(halves):
                 part = i * halves + h
-                out[section_of(k, n), :, h * HD : (h + 1) * HD] = shares[k, part * chunk : (part + 1) * chunk, :]
+                out[page_section_of(k, n), :, h * HD : (h + 1) * HD] = shares[k, part * chunk : (part + 1) * chunk, :]
+    copies = [pltpu.make_async_copy(x, out, sems.at[i]) for i, (x, out) in enumerate(zip(held, (keys, values)))]
+    for c in copies:
+        c.start()
     pages = 2 * halves * chunk
     stats = row_to_column(mine[every : every + 1, :])
     lines = []
@@ -385,7 +399,7 @@
         at = slice(g * rows, (g + 1) * rows)
         pieces = [(mine[at, :], stats[at], stats[every + g * rows : every + (g + 1) * rows])]
         for k in range(n):
-            away = pos != section_of(k, n)
+            away = pos != page_section_of(k, n)
             top = jnp.where(away, pick_column(lines[k][g : g + 1], rows, start), LOWEST)
             weight = jnp.where(away, pick_column(lines[k][kv_heads + g : kv_heads + g + 1], rows, start), 0.0)
             share = shares[k, pages + g * rows : pages + (g + 1) * rows, :].astype(F32)
@@ -398,6 +412,8 @@
         for h in range(rows // steps):
             to = (g * rows // steps + h) * HD
             attended[0, :, to : to + HD] = result[h * steps : (h + 1) * steps, :]
+    for c in copies:
+        c.wait()
 
 
 def body(
@@ -430,8 +446,8 @@
     def across(array):
         return lax.ppermute(array, "tensor", [(0, 1), (1, 0)])
 
-    def exchange(array):
-        order = [[section_of(rank, n) for rank in range(n)]]
+    def exchange(array, section_at):
+        order = [[section_at(rank, n) for rank in range(n)]]
         return lax.all_to_all(array, "section", split_axis=0, concat_axis=0, tiled=True, axis_index_groups=order)
 
     def remote(array):
@@ -448,8 +464,8 @@
     q_lots = q_rows * HD // (2 * kvw)
     gain = norm_gain.reshape(1, 2 * half)
     load = min(2048, half)
-    step = min(1024, load)
-    kept = load
+    step = min(1024, load // 2)
+    kept = load + load // 2
     arguments = (img_route.T, w_key, w_value, vis_rows, gain, query)
     info, key_held, value_held, vis_near, gain_near, query_near = call(
         lambda *refs: prepare_kernel(n, lot, *refs),
@@ -467,7 +483,7 @@
     )(*[remote(a) for a in arguments])
 
     left = 2 * half - kept
-    sizes = [load] * (left // load - 1) + [step] * (load // step)
+    sizes = [half - kept, *[load] * (half // load - 1), *[load // 2] * 2]
     packed = call(
         lambda *refs: vis_kernel(n, lot, sizes, step, *refs),
         pltpu.VMEM((n, q_lots + lot, 2 * kvw), BF16),
@@ -492,7 +508,7 @@
         remote(w_value),
         info,
     )
-    arrived = exchange(packed)
+    arrived = exchange(packed, section_of)
 
     block = page_cap * PAGE * 2 * kv_heads + q_rows + PAGE
     lists = (img_route.T, page_dest.T, page_count, tail_len, dec_req)
@@ -539,7 +555,7 @@
         flops=4 * n * q_rows * tok * HD,
         traffic=n * (q_rows + STAT) * HD * 4,
     )(slots, info, kv_text, arrived, bias, base)
-    shares = exchange(sent)
+    shares = exchange(sent, page_section_of)
 
     mine = call(
         lambda *refs: fresh_kernel(n, kv_heads, steps, *refs),
@@ -559,7 +575,12 @@
             jax.ShapeDtypeStruct((n, page_cap * PAGE, kvw), BF16),
         ),
         [VM, VM],
-        (VM, VM, VM),
+        (VM, ANY, ANY),
+        [
+            pltpu.VMEM((n, page_cap * PAGE, kvw), BF16),
+            pltpu.VMEM((n, page_cap * PAGE, kvw), BF16),
+            pltpu.SemaphoreType.DMA((2,)),
+        ],
         traffic=4 * tok * 2 * kvw,
     )(shares, mine)
     return (

time: 39 us -> 39.3 us (level)
  starting transfers between devices: 14.7 us -> 13.7 us
  waiting for transfers between devices: 6.79 us -> 7.5 us
  Pallas kernels: 16.3 us -> 17 us
    all_to_all x2, starting transfers between devices: 14.1 us -> 13.1 us  [exchange(): lax.all_to_all(array, 'section', split_axis=0, concat_axis=0, tiled=True,...]
    all_to_all x2, waiting for transfers between devices: 6.79 us -> 7.49 us  [exchange(): lax.all_to_all(array, 'section', split_axis=0, concat_axis=0, tiled=True,...]
    pallas_call x1, Pallas kernels: 0.93 us -> 1.54 us  [body(): call(lambda *refs: finish_kernel(kv_heads, steps, page_cap, *refs), (jax....]
where the time goes in v16:
time: 39.3 us; the launch traced here: 38.8 us
  Pallas kernels  17 us (43%)
  starting transfers between devices  13.7 us (35%)
  waiting for transfers between devices  7.5 us (19%)
  between operations  0.68 us (2%)
    all_to_all x2, starting transfers between devices, exchange(): lax.all_to_all(array, 'section', split_axis=0, concat_axis=0, tiled=True,...  13.1 us
    all_to_all x2, waiting for transfers between devices, exchange(): lax.all_to_all(array, 'section', split_axis=0, concat_axis=0, tiled=True,...  7.49 us
    pallas_call x1, Pallas kernels, body(): call(lambda *refs: text_kernel(n, img, lot, load, step, page_cap, *refs),...  6.25 us
    pallas_call x1, Pallas kernels, body(): call(lambda *refs: vis_kernel(n, lot, sizes, step, *refs), pltpu.VMEM((n,...  3.93 us
    pallas_call x1, Pallas kernels, body(): call(lambda *refs: prepare_kernel(n, lot, *refs), (jax.ShapeDtypeStruct((...  2.06 us
    pallas_call x1, Pallas kernels, body(): call(lambda *refs: attend_kernel(n, cap, lot, page_cap, kv_heads, *refs),...  1.91 us
    pallas_call x1, Pallas kernels, body(): call(lambda *refs: finish_kernel(kv_heads, steps, page_cap, *refs), (jax....  1.54 us
    pallas_call x1, Pallas kernels, body(): call(lambda *refs: fresh_kernel(n, kv_heads, steps, *refs), jax.ShapeDtyp...  1.3 us
  transfers between devices with their start and end apart: 4, of which 2 were waited for; matrix products, arithmetic and copies ran while one was open for 0% of the time, Pallas kernels for 35%

profile of v16, /device:TPU:0, one launch (start us, length us, event | category | flops | bytes accessed | tf_op | source)
XLA Modules:
  0.0 38.8 jit_solution(4032966008247269375)
XLA Ops:
  0.6 0.5 %collective-permute-start.1 = (bf16[64,4096]{1,0:T(8,128)(2,1)}, bf16[64,4096]{1,0:T(8,128)(2,1)S(1)}, u32[]{:S(2)}, u32[]{:S(2)}) collective-permute-start(bf16[64,4096]{1,0:T(8,128)(2,1)} %refs_3_.3), channel_id=1, source_target_pairs={{0,1},{1,0},{2,3},{3,2},{4,5},{5,4},{6,7},{7,6},{8,9},{9,8},{10,11... | collective-permute-start | bytes 1572872 | tf_op jit(solution)/shard_map/ppermute | solution.py:447
  1.1 0.1 collective-permute-start
  1.2 2.1 %shard_map.149 = (s32[8,64]{1,0:T(8,128)S(1)}, bf16[3072,256]{1,0:T(8,128)(2,1)S(1)}, bf16[3072,256]{1,0:T(8,128)(2,1)S(1)}, bf16[64,4096]{1,0:T(8,128)(2,1)S(1)...) custom-call(s32[1,512]{1,0:T(1,128)} %bitcast.16, bf16[8192,256]{1,0:T(8,128)(2,1)} %refs_6_.1, ...), custom_call_target="tpu_custom_call" | custom-call | flops 1048576 | bytes 16777216 | tf_op jit(solution)/shard_map/pallas_call | solution.py:470
  3.3 0.0 collective-permute-done.1.refs_1_
  3.3 3.9 %shard_map.150 = bf16[8,32,512]{2,1,0:T(8,128)(2,1)} custom-call(bf16[64,4096]{1,0:T(8,128)(2,1)S(1)} %get-tuple-element.22.refs_0_, bf16[64,4096]{1,0:T(8,128)(2,1)S(1)} %collective-permute-done.1.refs_1_, f32[1,8192]{1,0:T(1,128)S(1)} %get-tuple-element.23.refs_2_, bf16[64,128]{1,0:T(8,128)(2,1)S(1)} %get-tuple-element.24.refs_3_, ...), custom_call_target="tpu_custom_call" | custom-call | flops 17179869184 | bytes 9437184 | tf_op jit(solution)/shard_map/pallas_call | solution.py:487
  7.2 7.8 %all-to-all-start = ((bf16[8,32,512]{2,1,0:T(8,128)(2,1)}), bf16[8,32,512]{2,1,0:T(8,128)(2,1)S(1)}, u32[]{:S(2)}, u32[]{:S(2)}) async-start(bf16[8,32,512]{2,1,0:T(8,128)(2,1)} %shard_map.150), calls=%async_computation | async-start | bytes 524288 | tf_op jit(solution)/shard_map/all_to_all | solution.py:451
  15.1 0.0 collective-permute-done.refs_1_
  15.1 6.2 %shard_map.148 = (bf16[256,512]{1,0:T(8,128)(2,1)S(1)}, f32[256,256]{1,0:T(8,128)S(1)}, bf16[8,128,128]{2,1,0:T(8,128)(2,1)S(1)}, s32[8,128]{1,0:T(8,128)S(1)}, s32[16]{0:T(128)S(1)}) custom-call(bf16[256,4096]{1,0:T(8,128)(2,1)} %refs_0_.1, bf16[256,4096]{1,0:T(8,128)(2,1)S(1)} %collective-permute-done.refs_1_, f32[1,8192]{1,0:T(1,128)} %bitcast.13, ...), custom_call_target="tpu_custom_call" | custom-call | flops 2147483648 | bytes 12582912 | tf_op jit(solution)/shard_map/pallas_call | solution.py:515
  21.3 1.1 %all-to-all-done.refs_3_ = bf16[8,32,512]{2,1,0:T(8,128)(2,1)S(1)} async-done(((bf16[8,32,512]{2,1,0:T(8,128)(2,1)}), bf16[8,32,512]{2,1,0:T(8,128)(2,1)S(1)}, u32[]{:S(2)}, u32[]{:S(2)}) %all-to-all-start) | async-done | bytes 262176 | tf_op jit(solution)/shard_map/all_to_all | solution.py:451
  22.4 1.9 %shard_map.151 = (bf16[8,208,128]{2,1,0:T(8,128)(2,1)}, f32[72,128]{1,0:T(8,128)S(1)}) custom-call(s32[16]{0:T(128)S(1)} %get-tuple-element.19.refs_0_, s32[8,128]{1,0:T(8,128)S(1)} %get-tuple-element.20.refs_1_, bf16[256,512]{1,0:T(8,128)(2,1)S(1)} %get-tuple-element.21.refs_2_, bf16[8,32,512]{2,1,0:T(8,128)(2,1)S(1)} %all-to-all-done.refs_3_, ...), custom_call_target="tpu_custom_call" | custom-call | flops 67108864 | bytes 294912 | tf_op jit(solution)/shard_map/pallas_call | solution.py:540
  24.4 5.2 %all-to-all-start.1 = ((bf16[8,208,128]{2,1,0:T(8,128)(2,1)}), bf16[8,208,128]{2,1,0:T(8,128)(2,1)S(1)}, u32[]{:S(2)}, u32[]{:S(2)}) async-start(bf16[8,208,128]{2,1,0:T(8,128)(2,1)} %get-tuple-element.30), calls=%async_computation.1 | async-start | bytes 851968 | tf_op jit(solution)/shard_map/all_to_all | solution.py:451
  29.6 1.3 %shard_map.152.refs_1_ = f32[72,128]{1,0:T(8,128)S(1)} custom-call(bf16[64,128]{1,0:T(8,128)(2,1)} %bitcast.15, bf16[4,256]{1,0:T(4,128)(2,1)} %bitcast.18, bf16[4,256]{1,0:T(4,128)(2,1)} %bitcast.19, f32[72,128]{1,0:T(8,128)S(1)} %get-tuple-element.31.refs_3_), custom_call_target="tpu_custom_call" | custom-call | flops 1048576 | bytes 262144 | tf_op jit(solution)/shard_map/pallas_call | solution.py:560
  30.9 6.4 %all-to-all-done.1.refs_0_ = bf16[8,208,128]{2,1,0:T(8,128)(2,1)S(1)} async-done(((bf16[8,208,128]{2,1,0:T(8,128)(2,1)}), bf16[8,208,128]{2,1,0:T(8,128)(2,1)S(1)}, u32[]{:S(2)}, u32[]{:S(2)}) %all-to-all-start.1) | async-done | bytes 426016 | tf_op jit(solution)/shard_map/all_to_all | solution.py:451
  37.3 1.5 %shard_map.153 = (bf16[1,4,2048]{2,1,0:T(4,128)(2,1)}, bf16[8,32,256]{2,1,0:T(8,128)(2,1)}, bf16[8,32,256]{2,1,0:T(8,128)(2,1)}) custom-call(bf16[8,208,128]{2,1,0:T(8,128)(2,1)S(1)} %all-to-all-done.1.refs_0_, f32[72,128]{1,0:T(8,128)S(1)} %shard_map.152.refs_1_), custom_call_target="tpu_custom_call" | custom-call | bytes 524288 | tf_op jit(solution)/shard_map/pallas_call | solution.py:570
Async XLA Ops:
  0.6 2.7 %collective-permute-start.1 = (bf16[64,4096]{1,0:T(8,128)(2,1)}, bf16[64,4096]{1,0:T(8,128)(2,1)S(1)}, u32[]{:S(2)}, u32[]{:S(2)}) collective-permute-start(bf16[64,4096]{1,0:T(8,128)(2,1)} %refs_3_.3), channel_id=1, source_target_pairs={{0,1},{1,0},{2,3},{3,2},{4,5},{5,4},{6,7},{7,6},{8,9},{9,8},{10,11... | collective-permute-start | bytes 1572872 | tf_op jit(solution)/shard_map/ppermute | solution.py:447
  1.1 13.9 %collective-permute-start = (bf16[256,4096]{1,0:T(8,128)(2,1)}, bf16[256,4096]{1,0:T(8,128)(2,1)S(1)}, u32[]{:S(2)}, u32[]{:S(2)}) collective-permute-start(bf16[256,4096]{1,0:T(8,128)(2,1)} %refs_0_.1), channel_id=1, source_target_pairs={{0,1},{1,0},{2,3},{3,2},{4,5},{5,4},{6,7},{7,6},{8,9},{9,8},{10,11... | collective-permute-start | bytes 6291464 | tf_op jit(solution)/shard_map/ppermute | solution.py:447
  7.2 15.2 %all-to-all-start = ((bf16[8,32,512]{2,1,0:T(8,128)(2,1)}), bf16[8,32,512]{2,1,0:T(8,128)(2,1)S(1)}, u32[]{:S(2)}, u32[]{:S(2)}) async-start(bf16[8,32,512]{2,1,0:T(8,128)(2,1)} %shard_map.150), calls=%async_computation | async-start | bytes 524288 | tf_op jit(solution)/shard_map/all_to_all | solution.py:451
  24.4 12.9 %all-to-all-start.1 = ((bf16[8,208,128]{2,1,0:T(8,128)(2,1)}), bf16[8,208,128]{2,1,0:T(8,128)(2,1)S(1)}, u32[]{:S(2)}, u32[]{:S(2)}) async-start(bf16[8,208,128]{2,1,0:T(8,128)(2,1)} %get-tuple-element.30), calls=%async_computation.1 | async-start | bytes 851968 | tf_op jit(solution)/shard_map/all_to_all | solution.py:451

commit v17 on v16

--- a/solution.py
+++ b/solution.py
@@ -42,12 +42,12 @@
 
 def page_rank_of(section, n):
     z, y, length = section // 2, section % 2, n // 2
-    return (1 - y) * length + (2 * length - z - n // 4) % length
+    return ((1 - y) * length + (2 * length - z - n // 4) % length + n - 1) % n
 
 
 def page_section_of(rank, n):
-    length = n // 2
-    return 2 * (length - 1 - (rank % length + n // 4 - 1) % length) + 1 - rank // length
+    length, place = n // 2, (rank + 1) % n
+    return 2 * (length - 1 - (place % length + n // 4 - 1) % length) + 1 - place // length
 
 
 def dot(a, b):
@@ -371,7 +371,7 @@
     mine[every:, :] = jnp.broadcast_to(line, (STAT, line.shape[1]))
 
 
-def finish_kernel(kv_heads, steps, page_cap, shares, mine, attended, keys, values, *scratch):
+def finish_kernel(kv_heads, steps, page_cap, shares, mine, attended, keys, values):
     n = shares.shape[0]
     pos = lax.axis_index("section")
     every = mine.shape[0] - STAT
@@ -379,15 +379,11 @@
     start = rank_of(pos, n) % (HD // rows) * rows
     chunk = page_cap * PAGE
     halves = keys.shape[2] // HD
-    held, sems = scratch[:2], scratch[2]
     for k in range(n):
-        for i, out in enumerate(held):
+        for i, out in enumerate((keys, values)):
             for h in range(halves):
                 part = i * halves + h
                 out[page_section_of(k, n), :, h * HD : (h + 1) * HD] = shares[k, part * chunk : (part + 1) * chunk, :]
-    copies = [pltpu.make_async_copy(x, out, sems.at[i]) for i, (x, out) in enumerate(zip(held, (keys, values)))]
-    for c in copies:
-        c.start()
     pages = 2 * halves * chunk
     stats = row_to_column(mine[every : every + 1, :])
     lines = []
@@ -412,8 +408,6 @@
         for h in range(rows // steps):
             to = (g * rows // steps + h) * HD
             attended[0, :, to : to + HD] = result[h * steps : (h + 1) * steps, :]
-    for c in copies:
-        c.wait()
 
 
 def body(
@@ -575,12 +569,7 @@
             jax.ShapeDtypeStruct((n, page_cap * PAGE, kvw), BF16),
         ),
         [VM, VM],
-        (VM, ANY, ANY),
-        [
-            pltpu.VMEM((n, page_cap * PAGE, kvw), BF16),
-            pltpu.VMEM((n, page_cap * PAGE, kvw), BF16),
-            pltpu.SemaphoreType.DMA((2,)),
-        ],
+        (VM, VM, VM),
         traffic=4 * tok * 2 * kvw,
     )(shares, mine)
     return (

time: 39.3 us -> 39.2 us (level)
  waiting for transfers between devices: 7.5 us -> 9.06 us
  starting transfers between devices: 13.7 us -> 12.6 us
  Pallas kernels: 17 us -> 16.4 us
    all_to_all x2, waiting for transfers between devices: 7.49 us -> 9.06 us  [exchange(): lax.all_to_all(array, 'section', split_axis=0, concat_axis=0, tiled=True,...]
    all_to_all x2, starting transfers between devices: 13.1 us -> 12 us  [exchange(): lax.all_to_all(array, 'section', split_axis=0, concat_axis=0, tiled=True,...]
    pallas_call x1, Pallas kernels: 1.54 us -> 0.93 us  [body(): call(lambda *refs: finish_kernel(kv_heads, steps, page_cap, *refs), (jax....]
where the time goes in v17:
time: 39.2 us; the launch traced here: 38.8 us
  Pallas kernels  16.4 us (42%)
  starting transfers between devices  12.6 us (32%)
  waiting for transfers between devices  9.06 us (23%)
  between operations  0.68 us (2%)
    all_to_all x2, starting transfers between devices, exchange(): lax.all_to_all(array, 'section', split_axis=0, concat_axis=0, tiled=True,...  12 us
    all_to_all x2, waiting for transfers between devices, exchange(): lax.all_to_all(array, 'section', split_axis=0, concat_axis=0, tiled=True,...  9.06 us
    pallas_call x1, Pallas kernels, body(): call(lambda *refs: text_kernel(n, img, lot, load, step, page_cap, *refs),...  6.29 us
    pallas_call x1, Pallas kernels, body(): call(lambda *refs: vis_kernel(n, lot, sizes, step, *refs), pltpu.VMEM((n,...  3.93 us
    pallas_call x1, Pallas kernels, body(): call(lambda *refs: prepare_kernel(n, lot, *refs), (jax.ShapeDtypeStruct((...  2.06 us
    pallas_call x1, Pallas kernels, body(): call(lambda *refs: attend_kernel(n, cap, lot, page_cap, kv_heads, *refs),...  1.91 us
    pallas_call x1, Pallas kernels, body(): call(lambda *refs: fresh_kernel(n, kv_heads, steps, *refs), jax.ShapeDtyp...  1.3 us
    pallas_call x1, Pallas kernels, body(): call(lambda *refs: finish_kernel(kv_heads, steps, page_cap, *refs), (jax....  0.93 us
  transfers between devices with their start and end apart: 4, of which 2 were waited for; matrix products, arithmetic and copies ran while one was open for 0% of the time, Pallas kernels for 35%

profile of v17, /device:TPU:0, one launch (start us, length us, event | category | flops | bytes accessed | tf_op | source)
XLA Modules:
  0.0 38.8 jit_solution(6465699307769577226)
XLA Ops:
  0.6 0.5 %collective-permute-start.1 = (bf16[64,4096]{1,0:T(8,128)(2,1)}, bf16[64,4096]{1,0:T(8,128)(2,1)S(1)}, u32[]{:S(2)}, u32[]{:S(2)}) collective-permute-start(bf16[64,4096]{1,0:T(8,128)(2,1)} %refs_3_.3), channel_id=1, source_target_pairs={{0,1},{1,0},{2,3},{3,2},{4,5},{5,4},{6,7},{7,6},{8,9},{9,8},{10,11... | collective-permute-start | bytes 1572872 | tf_op jit(solution)/shard_map/ppermute | solution.py:441
  1.1 0.1 collective-permute-start
  1.2 2.1 %shard_map.149 = (s32[8,64]{1,0:T(8,128)S(1)}, bf16[3072,256]{1,0:T(8,128)(2,1)S(1)}, bf16[3072,256]{1,0:T(8,128)(2,1)S(1)}, bf16[64,4096]{1,0:T(8,128)(2,1)S(1)...) custom-call(s32[1,512]{1,0:T(1,128)} %bitcast.16, bf16[8192,256]{1,0:T(8,128)(2,1)} %refs_6_.1, ...), custom_call_target="tpu_custom_call" | custom-call | flops 1048576 | bytes 16777216 | tf_op jit(solution)/shard_map/pallas_call | solution.py:464
  3.3 0.0 collective-permute-done.1.refs_1_
  3.3 3.9 %shard_map.150 = bf16[8,32,512]{2,1,0:T(8,128)(2,1)} custom-call(bf16[64,4096]{1,0:T(8,128)(2,1)S(1)} %get-tuple-element.22.refs_0_, bf16[64,4096]{1,0:T(8,128)(2,1)S(1)} %collective-permute-done.1.refs_1_, f32[1,8192]{1,0:T(1,128)S(1)} %get-tuple-element.23.refs_2_, bf16[64,128]{1,0:T(8,128)(2,1)S(1)} %get-tuple-element.24.refs_3_, ...), custom_call_target="tpu_custom_call" | custom-call | flops 17179869184 | bytes 9437184 | tf_op jit(solution)/shard_map/pallas_call | solution.py:481
  7.2 7.8 %all-to-all-start = ((bf16[8,32,512]{2,1,0:T(8,128)(2,1)}), bf16[8,32,512]{2,1,0:T(8,128)(2,1)S(1)}, u32[]{:S(2)}, u32[]{:S(2)}) async-start(bf16[8,32,512]{2,1,0:T(8,128)(2,1)} %shard_map.150), calls=%async_computation | async-start | bytes 524288 | tf_op jit(solution)/shard_map/all_to_all | solution.py:445
  15.1 0.0 collective-permute-done.refs_1_
  15.1 6.3 %shard_map.148 = (bf16[256,512]{1,0:T(8,128)(2,1)S(1)}, f32[256,256]{1,0:T(8,128)S(1)}, bf16[8,128,128]{2,1,0:T(8,128)(2,1)S(1)}, s32[8,128]{1,0:T(8,128)S(1)}, s32[16]{0:T(128)S(1)}) custom-call(bf16[256,4096]{1,0:T(8,128)(2,1)} %refs_0_.1, bf16[256,4096]{1,0:T(8,128)(2,1)S(1)} %collective-permute-done.refs_1_, f32[1,8192]{1,0:T(1,128)} %bitcast.13, ...), custom_call_target="tpu_custom_call" | custom-call | flops 2147483648 | bytes 12582912 | tf_op jit(solution)/shard_map/pallas_call | solution.py:509
  21.4 1.1 %all-to-all-done.refs_3_ = bf16[8,32,512]{2,1,0:T(8,128)(2,1)S(1)} async-done(((bf16[8,32,512]{2,1,0:T(8,128)(2,1)}), bf16[8,32,512]{2,1,0:T(8,128)(2,1)S(1)}, u32[]{:S(2)}, u32[]{:S(2)}) %all-to-all-start) | async-done | bytes 262176 | tf_op jit(solution)/shard_map/all_to_all | solution.py:445
  22.4 1.9 %shard_map.151 = (bf16[8,208,128]{2,1,0:T(8,128)(2,1)}, f32[72,128]{1,0:T(8,128)S(1)}) custom-call(s32[16]{0:T(128)S(1)} %get-tuple-element.19.refs_0_, s32[8,128]{1,0:T(8,128)S(1)} %get-tuple-element.20.refs_1_, bf16[256,512]{1,0:T(8,128)(2,1)S(1)} %get-tuple-element.21.refs_2_, bf16[8,32,512]{2,1,0:T(8,128)(2,1)S(1)} %all-to-all-done.refs_3_, ...), custom_call_target="tpu_custom_call" | custom-call | flops 67108864 | bytes 294912 | tf_op jit(solution)/shard_map/pallas_call | solution.py:534
  24.4 4.2 %all-to-all-start.1 = ((bf16[8,208,128]{2,1,0:T(8,128)(2,1)}), bf16[8,208,128]{2,1,0:T(8,128)(2,1)S(1)}, u32[]{:S(2)}, u32[]{:S(2)}) async-start(bf16[8,208,128]{2,1,0:T(8,128)(2,1)} %get-tuple-element.30), calls=%async_computation.1 | async-start | bytes 851968 | tf_op jit(solution)/shard_map/all_to_all | solution.py:445
  28.6 1.3 %shard_map.152.refs_1_ = f32[72,128]{1,0:T(8,128)S(1)} custom-call(bf16[64,128]{1,0:T(8,128)(2,1)} %bitcast.15, bf16[4,256]{1,0:T(4,128)(2,1)} %bitcast.18, bf16[4,256]{1,0:T(4,128)(2,1)} %bitcast.19, f32[72,128]{1,0:T(8,128)S(1)} %get-tuple-element.31.refs_3_), custom_call_target="tpu_custom_call" | custom-call | flops 1048576 | bytes 262144 | tf_op jit(solution)/shard_map/pallas_call | solution.py:554
  29.9 8.0 %all-to-all-done.1.refs_0_ = bf16[8,208,128]{2,1,0:T(8,128)(2,1)S(1)} async-done(((bf16[8,208,128]{2,1,0:T(8,128)(2,1)}), bf16[8,208,128]{2,1,0:T(8,128)(2,1)S(1)}, u32[]{:S(2)}, u32[]{:S(2)}) %all-to-all-start.1) | async-done | bytes 426016 | tf_op jit(solution)/shard_map/all_to_all | solution.py:445
  37.9 0.9 %shard_map.153 = (bf16[1,4,2048]{2,1,0:T(4,128)(2,1)}, bf16[8,32,256]{2,1,0:T(8,128)(2,1)}, bf16[8,32,256]{2,1,0:T(8,128)(2,1)}) custom-call(bf16[8,208,128]{2,1,0:T(8,128)(2,1)S(1)} %all-to-all-done.1.refs_0_, f32[72,128]{1,0:T(8,128)S(1)} %shard_map.152.refs_1_), custom_call_target="tpu_custom_call" | custom-call | bytes 524288 | tf_op jit(solution)/shard_map/pallas_call | solution.py:564
Async XLA Ops:
  0.6 2.7 %collective-permute-start.1 = (bf16[64,4096]{1,0:T(8,128)(2,1)}, bf16[64,4096]{1,0:T(8,128)(2,1)S(1)}, u32[]{:S(2)}, u32[]{:S(2)}) collective-permute-start(bf16[64,4096]{1,0:T(8,128)(2,1)} %refs_3_.3), channel_id=1, source_target_pairs={{0,1},{1,0},{2,3},{3,2},{4,5},{5,4},{6,7},{7,6},{8,9},{9,8},{10,11... | collective-permute-start | bytes 1572872 | tf_op jit(solution)/shard_map/ppermute | solution.py:441
  1.1 13.9 %collective-permute-start = (bf16[256,4096]{1,0:T(8,128)(2,1)}, bf16[256,4096]{1,0:T(8,128)(2,1)S(1)}, u32[]{:S(2)}, u32[]{:S(2)}) collective-permute-start(bf16[256,4096]{1,0:T(8,128)(2,1)} %refs_0_.1), channel_id=1, source_target_pairs={{0,1},{1,0},{2,3},{3,2},{4,5},{5,4},{6,7},{7,6},{8,9},{9,8},{10,11... | collective-permute-start | bytes 6291464 | tf_op jit(solution)/shard_map/ppermute | solution.py:441
  7.2 15.2 %all-to-all-start = ((bf16[8,32,512]{2,1,0:T(8,128)(2,1)}), bf16[8,32,512]{2,1,0:T(8,128)(2,1)S(1)}, u32[]{:S(2)}, u32[]{:S(2)}) async-start(bf16[8,32,512]{2,1,0:T(8,128)(2,1)} %shard_map.150), calls=%async_computation | async-start | bytes 524288 | tf_op jit(solution)/shard_map/all_to_all | solution.py:445
  24.4 13.5 %all-to-all-start.1 = ((bf16[8,208,128]{2,1,0:T(8,128)(2,1)}), bf16[8,208,128]{2,1,0:T(8,128)(2,1)S(1)}, u32[]{:S(2)}, u32[]{:S(2)}) async-start(bf16[8,208,128]{2,1,0:T(8,128)(2,1)} %get-tuple-element.30), calls=%async_computation.1 | async-start | bytes 851968 | tf_op jit(solution)/shard_map/all_to_all | solution.py:445

commit v18 on v17

--- a/solution.py
+++ b/solution.py
@@ -42,12 +42,12 @@
 
 def page_rank_of(section, n):
     z, y, length = section // 2, section % 2, n // 2
-    return ((1 - y) * length + (2 * length - z - n // 4) % length + n - 1) % n
+    return (1 - y) * length + (2 * length - z - n // 4) % length
 
 
 def page_section_of(rank, n):
-    length, place = n // 2, (rank + 1) % n
-    return 2 * (length - 1 - (place % length + n // 4 - 1) % length) + 1 - place // length
+    length = n // 2
+    return 2 * (length - 1 - (rank % length + n // 4 - 1) % length) + 1 - rank // length
 
 
 def dot(a, b):

time: 39.2 us -> 38.7 us (0.987)
  waiting for transfers between devices: 9.06 us -> 7.5 us
  starting transfers between devices: 12.6 us -> 13.7 us
    all_to_all x2, waiting for transfers between devices: 9.06 us -> 7.49 us  [exchange(): lax.all_to_all(array, 'section', split_axis=0, concat_axis=0, tiled=True,...]
    all_to_all x2, starting transfers between devices: 12 us -> 13.1 us  [exchange(): lax.all_to_all(array, 'section', split_axis=0, concat_axis=0, tiled=True,...]
where the time goes in v18:
time: 38.7 us; the launch traced here: 38.2 us
  Pallas kernels  16.4 us (42%)
  starting transfers between devices  13.7 us (35%)
  waiting for transfers between devices  7.5 us (19%)
  between operations  0.68 us (2%)
    all_to_all x2, starting transfers between devices, exchange(): lax.all_to_all(array, 'section', split_axis=0, concat_axis=0, tiled=True,...  13.1 us
    all_to_all x2, waiting for transfers between devices, exchange(): lax.all_to_all(array, 'section', split_axis=0, concat_axis=0, tiled=True,...  7.49 us
    pallas_call x1, Pallas kernels, body(): call(lambda *refs: text_kernel(n, img, lot, load, step, page_cap, *refs),...  6.25 us
    pallas_call x1, Pallas kernels, body(): call(lambda *refs: vis_kernel(n, lot, sizes, step, *refs), pltpu.VMEM((n,...  3.93 us
    pallas_call x1, Pallas kernels, body(): call(lambda *refs: prepare_kernel(n, lot, *refs), (jax.ShapeDtypeStruct((...  2.06 us
    pallas_call x1, Pallas kernels, body(): call(lambda *refs: attend_kernel(n, cap, lot, page_cap, kv_heads, *refs),...  1.91 us
    pallas_call x1, Pallas kernels, body(): call(lambda *refs: fresh_kernel(n, kv_heads, steps, *refs), jax.ShapeDtyp...  1.3 us
    pallas_call x1, Pallas kernels, body(): call(lambda *refs: finish_kernel(kv_heads, steps, page_cap, *refs), (jax....  0.93 us
  transfers between devices with their start and end apart: 4, of which 2 were waited for; matrix products, arithmetic and copies ran while one was open for 0% of the time, Pallas kernels for 35%

profile of v18, /device:TPU:0, one launch (start us, length us, event | category | flops | bytes accessed | tf_op | source)
XLA Modules:
  0.0 38.2 jit_solution(15524082154592101702)
XLA Ops:
  0.6 0.5 %collective-permute-start.1 = (bf16[64,4096]{1,0:T(8,128)(2,1)}, bf16[64,4096]{1,0:T(8,128)(2,1)S(1)}, u32[]{:S(2)}, u32[]{:S(2)}) collective-permute-start(bf16[64,4096]{1,0:T(8,128)(2,1)} %refs_3_.3), channel_id=1, source_target_pairs={{0,1},{1,0},{2,3},{3,2},{4,5},{5,4},{6,7},{7,6},{8,9},{9,8},{10,11... | collective-permute-start | bytes 1572872 | tf_op jit(solution)/shard_map/ppermute | solution.py:441
  1.1 0.1 collective-permute-start
  1.2 2.1 %shard_map.149 = (s32[8,64]{1,0:T(8,128)S(1)}, bf16[3072,256]{1,0:T(8,128)(2,1)S(1)}, bf16[3072,256]{1,0:T(8,128)(2,1)S(1)}, bf16[64,4096]{1,0:T(8,128)(2,1)S(1)...) custom-call(s32[1,512]{1,0:T(1,128)} %bitcast.16, bf16[8192,256]{1,0:T(8,128)(2,1)} %refs_6_.1, ...), custom_call_target="tpu_custom_call" | custom-call | flops 1048576 | bytes 16777216 | tf_op jit(solution)/shard_map/pallas_call | solution.py:464
  3.3 0.0 collective-permute-done.1.refs_1_
  3.3 3.9 %shard_map.150 = bf16[8,32,512]{2,1,0:T(8,128)(2,1)} custom-call(bf16[64,4096]{1,0:T(8,128)(2,1)S(1)} %get-tuple-element.22.refs_0_, bf16[64,4096]{1,0:T(8,128)(2,1)S(1)} %collective-permute-done.1.refs_1_, f32[1,8192]{1,0:T(1,128)S(1)} %get-tuple-element.23.refs_2_, bf16[64,128]{1,0:T(8,128)(2,1)S(1)} %get-tuple-element.24.refs_3_, ...), custom_call_target="tpu_custom_call" | custom-call | flops 17179869184 | bytes 9437184 | tf_op jit(solution)/shard_map/pallas_call | solution.py:481
  7.2 7.8 %all-to-all-start = ((bf16[8,32,512]{2,1,0:T(8,128)(2,1)}), bf16[8,32,512]{2,1,0:T(8,128)(2,1)S(1)}, u32[]{:S(2)}, u32[]{:S(2)}) async-start(bf16[8,32,512]{2,1,0:T(8,128)(2,1)} %shard_map.150), calls=%async_computation | async-start | bytes 524288 | tf_op jit(solution)/shard_map/all_to_all | solution.py:445
  15.1 0.0 collective-permute-done.refs_1_
  15.1 6.2 %shard_map.148 = (bf16[256,512]{1,0:T(8,128)(2,1)S(1)}, f32[256,256]{1,0:T(8,128)S(1)}, bf16[8,128,128]{2,1,0:T(8,128)(2,1)S(1)}, s32[8,128]{1,0:T(8,128)S(1)}, s32[16]{0:T(128)S(1)}) custom-call(bf16[256,4096]{1,0:T(8,128)(2,1)} %refs_0_.1, bf16[256,4096]{1,0:T(8,128)(2,1)S(1)} %collective-permute-done.refs_1_, f32[1,8192]{1,0:T(1,128)} %bitcast.13, ...), custom_call_target="tpu_custom_call" | custom-call | flops 2147483648 | bytes 12582912 | tf_op jit(solution)/shard_map/pallas_call | solution.py:509
  21.3 1.1 %all-to-all-done.refs_3_ = bf16[8,32,512]{2,1,0:T(8,128)(2,1)S(1)} async-done(((bf16[8,32,512]{2,1,0:T(8,128)(2,1)}), bf16[8,32,512]{2,1,0:T(8,128)(2,1)S(1)}, u32[]{:S(2)}, u32[]{:S(2)}) %all-to-all-start) | async-done | bytes 262176 | tf_op jit(solution)/shard_map/all_to_all | solution.py:445
  22.4 1.9 %shard_map.151 = (bf16[8,208,128]{2,1,0:T(8,128)(2,1)}, f32[72,128]{1,0:T(8,128)S(1)}) custom-call(s32[16]{0:T(128)S(1)} %get-tuple-element.19.refs_0_, s32[8,128]{1,0:T(8,128)S(1)} %get-tuple-element.20.refs_1_, bf16[256,512]{1,0:T(8,128)(2,1)S(1)} %get-tuple-element.21.refs_2_, bf16[8,32,512]{2,1,0:T(8,128)(2,1)S(1)} %all-to-all-done.refs_3_, ...), custom_call_target="tpu_custom_call" | custom-call | flops 67108864 | bytes 294912 | tf_op jit(solution)/shard_map/pallas_call | solution.py:534
  24.4 5.2 %all-to-all-start.1 = ((bf16[8,208,128]{2,1,0:T(8,128)(2,1)}), bf16[8,208,128]{2,1,0:T(8,128)(2,1)S(1)}, u32[]{:S(2)}, u32[]{:S(2)}) async-start(bf16[8,208,128]{2,1,0:T(8,128)(2,1)} %get-tuple-element.30), calls=%async_computation.1 | async-start | bytes 851968 | tf_op jit(solution)/shard_map/all_to_all | solution.py:445
  29.6 1.3 %shard_map.152.refs_1_ = f32[72,128]{1,0:T(8,128)S(1)} custom-call(bf16[64,128]{1,0:T(8,128)(2,1)} %bitcast.15, bf16[4,256]{1,0:T(4,128)(2,1)} %bitcast.18, bf16[4,256]{1,0:T(4,128)(2,1)} %bitcast.19, f32[72,128]{1,0:T(8,128)S(1)} %get-tuple-element.31.refs_3_), custom_call_target="tpu_custom_call" | custom-call | flops 1048576 | bytes 262144 | tf_op jit(solution)/shard_map/pallas_call | solution.py:554
  30.9 6.4 %all-to-all-done.1.refs_0_ = bf16[8,208,128]{2,1,0:T(8,128)(2,1)S(1)} async-done(((bf16[8,208,128]{2,1,0:T(8,128)(2,1)}), bf16[8,208,128]{2,1,0:T(8,128)(2,1)S(1)}, u32[]{:S(2)}, u32[]{:S(2)}) %all-to-all-start.1) | async-done | bytes 426016 | tf_op jit(solution)/shard_map/all_to_all | solution.py:445
  37.3 0.9 %shard_map.153 = (bf16[1,4,2048]{2,1,0:T(4,128)(2,1)}, bf16[8,32,256]{2,1,0:T(8,128)(2,1)}, bf16[8,32,256]{2,1,0:T(8,128)(2,1)}) custom-call(bf16[8,208,128]{2,1,0:T(8,128)(2,1)S(1)} %all-to-all-done.1.refs_0_, f32[72,128]{1,0:T(8,128)S(1)} %shard_map.152.refs_1_), custom_call_target="tpu_custom_call" | custom-call | bytes 524288 | tf_op jit(solution)/shard_map/pallas_call | solution.py:564
Async XLA Ops:
  0.6 2.7 %collective-permute-start.1 = (bf16[64,4096]{1,0:T(8,128)(2,1)}, bf16[64,4096]{1,0:T(8,128)(2,1)S(1)}, u32[]{:S(2)}, u32[]{:S(2)}) collective-permute-start(bf16[64,4096]{1,0:T(8,128)(2,1)} %refs_3_.3), channel_id=1, source_target_pairs={{0,1},{1,0},{2,3},{3,2},{4,5},{5,4},{6,7},{7,6},{8,9},{9,8},{10,11... | collective-permute-start | bytes 1572872 | tf_op jit(solution)/shard_map/ppermute | solution.py:441
  1.1 13.9 %collective-permute-start = (bf16[256,4096]{1,0:T(8,128)(2,1)}, bf16[256,4096]{1,0:T(8,128)(2,1)S(1)}, u32[]{:S(2)}, u32[]{:S(2)}) collective-permute-start(bf16[256,4096]{1,0:T(8,128)(2,1)} %refs_0_.1), channel_id=1, source_target_pairs={{0,1},{1,0},{2,3},{3,2},{4,5},{5,4},{6,7},{7,6},{8,9},{9,8},{10,11... | collective-permute-start | bytes 6291464 | tf_op jit(solution)/shard_map/ppermute | solution.py:441
  7.2 15.2 %all-to-all-start = ((bf16[8,32,512]{2,1,0:T(8,128)(2,1)}), bf16[8,32,512]{2,1,0:T(8,128)(2,1)S(1)}, u32[]{:S(2)}, u32[]{:S(2)}) async-start(bf16[8,32,512]{2,1,0:T(8,128)(2,1)} %shard_map.150), calls=%async_computation | async-start | bytes 524288 | tf_op jit(solution)/shard_map/all_to_all | solution.py:445
  24.4 12.9 %all-to-all-start.1 = ((bf16[8,208,128]{2,1,0:T(8,128)(2,1)}), bf16[8,208,128]{2,1,0:T(8,128)(2,1)S(1)}, u32[]{:S(2)}, u32[]{:S(2)}) async-start(bf16[8,208,128]{2,1,0:T(8,128)(2,1)} %get-tuple-element.30), calls=%async_computation.1 | async-start | bytes 851968 | tf_op jit(solution)/shard_map/all_to_all | solution.py:445

commit v19 on v18

--- a/solution.py
+++ b/solution.py
@@ -42,12 +42,12 @@
 
 def page_rank_of(section, n):
     z, y, length = section // 2, section % 2, n // 2
-    return (1 - y) * length + (2 * length - z - n // 4) % length
+    return y * length + (2 * length - z - n // 4) % length
 
 
 def page_section_of(rank, n):
     length = n // 2
-    return 2 * (length - 1 - (rank % length + n // 4 - 1) % length) + 1 - rank // length
+    return 2 * (length - 1 - (rank % length + n // 4 - 1) % length) + rank // length
 
 
 def dot(a, b):

time: 38.7 us -> 38.1 us (0.984)
  starting transfers between devices: 13.7 us -> 13.2 us
    all_to_all x2, starting transfers between devices: 13.1 us -> 12.6 us  [exchange(): lax.all_to_all(array, 'section', split_axis=0, concat_axis=0, tiled=True,...]
  transfers between devices with their start and end apart: 4 -> 4, of which waited for: 2 -> 2; matrix products, arithmetic and copies ran while one was open for 0% -> 0% of each run, Pallas kernels for 35% -> 36%
where the time goes in v19:
time: 38.1 us; the launch traced here: 37.7 us
  Pallas kernels  16.4 us (43%)
  starting transfers between devices  13.2 us (35%)
  waiting for transfers between devices  7.45 us (20%)
  between operations  0.68 us (2%)
    all_to_all x2, starting transfers between devices, exchange(): lax.all_to_all(array, 'section', split_axis=0, concat_axis=0, tiled=True,...  12.6 us
    all_to_all x2, waiting for transfers between devices, exchange(): lax.all_to_all(array, 'section', split_axis=0, concat_axis=0, tiled=True,...  7.45 us
    pallas_call x1, Pallas kernels, body(): call(lambda *refs: text_kernel(n, img, lot, load, step, page_cap, *refs),...  6.24 us
    pallas_call x1, Pallas kernels, body(): call(lambda *refs: vis_kernel(n, lot, sizes, step, *refs), pltpu.VMEM((n,...  3.93 us
    pallas_call x1, Pallas kernels, body(): call(lambda *refs: prepare_kernel(n, lot, *refs), (jax.ShapeDtypeStruct((...  2.06 us
    pallas_call x1, Pallas kernels, body(): call(lambda *refs: attend_kernel(n, cap, lot, page_cap, kv_heads, *refs),...  1.91 us
    pallas_call x1, Pallas kernels, body(): call(lambda *refs: fresh_kernel(n, kv_heads, steps, *refs), jax.ShapeDtyp...  1.3 us
    pallas_call x1, Pallas kernels, body(): call(lambda *refs: finish_kernel(kv_heads, steps, page_cap, *refs), (jax....  0.93 us
  transfers between devices with their start and end apart: 4, of which 2 were waited for; matrix products, arithmetic and copies ran while one was open for 0% of the time, Pallas kernels for 36%

profile of v19, /device:TPU:0, one launch (start us, length us, event | category | flops | bytes accessed | tf_op | source)
XLA Modules:
  0.0 37.7 jit_solution(3345170835591946864)
XLA Ops:
  0.6 0.5 %collective-permute-start.1 = (bf16[64,4096]{1,0:T(8,128)(2,1)}, bf16[64,4096]{1,0:T(8,128)(2,1)S(1)}, u32[]{:S(2)}, u32[]{:S(2)}) collective-permute-start(bf16[64,4096]{1,0:T(8,128)(2,1)} %refs_3_.3), channel_id=1, source_target_pairs={{0,1},{1,0},{2,3},{3,2},{4,5},{5,4},{6,7},{7,6},{8,9},{9,8},{10,11... | collective-permute-start | bytes 1572872 | tf_op jit(solution)/shard_map/ppermute | solution.py:441
  1.1 0.1 collective-permute-start
  1.2 2.1 %shard_map.149 = (s32[8,64]{1,0:T(8,128)S(1)}, bf16[3072,256]{1,0:T(8,128)(2,1)S(1)}, bf16[3072,256]{1,0:T(8,128)(2,1)S(1)}, bf16[64,4096]{1,0:T(8,128)(2,1)S(1)...) custom-call(s32[1,512]{1,0:T(1,128)} %bitcast.16, bf16[8192,256]{1,0:T(8,128)(2,1)} %refs_6_.1, ...), custom_call_target="tpu_custom_call" | custom-call | flops 1048576 | bytes 16777216 | tf_op jit(solution)/shard_map/pallas_call | solution.py:464
  3.3 0.0 collective-permute-done.1.refs_1_
  3.3 3.9 %shard_map.150 = bf16[8,32,512]{2,1,0:T(8,128)(2,1)} custom-call(bf16[64,4096]{1,0:T(8,128)(2,1)S(1)} %get-tuple-element.22.refs_0_, bf16[64,4096]{1,0:T(8,128)(2,1)S(1)} %collective-permute-done.1.refs_1_, f32[1,8192]{1,0:T(1,128)S(1)} %get-tuple-element.23.refs_2_, bf16[64,128]{1,0:T(8,128)(2,1)S(1)} %get-tuple-element.24.refs_3_, ...), custom_call_target="tpu_custom_call" | custom-call | flops 17179869184 | bytes 9437184 | tf_op jit(solution)/shard_map/pallas_call | solution.py:481
  7.2 7.8 %all-to-all-start = ((bf16[8,32,512]{2,1,0:T(8,128)(2,1)}), bf16[8,32,512]{2,1,0:T(8,128)(2,1)S(1)}, u32[]{:S(2)}, u32[]{:S(2)}) async-start(bf16[8,32,512]{2,1,0:T(8,128)(2,1)} %shard_map.150), calls=%async_computation | async-start | bytes 524288 | tf_op jit(solution)/shard_map/all_to_all | solution.py:445
  15.1 0.0 collective-permute-done.refs_1_
  15.1 6.2 %shard_map.148 = (bf16[256,512]{1,0:T(8,128)(2,1)S(1)}, f32[256,256]{1,0:T(8,128)S(1)}, bf16[8,128,128]{2,1,0:T(8,128)(2,1)S(1)}, s32[8,128]{1,0:T(8,128)S(1)}, s32[16]{0:T(128)S(1)}) custom-call(bf16[256,4096]{1,0:T(8,128)(2,1)} %refs_0_.1, bf16[256,4096]{1,0:T(8,128)(2,1)S(1)} %collective-permute-done.refs_1_, f32[1,8192]{1,0:T(1,128)} %bitcast.13, ...), custom_call_target="tpu_custom_call" | custom-call | flops 2147483648 | bytes 12582912 | tf_op jit(solution)/shard_map/pallas_call | solution.py:509
  21.3 1.1 %all-to-all-done.refs_3_ = bf16[8,32,512]{2,1,0:T(8,128)(2,1)S(1)} async-done(((bf16[8,32,512]{2,1,0:T(8,128)(2,1)}), bf16[8,32,512]{2,1,0:T(8,128)(2,1)S(1)}, u32[]{:S(2)}, u32[]{:S(2)}) %all-to-all-start) | async-done | bytes 262176 | tf_op jit(solution)/shard_map/all_to_all | solution.py:445
  22.4 1.9 %shard_map.151 = (bf16[8,208,128]{2,1,0:T(8,128)(2,1)}, f32[72,128]{1,0:T(8,128)S(1)}) custom-call(s32[16]{0:T(128)S(1)} %get-tuple-element.19.refs_0_, s32[8,128]{1,0:T(8,128)S(1)} %get-tuple-element.20.refs_1_, bf16[256,512]{1,0:T(8,128)(2,1)S(1)} %get-tuple-element.21.refs_2_, bf16[8,32,512]{2,1,0:T(8,128)(2,1)S(1)} %all-to-all-done.refs_3_, ...), custom_call_target="tpu_custom_call" | custom-call | flops 67108864 | bytes 294912 | tf_op jit(solution)/shard_map/pallas_call | solution.py:534
  24.4 4.8 %all-to-all-start.1 = ((bf16[8,208,128]{2,1,0:T(8,128)(2,1)}), bf16[8,208,128]{2,1,0:T(8,128)(2,1)S(1)}, u32[]{:S(2)}, u32[]{:S(2)}) async-start(bf16[8,208,128]{2,1,0:T(8,128)(2,1)} %get-tuple-element.30), calls=%async_computation.1 | async-start | bytes 851968 | tf_op jit(solution)/shard_map/all_to_all | solution.py:445
  29.1 1.3 %shard_map.152.refs_1_ = f32[72,128]{1,0:T(8,128)S(1)} custom-call(bf16[64,128]{1,0:T(8,128)(2,1)} %bitcast.15, bf16[4,256]{1,0:T(4,128)(2,1)} %bitcast.18, bf16[4,256]{1,0:T(4,128)(2,1)} %bitcast.19, f32[72,128]{1,0:T(8,128)S(1)} %get-tuple-element.31.refs_3_), custom_call_target="tpu_custom_call" | custom-call | flops 1048576 | bytes 262144 | tf_op jit(solution)/shard_map/pallas_call | solution.py:554
  30.4 6.3 %all-to-all-done.1.refs_0_ = bf16[8,208,128]{2,1,0:T(8,128)(2,1)S(1)} async-done(((bf16[8,208,128]{2,1,0:T(8,128)(2,1)}), bf16[8,208,128]{2,1,0:T(8,128)(2,1)S(1)}, u32[]{:S(2)}, u32[]{:S(2)}) %all-to-all-start.1) | async-done | bytes 426016 | tf_op jit(solution)/shard_map/all_to_all | solution.py:445
  36.8 0.9 %shard_map.153 = (bf16[1,4,2048]{2,1,0:T(4,128)(2,1)}, bf16[8,32,256]{2,1,0:T(8,128)(2,1)}, bf16[8,32,256]{2,1,0:T(8,128)(2,1)}) custom-call(bf16[8,208,128]{2,1,0:T(8,128)(2,1)S(1)} %all-to-all-done.1.refs_0_, f32[72,128]{1,0:T(8,128)S(1)} %shard_map.152.refs_1_), custom_call_target="tpu_custom_call" | custom-call | bytes 524288 | tf_op jit(solution)/shard_map/pallas_call | solution.py:564
Async XLA Ops:
  0.6 2.7 %collective-permute-start.1 = (bf16[64,4096]{1,0:T(8,128)(2,1)}, bf16[64,4096]{1,0:T(8,128)(2,1)S(1)}, u32[]{:S(2)}, u32[]{:S(2)}) collective-permute-start(bf16[64,4096]{1,0:T(8,128)(2,1)} %refs_3_.3), channel_id=1, source_target_pairs={{0,1},{1,0},{2,3},{3,2},{4,5},{5,4},{6,7},{7,6},{8,9},{9,8},{10,11... | collective-permute-start | bytes 1572872 | tf_op jit(solution)/shard_map/ppermute | solution.py:441
  1.1 13.9 %collective-permute-start = (bf16[256,4096]{1,0:T(8,128)(2,1)}, bf16[256,4096]{1,0:T(8,128)(2,1)S(1)}, u32[]{:S(2)}, u32[]{:S(2)}) collective-permute-start(bf16[256,4096]{1,0:T(8,128)(2,1)} %refs_0_.1), channel_id=1, source_target_pairs={{0,1},{1,0},{2,3},{3,2},{4,5},{5,4},{6,7},{7,6},{8,9},{9,8},{10,11... | collective-permute-start | bytes 6291464 | tf_op jit(solution)/shard_map/ppermute | solution.py:441
  7.2 15.2 %all-to-all-start = ((bf16[8,32,512]{2,1,0:T(8,128)(2,1)}), bf16[8,32,512]{2,1,0:T(8,128)(2,1)S(1)}, u32[]{:S(2)}, u32[]{:S(2)}) async-start(bf16[8,32,512]{2,1,0:T(8,128)(2,1)} %shard_map.150), calls=%async_computation | async-start | bytes 524288 | tf_op jit(solution)/shard_map/all_to_all | solution.py:445
  24.4 12.4 %all-to-all-start.1 = ((bf16[8,208,128]{2,1,0:T(8,128)(2,1)}), bf16[8,208,128]{2,1,0:T(8,128)(2,1)S(1)}, u32[]{:S(2)}, u32[]{:S(2)}) async-start(bf16[8,208,128]{2,1,0:T(8,128)(2,1)} %get-tuple-element.30), calls=%async_computation.1 | async-start | bytes 851968 | tf_op jit(solution)/shard_map/all_to_all | solution.py:445

commit v20 on v19

--- a/solution.py
+++ b/solution.py
@@ -171,12 +171,22 @@
         total[:, columns] += part
 
 
-def vis_kernel(n, lot, sizes, step, *refs):
-    near, far, gain, query, key_held, value_held, w_key, w_value, info, out, key_rest, value_rest, total, sems = refs
+def start_lists(far, small, sems):
+    copies = [pltpu.make_async_copy(a, b, sems.at[i]) for i, (a, b) in enumerate(zip(far, small))]
+    for c in copies:
+        c.start()
+    return copies
+
+
+def vis_kernel(n, lot, page_cap, sizes, step, *refs):
+    near, far, gain, query, key_held, value_held, w_key, w_value, info = refs[:9]
+    lists, (out, *plan) = refs[9:14], refs[14:18]
+    (key_rest, value_rest, total, starts, sems, list_sems), small = refs[18:24], refs[24:]
     img, half = near.shape
     kvw = w_key.shape[1]
     me = lax.axis_index("tensor")
     held = key_held.shape[0]
+    copies = start_lists(lists, small, list_sems)
     loads = {}
     at = held
     for size in sizes:
@@ -209,6 +219,12 @@
         for j in range(query.shape[0] // q_lots):
             out[k, :q_lots, j * HD : (j + 1) * HD] = query[j * q_lots : (j + 1) * q_lots, :]
         out[k, q_lots:, :] = packed[k * lot : (k + 1) * lot, :]
+    for copy in copies:
+        copy.wait()
+
+    @pl.when(me == 1)
+    def _():
+        plan_tokens(n, img, lot, page_cap, small, *plan, starts)
 
 
 def put_page(out, page_cap, slot, rows):
@@ -219,17 +235,18 @@
 
 
 def text_kernel(n, img, lot, load, step, page_cap, *refs):
-    (near_far, far, gain, w_key_far, w_value_far), small_far, refs = refs[:5], refs[5:10], refs[10:]
-    (out, bias, base, info, slots), (near, w_key, w_value, total, starts, sems), small = refs[:5], refs[5:11], refs[11:]
+    (near_far, far, gain, w_key_far, w_value_far), lists, early, refs = refs[:5], refs[5:10], refs[10:13], refs[13:]
+    (out, base, info, slots, bias), (near, w_key, w_value, total, starts, sems, list_sems), small = (
+        refs[:5],
+        refs[5:12],
+        refs[12:],
+    )
     half = near.shape[1]
     kvw = w_key.shape[1]
     me = lax.axis_index("tensor")
     first = pltpu.make_async_copy(near_far, near, sems.at[0])
     first.start()
-    used = sems.shape[0] - len(small)
-    lists = [pltpu.make_async_copy(a, b, sems.at[used + i]) for i, (a, b) in enumerate(zip(small_far, small))]
-    for copy in lists:
-        copy.start()
+    copies = start_lists(lists, small, list_sems)
     loads = []
     for side in (me, 1 - me):
         for c in range(0, half, load):
@@ -243,9 +260,20 @@
                 copy.start()
             loads.append(pair)
     sums = squares_of(far)
-    for copy in lists:
+    for copy in copies:
         copy.wait()
-    plan_tokens(n, img, lot, page_cap, small, info, slots, bias, starts)
+
+    @pl.when(me == 0)
+    def _():
+        plan_tokens(n, img, lot, page_cap, small, info, slots, bias, starts)
+
+    @pl.when(me == 1)
+    def _():
+        info[...] = early[0][...]
+        bias[...] = early[2][...]
+        for g in range(slots.shape[0]):
+            slots[g] = early[1][g]
+
     first.wait()
     sums = jnp.sum(squares_of(near) + sums, axis=1, keepdims=True)
     scale = lax.rsqrt(sums / (2.0 * half) + EPS)
@@ -478,16 +506,26 @@
 
     left = 2 * half - kept
     sizes = [half - kept, *[load] * (half // load - 1), *[load // 2] * 2]
-    packed = call(
-        lambda *refs: vis_kernel(n, lot, sizes, step, *refs),
-        pltpu.VMEM((n, q_lots + lot, 2 * kvw), BF16),
-        [VM] * 6 + [ANY] * 2 + [VM],
-        VM,
+    lists = (img_route.T, page_dest.T, page_count, tail_len, dec_req)
+    held_lists = [(pltpu.VMEM if i == 0 else pltpu.SMEM)(a.shape, a.dtype) for i, a in enumerate(lists)]
+    plan_shapes = (
+        jax.ShapeDtypeStruct((STAT, n * lot), I32),
+        jax.ShapeDtypeStruct((blocks,), I32),
+        jax.ShapeDtypeStruct((tok, n * q_rows // kv_heads), F32),
+    )
+    packed, *early = call(
+        lambda *refs: vis_kernel(n, lot, page_cap, sizes, step, *refs),
+        (pltpu.VMEM((n, q_lots + lot, 2 * kvw), BF16), *plan_shapes),
+        [VM] * 6 + [ANY] * 2 + [VM] + [ANY] * len(lists),
+        (VM, VM, SM, VM),
         [
             pltpu.VMEM((left, kvw), BF16),
             pltpu.VMEM((left, kvw), BF16),
             pltpu.VMEM((img, 2 * kvw), F32),
+            pltpu.SMEM((n,), I32),
             pltpu.SemaphoreType.DMA((2 * len(sizes),)),
+            pltpu.SemaphoreType.DMA((len(lists),)),
+            *held_lists,
         ],
         flops=64 * img * 2 * half * 2 * kvw,
         traffic=2 * img * 2 * half + 8 * half * kvw,
@@ -501,35 +539,42 @@
         remote(w_key),
         remote(w_value),
         info,
+        *[remote(a) for a in lists],
     )
     arrived = exchange(packed, section_of)
 
     block = page_cap * PAGE * 2 * kv_heads + q_rows + PAGE
-    lists = (img_route.T, page_dest.T, page_count, tail_len, dec_req)
-    kv_text, bias, base, info, slots = call(
+    kv_text, base, info, slots, bias = call(
         lambda *refs: text_kernel(n, img, lot, load, step, page_cap, *refs),
         (
             jax.ShapeDtypeStruct((tok, 2 * kvw), BF16),
-            jax.ShapeDtypeStruct((tok, n * q_rows // kv_heads), F32),
             jax.ShapeDtypeStruct((n, block - q_rows - PAGE, HD), BF16),
-            jax.ShapeDtypeStruct((STAT, n * lot), I32),
-            jax.ShapeDtypeStruct((blocks,), I32),
+            *plan_shapes,
         ),
-        [ANY, VM, VM] + [ANY] * 7,
-        (VM, VM, VM, VM, SM),
+        [ANY, VM, VM] + [ANY] * 7 + [VM, SM, VM],
+        (VM, VM, VM, SM, VM),
         [
             pltpu.VMEM((tok, half), BF16),
             pltpu.VMEM(w_key.shape, BF16),
             pltpu.VMEM(w_value.shape, BF16),
             pltpu.VMEM((tok, 2 * kvw), F32),
             pltpu.SMEM((n,), I32),
-            pltpu.SemaphoreType.DMA((1 + 4 * half // load + len(lists),)),
-            *[(pltpu.VMEM if i == 0 else pltpu.SMEM)(a.shape, a.dtype) for i, a in enumerate(lists)],
+            pltpu.SemaphoreType.DMA((1 + 4 * half // load,)),
+            pltpu.SemaphoreType.DMA((len(lists),)),
+            *held_lists,
         ],
         limit=24,
         flops=2 * tok * 2 * half * 2 * kvw,
         traffic=2 * tok * 2 * half + 8 * half * kvw,
-    )(remote(text_rows), text_far, remote(gain), remote(w_key), remote(w_value), *[remote(a) for a in lists])
+    )(
+        remote(text_rows),
+        text_far,
+        remote(gain),
+        remote(w_key),
+        remote(w_value),
+        *[remote(a) for a in lists],
+        *early,
+    )
 
     sent, own = call(
         lambda *refs: attend_kernel(n, cap, lot, page_cap, kv_heads, *refs),

time: 38.1 us -> 39.4 us (1.034)
  waiting for transfers between devices: 7.45 us -> 8.24 us
  Pallas kernels: 16.4 us -> 16.9 us
    all_to_all x2, waiting for transfers between devices: 7.45 us -> 8.24 us  [exchange(): lax.all_to_all(array, 'section', split_axis=0, concat_axis=0, tiled=True,...]
    pallas_call x1, Pallas kernels: 3.93 us -> 4.44 us  [body(): call(lambda *refs: vis_kernel(n, lot, page_cap, sizes, step, *refs), (plt...]
where the time goes in v20:
time: 39.4 us; the launch traced here: 39 us
  Pallas kernels  16.9 us (43%)
  starting transfers between devices  13.1 us (33%)
  waiting for transfers between devices  8.24 us (21%)
  between operations  0.68 us (2%)
    all_to_all x2, starting transfers between devices, exchange(): lax.all_to_all(array, 'section', split_axis=0, concat_axis=0, tiled=True,...  12.6 us
    all_to_all x2, waiting for transfers between devices, exchange(): lax.all_to_all(array, 'section', split_axis=0, concat_axis=0, tiled=True,...  8.24 us
    pallas_call x1, Pallas kernels, body(): call(lambda *refs: text_kernel(n, img, lot, load, step, page_cap, *refs),...  6.26 us
    pallas_call x1, Pallas kernels, body(): call(lambda *refs: vis_kernel(n, lot, page_cap, sizes, step, *refs), (plt...  4.44 us
    pallas_call x1, Pallas kernels, body(): call(lambda *refs: prepare_kernel(n, lot, *refs), (jax.ShapeDtypeStruct((...  2.06 us
    pallas_call x1, Pallas kernels, body(): call(lambda *refs: attend_kernel(n, cap, lot, page_cap, kv_heads, *refs),...  1.92 us
    pallas_call x1, Pallas kernels, body(): call(lambda *refs: fresh_kernel(n, kv_heads, steps, *refs), jax.ShapeDtyp...  1.3 us
    pallas_call x1, Pallas kernels, body(): call(lambda *refs: finish_kernel(kv_heads, steps, page_cap, *refs), (jax....  0.93 us
  transfers between devices with their start and end apart: 4, of which 2 were waited for; matrix products, arithmetic and copies ran while one was open for 0% of the time, Pallas kernels for 36%

profile of v20, /device:TPU:0, one launch (start us, length us, event | category | flops | bytes accessed | tf_op | source)
XLA Modules:
  0.0 39.0 jit_solution(14601042149596230102)
XLA Ops:
  0.6 0.5 %collective-permute-start.1 = (bf16[64,4096]{1,0:T(8,128)(2,1)}, bf16[64,4096]{1,0:T(8,128)(2,1)S(1)}, u32[]{:S(2)}, u32[]{:S(2)}) collective-permute-start(bf16[64,4096]{1,0:T(8,128)(2,1)} %refs_3_.2), channel_id=1, source_target_pairs={{0,1},{1,0},{2,3},{3,2},{4,5},{5,4},{6,7},{7,6},{8,9},{9,8},{10,11... | collective-permute-start | bytes 1572872 | tf_op jit(solution)/shard_map/ppermute | solution.py:469
  1.1 0.1 collective-permute-start
  1.2 2.1 %shard_map.148 = (s32[8,64]{1,0:T(8,128)S(1)}, bf16[3072,256]{1,0:T(8,128)(2,1)S(1)}, bf16[3072,256]{1,0:T(8,128)(2,1)S(1)}, bf16[64,4096]{1,0:T(8,128)(2,1)S(1)...) custom-call(s32[1,512]{1,0:T(1,128)} %bitcast.16, bf16[8192,256]{1,0:T(8,128)(2,1)} %refs_3_.3, ...), custom_call_target="tpu_custom_call" | custom-call | flops 1048576 | bytes 16777216 | tf_op jit(solution)/shard_map/pallas_call | solution.py:492
  3.3 0.0 collective-permute-done.1.refs_1_
  3.3 4.4 %shard_map.149 = (bf16[8,32,512]{2,1,0:T(8,128)(2,1)}, s32[8,128]{1,0:T(8,128)S(1)}, s32[16]{0:T(128)S(1)}, f32[256,256]{1,0:T(8,128)S(1)}) custom-call(bf16[64,4096]{1,0:T(8,128)(2,1)S(1)} %get-tuple-element.23.refs_0_, bf16[64,4096]{1,0:T(8,128)(2,1)S(1)} %collective-permute-done.1.refs_1_, f32[1,8192]{1,0:T(1,128)S(1)} %get-tuple-element.24.refs_2_, ...), custom_call_target="tpu_custom_call" | custom-call | flops 17179869184 | bytes 9437184 | tf_op jit(solution)/shard_map/pallas_call | solution.py:516
  7.7 7.8 %all-to-all-start = ((bf16[8,32,512]{2,1,0:T(8,128)(2,1)}), bf16[8,32,512]{2,1,0:T(8,128)(2,1)S(1)}, u32[]{:S(2)}, u32[]{:S(2)}) async-start(bf16[8,32,512]{2,1,0:T(8,128)(2,1)} %get-tuple-element.35), calls=%async_computation | async-start | bytes 524288 | tf_op jit(solution)/shard_map/all_to_all | solution.py:473
  15.6 0.0 collective-permute-done.refs_1_
  15.6 6.3 %shard_map.150 = (bf16[256,512]{1,0:T(8,128)(2,1)S(1)}, bf16[8,128,128]{2,1,0:T(8,128)(2,1)S(1)}, s32[8,128]{1,0:T(8,128)S(1)}, s32[16]{0:T(128)S(1)}, f32[256,256]{1,0:T(8,128)S(1)}) custom-call(bf16[256,4096]{1,0:T(8,128)(2,1)} %refs_0_.1, bf16[256,4096]{1,0:T(8,128)(2,1)S(1)} %collective-permute-done.refs_1_, f32[1,8192]{1,0:T(1,128)} %bitcast.13, ...), custom_call_target="tpu_custom_call" | custom-call | flops 2147483648 | bytes 12582912 | tf_op jit(solution)/shard_map/pallas_call | solution.py:547
  21.8 1.5 %all-to-all-done.refs_3_ = bf16[8,32,512]{2,1,0:T(8,128)(2,1)S(1)} async-done(((bf16[8,32,512]{2,1,0:T(8,128)(2,1)}), bf16[8,32,512]{2,1,0:T(8,128)(2,1)S(1)}, u32[]{:S(2)}, u32[]{:S(2)}) %all-to-all-start) | async-done | bytes 262176 | tf_op jit(solution)/shard_map/all_to_all | solution.py:473
  23.3 1.9 %shard_map.151 = (bf16[8,208,128]{2,1,0:T(8,128)(2,1)}, f32[72,128]{1,0:T(8,128)S(1)}) custom-call(s32[16]{0:T(128)S(1)} %get-tuple-element.32.refs_0_, s32[8,128]{1,0:T(8,128)S(1)} %get-tuple-element.33.refs_1_, bf16[256,512]{1,0:T(8,128)(2,1)S(1)} %get-tuple-element.34.refs_2_, bf16[8,32,512]{2,1,0:T(8,128)(2,1)S(1)} %all-to-all-done.refs_3_, ...), custom_call_target="tpu_custom_call" | custom-call | flops 67108864 | bytes 294912 | tf_op jit(solution)/shard_map/pallas_call | solution.py:579
  25.3 4.7 %all-to-all-start.1 = ((bf16[8,208,128]{2,1,0:T(8,128)(2,1)}), bf16[8,208,128]{2,1,0:T(8,128)(2,1)S(1)}, u32[]{:S(2)}, u32[]{:S(2)}) async-start(bf16[8,208,128]{2,1,0:T(8,128)(2,1)} %get-tuple-element.38), calls=%async_computation.1 | async-start | bytes 851968 | tf_op jit(solution)/shard_map/all_to_all | solution.py:473
  30.0 1.3 %shard_map.152.refs_1_ = f32[72,128]{1,0:T(8,128)S(1)} custom-call(bf16[64,128]{1,0:T(8,128)(2,1)} %bitcast.15, bf16[4,256]{1,0:T(4,128)(2,1)} %bitcast.19, bf16[4,256]{1,0:T(4,128)(2,1)} %bitcast.20, f32[72,128]{1,0:T(8,128)S(1)} %get-tuple-element.39.refs_3_), custom_call_target="tpu_custom_call" | custom-call | flops 1048576 | bytes 262144 | tf_op jit(solution)/shard_map/pallas_call | solution.py:599
  31.3 6.7 %all-to-all-done.1.refs_0_ = bf16[8,208,128]{2,1,0:T(8,128)(2,1)S(1)} async-done(((bf16[8,208,128]{2,1,0:T(8,128)(2,1)}), bf16[8,208,128]{2,1,0:T(8,128)(2,1)S(1)}, u32[]{:S(2)}, u32[]{:S(2)}) %all-to-all-start.1) | async-done | bytes 426016 | tf_op jit(solution)/shard_map/all_to_all | solution.py:473
  38.0 0.9 %shard_map.153 = (bf16[1,4,2048]{2,1,0:T(4,128)(2,1)}, bf16[8,32,256]{2,1,0:T(8,128)(2,1)}, bf16[8,32,256]{2,1,0:T(8,128)(2,1)}) custom-call(bf16[8,208,128]{2,1,0:T(8,128)(2,1)S(1)} %all-to-all-done.1.refs_0_, f32[72,128]{1,0:T(8,128)S(1)} %shard_map.152.refs_1_), custom_call_target="tpu_custom_call" | custom-call | bytes 524288 | tf_op jit(solution)/shard_map/pallas_call | solution.py:609
Async XLA Ops:
  0.6 2.7 %collective-permute-start.1 = (bf16[64,4096]{1,0:T(8,128)(2,1)}, bf16[64,4096]{1,0:T(8,128)(2,1)S(1)}, u32[]{:S(2)}, u32[]{:S(2)}) collective-permute-start(bf16[64,4096]{1,0:T(8,128)(2,1)} %refs_3_.2), channel_id=1, source_target_pairs={{0,1},{1,0},{2,3},{3,2},{4,5},{5,4},{6,7},{7,6},{8,9},{9,8},{10,11... | collective-permute-start | bytes 1572872 | tf_op jit(solution)/shard_map/ppermute | solution.py:469
  1.1 14.4 %collective-permute-start = (bf16[256,4096]{1,0:T(8,128)(2,1)}, bf16[256,4096]{1,0:T(8,128)(2,1)S(1)}, u32[]{:S(2)}, u32[]{:S(2)}) collective-permute-start(bf16[256,4096]{1,0:T(8,128)(2,1)} %refs_0_.1), channel_id=1, source_target_pairs={{0,1},{1,0},{2,3},{3,2},{4,5},{5,4},{6,7},{7,6},{8,9},{9,8},{10,11... | collective-permute-start | bytes 6291464 | tf_op jit(solution)/shard_map/ppermute | solution.py:469
  7.7 15.6 %all-to-all-start = ((bf16[8,32,512]{2,1,0:T(8,128)(2,1)}), bf16[8,32,512]{2,1,0:T(8,128)(2,1)S(1)}, u32[]{:S(2)}, u32[]{:S(2)}) async-start(bf16[8,32,512]{2,1,0:T(8,128)(2,1)} %get-tuple-element.35), calls=%async_computation | async-start | bytes 524288 | tf_op jit(solution)/shard_map/all_to_all | solution.py:473
  25.3 12.8 %all-to-all-start.1 = ((bf16[8,208,128]{2,1,0:T(8,128)(2,1)}), bf16[8,208,128]{2,1,0:T(8,128)(2,1)S(1)}, u32[]{:S(2)}, u32[]{:S(2)}) async-start(bf16[8,208,128]{2,1,0:T(8,128)(2,1)} %get-tuple-element.38), calls=%async_computation.1 | async-start | bytes 851968 | tf_op jit(solution)/shard_map/all_to_all | solution.py:473

commit v21 on v19

--- a/solution.py
+++ b/solution.py
@@ -117,7 +117,7 @@
         c.wait()
 
 
-def plan_tokens(n, img, lot, page_cap, small, info, slots, bias, starts):
+def plan_tokens(n, img, lot, page_cap, small, hot, covered, slots, bias, starts):
     route, pages, count, tail, req = small
     pos = lax.axis_index("section")
     tok, width = bias.shape
@@ -131,7 +131,10 @@
         arriving = jnp.sum(here, axis=1, keepdims=True)
         fits = fits + jnp.where(source == e, arriving, 0)
         offset = offset + jnp.where(source > e, arriving, 0)
-    info[...] = jnp.broadcast_to(jnp.where(inner < fits, offset + inner, -1), info.shape)
+    target = jnp.where(inner < fits, offset + inner, -1)
+    chosen = jnp.where(lax.broadcasted_iota(I32, hot.shape, 0) == target, 1.0, 0.0)
+    hot[...] = chosen.astype(BF16)
+    covered[...] = jnp.broadcast_to(jnp.sum(chosen, axis=1, keepdims=True), covered.shape)
     total = jnp.int32(0)
     for r in range(n):
         starts[r] = total
@@ -191,16 +194,18 @@
             copy.start()
         at += size
     scale = scale_of(near, far)
-    for at in range(0, 2 * half, step):
+    points = [*range(0, 2 * half - step, step), *range(2 * half - step, 2 * half, sizes[-1])]
+    for at, end in zip(points, [*points[1:], 2 * half]):
         for copy in loads.get(at, ()):
             copy.wait()
         rows, side = (near, me) if at < half else (far, 1 - me)
         weights, w_at = ((key_held, value_held), at) if at < held else ((key_rest, value_rest), at - held)
         c = at % half
-        columns = pl.ds(pl.multiple_of(side * half + c, step), step)
-        normed = normed_rows(rows, c, step, scale, gain[:, columns])
+        size = end - at
+        columns = pl.ds(pl.multiple_of(side * half + c, size), size)
+        normed = normed_rows(rows, c, size, scale, gain[:, columns])
         for w, col in zip(weights, (0, kvw)):
-            add_part(total, col, normed, w[w_at : w_at + step, :], at == 0)
+            add_part(total, col, normed, w[w_at : w_at + size, :], at == 0)
     slot = lax.broadcasted_iota(I32, (n * lot, img), 0)
     chosen = jnp.where(slot == info[0:1, :img], 1.0, 0.0).astype(BF16)
     packed = dot(chosen, total[...].astype(BF16)).astype(BF16)
@@ -220,7 +225,11 @@
 
 def text_kernel(n, img, lot, load, step, page_cap, *refs):
     (near_far, far, gain, w_key_far, w_value_far), small_far, refs = refs[:5], refs[5:10], refs[10:]
-    (out, bias, base, info, slots), (near, w_key, w_value, total, starts, sems), small = refs[:5], refs[5:11], refs[11:]
+    (out, bias, base, hot, covered, slots), (near, w_key, w_value, total, starts, sems), small = (
+        refs[:6],
+        refs[6:12],
+        refs[12:],
+    )
     half = near.shape[1]
     kvw = w_key.shape[1]
     me = lax.axis_index("tensor")
@@ -245,7 +254,7 @@
     sums = squares_of(far)
     for copy in lists:
         copy.wait()
-    plan_tokens(n, img, lot, page_cap, small, info, slots, bias, starts)
+    plan_tokens(n, img, lot, page_cap, small, hot, covered, slots, bias, starts)
     first.wait()
     sums = jnp.sum(squares_of(near) + sums, axis=1, keepdims=True)
     scale = lax.rsqrt(sums / (2.0 * half) + EPS)
@@ -266,7 +275,7 @@
         put_page(base, page_cap, slots[g], out[g * PAGE : (g + 1) * PAGE, :])
 
 
-def attend_kernel(n, cap, lot, page_cap, kv_heads, slots, info, kv_text, arrived, bias, base, sent, own, *scratch):
+def attend_kernel(n, cap, lot, page_cap, kv_heads, slots, hot, covered, kv_text, arrived, bias, base, sent, own, *scratch):
     out, mixed, held, rows_held, sems = scratch
     order = [page_section_of(k, n) for k in range(n)]
     rank = rank_of(lax.axis_index("section"), n)
@@ -274,12 +283,9 @@
     kvw = kv_heads * HD
     q_lots = arrived.shape[1] - lot
     reach = min(tok, n * cap)
-    hit = lax.broadcasted_iota(I32, (reach, n * lot), 0) == info[0:1, :]
-    hot = jnp.where(hit, 1.0, 0.0)
-    covered = jnp.sum(hot, axis=1, keepdims=True) > 0.0
     incoming = jnp.concatenate([arrived[k, q_lots:, :] for k in range(n)], axis=0)
-    placed = dot(hot.astype(BF16), incoming)
-    mixed[...] = jnp.where(covered, placed, kv_text[:reach, :].astype(F32)).astype(BF16)
+    placed = dot(hot[...], incoming)
+    mixed[...] = jnp.where(covered[:, :1] > 0.0, placed, kv_text[:reach, :].astype(F32)).astype(BF16)
     groups = arrived.shape[2] // HD // kv_heads
     rows = groups * q_lots
     pages = base.shape[1]
@@ -459,6 +465,7 @@
     gain = norm_gain.reshape(1, 2 * half)
     load = min(2048, half)
     step = min(1024, load // 2)
+    fine = step // 2
     kept = load + load // 2
     arguments = (img_route.T, w_key, w_value, vis_rows, gain, query)
     info, key_held, value_held, vis_near, gain_near, query_near = call(
@@ -477,7 +484,7 @@
     )(*[remote(a) for a in arguments])
 
     left = 2 * half - kept
-    sizes = [half - kept, *[load] * (half // load - 1), *[load // 2] * 2]
+    sizes = [half - kept, *[load] * (half // load - 1), load // 2, fine, fine]
     packed = call(
         lambda *refs: vis_kernel(n, lot, sizes, step, *refs),
         pltpu.VMEM((n, q_lots + lot, 2 * kvw), BF16),
@@ -506,17 +513,19 @@
 
     block = page_cap * PAGE * 2 * kv_heads + q_rows + PAGE
     lists = (img_route.T, page_dest.T, page_count, tail_len, dec_req)
-    kv_text, bias, base, info, slots = call(
+    reach = min(tok, n * cap)
+    kv_text, bias, base, hot, covered, slots = call(
         lambda *refs: text_kernel(n, img, lot, load, step, page_cap, *refs),
         (
             jax.ShapeDtypeStruct((tok, 2 * kvw), BF16),
             jax.ShapeDtypeStruct((tok, n * q_rows // kv_heads), F32),
             jax.ShapeDtypeStruct((n, block - q_rows - PAGE, HD), BF16),
-            jax.ShapeDtypeStruct((STAT, n * lot), I32),
+            jax.ShapeDtypeStruct((reach, n * lot), BF16),
+            jax.ShapeDtypeStruct((reach, HD), F32),
             jax.ShapeDtypeStruct((blocks,), I32),
         ),
         [ANY, VM, VM] + [ANY] * 7,
-        (VM, VM, VM, VM, SM),
+        (VM, VM, VM, VM, VM, SM),
         [
             pltpu.VMEM((tok, half), BF16),
             pltpu.VMEM(w_key.shape, BF16),
@@ -537,7 +546,7 @@
             jax.ShapeDtypeStruct((n, block, HD), BF16),
             jax.ShapeDtypeStruct((q_rows + STAT, HD), F32),
         ),
-        [SM] + [VM] * 5,
+        [SM] + [VM] * 6,
         (ANY, VM),
         [
             pltpu.VMEM((n, block, HD), BF16),
@@ -548,7 +557,7 @@
         ],
         flops=4 * n * q_rows * tok * HD,
         traffic=n * (q_rows + STAT) * HD * 4,
-    )(slots, info, kv_text, arrived, bias, base)
+    )(slots, hot, covered, kv_text, arrived, bias, base)
     shares = exchange(sent, page_section_of)
 
     mine = call(

time: 38.1 us -> 38.2 us (level)
  no operation moved by 1% of the time
where the time goes in v21:
time: 38.2 us; the launch traced here: 37.7 us
  Pallas kernels  16.4 us (43%)
  starting transfers between devices  13.2 us (35%)
  waiting for transfers between devices  7.45 us (20%)
  between operations  0.68 us (2%)
    all_to_all x2, starting transfers between devices, exchange(): lax.all_to_all(array, 'section', split_axis=0, concat_axis=0, tiled=True,...  12.6 us
    all_to_all x2, waiting for transfers between devices, exchange(): lax.all_to_all(array, 'section', split_axis=0, concat_axis=0, tiled=True,...  7.44 us
    pallas_call x1, Pallas kernels, body(): call(lambda *refs: text_kernel(n, img, lot, load, step, page_cap, *refs),...  6.27 us
    pallas_call x1, Pallas kernels, body(): call(lambda *refs: vis_kernel(n, lot, sizes, step, *refs), pltpu.VMEM((n,...  3.95 us
    pallas_call x1, Pallas kernels, body(): call(lambda *refs: prepare_kernel(n, lot, *refs), (jax.ShapeDtypeStruct((...  2.06 us
    pallas_call x1, Pallas kernels, body(): call(lambda *refs: attend_kernel(n, cap, lot, page_cap, kv_heads, *refs),...  1.91 us
    pallas_call x1, Pallas kernels, body(): call(lambda *refs: fresh_kernel(n, kv_heads, steps, *refs), jax.ShapeDtyp...  1.3 us
    pallas_call x1, Pallas kernels, body(): call(lambda *refs: finish_kernel(kv_heads, steps, page_cap, *refs), (jax....  0.93 us
  transfers between devices with their start and end apart: 4, of which 2 were waited for; matrix products, arithmetic and copies ran while one was open for 0% of the time, Pallas kernels for 36%

profile of v21, /device:TPU:0, one launch (start us, length us, event | category | flops | bytes accessed | tf_op | source)
XLA Modules:
  0.0 37.7 jit_solution(8580974375045978778)
XLA Ops:
  0.6 0.5 %collective-permute-start.1 = (bf16[64,4096]{1,0:T(8,128)(2,1)}, bf16[64,4096]{1,0:T(8,128)(2,1)S(1)}, u32[]{:S(2)}, u32[]{:S(2)}) collective-permute-start(bf16[64,4096]{1,0:T(8,128)(2,1)} %refs_3_.3), channel_id=1, source_target_pairs={{0,1},{1,0},{2,3},{3,2},{4,5},{5,4},{6,7},{7,6},{8,9},{9,8},{10,11... | collective-permute-start | bytes 1572872 | tf_op jit(solution)/shard_map/ppermute | solution.py:447
  1.1 0.1 collective-permute-start
  1.2 2.1 %shard_map.149 = (s32[8,64]{1,0:T(8,128)S(1)}, bf16[3072,256]{1,0:T(8,128)(2,1)S(1)}, bf16[3072,256]{1,0:T(8,128)(2,1)S(1)}, bf16[64,4096]{1,0:T(8,128)(2,1)S(1)...) custom-call(s32[1,512]{1,0:T(1,128)} %bitcast.16, bf16[8192,256]{1,0:T(8,128)(2,1)} %refs_6_.1, ...), custom_call_target="tpu_custom_call" | custom-call | flops 1048576 | bytes 16777216 | tf_op jit(solution)/shard_map/pallas_call | solution.py:471
  3.3 0.0 collective-permute-done.1.refs_1_
  3.3 3.9 %shard_map.150 = bf16[8,32,512]{2,1,0:T(8,128)(2,1)} custom-call(bf16[64,4096]{1,0:T(8,128)(2,1)S(1)} %get-tuple-element.24.refs_0_, bf16[64,4096]{1,0:T(8,128)(2,1)S(1)} %collective-permute-done.1.refs_1_, f32[1,8192]{1,0:T(1,128)S(1)} %get-tuple-element.25.refs_2_, bf16[64,128]{1,0:T(8,128)(2,1)S(1)} %get-tuple-element.26.refs_3_, ...), custom_call_target="tpu_custom_call" | custom-call | flops 17179869184 | bytes 9437184 | tf_op jit(solution)/shard_map/pallas_call | solution.py:488
  7.3 7.8 %all-to-all-start = ((bf16[8,32,512]{2,1,0:T(8,128)(2,1)}), bf16[8,32,512]{2,1,0:T(8,128)(2,1)S(1)}, u32[]{:S(2)}, u32[]{:S(2)}) async-start(bf16[8,32,512]{2,1,0:T(8,128)(2,1)} %shard_map.150), calls=%async_computation | async-start | bytes 524288 | tf_op jit(solution)/shard_map/all_to_all | solution.py:451
  15.1 0.0 collective-permute-done.refs_1_
  15.1 6.3 %shard_map.148 = (bf16[256,512]{1,0:T(8,128)(2,1)S(1)}, f32[256,256]{1,0:T(8,128)S(1)}, bf16[8,128,128]{2,1,0:T(8,128)(2,1)S(1)}, bf16[128,128]{1,0:T(8,128)(2,1...) custom-call(bf16[256,4096]{1,0:T(8,128)(2,1)} %refs_0_.1, bf16[256,4096]{1,0:T(8,128)(2,1)S(1)} %collective-permute-done.refs_1_, ...), custom_call_target="tpu_custom_call" | custom-call | flops 2147483648 | bytes 12582912 | tf_op jit(solution)/shard_map/pallas_call | solution.py:517
  21.4 1.1 %all-to-all-done.refs_4_ = bf16[8,32,512]{2,1,0:T(8,128)(2,1)S(1)} async-done(((bf16[8,32,512]{2,1,0:T(8,128)(2,1)}), bf16[8,32,512]{2,1,0:T(8,128)(2,1)S(1)}, u32[]{:S(2)}, u32[]{:S(2)}) %all-to-all-start) | async-done | bytes 262176 | tf_op jit(solution)/shard_map/all_to_all | solution.py:451
  22.5 1.9 %shard_map.151 = (bf16[8,208,128]{2,1,0:T(8,128)(2,1)}, f32[72,128]{1,0:T(8,128)S(1)}) custom-call(s32[16]{0:T(128)S(1)} %get-tuple-element.20.refs_0_, bf16[128,128]{1,0:T(8,128)(2,1)S(1)} %get-tuple-element.21.refs_1_, f32[128,128]{1,0:T(8,128)S(1)} %get-tuple-element.22.refs_2_, bf16[256,512]{1,0:T(8,128)(2,1)S(1)} %get-tuple-element.23.refs_3_, ...), custom_call_target="tpu_custom_call" | custom-call | flops 67108864 | bytes 294912 | tf_op jit(solution)/shard_map/pallas_call | solution.py:543
  24.4 4.8 %all-to-all-start.1 = ((bf16[8,208,128]{2,1,0:T(8,128)(2,1)}), bf16[8,208,128]{2,1,0:T(8,128)(2,1)S(1)}, u32[]{:S(2)}, u32[]{:S(2)}) async-start(bf16[8,208,128]{2,1,0:T(8,128)(2,1)} %get-tuple-element.32), calls=%async_computation.1 | async-start | bytes 851968 | tf_op jit(solution)/shard_map/all_to_all | solution.py:451
  29.1 1.3 %shard_map.152.refs_1_ = f32[72,128]{1,0:T(8,128)S(1)} custom-call(bf16[64,128]{1,0:T(8,128)(2,1)} %bitcast.15, bf16[4,256]{1,0:T(4,128)(2,1)} %bitcast.18, bf16[4,256]{1,0:T(4,128)(2,1)} %bitcast.19, f32[72,128]{1,0:T(8,128)S(1)} %get-tuple-element.33.refs_3_), custom_call_target="tpu_custom_call" | custom-call | flops 1048576 | bytes 262144 | tf_op jit(solution)/shard_map/pallas_call | solution.py:563
  30.5 6.3 %all-to-all-done.1.refs_0_ = bf16[8,208,128]{2,1,0:T(8,128)(2,1)S(1)} async-done(((bf16[8,208,128]{2,1,0:T(8,128)(2,1)}), bf16[8,208,128]{2,1,0:T(8,128)(2,1)S(1)}, u32[]{:S(2)}, u32[]{:S(2)}) %all-to-all-start.1) | async-done | bytes 426016 | tf_op jit(solution)/shard_map/all_to_all | solution.py:451
  36.8 0.9 %shard_map.153 = (bf16[1,4,2048]{2,1,0:T(4,128)(2,1)}, bf16[8,32,256]{2,1,0:T(8,128)(2,1)}, bf16[8,32,256]{2,1,0:T(8,128)(2,1)}) custom-call(bf16[8,208,128]{2,1,0:T(8,128)(2,1)S(1)} %all-to-all-done.1.refs_0_, f32[72,128]{1,0:T(8,128)S(1)} %shard_map.152.refs_1_), custom_call_target="tpu_custom_call" | custom-call | bytes 524288 | tf_op jit(solution)/shard_map/pallas_call | solution.py:573
Async XLA Ops:
  0.6 2.7 %collective-permute-start.1 = (bf16[64,4096]{1,0:T(8,128)(2,1)}, bf16[64,4096]{1,0:T(8,128)(2,1)S(1)}, u32[]{:S(2)}, u32[]{:S(2)}) collective-permute-start(bf16[64,4096]{1,0:T(8,128)(2,1)} %refs_3_.3), channel_id=1, source_target_pairs={{0,1},{1,0},{2,3},{3,2},{4,5},{5,4},{6,7},{7,6},{8,9},{9,8},{10,11... | collective-permute-start | bytes 1572872 | tf_op jit(solution)/shard_map/ppermute | solution.py:447
  1.1 13.9 %collective-permute-start = (bf16[256,4096]{1,0:T(8,128)(2,1)}, bf16[256,4096]{1,0:T(8,128)(2,1)S(1)}, u32[]{:S(2)}, u32[]{:S(2)}) collective-permute-start(bf16[256,4096]{1,0:T(8,128)(2,1)} %refs_0_.1), channel_id=1, source_target_pairs={{0,1},{1,0},{2,3},{3,2},{4,5},{5,4},{6,7},{7,6},{8,9},{9,8},{10,11... | collective-permute-start | bytes 6291464 | tf_op jit(solution)/shard_map/ppermute | solution.py:447
  7.3 15.2 %all-to-all-start = ((bf16[8,32,512]{2,1,0:T(8,128)(2,1)}), bf16[8,32,512]{2,1,0:T(8,128)(2,1)S(1)}, u32[]{:S(2)}, u32[]{:S(2)}) async-start(bf16[8,32,512]{2,1,0:T(8,128)(2,1)} %shard_map.150), calls=%async_computation | async-start | bytes 524288 | tf_op jit(solution)/shard_map/all_to_all | solution.py:451
  24.4 12.4 %all-to-all-start.1 = ((bf16[8,208,128]{2,1,0:T(8,128)(2,1)}), bf16[8,208,128]{2,1,0:T(8,128)(2,1)S(1)}, u32[]{:S(2)}, u32[]{:S(2)}) async-start(bf16[8,208,128]{2,1,0:T(8,128)(2,1)} %get-tuple-element.32), calls=%async_computation.1 | async-start | bytes 851968 | tf_op jit(solution)/shard_map/all_to_all | solution.py:451

commit v22 on v21

--- a/solution.py
+++ b/solution.py
@@ -233,12 +233,12 @@
     half = near.shape[1]
     kvw = w_key.shape[1]
     me = lax.axis_index("tensor")
-    first = pltpu.make_async_copy(near_far, near, sems.at[0])
-    first.start()
     used = sems.shape[0] - len(small)
     lists = [pltpu.make_async_copy(a, b, sems.at[used + i]) for i, (a, b) in enumerate(zip(small_far, small))]
     for copy in lists:
         copy.start()
+    first = pltpu.make_async_copy(near_far, near, sems.at[0])
+    first.start()
     loads = []
     for side in (me, 1 - me):
         for c in range(0, half, load):
@@ -252,15 +252,16 @@
                 copy.start()
             loads.append(pair)
     sums = squares_of(far)
-    for copy in lists:
-        copy.wait()
-    plan_tokens(n, img, lot, page_cap, small, hot, covered, slots, bias, starts)
     first.wait()
     sums = jnp.sum(squares_of(near) + sums, axis=1, keepdims=True)
     scale = lax.rsqrt(sums / (2.0 * half) + EPS)
     for i, pair in enumerate(loads):
         for copy in pair:
             copy.wait()
+        if i == 1:
+            for copy in lists:
+                copy.wait()
+            plan_tokens(n, img, lot, page_cap, small, hot, covered, slots, bias, starts)
         for at in range(i * load, (i + 1) * load, step):
             rows, side = (near, me) if at < half else (far, 1 - me)
             c = at % half

time: 38.2 us -> 38.3 us (level)
  no operation moved by 1% of the time
where the time goes in v22:
time: 38.3 us; the launch traced here: 37.8 us
  Pallas kernels  16.5 us (43%)
  starting transfers between devices  13.2 us (34%)
  waiting for transfers between devices  7.45 us (19%)
  between operations  0.68 us (2%)
    all_to_all x2, starting transfers between devices, exchange(): lax.all_to_all(array, 'section', split_axis=0, concat_axis=0, tiled=True,...  12.6 us
    all_to_all x2, waiting for transfers between devices, exchange(): lax.all_to_all(array, 'section', split_axis=0, concat_axis=0, tiled=True,...  7.44 us
    pallas_call x1, Pallas kernels, body(): call(lambda *refs: text_kernel(n, img, lot, load, step, page_cap, *refs),...  6.36 us
    pallas_call x1, Pallas kernels, body(): call(lambda *refs: vis_kernel(n, lot, sizes, step, *refs), pltpu.VMEM((n,...  3.95 us
    pallas_call x1, Pallas kernels, body(): call(lambda *refs: prepare_kernel(n, lot, *refs), (jax.ShapeDtypeStruct((...  2.06 us
    pallas_call x1, Pallas kernels, body(): call(lambda *refs: attend_kernel(n, cap, lot, page_cap, kv_heads, *refs),...  1.91 us
    pallas_call x1, Pallas kernels, body(): call(lambda *refs: fresh_kernel(n, kv_heads, steps, *refs), jax.ShapeDtyp...  1.3 us
    pallas_call x1, Pallas kernels, body(): call(lambda *refs: finish_kernel(kv_heads, steps, page_cap, *refs), (jax....  0.93 us
  transfers between devices with their start and end apart: 4, of which 2 were waited for; matrix products, arithmetic and copies ran while one was open for 0% of the time, Pallas kernels for 36%

profile of v22, /device:TPU:0, one launch (start us, length us, event | category | flops | bytes accessed | tf_op | source)
XLA Modules:
  0.0 37.8 jit_solution(7454912629647298810)
XLA Ops:
  0.6 0.5 %collective-permute-start.1 = (bf16[64,4096]{1,0:T(8,128)(2,1)}, bf16[64,4096]{1,0:T(8,128)(2,1)S(1)}, u32[]{:S(2)}, u32[]{:S(2)}) collective-permute-start(bf16[64,4096]{1,0:T(8,128)(2,1)} %refs_3_.3), channel_id=1, source_target_pairs={{0,1},{1,0},{2,3},{3,2},{4,5},{5,4},{6,7},{7,6},{8,9},{9,8},{10,11... | collective-permute-start | bytes 1572872 | tf_op jit(solution)/shard_map/ppermute | solution.py:448
  1.1 0.1 collective-permute-start
  1.2 2.1 %shard_map.149 = (s32[8,64]{1,0:T(8,128)S(1)}, bf16[3072,256]{1,0:T(8,128)(2,1)S(1)}, bf16[3072,256]{1,0:T(8,128)(2,1)S(1)}, bf16[64,4096]{1,0:T(8,128)(2,1)S(1)...) custom-call(s32[1,512]{1,0:T(1,128)} %bitcast.16, bf16[8192,256]{1,0:T(8,128)(2,1)} %refs_6_.1, ...), custom_call_target="tpu_custom_call" | custom-call | flops 1048576 | bytes 16777216 | tf_op jit(solution)/shard_map/pallas_call | solution.py:472
  3.3 0.0 collective-permute-done.1.refs_1_
  3.3 3.9 %shard_map.150 = bf16[8,32,512]{2,1,0:T(8,128)(2,1)} custom-call(bf16[64,4096]{1,0:T(8,128)(2,1)S(1)} %get-tuple-element.24.refs_0_, bf16[64,4096]{1,0:T(8,128)(2,1)S(1)} %collective-permute-done.1.refs_1_, f32[1,8192]{1,0:T(1,128)S(1)} %get-tuple-element.25.refs_2_, bf16[64,128]{1,0:T(8,128)(2,1)S(1)} %get-tuple-element.26.refs_3_, ...), custom_call_target="tpu_custom_call" | custom-call | flops 17179869184 | bytes 9437184 | tf_op jit(solution)/shard_map/pallas_call | solution.py:489
  7.3 7.8 %all-to-all-start = ((bf16[8,32,512]{2,1,0:T(8,128)(2,1)}), bf16[8,32,512]{2,1,0:T(8,128)(2,1)S(1)}, u32[]{:S(2)}, u32[]{:S(2)}) async-start(bf16[8,32,512]{2,1,0:T(8,128)(2,1)} %shard_map.150), calls=%async_computation | async-start | bytes 524288 | tf_op jit(solution)/shard_map/all_to_all | solution.py:452
  15.1 0.0 collective-permute-done.refs_1_
  15.1 6.4 %shard_map.148 = (bf16[256,512]{1,0:T(8,128)(2,1)S(1)}, f32[256,256]{1,0:T(8,128)S(1)}, bf16[8,128,128]{2,1,0:T(8,128)(2,1)S(1)}, bf16[128,128]{1,0:T(8,128)(2,1...) custom-call(bf16[256,4096]{1,0:T(8,128)(2,1)} %refs_0_.1, bf16[256,4096]{1,0:T(8,128)(2,1)S(1)} %collective-permute-done.refs_1_, ...), custom_call_target="tpu_custom_call" | custom-call | flops 2147483648 | bytes 12582912 | tf_op jit(solution)/shard_map/pallas_call | solution.py:518
  21.5 1.0 %all-to-all-done.refs_4_ = bf16[8,32,512]{2,1,0:T(8,128)(2,1)S(1)} async-done(((bf16[8,32,512]{2,1,0:T(8,128)(2,1)}), bf16[8,32,512]{2,1,0:T(8,128)(2,1)S(1)}, u32[]{:S(2)}, u32[]{:S(2)}) %all-to-all-start) | async-done | bytes 262176 | tf_op jit(solution)/shard_map/all_to_all | solution.py:452
  22.5 1.9 %shard_map.151 = (bf16[8,208,128]{2,1,0:T(8,128)(2,1)}, f32[72,128]{1,0:T(8,128)S(1)}) custom-call(s32[16]{0:T(128)S(1)} %get-tuple-element.20.refs_0_, bf16[128,128]{1,0:T(8,128)(2,1)S(1)} %get-tuple-element.21.refs_1_, f32[128,128]{1,0:T(8,128)S(1)} %get-tuple-element.22.refs_2_, bf16[256,512]{1,0:T(8,128)(2,1)S(1)} %get-tuple-element.23.refs_3_, ...), custom_call_target="tpu_custom_call" | custom-call | flops 67108864 | bytes 294912 | tf_op jit(solution)/shard_map/pallas_call | solution.py:544
  24.4 4.8 %all-to-all-start.1 = ((bf16[8,208,128]{2,1,0:T(8,128)(2,1)}), bf16[8,208,128]{2,1,0:T(8,128)(2,1)S(1)}, u32[]{:S(2)}, u32[]{:S(2)}) async-start(bf16[8,208,128]{2,1,0:T(8,128)(2,1)} %get-tuple-element.32), calls=%async_computation.1 | async-start | bytes 851968 | tf_op jit(solution)/shard_map/all_to_all | solution.py:452
  29.1 1.3 %shard_map.152.refs_1_ = f32[72,128]{1,0:T(8,128)S(1)} custom-call(bf16[64,128]{1,0:T(8,128)(2,1)} %bitcast.15, bf16[4,256]{1,0:T(4,128)(2,1)} %bitcast.18, bf16[4,256]{1,0:T(4,128)(2,1)} %bitcast.19, f32[72,128]{1,0:T(8,128)S(1)} %get-tuple-element.33.refs_3_), custom_call_target="tpu_custom_call" | custom-call | flops 1048576 | bytes 262144 | tf_op jit(solution)/shard_map/pallas_call | solution.py:564
  30.5 6.4 %all-to-all-done.1.refs_0_ = bf16[8,208,128]{2,1,0:T(8,128)(2,1)S(1)} async-done(((bf16[8,208,128]{2,1,0:T(8,128)(2,1)}), bf16[8,208,128]{2,1,0:T(8,128)(2,1)S(1)}, u32[]{:S(2)}, u32[]{:S(2)}) %all-to-all-start.1) | async-done | bytes 426016 | tf_op jit(solution)/shard_map/all_to_all | solution.py:452
  36.9 0.9 %shard_map.153 = (bf16[1,4,2048]{2,1,0:T(4,128)(2,1)}, bf16[8,32,256]{2,1,0:T(8,128)(2,1)}, bf16[8,32,256]{2,1,0:T(8,128)(2,1)}) custom-call(bf16[8,208,128]{2,1,0:T(8,128)(2,1)S(1)} %all-to-all-done.1.refs_0_, f32[72,128]{1,0:T(8,128)S(1)} %shard_map.152.refs_1_), custom_call_target="tpu_custom_call" | custom-call | bytes 524288 | tf_op jit(solution)/shard_map/pallas_call | solution.py:574
Async XLA Ops:
  0.6 2.7 %collective-permute-start.1 = (bf16[64,4096]{1,0:T(8,128)(2,1)}, bf16[64,4096]{1,0:T(8,128)(2,1)S(1)}, u32[]{:S(2)}, u32[]{:S(2)}) collective-permute-start(bf16[64,4096]{1,0:T(8,128)(2,1)} %refs_3_.3), channel_id=1, source_target_pairs={{0,1},{1,0},{2,3},{3,2},{4,5},{5,4},{6,7},{7,6},{8,9},{9,8},{10,11... | collective-permute-start | bytes 1572872 | tf_op jit(solution)/shard_map/ppermute | solution.py:448
  1.1 13.9 %collective-permute-start = (bf16[256,4096]{1,0:T(8,128)(2,1)}, bf16[256,4096]{1,0:T(8,128)(2,1)S(1)}, u32[]{:S(2)}, u32[]{:S(2)}) collective-permute-start(bf16[256,4096]{1,0:T(8,128)(2,1)} %refs_0_.1), channel_id=1, source_target_pairs={{0,1},{1,0},{2,3},{3,2},{4,5},{5,4},{6,7},{7,6},{8,9},{9,8},{10,11... | collective-permute-start | bytes 6291464 | tf_op jit(solution)/shard_map/ppermute | solution.py:448
  7.3 15.2 %all-to-all-start = ((bf16[8,32,512]{2,1,0:T(8,128)(2,1)}), bf16[8,32,512]{2,1,0:T(8,128)(2,1)S(1)}, u32[]{:S(2)}, u32[]{:S(2)}) async-start(bf16[8,32,512]{2,1,0:T(8,128)(2,1)} %shard_map.150), calls=%async_computation | async-start | bytes 524288 | tf_op jit(solution)/shard_map/all_to_all | solution.py:452
  24.4 12.5 %all-to-all-start.1 = ((bf16[8,208,128]{2,1,0:T(8,128)(2,1)}), bf16[8,208,128]{2,1,0:T(8,128)(2,1)S(1)}, u32[]{:S(2)}, u32[]{:S(2)}) async-start(bf16[8,208,128]{2,1,0:T(8,128)(2,1)} %get-tuple-element.32), calls=%async_computation.1 | async-start | bytes 851968 | tf_op jit(solution)/shard_map/all_to_all | solution.py:452

commit v23 on v19

--- a/solution.py
+++ b/solution.py
@@ -32,12 +32,17 @@
     )
 
 
+def mirrored(section, n):
+    return n - 2 - section + 2 * (section % 2)
+
+
 def rank_of(section, n):
-    return jnp.where(section < n // 2, n - 2 - 2 * section, 2 * section - n + 1)
+    other = mirrored(section, n)
+    return jnp.where(other < n // 2, n - 2 - 2 * other, 2 * other - n + 1)
 
 
 def section_of(rank, n):
-    return n // 2 - 1 - rank // 2 + rank % 2 * (rank // 2 * 2 + 1)
+    return mirrored(n // 2 - 1 - rank // 2 + rank % 2 * (rank // 2 * 2 + 1), n)
 
 
 def page_rank_of(section, n):

time: 38.1 us -> 38.6 us (1.013)
  starting transfers between devices: 13.2 us -> 14.3 us
  waiting for transfers between devices: 7.45 us -> 6.79 us
    all_to_all x2, starting transfers between devices: 12.6 us -> 13.7 us  [exchange(): lax.all_to_all(array, 'section', split_axis=0, concat_axis=0, tiled=True,...]
    all_to_all x2, waiting for transfers between devices: 7.45 us -> 6.78 us  [exchange(): lax.all_to_all(array, 'section', split_axis=0, concat_axis=0, tiled=True,...]
  transfers between devices with their start and end apart: 4 -> 4, of which waited for: 2 -> 2; matrix products, arithmetic and copies ran while one was open for 0% -> 0% of each run, Pallas kernels for 36% -> 35%
where the time goes in v23:
time: 38.6 us; the launch traced here: 38.2 us
  Pallas kernels  16.4 us (42%)
  starting transfers between devices  14.3 us (37%)
  waiting for transfers between devices  6.79 us (18%)
  between operations  0.68 us (2%)
    all_to_all x2, starting transfers between devices, exchange(): lax.all_to_all(array, 'section', split_axis=0, concat_axis=0, tiled=True,...  13.7 us
    all_to_all x2, waiting for transfers between devices, exchange(): lax.all_to_all(array, 'section', split_axis=0, concat_axis=0, tiled=True,...  6.78 us
    pallas_call x1, Pallas kernels, body(): call(lambda *refs: text_kernel(n, img, lot, load, step, page_cap, *refs),...  6.24 us
    pallas_call x1, Pallas kernels, body(): call(lambda *refs: vis_kernel(n, lot, sizes, step, *refs), pltpu.VMEM((n,...  3.93 us
    pallas_call x1, Pallas kernels, body(): call(lambda *refs: prepare_kernel(n, lot, *refs), (jax.ShapeDtypeStruct((...  2.06 us
    pallas_call x1, Pallas kernels, body(): call(lambda *refs: attend_kernel(n, cap, lot, page_cap, kv_heads, *refs),...  1.91 us
    pallas_call x1, Pallas kernels, body(): call(lambda *refs: fresh_kernel(n, kv_heads, steps, *refs), jax.ShapeDtyp...  1.3 us
    pallas_call x1, Pallas kernels, body(): call(lambda *refs: finish_kernel(kv_heads, steps, page_cap, *refs), (jax....  0.93 us
  transfers between devices with their start and end apart: 4, of which 2 were waited for; matrix products, arithmetic and copies ran while one was open for 0% of the time, Pallas kernels for 35%

profile of v23, /device:TPU:0, one launch (start us, length us, event | category | flops | bytes accessed | tf_op | source)
XLA Modules:
  0.0 38.2 jit_solution(572691279155601315)
XLA Ops:
  0.6 0.5 %collective-permute-start.1 = (bf16[64,4096]{1,0:T(8,128)(2,1)}, bf16[64,4096]{1,0:T(8,128)(2,1)S(1)}, u32[]{:S(2)}, u32[]{:S(2)}) collective-permute-start(bf16[64,4096]{1,0:T(8,128)(2,1)} %refs_3_.3), channel_id=1, source_target_pairs={{0,1},{1,0},{2,3},{3,2},{4,5},{5,4},{6,7},{7,6},{8,9},{9,8},{10,11... | collective-permute-start | bytes 1572872 | tf_op jit(solution)/shard_map/ppermute | solution.py:446
  1.1 0.1 collective-permute-start
  1.2 2.1 %shard_map.149 = (s32[8,64]{1,0:T(8,128)S(1)}, bf16[3072,256]{1,0:T(8,128)(2,1)S(1)}, bf16[3072,256]{1,0:T(8,128)(2,1)S(1)}, bf16[64,4096]{1,0:T(8,128)(2,1)S(1)...) custom-call(s32[1,512]{1,0:T(1,128)} %bitcast.16, bf16[8192,256]{1,0:T(8,128)(2,1)} %refs_6_.1, ...), custom_call_target="tpu_custom_call" | custom-call | flops 1048576 | bytes 16777216 | tf_op jit(solution)/shard_map/pallas_call | solution.py:469
  3.3 0.0 collective-permute-done.1.refs_1_
  3.3 3.9 %shard_map.150 = bf16[8,32,512]{2,1,0:T(8,128)(2,1)} custom-call(bf16[64,4096]{1,0:T(8,128)(2,1)S(1)} %get-tuple-element.22.refs_0_, bf16[64,4096]{1,0:T(8,128)(2,1)S(1)} %collective-permute-done.1.refs_1_, f32[1,8192]{1,0:T(1,128)S(1)} %get-tuple-element.23.refs_2_, bf16[64,128]{1,0:T(8,128)(2,1)S(1)} %get-tuple-element.24.refs_3_, ...), custom_call_target="tpu_custom_call" | custom-call | flops 17179869184 | bytes 9437184 | tf_op jit(solution)/shard_map/pallas_call | solution.py:486
  7.2 8.3 %all-to-all-start = ((bf16[8,32,512]{2,1,0:T(8,128)(2,1)}), bf16[8,32,512]{2,1,0:T(8,128)(2,1)S(1)}, u32[]{:S(2)}, u32[]{:S(2)}) async-start(bf16[8,32,512]{2,1,0:T(8,128)(2,1)} %shard_map.150), calls=%async_computation | async-start | bytes 524288 | tf_op jit(solution)/shard_map/all_to_all | solution.py:450
  15.6 0.0 collective-permute-done.refs_1_
  15.6 6.2 %shard_map.148 = (bf16[256,512]{1,0:T(8,128)(2,1)S(1)}, f32[256,256]{1,0:T(8,128)S(1)}, bf16[8,128,128]{2,1,0:T(8,128)(2,1)S(1)}, s32[8,128]{1,0:T(8,128)S(1)}, s32[16]{0:T(128)S(1)}) custom-call(bf16[256,4096]{1,0:T(8,128)(2,1)} %refs_0_.1, bf16[256,4096]{1,0:T(8,128)(2,1)S(1)} %collective-permute-done.refs_1_, f32[1,8192]{1,0:T(1,128)} %bitcast.13, ...), custom_call_target="tpu_custom_call" | custom-call | flops 2147483648 | bytes 12582912 | tf_op jit(solution)/shard_map/pallas_call | solution.py:514
  21.8 0.2 all-to-all-done.refs_3_
  22.0 1.9 %shard_map.151 = (bf16[8,208,128]{2,1,0:T(8,128)(2,1)}, f32[72,128]{1,0:T(8,128)S(1)}) custom-call(s32[16]{0:T(128)S(1)} %get-tuple-element.19.refs_0_, s32[8,128]{1,0:T(8,128)S(1)} %get-tuple-element.20.refs_1_, bf16[256,512]{1,0:T(8,128)(2,1)S(1)} %get-tuple-element.21.refs_2_, bf16[8,32,512]{2,1,0:T(8,128)(2,1)S(1)} %all-to-all-done.refs_3_, ...), custom_call_target="tpu_custom_call" | custom-call | flops 67108864 | bytes 294912 | tf_op jit(solution)/shard_map/pallas_call | solution.py:539
  23.9 5.4 %all-to-all-start.1 = ((bf16[8,208,128]{2,1,0:T(8,128)(2,1)}), bf16[8,208,128]{2,1,0:T(8,128)(2,1)S(1)}, u32[]{:S(2)}, u32[]{:S(2)}) async-start(bf16[8,208,128]{2,1,0:T(8,128)(2,1)} %get-tuple-element.30), calls=%async_computation.1 | async-start | bytes 851968 | tf_op jit(solution)/shard_map/all_to_all | solution.py:450
  29.4 1.3 %shard_map.152.refs_1_ = f32[72,128]{1,0:T(8,128)S(1)} custom-call(bf16[64,128]{1,0:T(8,128)(2,1)} %bitcast.15, bf16[4,256]{1,0:T(4,128)(2,1)} %bitcast.18, bf16[4,256]{1,0:T(4,128)(2,1)} %bitcast.19, f32[72,128]{1,0:T(8,128)S(1)} %get-tuple-element.31.refs_3_), custom_call_target="tpu_custom_call" | custom-call | flops 1048576 | bytes 262144 | tf_op jit(solution)/shard_map/pallas_call | solution.py:559
  30.7 6.6 %all-to-all-done.1.refs_0_ = bf16[8,208,128]{2,1,0:T(8,128)(2,1)S(1)} async-done(((bf16[8,208,128]{2,1,0:T(8,128)(2,1)}), bf16[8,208,128]{2,1,0:T(8,128)(2,1)S(1)}, u32[]{:S(2)}, u32[]{:S(2)}) %all-to-all-start.1) | async-done | bytes 426016 | tf_op jit(solution)/shard_map/all_to_all | solution.py:450
  37.3 0.9 %shard_map.153 = (bf16[1,4,2048]{2,1,0:T(4,128)(2,1)}, bf16[8,32,256]{2,1,0:T(8,128)(2,1)}, bf16[8,32,256]{2,1,0:T(8,128)(2,1)}) custom-call(bf16[8,208,128]{2,1,0:T(8,128)(2,1)S(1)} %all-to-all-done.1.refs_0_, f32[72,128]{1,0:T(8,128)S(1)} %shard_map.152.refs_1_), custom_call_target="tpu_custom_call" | custom-call | bytes 524288 | tf_op jit(solution)/shard_map/pallas_call | solution.py:569
Async XLA Ops:
  0.6 2.7 %collective-permute-start.1 = (bf16[64,4096]{1,0:T(8,128)(2,1)}, bf16[64,4096]{1,0:T(8,128)(2,1)S(1)}, u32[]{:S(2)}, u32[]{:S(2)}) collective-permute-start(bf16[64,4096]{1,0:T(8,128)(2,1)} %refs_3_.3), channel_id=1, source_target_pairs={{0,1},{1,0},{2,3},{3,2},{4,5},{5,4},{6,7},{7,6},{8,9},{9,8},{10,11... | collective-permute-start | bytes 1572872 | tf_op jit(solution)/shard_map/ppermute | solution.py:446
  1.1 14.4 %collective-permute-start = (bf16[256,4096]{1,0:T(8,128)(2,1)}, bf16[256,4096]{1,0:T(8,128)(2,1)S(1)}, u32[]{:S(2)}, u32[]{:S(2)}) collective-permute-start(bf16[256,4096]{1,0:T(8,128)(2,1)} %refs_0_.1), channel_id=1, source_target_pairs={{0,1},{1,0},{2,3},{3,2},{4,5},{5,4},{6,7},{7,6},{8,9},{9,8},{10,11... | collective-permute-start | bytes 6291464 | tf_op jit(solution)/shard_map/ppermute | solution.py:446
  7.2 14.8 %all-to-all-start = ((bf16[8,32,512]{2,1,0:T(8,128)(2,1)}), bf16[8,32,512]{2,1,0:T(8,128)(2,1)S(1)}, u32[]{:S(2)}, u32[]{:S(2)}) async-start(bf16[8,32,512]{2,1,0:T(8,128)(2,1)} %shard_map.150), calls=%async_computation | async-start | bytes 524288 | tf_op jit(solution)/shard_map/all_to_all | solution.py:450
  23.9 13.3 %all-to-all-start.1 = ((bf16[8,208,128]{2,1,0:T(8,128)(2,1)}), bf16[8,208,128]{2,1,0:T(8,128)(2,1)S(1)}, u32[]{:S(2)}, u32[]{:S(2)}) async-start(bf16[8,208,128]{2,1,0:T(8,128)(2,1)} %get-tuple-element.30), calls=%async_computation.1 | async-start | bytes 851968 | tf_op jit(solution)/shard_map/all_to_all | solution.py:450

commit v24 on v19

--- a/solution.py
+++ b/solution.py
@@ -459,7 +459,7 @@
     gain = norm_gain.reshape(1, 2 * half)
     load = min(2048, half)
     step = min(1024, load // 2)
-    kept = load + load // 2
+    kept = half
     arguments = (img_route.T, w_key, w_value, vis_rows, gain, query)
     info, key_held, value_held, vis_near, gain_near, query_near = call(
         lambda *refs: prepare_kernel(n, lot, *refs),
@@ -477,7 +477,7 @@
     )(*[remote(a) for a in arguments])
 
     left = 2 * half - kept
-    sizes = [half - kept, *[load] * (half // load - 1), *[load // 2] * 2]
+    sizes = [*[load] * (half // load - 1), *[load // 2] * 2]
     packed = call(
         lambda *refs: vis_kernel(n, lot, sizes, step, *refs),
         pltpu.VMEM((n, q_lots + lot, 2 * kvw), BF16),

time: 38.1 us -> 38.3 us (level)
  no operation moved by 1% of the time
where the time goes in v24:
time: 38.3 us; the launch traced here: 37.8 us
  Pallas kernels  16.5 us (43%)
  starting transfers between devices  13.2 us (34%)
  waiting for transfers between devices  7.48 us (20%)
  between operations  0.68 us (2%)
    all_to_all x2, starting transfers between devices, exchange(): lax.all_to_all(array, 'section', split_axis=0, concat_axis=0, tiled=True,...  12.6 us
    all_to_all x2, waiting for transfers between devices, exchange(): lax.all_to_all(array, 'section', split_axis=0, concat_axis=0, tiled=True,...  7.47 us
    pallas_call x1, Pallas kernels, body(): call(lambda *refs: text_kernel(n, img, lot, load, step, page_cap, *refs),...  6.24 us
    pallas_call x1, Pallas kernels, body(): call(lambda *refs: vis_kernel(n, lot, sizes, step, *refs), pltpu.VMEM((n,...  3.72 us
    pallas_call x1, Pallas kernels, body(): call(lambda *refs: prepare_kernel(n, lot, *refs), (jax.ShapeDtypeStruct((...  2.37 us
    pallas_call x1, Pallas kernels, body(): call(lambda *refs: attend_kernel(n, cap, lot, page_cap, kv_heads, *refs),...  1.91 us
    pallas_call x1, Pallas kernels, body(): call(lambda *refs: fresh_kernel(n, kv_heads, steps, *refs), jax.ShapeDtyp...  1.3 us
    pallas_call x1, Pallas kernels, body(): call(lambda *refs: finish_kernel(kv_heads, steps, page_cap, *refs), (jax....  0.93 us
  transfers between devices with their start and end apart: 4, of which 2 were waited for; matrix products, arithmetic and copies ran while one was open for 0% of the time, Pallas kernels for 36%

profile of v24, /device:TPU:0, one launch (start us, length us, event | category | flops | bytes accessed | tf_op | source)
XLA Modules:
  0.0 37.8 jit_solution(8256443076801514538)
XLA Ops:
  0.6 0.5 %collective-permute-start.1 = (bf16[64,4096]{1,0:T(8,128)(2,1)}, bf16[64,4096]{1,0:T(8,128)(2,1)S(1)}, u32[]{:S(2)}, u32[]{:S(2)}) collective-permute-start(bf16[64,4096]{1,0:T(8,128)(2,1)} %refs_3_.3), channel_id=1, source_target_pairs={{0,1},{1,0},{2,3},{3,2},{4,5},{5,4},{6,7},{7,6},{8,9},{9,8},{10,11... | collective-permute-start | bytes 1572872 | tf_op jit(solution)/shard_map/ppermute | solution.py:441
  1.1 0.1 collective-permute-start
  1.2 2.4 %shard_map.149 = (s32[8,64]{1,0:T(8,128)S(1)}, bf16[4096,256]{1,0:T(8,128)(2,1)S(1)}, bf16[4096,256]{1,0:T(8,128)(2,1)S(1)}, bf16[64,4096]{1,0:T(8,128)(2,1)S(1)...) custom-call(s32[1,512]{1,0:T(1,128)} %bitcast.16, bf16[8192,256]{1,0:T(8,128)(2,1)} %refs_6_.1, ...), custom_call_target="tpu_custom_call" | custom-call | flops 1048576 | bytes 16777216 | tf_op jit(solution)/shard_map/pallas_call | solution.py:464
  3.6 0.0 collective-permute-done.1.refs_1_
  3.6 3.7 %shard_map.150 = bf16[8,32,512]{2,1,0:T(8,128)(2,1)} custom-call(bf16[64,4096]{1,0:T(8,128)(2,1)S(1)} %get-tuple-element.22.refs_0_, bf16[64,4096]{1,0:T(8,128)(2,1)S(1)} %collective-permute-done.1.refs_1_, f32[1,8192]{1,0:T(1,128)S(1)} %get-tuple-element.23.refs_2_, bf16[64,128]{1,0:T(8,128)(2,1)S(1)} %get-tuple-element.24.refs_3_, ...), custom_call_target="tpu_custom_call" | custom-call | flops 17179869184 | bytes 9437184 | tf_op jit(solution)/shard_map/pallas_call | solution.py:481
  7.3 7.8 %all-to-all-start = ((bf16[8,32,512]{2,1,0:T(8,128)(2,1)}), bf16[8,32,512]{2,1,0:T(8,128)(2,1)S(1)}, u32[]{:S(2)}, u32[]{:S(2)}) async-start(bf16[8,32,512]{2,1,0:T(8,128)(2,1)} %shard_map.150), calls=%async_computation | async-start | bytes 524288 | tf_op jit(solution)/shard_map/all_to_all | solution.py:445
  15.2 0.0 collective-permute-done.refs_1_
  15.2 6.2 %shard_map.148 = (bf16[256,512]{1,0:T(8,128)(2,1)S(1)}, f32[256,256]{1,0:T(8,128)S(1)}, bf16[8,128,128]{2,1,0:T(8,128)(2,1)S(1)}, s32[8,128]{1,0:T(8,128)S(1)}, s32[16]{0:T(128)S(1)}) custom-call(bf16[256,4096]{1,0:T(8,128)(2,1)} %refs_0_.1, bf16[256,4096]{1,0:T(8,128)(2,1)S(1)} %collective-permute-done.refs_1_, f32[1,8192]{1,0:T(1,128)} %bitcast.13, ...), custom_call_target="tpu_custom_call" | custom-call | flops 2147483648 | bytes 12582912 | tf_op jit(solution)/shard_map/pallas_call | solution.py:509
  21.4 1.2 %all-to-all-done.refs_3_ = bf16[8,32,512]{2,1,0:T(8,128)(2,1)S(1)} async-done(((bf16[8,32,512]{2,1,0:T(8,128)(2,1)}), bf16[8,32,512]{2,1,0:T(8,128)(2,1)S(1)}, u32[]{:S(2)}, u32[]{:S(2)}) %all-to-all-start) | async-done | bytes 262176 | tf_op jit(solution)/shard_map/all_to_all | solution.py:445
  22.6 1.9 %shard_map.151 = (bf16[8,208,128]{2,1,0:T(8,128)(2,1)}, f32[72,128]{1,0:T(8,128)S(1)}) custom-call(s32[16]{0:T(128)S(1)} %get-tuple-element.19.refs_0_, s32[8,128]{1,0:T(8,128)S(1)} %get-tuple-element.20.refs_1_, bf16[256,512]{1,0:T(8,128)(2,1)S(1)} %get-tuple-element.21.refs_2_, bf16[8,32,512]{2,1,0:T(8,128)(2,1)S(1)} %all-to-all-done.refs_3_, ...), custom_call_target="tpu_custom_call" | custom-call | flops 67108864 | bytes 294912 | tf_op jit(solution)/shard_map/pallas_call | solution.py:534
  24.5 4.8 %all-to-all-start.1 = ((bf16[8,208,128]{2,1,0:T(8,128)(2,1)}), bf16[8,208,128]{2,1,0:T(8,128)(2,1)S(1)}, u32[]{:S(2)}, u32[]{:S(2)}) async-start(bf16[8,208,128]{2,1,0:T(8,128)(2,1)} %get-tuple-element.30), calls=%async_computation.1 | async-start | bytes 851968 | tf_op jit(solution)/shard_map/all_to_all | solution.py:445
  29.3 1.3 %shard_map.152.refs_1_ = f32[72,128]{1,0:T(8,128)S(1)} custom-call(bf16[64,128]{1,0:T(8,128)(2,1)} %bitcast.15, bf16[4,256]{1,0:T(4,128)(2,1)} %bitcast.18, bf16[4,256]{1,0:T(4,128)(2,1)} %bitcast.19, f32[72,128]{1,0:T(8,128)S(1)} %get-tuple-element.31.refs_3_), custom_call_target="tpu_custom_call" | custom-call | flops 1048576 | bytes 262144 | tf_op jit(solution)/shard_map/pallas_call | solution.py:554
  30.6 6.3 %all-to-all-done.1.refs_0_ = bf16[8,208,128]{2,1,0:T(8,128)(2,1)S(1)} async-done(((bf16[8,208,128]{2,1,0:T(8,128)(2,1)}), bf16[8,208,128]{2,1,0:T(8,128)(2,1)S(1)}, u32[]{:S(2)}, u32[]{:S(2)}) %all-to-all-start.1) | async-done | bytes 426016 | tf_op jit(solution)/shard_map/all_to_all | solution.py:445
  36.9 0.9 %shard_map.153 = (bf16[1,4,2048]{2,1,0:T(4,128)(2,1)}, bf16[8,32,256]{2,1,0:T(8,128)(2,1)}, bf16[8,32,256]{2,1,0:T(8,128)(2,1)}) custom-call(bf16[8,208,128]{2,1,0:T(8,128)(2,1)S(1)} %all-to-all-done.1.refs_0_, f32[72,128]{1,0:T(8,128)S(1)} %shard_map.152.refs_1_), custom_call_target="tpu_custom_call" | custom-call | bytes 524288 | tf_op jit(solution)/shard_map/pallas_call | solution.py:564
Async XLA Ops:
  0.6 3.0 %collective-permute-start.1 = (bf16[64,4096]{1,0:T(8,128)(2,1)}, bf16[64,4096]{1,0:T(8,128)(2,1)S(1)}, u32[]{:S(2)}, u32[]{:S(2)}) collective-permute-start(bf16[64,4096]{1,0:T(8,128)(2,1)} %refs_3_.3), channel_id=1, source_target_pairs={{0,1},{1,0},{2,3},{3,2},{4,5},{5,4},{6,7},{7,6},{8,9},{9,8},{10,11... | collective-permute-start | bytes 1572872 | tf_op jit(solution)/shard_map/ppermute | solution.py:441
  1.1 14.0 %collective-permute-start = (bf16[256,4096]{1,0:T(8,128)(2,1)}, bf16[256,4096]{1,0:T(8,128)(2,1)S(1)}, u32[]{:S(2)}, u32[]{:S(2)}) collective-permute-start(bf16[256,4096]{1,0:T(8,128)(2,1)} %refs_0_.1), channel_id=1, source_target_pairs={{0,1},{1,0},{2,3},{3,2},{4,5},{5,4},{6,7},{7,6},{8,9},{9,8},{10,11... | collective-permute-start | bytes 6291464 | tf_op jit(solution)/shard_map/ppermute | solution.py:441
  7.3 15.2 %all-to-all-start = ((bf16[8,32,512]{2,1,0:T(8,128)(2,1)}), bf16[8,32,512]{2,1,0:T(8,128)(2,1)S(1)}, u32[]{:S(2)}, u32[]{:S(2)}) async-start(bf16[8,32,512]{2,1,0:T(8,128)(2,1)} %shard_map.150), calls=%async_computation | async-start | bytes 524288 | tf_op jit(solution)/shard_map/all_to_all | solution.py:445
  24.5 12.4 %all-to-all-start.1 = ((bf16[8,208,128]{2,1,0:T(8,128)(2,1)}), bf16[8,208,128]{2,1,0:T(8,128)(2,1)S(1)}, u32[]{:S(2)}, u32[]{:S(2)}) async-start(bf16[8,208,128]{2,1,0:T(8,128)(2,1)} %get-tuple-element.30), calls=%async_computation.1 | async-start | bytes 851968 | tf_op jit(solution)/shard_map/all_to_all | solution.py:445

commit v25 on v19

--- a/solution.py
+++ b/solution.py
@@ -267,7 +267,7 @@
 
 
 def attend_kernel(n, cap, lot, page_cap, kv_heads, slots, info, kv_text, arrived, bias, base, sent, own, *scratch):
-    out, mixed, held, rows_held, sems = scratch
+    out, mixed, rows_held, sems = scratch
     order = [page_section_of(k, n) for k in range(n)]
     rank = rank_of(lax.axis_index("section"), n)
     tok = kv_text.shape[0]
@@ -309,12 +309,12 @@
         numerator = lax.dot_general(
             weights.astype(BF16), value, (((0,), (0,)), ((), ())), preferred_element_type=F32
         )
-        held[g * n * rows : (g + 1) * n * rows, :] = numerator
-        own[g * rows : (g + 1) * rows, :] = held[pl.ds(pl.multiple_of((g * n + rank) * rows, rows), rows), :]
         numerator = numerator.astype(BF16)
         for k in range(n):
             to = order.index(section_of(k, n))
             out[to, pages + g * rows : pages + (g + 1) * rows, :] = numerator[k * rows : (k + 1) * rows, :]
+    mine = page_rank_of(lax.axis_index("section"), n)
+    own[: kv_heads * rows, :] = out[mine, pages : pages + kv_heads * rows, :].astype(F32)
     stat_rows = 2 * kv_heads
     share = HD // rows
     window = pl.ds(pl.multiple_of(rank // share * HD, HD), HD)
@@ -542,7 +542,6 @@
         [
             pltpu.VMEM((n, block, HD), BF16),
             pltpu.VMEM((min(tok, n * cap), 2 * kvw), BF16),
-            pltpu.VMEM((n * q_rows, HD), F32),
             pltpu.VMEM((STAT, n * q_rows // kv_heads), F32),
             pltpu.SemaphoreType.DMA((2,)),
         ],

time: 38.1 us -> 38.1 us (level)
  no operation moved by 1% of the time
where the time goes in v25:
time: 38.1 us; the launch traced here: 37.7 us
  Pallas kernels  16.4 us (43%)
  starting transfers between devices  13.2 us (35%)
  waiting for transfers between devices  7.45 us (20%)
  between operations  0.68 us (2%)
    all_to_all x2, starting transfers between devices, exchange(): lax.all_to_all(array, 'section', split_axis=0, concat_axis=0, tiled=True,...  12.6 us
    all_to_all x2, waiting for transfers between devices, exchange(): lax.all_to_all(array, 'section', split_axis=0, concat_axis=0, tiled=True,...  7.45 us
    pallas_call x1, Pallas kernels, body(): call(lambda *refs: text_kernel(n, img, lot, load, step, page_cap, *refs),...  6.24 us
    pallas_call x1, Pallas kernels, body(): call(lambda *refs: vis_kernel(n, lot, sizes, step, *refs), pltpu.VMEM((n,...  3.93 us
    pallas_call x1, Pallas kernels, body(): call(lambda *refs: prepare_kernel(n, lot, *refs), (jax.ShapeDtypeStruct((...  2.06 us
    pallas_call x1, Pallas kernels, body(): call(lambda *refs: attend_kernel(n, cap, lot, page_cap, kv_heads, *refs),...  1.91 us
    pallas_call x1, Pallas kernels, body(): call(lambda *refs: fresh_kernel(n, kv_heads, steps, *refs), jax.ShapeDtyp...  1.3 us
    pallas_call x1, Pallas kernels, body(): call(lambda *refs: finish_kernel(kv_heads, steps, page_cap, *refs), (jax....  0.93 us
  transfers between devices with their start and end apart: 4, of which 2 were waited for; matrix products, arithmetic and copies ran while one was open for 0% of the time, Pallas kernels for 36%

profile of v25, /device:TPU:0, one launch (start us, length us, event | category | flops | bytes accessed | tf_op | source)
XLA Modules:
  0.0 37.7 jit_solution(15396120428995351797)
XLA Ops:
  0.6 0.5 %collective-permute-start.1 = (bf16[64,4096]{1,0:T(8,128)(2,1)}, bf16[64,4096]{1,0:T(8,128)(2,1)S(1)}, u32[]{:S(2)}, u32[]{:S(2)}) collective-permute-start(bf16[64,4096]{1,0:T(8,128)(2,1)} %refs_3_.3), channel_id=1, source_target_pairs={{0,1},{1,0},{2,3},{3,2},{4,5},{5,4},{6,7},{7,6},{8,9},{9,8},{10,11... | collective-permute-start | bytes 1572872 | tf_op jit(solution)/shard_map/ppermute | solution.py:441
  1.1 0.1 collective-permute-start
  1.2 2.1 %shard_map.149 = (s32[8,64]{1,0:T(8,128)S(1)}, bf16[3072,256]{1,0:T(8,128)(2,1)S(1)}, bf16[3072,256]{1,0:T(8,128)(2,1)S(1)}, bf16[64,4096]{1,0:T(8,128)(2,1)S(1)...) custom-call(s32[1,512]{1,0:T(1,128)} %bitcast.16, bf16[8192,256]{1,0:T(8,128)(2,1)} %refs_6_.1, ...), custom_call_target="tpu_custom_call" | custom-call | flops 1048576 | bytes 16777216 | tf_op jit(solution)/shard_map/pallas_call | solution.py:464
  3.3 0.0 collective-permute-done.1.refs_1_
  3.3 3.9 %shard_map.150 = bf16[8,32,512]{2,1,0:T(8,128)(2,1)} custom-call(bf16[64,4096]{1,0:T(8,128)(2,1)S(1)} %get-tuple-element.22.refs_0_, bf16[64,4096]{1,0:T(8,128)(2,1)S(1)} %collective-permute-done.1.refs_1_, f32[1,8192]{1,0:T(1,128)S(1)} %get-tuple-element.23.refs_2_, bf16[64,128]{1,0:T(8,128)(2,1)S(1)} %get-tuple-element.24.refs_3_, ...), custom_call_target="tpu_custom_call" | custom-call | flops 17179869184 | bytes 9437184 | tf_op jit(solution)/shard_map/pallas_call | solution.py:481
  7.2 7.8 %all-to-all-start = ((bf16[8,32,512]{2,1,0:T(8,128)(2,1)}), bf16[8,32,512]{2,1,0:T(8,128)(2,1)S(1)}, u32[]{:S(2)}, u32[]{:S(2)}) async-start(bf16[8,32,512]{2,1,0:T(8,128)(2,1)} %shard_map.150), calls=%async_computation | async-start | bytes 524288 | tf_op jit(solution)/shard_map/all_to_all | solution.py:445
  15.1 0.0 collective-permute-done.refs_1_
  15.1 6.2 %shard_map.148 = (bf16[256,512]{1,0:T(8,128)(2,1)S(1)}, f32[256,256]{1,0:T(8,128)S(1)}, bf16[8,128,128]{2,1,0:T(8,128)(2,1)S(1)}, s32[8,128]{1,0:T(8,128)S(1)}, s32[16]{0:T(128)S(1)}) custom-call(bf16[256,4096]{1,0:T(8,128)(2,1)} %refs_0_.1, bf16[256,4096]{1,0:T(8,128)(2,1)S(1)} %collective-permute-done.refs_1_, f32[1,8192]{1,0:T(1,128)} %bitcast.13, ...), custom_call_target="tpu_custom_call" | custom-call | flops 2147483648 | bytes 12582912 | tf_op jit(solution)/shard_map/pallas_call | solution.py:509
  21.3 1.1 %all-to-all-done.refs_3_ = bf16[8,32,512]{2,1,0:T(8,128)(2,1)S(1)} async-done(((bf16[8,32,512]{2,1,0:T(8,128)(2,1)}), bf16[8,32,512]{2,1,0:T(8,128)(2,1)S(1)}, u32[]{:S(2)}, u32[]{:S(2)}) %all-to-all-start) | async-done | bytes 262176 | tf_op jit(solution)/shard_map/all_to_all | solution.py:445
  22.4 1.9 %shard_map.151 = (bf16[8,208,128]{2,1,0:T(8,128)(2,1)}, f32[72,128]{1,0:T(8,128)S(1)}) custom-call(s32[16]{0:T(128)S(1)} %get-tuple-element.19.refs_0_, s32[8,128]{1,0:T(8,128)S(1)} %get-tuple-element.20.refs_1_, bf16[256,512]{1,0:T(8,128)(2,1)S(1)} %get-tuple-element.21.refs_2_, bf16[8,32,512]{2,1,0:T(8,128)(2,1)S(1)} %all-to-all-done.refs_3_, ...), custom_call_target="tpu_custom_call" | custom-call | flops 67108864 | bytes 294912 | tf_op jit(solution)/shard_map/pallas_call | solution.py:534
  24.4 4.8 %all-to-all-start.1 = ((bf16[8,208,128]{2,1,0:T(8,128)(2,1)}), bf16[8,208,128]{2,1,0:T(8,128)(2,1)S(1)}, u32[]{:S(2)}, u32[]{:S(2)}) async-start(bf16[8,208,128]{2,1,0:T(8,128)(2,1)} %get-tuple-element.30), calls=%async_computation.1 | async-start | bytes 851968 | tf_op jit(solution)/shard_map/all_to_all | solution.py:445
  29.1 1.3 %shard_map.152.refs_1_ = f32[72,128]{1,0:T(8,128)S(1)} custom-call(bf16[64,128]{1,0:T(8,128)(2,1)} %bitcast.15, bf16[4,256]{1,0:T(4,128)(2,1)} %bitcast.18, bf16[4,256]{1,0:T(4,128)(2,1)} %bitcast.19, f32[72,128]{1,0:T(8,128)S(1)} %get-tuple-element.31.refs_3_), custom_call_target="tpu_custom_call" | custom-call | flops 1048576 | bytes 262144 | tf_op jit(solution)/shard_map/pallas_call | solution.py:553
  30.4 6.3 %all-to-all-done.1.refs_0_ = bf16[8,208,128]{2,1,0:T(8,128)(2,1)S(1)} async-done(((bf16[8,208,128]{2,1,0:T(8,128)(2,1)}), bf16[8,208,128]{2,1,0:T(8,128)(2,1)S(1)}, u32[]{:S(2)}, u32[]{:S(2)}) %all-to-all-start.1) | async-done | bytes 426016 | tf_op jit(solution)/shard_map/all_to_all | solution.py:445
  36.8 0.9 %shard_map.153 = (bf16[1,4,2048]{2,1,0:T(4,128)(2,1)}, bf16[8,32,256]{2,1,0:T(8,128)(2,1)}, bf16[8,32,256]{2,1,0:T(8,128)(2,1)}) custom-call(bf16[8,208,128]{2,1,0:T(8,128)(2,1)S(1)} %all-to-all-done.1.refs_0_, f32[72,128]{1,0:T(8,128)S(1)} %shard_map.152.refs_1_), custom_call_target="tpu_custom_call" | custom-call | bytes 524288 | tf_op jit(solution)/shard_map/pallas_call | solution.py:563
Async XLA Ops:
  0.6 2.7 %collective-permute-start.1 = (bf16[64,4096]{1,0:T(8,128)(2,1)}, bf16[64,4096]{1,0:T(8,128)(2,1)S(1)}, u32[]{:S(2)}, u32[]{:S(2)}) collective-permute-start(bf16[64,4096]{1,0:T(8,128)(2,1)} %refs_3_.3), channel_id=1, source_target_pairs={{0,1},{1,0},{2,3},{3,2},{4,5},{5,4},{6,7},{7,6},{8,9},{9,8},{10,11... | collective-permute-start | bytes 1572872 | tf_op jit(solution)/shard_map/ppermute | solution.py:441
  1.1 13.9 %collective-permute-start = (bf16[256,4096]{1,0:T(8,128)(2,1)}, bf16[256,4096]{1,0:T(8,128)(2,1)S(1)}, u32[]{:S(2)}, u32[]{:S(2)}) collective-permute-start(bf16[256,4096]{1,0:T(8,128)(2,1)} %refs_0_.1), channel_id=1, source_target_pairs={{0,1},{1,0},{2,3},{3,2},{4,5},{5,4},{6,7},{7,6},{8,9},{9,8},{10,11... | collective-permute-start | bytes 6291464 | tf_op jit(solution)/shard_map/ppermute | solution.py:441
  7.2 15.2 %all-to-all-start = ((bf16[8,32,512]{2,1,0:T(8,128)(2,1)}), bf16[8,32,512]{2,1,0:T(8,128)(2,1)S(1)}, u32[]{:S(2)}, u32[]{:S(2)}) async-start(bf16[8,32,512]{2,1,0:T(8,128)(2,1)} %shard_map.150), calls=%async_computation | async-start | bytes 524288 | tf_op jit(solution)/shard_map/all_to_all | solution.py:445
  24.4 12.4 %all-to-all-start.1 = ((bf16[8,208,128]{2,1,0:T(8,128)(2,1)}), bf16[8,208,128]{2,1,0:T(8,128)(2,1)S(1)}, u32[]{:S(2)}, u32[]{:S(2)}) async-start(bf16[8,208,128]{2,1,0:T(8,128)(2,1)} %get-tuple-element.30), calls=%async_computation.1 | async-start | bytes 851968 | tf_op jit(solution)/shard_map/all_to_all | solution.py:445

commit v26 on v19

--- a/solution.py
+++ b/solution.py
@@ -459,7 +459,7 @@
     gain = norm_gain.reshape(1, 2 * half)
     load = min(2048, half)
     step = min(1024, load // 2)
-    kept = load + load // 2
+    kept = load
     arguments = (img_route.T, w_key, w_value, vis_rows, gain, query)
     info, key_held, value_held, vis_near, gain_near, query_near = call(
         lambda *refs: prepare_kernel(n, lot, *refs),

time: 38.1 us -> 38.1 us (level)
  no operation moved by 1% of the time
where the time goes in v26:
time: 38.1 us; the launch traced here: 37.6 us
  Pallas kernels  16.3 us (43%)
  starting transfers between devices  13.2 us (35%)
  waiting for transfers between devices  7.42 us (19%)
  between operations  0.68 us (2%)
    all_to_all x2, starting transfers between devices, exchange(): lax.all_to_all(array, 'section', split_axis=0, concat_axis=0, tiled=True,...  12.6 us
    all_to_all x2, waiting for transfers between devices, exchange(): lax.all_to_all(array, 'section', split_axis=0, concat_axis=0, tiled=True,...  7.41 us
    pallas_call x1, Pallas kernels, body(): call(lambda *refs: text_kernel(n, img, lot, load, step, page_cap, *refs),...  6.24 us
    pallas_call x1, Pallas kernels, body(): call(lambda *refs: vis_kernel(n, lot, sizes, step, *refs), pltpu.VMEM((n,...  4.21 us
    pallas_call x1, Pallas kernels, body(): call(lambda *refs: attend_kernel(n, cap, lot, page_cap, kv_heads, *refs),...  1.91 us
    pallas_call x1, Pallas kernels, body(): call(lambda *refs: prepare_kernel(n, lot, *refs), (jax.ShapeDtypeStruct((...  1.74 us
    pallas_call x1, Pallas kernels, body(): call(lambda *refs: fresh_kernel(n, kv_heads, steps, *refs), jax.ShapeDtyp...  1.3 us
    pallas_call x1, Pallas kernels, body(): call(lambda *refs: finish_kernel(kv_heads, steps, page_cap, *refs), (jax....  0.93 us
  transfers between devices with their start and end apart: 4, of which 2 were waited for; matrix products, arithmetic and copies ran while one was open for 0% of the time, Pallas kernels for 36%

profile of v26, /device:TPU:0, one launch (start us, length us, event | category | flops | bytes accessed | tf_op | source)
XLA Modules:
  0.0 37.6 jit_solution(5138168547852025052)
XLA Ops:
  0.6 0.5 %collective-permute-start.1 = (bf16[64,4096]{1,0:T(8,128)(2,1)}, bf16[64,4096]{1,0:T(8,128)(2,1)S(1)}, u32[]{:S(2)}, u32[]{:S(2)}) collective-permute-start(bf16[64,4096]{1,0:T(8,128)(2,1)} %refs_3_.3), channel_id=1, source_target_pairs={{0,1},{1,0},{2,3},{3,2},{4,5},{5,4},{6,7},{7,6},{8,9},{9,8},{10,11... | collective-permute-start | bytes 1572872 | tf_op jit(solution)/shard_map/ppermute | solution.py:441
  1.1 0.1 collective-permute-start
  1.2 1.7 %shard_map.149 = (s32[8,64]{1,0:T(8,128)S(1)}, bf16[2048,256]{1,0:T(8,128)(2,1)S(1)}, bf16[2048,256]{1,0:T(8,128)(2,1)S(1)}, bf16[64,4096]{1,0:T(8,128)(2,1)S(1)...) custom-call(s32[1,512]{1,0:T(1,128)} %bitcast.16, bf16[8192,256]{1,0:T(8,128)(2,1)} %refs_6_.1, ...), custom_call_target="tpu_custom_call" | custom-call | flops 1048576 | bytes 16777216 | tf_op jit(solution)/shard_map/pallas_call | solution.py:464
  3.0 0.0 collective-permute-done.1.refs_1_
  3.0 4.2 %shard_map.150 = bf16[8,32,512]{2,1,0:T(8,128)(2,1)} custom-call(bf16[64,4096]{1,0:T(8,128)(2,1)S(1)} %get-tuple-element.22.refs_0_, bf16[64,4096]{1,0:T(8,128)(2,1)S(1)} %collective-permute-done.1.refs_1_, f32[1,8192]{1,0:T(1,128)S(1)} %get-tuple-element.23.refs_2_, bf16[64,128]{1,0:T(8,128)(2,1)S(1)} %get-tuple-element.24.refs_3_, ...), custom_call_target="tpu_custom_call" | custom-call | flops 17179869184 | bytes 9437184 | tf_op jit(solution)/shard_map/pallas_call | solution.py:481
  7.2 7.8 %all-to-all-start = ((bf16[8,32,512]{2,1,0:T(8,128)(2,1)}), bf16[8,32,512]{2,1,0:T(8,128)(2,1)S(1)}, u32[]{:S(2)}, u32[]{:S(2)}) async-start(bf16[8,32,512]{2,1,0:T(8,128)(2,1)} %shard_map.150), calls=%async_computation | async-start | bytes 524288 | tf_op jit(solution)/shard_map/all_to_all | solution.py:445
  15.0 0.0 collective-permute-done.refs_1_
  15.0 6.2 %shard_map.148 = (bf16[256,512]{1,0:T(8,128)(2,1)S(1)}, f32[256,256]{1,0:T(8,128)S(1)}, bf16[8,128,128]{2,1,0:T(8,128)(2,1)S(1)}, s32[8,128]{1,0:T(8,128)S(1)}, s32[16]{0:T(128)S(1)}) custom-call(bf16[256,4096]{1,0:T(8,128)(2,1)} %refs_0_.1, bf16[256,4096]{1,0:T(8,128)(2,1)S(1)} %collective-permute-done.refs_1_, f32[1,8192]{1,0:T(1,128)} %bitcast.13, ...), custom_call_target="tpu_custom_call" | custom-call | flops 2147483648 | bytes 12582912 | tf_op jit(solution)/shard_map/pallas_call | solution.py:509
  21.3 1.1 %all-to-all-done.refs_3_ = bf16[8,32,512]{2,1,0:T(8,128)(2,1)S(1)} async-done(((bf16[8,32,512]{2,1,0:T(8,128)(2,1)}), bf16[8,32,512]{2,1,0:T(8,128)(2,1)S(1)}, u32[]{:S(2)}, u32[]{:S(2)}) %all-to-all-start) | async-done | bytes 262176 | tf_op jit(solution)/shard_map/all_to_all | solution.py:445
  22.4 1.9 %shard_map.151 = (bf16[8,208,128]{2,1,0:T(8,128)(2,1)}, f32[72,128]{1,0:T(8,128)S(1)}) custom-call(s32[16]{0:T(128)S(1)} %get-tuple-element.19.refs_0_, s32[8,128]{1,0:T(8,128)S(1)} %get-tuple-element.20.refs_1_, bf16[256,512]{1,0:T(8,128)(2,1)S(1)} %get-tuple-element.21.refs_2_, bf16[8,32,512]{2,1,0:T(8,128)(2,1)S(1)} %all-to-all-done.refs_3_, ...), custom_call_target="tpu_custom_call" | custom-call | flops 67108864 | bytes 294912 | tf_op jit(solution)/shard_map/pallas_call | solution.py:534
  24.3 4.8 %all-to-all-start.1 = ((bf16[8,208,128]{2,1,0:T(8,128)(2,1)}), bf16[8,208,128]{2,1,0:T(8,128)(2,1)S(1)}, u32[]{:S(2)}, u32[]{:S(2)}) async-start(bf16[8,208,128]{2,1,0:T(8,128)(2,1)} %get-tuple-element.30), calls=%async_computation.1 | async-start | bytes 851968 | tf_op jit(solution)/shard_map/all_to_all | solution.py:445
  29.0 1.3 %shard_map.152.refs_1_ = f32[72,128]{1,0:T(8,128)S(1)} custom-call(bf16[64,128]{1,0:T(8,128)(2,1)} %bitcast.15, bf16[4,256]{1,0:T(4,128)(2,1)} %bitcast.18, bf16[4,256]{1,0:T(4,128)(2,1)} %bitcast.19, f32[72,128]{1,0:T(8,128)S(1)} %get-tuple-element.31.refs_3_), custom_call_target="tpu_custom_call" | custom-call | flops 1048576 | bytes 262144 | tf_op jit(solution)/shard_map/pallas_call | solution.py:554
  30.4 6.3 %all-to-all-done.1.refs_0_ = bf16[8,208,128]{2,1,0:T(8,128)(2,1)S(1)} async-done(((bf16[8,208,128]{2,1,0:T(8,128)(2,1)}), bf16[8,208,128]{2,1,0:T(8,128)(2,1)S(1)}, u32[]{:S(2)}, u32[]{:S(2)}) %all-to-all-start.1) | async-done | bytes 426016 | tf_op jit(solution)/shard_map/all_to_all | solution.py:445
  36.7 0.9 %shard_map.153 = (bf16[1,4,2048]{2,1,0:T(4,128)(2,1)}, bf16[8,32,256]{2,1,0:T(8,128)(2,1)}, bf16[8,32,256]{2,1,0:T(8,128)(2,1)}) custom-call(bf16[8,208,128]{2,1,0:T(8,128)(2,1)S(1)} %all-to-all-done.1.refs_0_, f32[72,128]{1,0:T(8,128)S(1)} %shard_map.152.refs_1_), custom_call_target="tpu_custom_call" | custom-call | bytes 524288 | tf_op jit(solution)/shard_map/pallas_call | solution.py:564
Async XLA Ops:
  0.6 2.4 %collective-permute-start.1 = (bf16[64,4096]{1,0:T(8,128)(2,1)}, bf16[64,4096]{1,0:T(8,128)(2,1)S(1)}, u32[]{:S(2)}, u32[]{:S(2)}) collective-permute-start(bf16[64,4096]{1,0:T(8,128)(2,1)} %refs_3_.3), channel_id=1, source_target_pairs={{0,1},{1,0},{2,3},{3,2},{4,5},{5,4},{6,7},{7,6},{8,9},{9,8},{10,11... | collective-permute-start | bytes 1572872 | tf_op jit(solution)/shard_map/ppermute | solution.py:441
  1.1 13.9 %collective-permute-start = (bf16[256,4096]{1,0:T(8,128)(2,1)}, bf16[256,4096]{1,0:T(8,128)(2,1)S(1)}, u32[]{:S(2)}, u32[]{:S(2)}) collective-permute-start(bf16[256,4096]{1,0:T(8,128)(2,1)} %refs_0_.1), channel_id=1, source_target_pairs={{0,1},{1,0},{2,3},{3,2},{4,5},{5,4},{6,7},{7,6},{8,9},{9,8},{10,11... | collective-permute-start | bytes 6291464 | tf_op jit(solution)/shard_map/ppermute | solution.py:441
  7.2 15.2 %all-to-all-start = ((bf16[8,32,512]{2,1,0:T(8,128)(2,1)}), bf16[8,32,512]{2,1,0:T(8,128)(2,1)S(1)}, u32[]{:S(2)}, u32[]{:S(2)}) async-start(bf16[8,32,512]{2,1,0:T(8,128)(2,1)} %shard_map.150), calls=%async_computation | async-start | bytes 524288 | tf_op jit(solution)/shard_map/all_to_all | solution.py:445
  24.3 12.4 %all-to-all-start.1 = ((bf16[8,208,128]{2,1,0:T(8,128)(2,1)}), bf16[8,208,128]{2,1,0:T(8,128)(2,1)S(1)}, u32[]{:S(2)}, u32[]{:S(2)}) async-start(bf16[8,208,128]{2,1,0:T(8,128)(2,1)} %get-tuple-element.30), calls=%async_computation.1 | async-start | bytes 851968 | tf_op jit(solution)/shard_map/all_to_all | solution.py:445
